TPU v7x, 256 devices: a whole 4x4x8 slice. The times are simulated.
256 devices in a mesh: ctx: 32 (over x, y, core), tp: 8 (over z).
Axes of the slice: x: 4, y: 4, z: 8, core: 2. Of those that a mesh axis runs over, the one named last changes fastest.
Arguments:
- query: bfloat16 [8192, 4096], P('ctx', 'tp'), may hold values from -6 to 6
- key_branch: bfloat16 [8192, 4096], P('ctx', 'tp'), may hold values from -6 to 6
- value_branch: bfloat16 [8192, 4096], P('ctx', 'tp'), may hold values from -6 to 6
- decay: float32 [16, 4096], P(None, 'tp'), may hold values from 1.2207031e-06 to 0.05
- frequency: float32 [16, 4096], P(None, 'tp'), may hold values from -3.140625 to 3.140625
- residue: float32 [2, 16, 4096], P(None, None, 'tp'), may hold values from -1.5 to 1.5
- skip_gain: float32 [4096], P('tp'), may hold values from -6 to 6
- out_weight: bfloat16 [4096, 4096], P('ctx', 'tp'), may hold values from -0.09375 to 0.09375
- doc_starts: int32 [8192], P('ctx'), may hold values from 0 to 1, as said below
Outputs:
- mixed: bfloat16 [8192, 4096], P('ctx', 'tp')
Inputs may be any that keep to these rules, and one draw needn't show every extreme that they name: `doc_starts`: token 0 starts a document; documents between starts are 256 to 4096 tokens long, the last one possibly shorter.
All inputs are finite; a program needn't handle non-finite values.
Results may differ from a plain program's by a relative error of at most 0.0049.
Values may be sent and summed in bfloat16 or wider, within the bound.
No kernel may reach another device: no remote copies, remote signals or barrier semaphores. Data moves between devices by JAX's collectives and lax.ppermute only.
A program may use at most 128 MiB of HBM per device.

v0:
```python
import jax
import jax.numpy as jnp
from jax import lax
from jax.sharding import PartitionSpec as P

BLOCK = 64


def carried_in(value, axis, join, neutral):
    count, mine = (lax.axis_size(axis), lax.axis_index(axis))
    pieces = jax.tree.map(lambda part: lax.all_gather(part, axis), value)
    subtotal = jax.tree.map(
        lambda part, zero: jnp.full_like(part, 0) + jnp.asarray(zero, part.dtype), value, neutral
    )

    def lap(position, subtotal):
        longer = join(subtotal, jax.tree.map(lambda part: part[position], pieces))
        return jax.tree.map(lambda new, old: jnp.where(position < mine, new, old), longer, subtotal)

    return lax.fori_loop(0, count - 1, lap, subtotal)


def build_tables(decay, frequency, residue, blen):
    steps = jnp.arange(blen + 1, dtype=jnp.float32)[:, None, None]
    magnitude = jnp.exp(-decay[None] * steps)
    pole_re = magnitude * jnp.cos(frequency[None] * steps)
    pole_im = magnitude * jnp.sin(frequency[None] * steps)
    scaling = jnp.sqrt(-jnp.expm1(-2.0 * decay))
    weight_re = residue[0] * scaling
    weight_im = residue[1] * scaling
    taps = jnp.sum(weight_re * pole_re[:blen] - weight_im * pole_im[:blen], axis=1)
    lagged = jnp.arange(blen)[:, None] - jnp.arange(blen)[None, :]
    toeplitz = jnp.where((lagged >= 0)[:, :, None], taps[jnp.clip(lagged, 0, blen - 1)], 0.0)
    out_re = weight_re * pole_re[1:] - weight_im * pole_im[1:]
    out_im = weight_re * pole_im[1:] + weight_im * pole_re[1:]
    into_re = pole_re[:blen][::-1]
    into_im = pole_im[:blen][::-1]
    return (toeplitz, out_re, out_im, into_re, into_im, pole_re[blen], pole_im[blen])


def block_step(tables, carry, signal_blk, starts_blk, want_out):
    toeplitz, out_re, out_im, into_re, into_im, jump_re, jump_im = tables
    hp = lax.Precision.HIGHEST
    state_re, state_im = carry
    running = jnp.cumsum(starts_blk)
    keep = (running == 0).astype(jnp.float32)
    result = None
    if want_out:
        result = keep[:, None] * (
            jnp.einsum("tmc,mc->tc", out_re, state_re, precision=hp)
            - jnp.einsum("tmc,mc->tc", out_im, state_im, precision=hp)
        )
        same = (running[:, None] == running[None, :]).astype(jnp.float32)
        result = result + jnp.einsum(
            "tsc,sc->tc", toeplitz * same[:, :, None], signal_blk, precision=hp
        )
    through = keep[-1]
    new_re = through * (jump_re * state_re - jump_im * state_im)
    new_im = through * (jump_re * state_im + jump_im * state_re)
    tail = (running == running[-1]).astype(jnp.float32)
    weighted = signal_blk * tail[:, None]
    new_re = new_re + jnp.einsum("smc,sc->mc", into_re, weighted, precision=hp)
    new_im = new_im + jnp.einsum("smc,sc->mc", into_im, weighted, precision=hp)
    return ((new_re, new_im), result)


def run_blocks(tables, carry, signal, starts, want_out):
    blocks = signal.shape[0] // BLOCK
    sig_blocks = signal.reshape(blocks, BLOCK, signal.shape[1])
    start_blocks = starts.reshape(blocks, BLOCK)

    def stepper(state, pieces):
        return block_step(tables, state, pieces[0], pieces[1], want_out)

    final, outs = lax.scan(stepper, carry, (sig_blocks, start_blocks))
    if want_out:
        outs = outs.reshape(signal.shape)
    return (final, outs)


def combine_states(earlier, later):
    e_re, e_im, e_are, e_aim = earlier
    l_re, l_im, l_are, l_aim = later
    return (
        l_are * e_re - l_aim * e_im + l_re,
        l_are * e_im + l_aim * e_re + l_im,
        l_are * e_are - l_aim * e_aim,
        l_are * e_aim + l_aim * e_are,
    )


def incoming_state(end_state, doc_starts, decay, frequency):
    tokens = doc_starts.shape[0]
    through = (jnp.sum(doc_starts) == 0).astype(jnp.float32)
    magnitude = jnp.exp(-decay * float(tokens))
    factor_re = through * magnitude * jnp.cos(frequency * float(tokens))
    factor_im = through * magnitude * jnp.sin(frequency * float(tokens))
    zeros = jnp.zeros_like(decay)
    ones = jnp.ones_like(decay)
    element = (end_state[0], end_state[1], factor_re, factor_im)
    prefix = carried_in(element, "ctx", combine_states, (zeros, zeros, ones, zeros))
    return (prefix[0], prefix[1])


def shards(
    query, key_branch, value_branch, decay, frequency, residue, skip_gain, out_weight, doc_starts
):
    signal = key_branch.astype(jnp.float32) * value_branch.astype(jnp.float32)
    tables = build_tables(decay, frequency, residue, BLOCK)
    zeros = jnp.zeros(decay.shape, jnp.float32)
    end_state, unused = run_blocks(tables, (zeros, zeros), signal, doc_starts, False)
    carried = incoming_state(end_state, doc_starts, decay, frequency)
    final, conv = run_blocks(tables, carried, signal, doc_starts, True)
    conv = conv + skip_gain[None, :] * signal
    hidden = (query.astype(jnp.float32) * conv).astype(jnp.bfloat16)
    all_hidden = lax.all_gather(hidden, "tp", axis=1, tiled=True)
    mixed = jnp.dot(
        all_hidden,
        lax.all_gather(out_weight, "ctx", axis=0, tiled=True),
        preferred_element_type=jnp.float32,
    )
    return mixed.astype(jnp.bfloat16)


def solution(mesh):
    in_specs = (
        P("ctx", "tp"),
        P("ctx", "tp"),
        P("ctx", "tp"),
        P(None, "tp"),
        P(None, "tp"),
        P(None, None, "tp"),
        P("tp"),
        P("ctx", "tp"),
        P("ctx"),
    )
    out_specs = P("ctx", "tp")
    return jax.shard_map(shards, mesh=mesh, in_specs=in_specs, out_specs=out_specs, check_vma=False)
```

profile of v0, /device:TPU:1, one launch (start us, length us, event | category | flops | bytes accessed | tf_op | source)
XLA Modules:
  0.0 425.0 jit_solution(9783097207292885011)
XLA Ops:
  10.9 8.4 %sine_multiply_fusion = (f32[65,16,512]{2,1,0:T(8,128)S(1)}, f32[65,16,512]{2,1,0:T(8,128)S(1)}) fusion(f32[16,512]{1,0:T(8,128)} %param.19, f32[16,512]{1,0:T(8,128)S(1)} %get-tuple-element.409), kind=kLoop, calls=%fused_computation.36 | loop fusion | flops 2129920 | bytes 4325376 | tf_op jit(solution)/shard_map/mul | solution.py:27
  19.3 4.0 subtract_reduce_fusion
  25.2 3.3 rev.7
  28.6 17.1 %while.44 = (s32[]{:T(128)}, f32[16,512]{1,0:T(8,128)S(1)}, f32[16,512]{1,0:T(8,128)S(1)}, s32[4,64]{1,0:T(4,128)S(1)}, f32[16,512]{1,0:T(8,128)S(1)}, /*index=5...) while((s32[]{:T(128)}, f32[16,512]{1,0:T(8,128)S(1)}, ...), condition=%wide.region_2.3_spmd.clone, body=%wide.region_0.2_spmd.clone.sunk | while | flops 2216005 | bytes 4917665 | solution.py:75
  34.4 2.1 multiply_reduce_fusion.14
  48.7 16.8 %gather_fusion = f32[4096,512]{1,0:T(8,128)} fusion(f32[64,512]{1,0:T(8,128)S(1)} %get-tuple-element.396, s32[4096]{0:T(1024)S(1)} %broadcast_clamp_fusion), kind=kCustom, calls=%fused_computation | custom fusion | bytes 16793600 | tf_op jit(solution)/shard_map/gather | solution.py:33
  65.5 5.9 %broadcast_select_fusion = f32[64,64,512]{2,1,0:T(8,128)} fusion(f32[64,64,512]{2,1,0:T(8,128)} %bitcast.152, pred[64,64]{1,0:T(8,128)(4,1)S(1)} %subtract_compare_fusion), kind=kLoop, calls=%fused_computation.35 | loop fusion | flops 2097152 | bytes 16781312 | tf_op jit(solution)/shard_map/jit(_where)/select_n | solution.py:33
  71.4 27.1 %all-gather.19.cloned.1.call-done = f32[512,512]{1,0:T(8,128)} async-done(((f32[16,512]{1,0:T(8,128)}), f32[512,512]{1,0:T(8,128)}) %all-gather.19.cloned.1.call-update) | async-done | bytes 1048592 | tf_op jit(solution)/shard_map/all_gather | solution.py:11
  98.5 49.8 %all-gather.21.cloned.1.call-done = f32[512,512]{1,0:T(8,128)} async-done(((f32[16,512]{1,0:T(8,128)}), f32[512,512]{1,0:T(8,128)}) %all-gather.21.cloned.1.call-update) | async-done | bytes 1048592 | tf_op jit(solution)/shard_map/all_gather | solution.py:11
  148.2 49.8 %all-gather.15.cloned.1.call-done = f32[512,512]{1,0:T(8,128)} async-done(((f32[16,512]{1,0:T(8,128)}), f32[512,512]{1,0:T(8,128)}) %all-gather.15.cloned.1.call-update) | async-done | bytes 1048592 | tf_op jit(solution)/shard_map/all_gather | solution.py:11
  198.0 49.6 %all-gather.17.cloned.1.call-done = f32[512,512]{1,0:T(8,128)} async-done(((f32[16,512]{1,0:T(8,128)}), f32[512,512]{1,0:T(8,128)}) %all-gather.17.cloned.1.call-update) | async-done | bytes 1048592 | tf_op jit(solution)/shard_map/all_gather | solution.py:11
  247.6 26.6 %while.45 = (s32[]{:T(128)}, f32[16,512]{1,0:T(8,128)S(1)}, f32[16,512]{1,0:T(8,128)S(1)}, s32[]{:T(128)}, f32[32,16,512]{2,1,0:T(8,128)}, /*index=5*/f32[32,16,...) while((s32[]{:T(128)}, f32[16,512]{1,0:T(8,128)S(1)}, ...), condition=%wide.region_5.6_spmd.clone, body=%wide.region_4.5_spmd.clone.sunk | while | flops 98308 | bytes 262269 | solution.py:20
  274.3 44.4 %while.43 = (s32[]{:T(128)}, f32[16,512]{1,0:T(8,128)S(1)}, f32[16,512]{1,0:T(8,128)S(1)}, f32[4,64,512]{2,1,0:T(8,128)}, s32[4,64]{1,0:T(4,128)S(1)}, /*index=5...) while((s32[]{:T(128)}, f32[16,512]{1,0:T(8,128)S(1)}, ...), condition=%wide.region_9.10_spmd, body=%wide.region_7.9_spmd.sunk | while | flops 10596546 | bytes 52465876 | solution.py:75
  275.9 2.3 multiply_reduce_fusion.11
  278.7 3.4 multiply_reduce_fusion.13
  287.0 2.3 multiply_reduce_fusion.11
  289.8 3.4 multiply_reduce_fusion.13
  298.0 2.3 multiply_reduce_fusion.11
  300.9 3.4 multiply_reduce_fusion.13
  309.1 2.3 multiply_reduce_fusion.11
  312.0 3.4 multiply_reduce_fusion.13
  321.2 35.9 %all-gather.11.cloned.1.call-done = bf16[256,4096]{1,0:T(8,128)(2,1)} async-done(((bf16[256,512]{1,0:T(8,128)(2,1)}), bf16[256,4096]{1,0:T(8,128)(2,1)}) %all-gather.11.cloned.1.call-update) | async-done | bytes 2097168 | tf_op jit(solution)/shard_map/all_gather | solution.py:116
  357.2 56.2 %all-gather.13.cloned.1.call-done = bf16[4096,512]{1,0:T(8,128)(2,1)} async-done(((bf16[128,512]{1,0:T(8,128)(2,1)}), bf16[4096,512]{1,0:T(8,128)(2,1)}) %all-gather.13.cloned.1.call-update) | async-done | bytes 4194320 | tf_op jit(solution)/shard_map/all_gather | solution.py:119
  413.4 4.8 %convolution_convert_fusion = bf16[256,512]{1,0:T(8,128)(2,1)} fusion(bf16[256,4096]{1,0:T(8,128)(2,1)} %all-gather.11.cloned.1.call-done, bf16[4096,512]{1,0:T(8,128)(2,1)} %all-gather.13.cloned.1.call-done), kind=kOutput, calls=%fused_computation.43 | convolution fusion | flops 1073872896 | bytes 6553600 | tf_op jit(solution)/shard_map/dot_general | solution.py:117
  (160 shorter events, 70.9 us)
Async XLA Ops:
  6.5 91.9 %all-gather.19.cloned.1.call-start = ((), (), s32[]{:S(2)}) async-start(), calls=%async_computation.4 | async-start | bytes 1081344 | tf_op jit(solution)/shard_map/all_gather | solution.py:11
  25.2 3.3 copy-start.3
  25.2 3.3 copy-start.4
  45.7 0.6 copy-start.1
  45.7 0.7 copy-start.2
  46.3 101.9 %all-gather.21.cloned.1.call-start = ((), (), s32[]{:S(2)}) async-start(), calls=%async_computation.5 | async-start | bytes 1081344 | tf_op jit(solution)/shard_map/all_gather | solution.py:11
  47.1 151.0 %all-gather.15.cloned.1.call-start = ((), (), s32[]{:S(2)}) async-start(), calls=%async_computation.2 | async-start | bytes 1081344 | tf_op jit(solution)/shard_map/all_gather | solution.py:11
  47.8 199.8 %all-gather.17.cloned.1.call-start = ((), (), s32[]{:S(2)}) async-start(), calls=%async_computation.3 | async-start | bytes 1081344 | tf_op jit(solution)/shard_map/all_gather | solution.py:11
  48.4 308.8 %all-gather.11.cloned.1.call-start = ((), (), s32[]{:S(2)}) async-start(), calls=%async_computation | async-start | bytes 2359296 | tf_op jit(solution)/shard_map/all_gather | solution.py:116
  274.2 44.4 %copy-start.5 = (f32[512]{0:T(512)S(1)}, f32[512]{0:T(512)}, u32[]{:S(2)}) copy-start(f32[512]{0:T(512)} %param.21) | copy-start | bytes 6148
  275.9 7.0 %copy-start = (f32[64,64,512]{2,1,0:T(8,128)S(1)}, f32[64,64,512]{2,1,0:T(8,128)}, u32[]{:S(2)}) copy-start(f32[64,64,512]{2,1,0:T(8,128)} %get-tuple-element.728) | copy-start | bytes 25165828 | tf_op jit(solution)/shard_map/while
  286.9 7.0 %copy-start = (f32[64,64,512]{2,1,0:T(8,128)S(1)}, f32[64,64,512]{2,1,0:T(8,128)}, u32[]{:S(2)}) copy-start(f32[64,64,512]{2,1,0:T(8,128)} %get-tuple-element.728) | copy-start | bytes 25165828 | tf_op jit(solution)/shard_map/while
  298.0 7.0 %copy-start = (f32[64,64,512]{2,1,0:T(8,128)S(1)}, f32[64,64,512]{2,1,0:T(8,128)}, u32[]{:S(2)}) copy-start(f32[64,64,512]{2,1,0:T(8,128)} %get-tuple-element.728) | copy-start | bytes 25165828 | tf_op jit(solution)/shard_map/while
  309.1 7.0 %copy-start = (f32[64,64,512]{2,1,0:T(8,128)S(1)}, f32[64,64,512]{2,1,0:T(8,128)}, u32[]{:S(2)}) copy-start(f32[64,64,512]{2,1,0:T(8,128)} %get-tuple-element.728) | copy-start | bytes 25165828 | tf_op jit(solution)/shard_map/while
  320.6 92.7 %all-gather.13.cloned.1.call-start = ((), (), s32[]{:S(2)}) async-start(), calls=%async_computation.1 | async-start | bytes 4325376 | tf_op jit(solution)/shard_map/all_gather | solution.py:119
Sparse Core Ops, SparseCore 0:
  46.4 52.0 all-gather.18
  101.0 47.1 all-gather.20
  150.8 47.1 all-gather.14
  200.4 47.1 all-gather.16
  320.8 36.3 all-gather.10
  359.6 53.7 all-gather.12
where the time goes:
time: 428 us; the launch traced here: 425 us
  waiting for transfers between devices  271 us (63%)
  other arithmetic  100 us (23%)
  local copies, waits for them, and re-layouts  30.8 us (7%)
  between operations  14.3 us (3%)
  matrix products  4.77 us (1%)
    all_gather x4, waiting for transfers between devices, carried_in(): pieces = jax.tree.map(lambda part: lax.all_gather(part, axis), value)  176 us
    all_gather x1, waiting for transfers between devices, shards(): lax.all_gather(out_weight, 'ctx', axis=0, tiled=True)  56.2 us
    all_gather x1, waiting for transfers between devices, shards(): all_hidden = lax.all_gather(hidden, 'tp', axis=1, tiled=True)  35.9 us
    select_n x31, other arithmetic, lap(): jnp.where(position < mine, new, old)  25.9 us
    dot_general x8, other arithmetic, block_step(): new_im = new_im + jnp.einsum('smc,sc->mc', into_im, weighted, precision=hp)  17.7 us
    gather x1, local copies, waits for them, and re-layouts, build_tables(): taps[jnp.clip(lagged, 0, blen - 1)]  16.8 us
    dot_general x4, other arithmetic, block_step(): jnp.einsum('tmc,mc->tc', out_im, state_im, precision=hp)  13.5 us
  transfers between devices with their start and end apart: 6, of which 6 were waited for; matrix products, arithmetic and copies ran while one was open for 5% of the time, Pallas kernels for 0%

commit v1 on v0

v1 whole, which is shorter than its diff:
```python
import jax
import jax.numpy as jnp
from jax import lax
from jax.experimental import pallas as pl
from jax.experimental.pallas import tpu as pltpu
from jax.sharding import PartitionSpec as P

F32 = jnp.float32
BF16 = jnp.bfloat16
NX, NY, NC, NZ = 4, 4, 2, 8
TOK, CH, MODES = 256, 512, 16
LANES = 128
GROUPS = CH // LANES
STEPS = 32
BLOCKS = TOK // STEPS
ROWS = 2 * MODES
PAY = ROWS + 8
VMEM = pl.BlockSpec(memory_space=pltpu.VMEM)
PARAMS = pltpu.CompilerParams(vmem_limit_bytes=48 * 1024 * 1024)


def call(kernel, outs, args, scratch=(), flops=0, nbytes=0):
    return pl.pallas_call(
        kernel,
        out_shape=outs,
        in_specs=[VMEM] * len(args),
        out_specs=jax.tree.map(lambda unused: VMEM, outs),
        scratch_shapes=list(scratch),
        compiler_params=PARAMS,
        cost_estimate=pl.CostEstimate(flops=flops, bytes_accessed=nbytes, transcendentals=0),
    )(*args)


def struct(*shape, dtype=F32):
    return jax.ShapeDtypeStruct(shape, dtype)


def cmul(a, b):
    return a[0] * b[0] - a[1] * b[1], a[0] * b[1] + a[1] * b[0]


def cadd(a, b):
    return a[0] + b[0], a[1] + b[1]


def square(a):
    return a[0] * a[0] - a[1] * a[1], 2.0 * a[0] * a[1]


def halves(ref):
    return ref[:MODES, :], ref[MODES:ROWS, :]


def first_start(starts_ref):
    starts = starts_ref[...]
    at = lax.broadcasted_iota(jnp.int32, starts.shape, 0) * LANES
    at = at + lax.broadcasted_iota(jnp.int32, starts.shape, 1)
    where = jnp.where(starts > 0, at, TOK)
    return jnp.min(jnp.min(where, axis=1, keepdims=True), axis=0, keepdims=True)


def poles(decay_ref, freq_ref):
    magnitude = jnp.exp(-decay_ref[...])
    freq = freq_ref[...]
    return magnitude * jnp.cos(freq), magnitude * jnp.sin(freq)


def fill_powers(pole, table_re, table_im, count):
    def put(k, value):
        for g in range(GROUPS):
            rows = pl.ds(pl.multiple_of(k * MODES, MODES), MODES)
            lanes = slice(g * LANES, (g + 1) * LANES)
            table_re[g, rows, :] = value[0][:, lanes]
            table_im[g, rows, :] = value[1][:, lanes]

    def step(k, value):
        put(k, value)
        return cmul(value, pole)

    one = (jnp.ones((MODES, CH), F32), jnp.zeros((MODES, CH), F32))
    last = lax.fori_loop(0, count, step, one)
    return last


def fill_signal(key_ref, value_ref, sig):
    for g in range(GROUPS):
        lanes = slice(g * LANES, (g + 1) * LANES)
        sig[g] = key_ref[:, lanes].astype(F32) * value_ref[:, lanes].astype(F32)


def block_iota():
    return lax.broadcasted_iota(jnp.int32, (BLOCKS, LANES), 0)


def ends_kernel(key_ref, value_ref, decay_ref, freq_ref, starts_ref, pay_ref, eb_ref, p256_ref,
                sig, tre, tim, qre, qim):
    s0 = first_start(starts_ref)
    b0 = s0 // STEPS
    fill_signal(key_ref, value_ref, sig)
    pole = poles(decay_ref, freq_ref)
    q = fill_powers(pole, tre, tim, STEPS)
    one = (jnp.ones((MODES, CH), F32), jnp.zeros((MODES, CH), F32))
    value = one
    for n in range(BLOCKS):
        row = (BLOCKS - 1 - n) * MODES
        for g in range(GROUPS):
            lanes = slice(g * LANES, (g + 1) * LANES)
            qre[g, row:row + MODES, :] = value[0][:, lanes]
            qim[g, row:row + MODES, :] = value[1][:, lanes]
        value = cmul(value, q)
    p256_ref[:MODES, :] = value[0]
    p256_ref[MODES:, :] = value[1]
    blocks = block_iota()
    reach = (s0 >= TOK) | (blocks >= b0)

    def group(g, unused):
        def step(j, acc):
            x = sig[g, pl.ds(j, BLOCKS, stride=STEPS), :]
            x = jnp.where((blocks * STEPS + j >= s0) | (blocks != b0), x, 0.0)
            base = (STEPS - 1 - j) * MODES
            out = []
            for m in range(MODES):
                out.append(acc[2 * m] + tre[g, pl.ds(base + m, 1), :] * x)
                out.append(acc[2 * m + 1] + tim[g, pl.ds(base + m, 1), :] * x)
            return tuple(out)

        zero = jnp.zeros((BLOCKS, LANES), F32)
        acc = lax.fori_loop(0, STEPS, step, (zero,) * ROWS, unroll=4)
        for m in range(MODES):
            re, im = acc[2 * m], acc[2 * m + 1]
            eb_ref[g, m] = re
            eb_ref[g, MODES + m] = im
            w = (qre[g, pl.ds(m, BLOCKS, stride=MODES), :], qim[g, pl.ds(m, BLOCKS, stride=MODES), :])
            end = cmul(w, (re, im))
            pay3 = pl.ds(pl.multiple_of(g * LANES, LANES), LANES)
            pay_ref[pl.ds(m, 1), pay3] = jnp.sum(jnp.where(reach, end[0], 0.0), axis=0, keepdims=True)
            pay_ref[pl.ds(MODES + m, 1), pay3] = jnp.sum(jnp.where(reach, end[1], 0.0), axis=0, keepdims=True)
        return unused

    lax.fori_loop(0, GROUPS, group, 0)
    pay_ref[ROWS:, :] = jnp.broadcast_to((s0 >= TOK).astype(F32), (PAY - ROWS, CH))


def local_kernel(key_ref, value_ref, decay_ref, freq_ref, res_ref, skip_ref, starts_ref, eb_ref,
                 y_ref, pz_ref, gz_ref, tre, tim, sig, qre, qim, taps, rows_):
    s0 = first_start(starts_ref)
    b0 = s0 // STEPS
    blocks = block_iota()
    fill_signal(key_ref, value_ref, sig)
    pole = poles(decay_ref, freq_ref)
    q = fill_powers(pole, tre, tim, STEPS + 1)
    q = (jnp.concatenate([tre[g, STEPS * MODES:, :] for g in range(GROUPS)], axis=1),
         jnp.concatenate([tim[g, STEPS * MODES:, :] for g in range(GROUPS)], axis=1))
    y = 2.0 * decay_ref[...]
    series = jnp.ones_like(y)
    for n in range(10, 1, -1):
        series = 1.0 - y * (1.0 / n) * series
    scale = jnp.sqrt(y * series)
    weight = (res_ref[0] * scale, res_ref[1] * scale)
    for g in range(GROUPS):
        lanes = slice(g * LANES, (g + 1) * LANES)
        w_re, w_im = weight[0][:, lanes], weight[1][:, lanes]
        for k in range(STEPS):
            term = w_re * tre[g, k * MODES:(k + 1) * MODES, :] - w_im * tim[g, k * MODES:(k + 1) * MODES, :]
            row = jnp.sum(term, axis=0, keepdims=True)
            if k == 0:
                row = row + skip_ref[:, lanes]
            taps[g, k:k + 1, :] = row
    value = weight
    for n in range(BLOCKS):
        for g in range(GROUPS):
            lanes = slice(g * LANES, (g + 1) * LANES)
            qre[g, n * MODES:(n + 1) * MODES, :] = value[0][:, lanes]
            qim[g, n * MODES:(n + 1) * MODES, :] = value[1][:, lanes]
        value = cmul(value, q)
    power = q
    for n in range(3):
        for g in range(GROUPS):
            lanes = slice(g * LANES, (g + 1) * LANES)
            rows_[g, n * ROWS:n * ROWS + MODES, :] = power[0][:, lanes]
            rows_[g, n * ROWS + MODES:(n + 1) * ROWS, :] = power[1][:, lanes]
        power = square(power)
    for g in range(GROUPS):
        lanes = slice(g * LANES, (g + 1) * LANES)
        rows_[g, 3 * ROWS:3 * ROWS + MODES, :] = weight[0][:, lanes]
        rows_[g, 3 * ROWS + MODES:4 * ROWS, :] = weight[1][:, lanes]

    keeps = []
    for n in range(3):
        s = 1 << n
        keeps.append((blocks >= s) & jnp.logical_not((blocks - s < b0) & (b0 <= blocks)))
    heard = blocks <= b0

    def group(g, unused):
        for m in range(MODES):
            state = (eb_ref[g, m], eb_ref[g, MODES + m])
            for n in range(3):
                moved = [jnp.where(keeps[n], pltpu.roll(part, 1 << n, 0), 0.0) for part in state]
                step = (rows_[g, n * ROWS + m:n * ROWS + m + 1, :],
                        rows_[g, n * ROWS + MODES + m:n * ROWS + MODES + m + 1, :])
                state = cadd(state, cmul(step, moved))
            before = [jnp.where(blocks >= 1, pltpu.roll(part, 1, 0), 0.0) for part in state]
            w = (rows_[g, 3 * ROWS + m:3 * ROWS + m + 1, :],
                 rows_[g, 3 * ROWS + MODES + m:3 * ROWS + MODES + m + 1, :])
            scaled = cmul(w, before)
            pz_ref[g, m] = scaled[0]
            pz_ref[g, MODES + m] = scaled[1]
            gz_ref[g, m] = jnp.where(heard, qre[g, pl.ds(m, BLOCKS, stride=MODES), :], 0.0)
            gz_ref[g, MODES + m] = jnp.where(heard, qim[g, pl.ds(m, BLOCKS, stride=MODES), :], 0.0)

        tile = 8

        def fir(select):
            xs = []
            for j in range(STEPS):
                x = sig[g, pl.ds(j, BLOCKS, stride=STEPS), :]
                late = (blocks * STEPS + j >= s0) | (blocks != b0)
                xs.append(jnp.where(late if select else jnp.logical_not(late), x, 0.0))
            for top in range(0, STEPS, tile):
                acc = [jnp.zeros((BLOCKS, LANES), F32)] * tile
                for k in range(top + tile):
                    tap = taps[g, k:k + 1, :]
                    for i in range(tile):
                        if top + i - k >= 0:
                            acc[i] = acc[i] + tap * xs[top + i - k]
                for i in range(tile):
                    if select:
                        y_ref[g, top + i] = acc[i]
                    else:
                        early = (blocks * STEPS + top + i < s0) & (blocks == b0)
                        y_ref[g, top + i] = y_ref[g, top + i] + jnp.where(early, acc[i], 0.0)

        fir(True)
        fir(False)
        return unused

    lax.fori_loop(0, GROUPS, group, 0)


def chip_kernel(own_ref, other_ref, p256_ref, pay_ref):
    core = lax.axis_index("ctx") % NC
    first = (core == 0).astype(F32)
    own, other = halves(own_ref), halves(other_ref)
    own_thru, other_thru = own_ref[ROWS:ROWS + 1, :], other_ref[ROWS:ROWS + 1, :]
    early = [first * a + (1.0 - first) * b for a, b in zip(own, other)]
    late = [first * b + (1.0 - first) * a for a, b in zip(own, other)]
    late_thru = first * other_thru + (1.0 - first) * own_thru
    moved = cmul(halves(p256_ref), early)
    pay_ref[:MODES, :] = late_thru * moved[0] + late[0]
    pay_ref[MODES:ROWS, :] = late_thru * moved[1] + late[1]
    pay_ref[ROWS:, :] = jnp.broadcast_to(own_thru * other_thru, (PAY - ROWS, CH))


def row_kernel(own_ref, one_ref, two_ref, three_ref, p256_ref, pay_ref, before_ref, factor_ref, held):
    mine = (lax.axis_index("ctx") // NC) % NY
    for k, ref in enumerate((own_ref, one_ref, two_ref, three_ref)):
        held[lax.rem(mine - k + NY, NY)] = ref[...]
    p512 = square(halves(p256_ref))
    state = (jnp.zeros((MODES, CH), F32),) * 2
    factor = (jnp.ones((MODES, CH), F32), jnp.zeros((MODES, CH), F32))
    thru = jnp.ones((1, CH), F32)
    for i in range(NY):
        @pl.when(mine == i)
        def put():
            before_ref[:MODES, :] = state[0]
            before_ref[MODES:, :] = state[1]
            factor_ref[:MODES, :] = factor[0]
            factor_ref[MODES:, :] = factor[1]
        open_ = held[i, ROWS:ROWS + 1, :]
        step = (open_ * p512[0], open_ * p512[1])
        state = cadd(cmul(step, state), (held[i, :MODES, :], held[i, MODES:ROWS, :]))
        factor = cmul(step, factor)
        thru = thru * open_
    pay_ref[:MODES, :] = state[0]
    pay_ref[MODES:ROWS, :] = state[1]
    pay_ref[ROWS:, :] = jnp.broadcast_to(thru, (PAY - ROWS, CH))


def gate_kernel(query_ref, y_ref, pz_ref, gz_ref, tre, tim, starts_ref, own_ref, other_ref, p256_ref,
                before_ref, factor_ref, one_ref, two_ref, hidden_ref, conv, sin):
    index = lax.axis_index("ctx")
    core, row = index % NC, index // (NC * NY)
    p256 = halves(p256_ref)
    p2048 = square(square(square(p256)))
    has_one = (row >= 1).astype(F32)
    has_two = (row >= 2).astype(F32)
    far = cmul(p2048, halves(two_ref))
    open_one = has_two * one_ref[ROWS:ROWS + 1, :]
    incoming = [has_one * a + open_one * b for a, b in zip(halves(one_ref), far)]
    state = cadd(halves(before_ref), cmul(halves(factor_ref), incoming))
    second = (core == 1).astype(F32)
    moved = cmul(p256, state)
    early_thru = other_ref[ROWS:ROWS + 1, :]
    state = [(1.0 - second) * a + second * (early_thru * b + c)
             for a, b, c in zip(state, moved, halves(other_ref))]
    for g in range(GROUPS):
        lanes = slice(g * LANES, (g + 1) * LANES)
        sin[g, :MODES, :] = state[0][:, lanes]
        sin[g, MODES:, :] = state[1][:, lanes]
    s0 = first_start(starts_ref)
    b0 = s0 // STEPS
    blocks = block_iota()

    def group(g, unused):
        z = []
        for m in range(MODES):
            s = (sin[g, m:m + 1, :], sin[g, MODES + m:MODES + m + 1, :])
            z.append(cadd((pz_ref[g, m], pz_ref[g, MODES + m]),
                          cmul((gz_ref[g, m], gz_ref[g, MODES + m]), s)))

        def step(j, unused):
            base = (j + 1) * MODES
            total = [None] * 4
            for m in range(MODES):
                term = tre[g, pl.ds(base + m, 1), :] * z[m][0] - tim[g, pl.ds(base + m, 1), :] * z[m][1]
                total[m % 4] = term if total[m % 4] is None else total[m % 4] + term
            total = (total[0] + total[1]) + (total[2] + total[3])
            late = (blocks * STEPS + j >= s0) & (blocks == b0)
            conv[g, pl.ds(j, BLOCKS, stride=STEPS), :] = y_ref[g, j] + jnp.where(late, 0.0, total)
            return unused

        return lax.fori_loop(0, STEPS, step, unused, unroll=4)

    lax.fori_loop(0, GROUPS, group, 0)
    for g in range(GROUPS):
        lanes = slice(g * LANES, (g + 1) * LANES)
        hidden_ref[:, lanes] = (query_ref[:, lanes].astype(F32) * conv[g]).astype(BF16)


def weight_kernel(*refs):
    pieces, out_ref = refs[:8], refs[8]
    index = lax.axis_index("ctx")
    core, y, x = index % NC, (index // NC) % NY, index // (NC * NY)
    for side in range(2):
        c = core if side == 0 else 1 - core
        for dx in range(NX):
            there = lax.rem(x - dx + NX, NX)
            for dy in range(NY):
                chip = there * NY + lax.rem(y - dy + NY, NY)
                rows = pl.ds(pl.multiple_of((chip * NC + c) * 128, 128), 128)
                out_ref[rows, :] = pieces[side * NX + dx][dy * 128:(dy + 1) * 128, :]


def near_kernel(own, up1, down1, up2, down2, weight_ref, out_ref):
    z = lax.axis_index("tp")
    total = None
    for k, ref in ((0, own), (1, up1), (-1, down1), (2, up2), (-2, down2)):
        rows = pl.ds(pl.multiple_of(lax.rem(z - k + NZ, NZ) * CH, CH), CH)
        term = jnp.dot(ref[...], weight_ref[rows, :], preferred_element_type=F32)
        total = term if total is None else total + term
    out_ref[...] = total


def far_kernel(near_ref, up3, down3, up4, down4, weight_ref, out_ref):
    z = lax.axis_index("tp")

    def rows(k):
        return pl.ds(pl.multiple_of(lax.rem(z - k + NZ, NZ) * CH, CH), CH)

    total = near_ref[...]
    for k, ref in ((3, up3), (-3, down3)):
        total = total + jnp.dot(ref[...], weight_ref[rows(k), :], preferred_element_type=F32)
    half = TOK // 2
    last = weight_ref[rows(4), :]
    out_ref[:half, :] = (total[:half] + jnp.dot(up4[...], last, preferred_element_type=F32)).astype(BF16)
    out_ref[half:, :] = (total[half:] + jnp.dot(down4[...], last, preferred_element_type=F32)).astype(BF16)


def ctx_index(x, y, c):
    return ((x % NX) * NY + y % NY) * NC + c % NC


def move(value, dx, dy, dc):
    pairs = [(ctx_index(x, y, c), ctx_index(x + dx, y + dy, c + dc))
             for x in range(NX) for y in range(NY) for c in range(NC)]
    return lax.ppermute(value, "ctx", pairs)


def turn(value, k):
    return lax.ppermute(value, "tp", [(i, (i + k) % NZ) for i in range(NZ)])


def shards(query, key, value, decay, freq, residue, skip, out_weight, doc_starts):
    starts = doc_starts.reshape(TOK // LANES, LANES)
    skip = skip.reshape(1, CH)
    sig = pltpu.VMEM((GROUPS, TOK, LANES), F32)
    qs = pltpu.VMEM((GROUPS, BLOCKS * MODES, LANES), F32)
    state_shape = struct(ROWS, CH)
    pay_shape = struct(PAY, CH)
    block_shape = struct(GROUPS, ROWS, BLOCKS, LANES)
    table = (GROUPS, (STEPS + 1) * MODES, LANES)

    pay, eb, p256 = call(
        ends_kernel, (pay_shape, block_shape, state_shape), (key, value, decay, freq, starts),
        [sig, pltpu.VMEM(table, F32), pltpu.VMEM(table, F32), qs, qs], 20_000_000, 1_500_000)
    other = move(pay, 0, 0, 1)

    wy = jnp.concatenate([out_weight] + [move(out_weight, 0, k, 0) for k in (1, 2, 3)], axis=0)
    wx = [wy] + [move(wy, k, 0, 0) for k in (1, 2, 3)]
    wo = [move(w, 0, 0, 1) for w in wx]
    weight = call(weight_kernel, struct(NZ * CH, CH, dtype=BF16), (*wx, *wo), (), 0, 8_000_000)

    chip = call(chip_kernel, pay_shape, (pay, other, p256))
    near = [move(chip, 0, k, 0) for k in (1, 2, 3)]
    y, pz, gz, tre, tim = call(
        local_kernel,
        (struct(GROUPS, STEPS, BLOCKS, LANES), block_shape, block_shape, struct(*table), struct(*table)),
        (key, value, decay, freq, residue, skip, starts, eb),
        [sig, qs, qs, pltpu.VMEM((GROUPS, STEPS, LANES), F32), pltpu.VMEM((GROUPS, 4 * ROWS, LANES), F32)],
        30_000_000, 5_000_000)
    row, before, factor = call(
        row_kernel, (pay_shape, state_shape, state_shape), (chip, *near, p256),
        [pltpu.VMEM((NY, PAY, CH), F32)])
    back = [move(row, k, 0, 0) for k in (1, 2)]
    hidden = call(
        gate_kernel, struct(TOK, CH, dtype=BF16),
        (query, y, pz, gz, tre, tim, starts, pay, other, p256, before, factor, *back),
        [sig, pltpu.VMEM((GROUPS, ROWS, LANES), F32)], 20_000_000, 5_000_000)

    half = TOK // 2
    up1, down1, up2, down2 = turn(hidden, 1), turn(hidden, -1), turn(hidden, 2), turn(hidden, -2)
    up3, down3 = turn(up2, 1), turn(down2, -1)
    up4, down4 = turn(up2[:half], 2), turn(down2[half:], -2)
    total = call(near_kernel, struct(TOK, CH), (hidden, up1, down1, up2, down2, weight), (),
                 5 * 2 * TOK * CH * CH, 4_000_000)
    return call(far_kernel, struct(TOK, CH, dtype=BF16), (total, up3, down3, up4, down4, weight), (),
                3 * 2 * TOK * CH * CH, 4_000_000)


def solution(mesh):
    in_specs = (
        P("ctx", "tp"),
        P("ctx", "tp"),
        P("ctx", "tp"),
        P(None, "tp"),
        P(None, "tp"),
        P(None, None, "tp"),
        P("tp"),
        P("ctx", "tp"),
        P("ctx"),
    )
    return jax.shard_map(
        shards, mesh=mesh, in_specs=in_specs, out_specs=P("ctx", "tp"), check_vma=False
    )
```

time: 428 us -> 100 us (0.23)
  the two profiles are of different devices: /device:TPU:1 before, /device:TPU:32 now
where the time goes in v1:
time: 100 us
  waiting for transfers between devices  52.5 us (52%)
  starting transfers between devices  27.6 us (28%)
  Pallas kernels  12.5 us (12%)
  local copies, waits for them, and re-layouts  7.28 us (7%)
    ppermute x8, waiting for transfers between devices, turn(): return lax.ppermute(value, 'tp', [(i, (i + k) % NZ) for i in range(NZ)])  28.6 us
    ppermute x16, waiting for transfers between devices, move(): return lax.ppermute(value, 'ctx', pairs)  23.9 us
    ppermute x16, starting transfers between devices, move(): return lax.ppermute(value, 'ctx', pairs)  15.2 us
    pallas_call x8, Pallas kernels, call(): pl.pallas_call(kernel, out_shape=outs, in_specs=[VMEM] * len(args), out_s...  12.5 us
    ppermute x8, starting transfers between devices, turn(): return lax.ppermute(value, 'tp', [(i, (i + k) % NZ) for i in range(NZ)])  12.4 us
    unnamed x31, local copies, waits for them, and re-layouts  7.25 us
  transfers between devices with their start and end apart: 24, of which 10 were waited for; matrix products, arithmetic and copies ran while one was open for 1% of the time, Pallas kernels for 11%

profile of v1, /device:TPU:32, one launch (start us, length us, event | category | flops | bytes accessed | tf_op | source)
XLA Modules:
  0.0 100.1 jit_solution(16891485737671126250)
XLA Ops:
  0.0 1.6 %collective-permute-start.10 = (bf16[128,512]{1,0:T(8,128)(2,1)}, bf16[128,512]{1,0:T(8,128)(2,1)S(1)}, u32[]{:S(2)}, u32[]{:S(2)}) collective-permute-start(bf16[128,512]{1,0:T(8,128)(2,1)} %param.16), channel_id=1, source_target_pairs={{0,16},{8,24},{16,32},{24,40},{32,48},{40,56},{48,0},{56,8},{64,80... | collective-permute-start | bytes 393224 | tf_op jit(solution)/shard_map/ppermute | solution.py:376
  1.6 2.9 %collective-permute-start.11 = (bf16[128,512]{1,0:T(8,128)(2,1)}, bf16[128,512]{1,0:T(8,128)(2,1)S(1)}, u32[]{:S(2)}, u32[]{:S(2)}) collective-permute-start(bf16[128,512]{1,0:T(8,128)(2,1)} %param.16), channel_id=1, source_target_pairs={{0,32},{8,40},{16,48},{24,56},{32,0},{40,8},{48,16},{56,24},{64,96... | collective-permute-start | bytes 393224 | tf_op jit(solution)/shard_map/ppermute | solution.py:376
  4.5 1.3 %collective-permute-start.12 = (bf16[128,512]{1,0:T(8,128)(2,1)}, bf16[128,512]{1,0:T(8,128)(2,1)S(1)}, u32[]{:S(2)}, u32[]{:S(2)}) collective-permute-start(bf16[128,512]{1,0:T(8,128)(2,1)} %param.16), channel_id=1, source_target_pairs={{0,48},{8,56},{16,0},{24,8},{32,16},{40,24},{48,32},{56,40},{64,11... | collective-permute-start | bytes 393224 | tf_op jit(solution)/shard_map/ppermute | solution.py:376
  5.8 0.9 copy-done.2
  6.8 0.9 copy-done.4
  10.0 3.0 %shard_map.91 = (f32[40,512]{1,0:T(8,128)S(1)}, f32[4,32,8,128]{3,2,1,0:T(8,128)S(1)}, f32[32,512]{1,0:T(8,128)S(1)}) custom-call(bf16[256,512]{1,0:T(8,128)(2,1)S(1)} %copy-done.2, bf16[256,512]{1,0:T(8,128)(2,1)S(1)} %copy-done.4, f32[16,512]{1,0:T(8,128)S(1)} %copy-done.7, f32[16,512]{1,0:T(8,128)S(1)} %copy-done.9, s32[2,128]{1,0:T(2,128)S(1)} %bitcast.2), custom_call_target="tpu_custom_call" | custom-call | flops 20000000 | bytes 1500000 | tf_op jit(solution)/shard_map/pallas_call | solution.py:23
  13.0 0.9 constant_dynamic-update-slice_fusion.3
  14.0 2.8 %collective-permute-start.15 = (bf16[512,512]{1,0:T(8,128)(2,1)S(1)}, bf16[512,512]{1,0:T(8,128)(2,1)S(1)}, u32[]{:S(2)}, u32[]{:S(2)}) collective-permute-start(bf16[512,512]{1,0:T(8,128)(2,1)S(1)} %constant_dynamic-update-slice_fusion.refs_0_), channel_id=1, source_target_pairs={{0,192},{8,200},{16,208},{24,216},{32,224},{40,232},{48,240},{56,2... | collective-permute-start | bytes 1572872 | tf_op jit(solution)/shard_map/ppermute | solution.py:376
  17.0 2.7 %collective-permute-start.2 = (f32[40,512]{1,0:T(8,128)S(1)}, f32[40,512]{1,0:T(8,128)S(1)}, u32[]{:S(2)}, u32[]{:S(2)}) collective-permute-start(f32[40,512]{1,0:T(8,128)S(1)} %shard_map.93.own_ref), channel_id=1, source_target_pairs={{0,32},{8,40},{16,48},{24,56},{32,0},{40,8},{48,16},{56,24},{64,96... | collective-permute-start | bytes 245768 | tf_op jit(solution)/shard_map/ppermute | solution.py:376
  20.5 1.7 %collective-permute-done.3.three_ref = f32[40,512]{1,0:T(8,128)S(1)} collective-permute-done((f32[40,512]{1,0:T(8,128)S(1)}, f32[40,512]{1,0:T(8,128)S(1)}, u32[]{:S(2)}, u32[]{:S(2)}) %collective-permute-start.3) | collective-permute-done | bytes 81952 | tf_op jit(solution)/shard_map/ppermute | solution.py:376
  23.2 2.2 %collective-permute-done.1.one_ref = f32[40,512]{1,0:T(8,128)S(1)} collective-permute-done((f32[40,512]{1,0:T(8,128)S(1)}, f32[40,512]{1,0:T(8,128)S(1)}, u32[]{:S(2)}, u32[]{:S(2)}) %collective-permute-start.1) | collective-permute-done | bytes 81952 | tf_op jit(solution)/shard_map/ppermute | solution.py:376
  27.3 3.1 %shard_map.92 = (f32[4,32,8,128]{3,2,1,0:T(8,128)S(1)}, f32[4,32,8,128]{3,2,1,0:T(8,128)S(1)}, f32[4,32,8,128]{3,2,1,0:T(8,128)S(1)}, f32[4,528,128]{2,1,0:T(8,128)S(1)}, f32[4,528,128]{2,1,0:T(8,128)S(1)}) custom-call(bf16[256,512]{1,0:T(8,128)(2,1)S(1)} %copy-done.3, bf16[256,512]{1,0:T(8,128)(2,1)S(1)} %copy-done.5, f32[16,512]{1,0:T(8,128)S(1)} %copy-done.8, ...), custom_call_target="tpu_custom_call" | custom-call | flops 30000000 | bytes 5000000 | tf_op jit(solution)/shard_map/pallas_call | solution.py:23
  30.4 18.3 %collective-permute-done.5.two_ref = f32[40,512]{1,0:T(8,128)S(1)} collective-permute-done((f32[40,512]{1,0:T(8,128)S(1)}, f32[40,512]{1,0:T(8,128)S(1)}, u32[]{:S(2)}, u32[]{:S(2)}) %collective-permute-start.5) | collective-permute-done | bytes 81952 | tf_op jit(solution)/shard_map/ppermute | solution.py:376
  49.5 1.9 %shard_map.95.own = bf16[256,512]{1,0:T(8,128)(2,1)S(1)} custom-call(bf16[256,512]{1,0:T(8,128)(2,1)S(1)} %copy-done.6, f32[4,32,8,128]{3,2,1,0:T(8,128)S(1)} %get-tuple-element.17.y_ref, f32[4,32,8,128]{3,2,1,0:T(8,128)S(1)} %get-tuple-element.18.pz_ref, f32[4,32,8,128]{3,2,1,0:T(8,128)S(1)} %get-tuple-element.19.gz_ref, ...), custom_call_target="tpu_custom_call" | custom-call | flops 20000000 | bytes 5000000 | tf_op jit(solution)/shard_map/pallas_call | solution.py:23
  51.4 5.5 %collective-permute-start.9 = (bf16[256,512]{1,0:T(8,128)(2,1)S(1)}, bf16[256,512]{1,0:T(8,128)(2,1)S(1)}, u32[]{:S(2)}, u32[]{:S(2)}) collective-permute-start(bf16[256,512]{1,0:T(8,128)(2,1)S(1)} %shard_map.95.own), channel_id=1, source_target_pairs={{0,6},{1,7},{2,0},{3,1},{4,2},{5,3},{6,4},{7,5},{8,14},{9,15},{10,... | collective-permute-start | bytes 786440 | tf_op jit(solution)/shard_map/ppermute | solution.py:380
  56.9 10.0 %collective-permute-done.9.down2 = bf16[256,512]{1,0:T(8,128)(2,1)S(1)} collective-permute-done((bf16[256,512]{1,0:T(8,128)(2,1)S(1)}, bf16[256,512]{1,0:T(8,128)(2,1)S(1)}, u32[]{:S(2)}, u32[]{:S(2)}) %collective-permute-start.9) | collective-permute-done | bytes 262176 | tf_op jit(solution)/shard_map/ppermute | solution.py:380
  67.9 4.6 %collective-permute-done.8.up2 = bf16[256,512]{1,0:T(8,128)(2,1)S(1)} collective-permute-done((bf16[256,512]{1,0:T(8,128)(2,1)S(1)}, bf16[256,512]{1,0:T(8,128)(2,1)S(1)}, u32[]{:S(2)}, u32[]{:S(2)}) %collective-permute-start.8) | collective-permute-done | bytes 262176 | tf_op jit(solution)/shard_map/ppermute | solution.py:380
  73.1 7.1 %collective-permute-done.7.down1 = bf16[256,512]{1,0:T(8,128)(2,1)S(1)} collective-permute-done((bf16[256,512]{1,0:T(8,128)(2,1)S(1)}, bf16[256,512]{1,0:T(8,128)(2,1)S(1)}, u32[]{:S(2)}, u32[]{:S(2)}) %collective-permute-start.7) | collective-permute-done | bytes 262176 | tf_op jit(solution)/shard_map/ppermute | solution.py:380
  80.2 2.0 %collective-permute-start.21 = (bf16[256,512]{1,0:T(8,128)(2,1)S(1)}, bf16[256,512]{1,0:T(8,128)(2,1)S(1)}, u32[]{:S(2)}, u32[]{:S(2)}) collective-permute-start(bf16[256,512]{1,0:T(8,128)(2,1)S(1)} %collective-permute-done.9.down2), channel_id=1, source_target_pairs={{0,7},{1,0},{2,1},{3,2},{4,3},{5,4},{6,5},{7,6},{8,15},{9,8},{10,9... | collective-permute-start | bytes 786440 | tf_op jit(solution)/shard_map/ppermute | solution.py:380
  82.3 4.2 %collective-permute-start.23 = (bf16[128,512]{1,0:T(8,128)(2,1)S(1)}, bf16[128,512]{1,0:T(8,128)(2,1)S(1)}, u32[]{:S(2)}, u32[]{:S(2)}) collective-permute-start(bf16[128,512]{1,0:T(8,128)(2,1)S(1)} %slice.9), channel_id=1, source_target_pairs={{0,6},{1,7},{2,0},{3,1},{4,2},{5,3},{6,4},{7,5},{8,14},{9,15},{10,... | collective-permute-start | bytes 393224 | tf_op jit(solution)/shard_map/ppermute | solution.py:380
  86.5 2.3 %shard_map.96.weight_ref = bf16[4096,512]{1,0:T(8,128)(2,1)} custom-call(bf16[512,512]{1,0:T(8,128)(2,1)S(1)} %constant_dynamic-update-slice_fusion.refs_0_, bf16[512,512]{1,0:T(8,128)(2,1)S(1)} %collective-permute-done.13.refs_1_, bf16[512,512]{1,0:T(8,128)(2,1)S(1)} %collective-permute-done.14.refs_2_, ...), custom_call_target="tpu_custom_call" | custom-call | bytes 8000000 | tf_op jit(solution)/shard_map/pallas_call | solution.py:23
  89.4 2.2 %copy-done = bf16[4096,512]{1,0:T(8,128)(2,1)S(1)} copy-done((bf16[4096,512]{1,0:T(8,128)(2,1)S(1)}, bf16[4096,512]{1,0:T(8,128)(2,1)}, u32[]{:S(2)}) %copy-start) | copy-done | bytes 4194328
  92.5 6.3 %collective-permute-done.22.up4 = bf16[128,512]{1,0:T(8,128)(2,1)S(1)} collective-permute-done((bf16[128,512]{1,0:T(8,128)(2,1)S(1)}, bf16[128,512]{1,0:T(8,128)(2,1)S(1)}, u32[]{:S(2)}, u32[]{:S(2)}) %collective-permute-start.22) | collective-permute-done | bytes 131104 | tf_op jit(solution)/shard_map/ppermute | solution.py:380
  98.8 1.3 %shard_map.98 = bf16[256,512]{1,0:T(8,128)(2,1)} custom-call(f32[256,512]{1,0:T(8,128)S(1)} %shard_map.97.near_ref, bf16[256,512]{1,0:T(8,128)(2,1)S(1)} %collective-permute-done.20.up3, bf16[256,512]{1,0:T(8,128)(2,1)S(1)} %collective-permute-done.21.down3, bf16[128,512]{1,0:T(8,128)(2,1)S(1)} %collective-permute-done.22.up4, ...), custom_call_target="tpu_custom_call" | custom-call | flops 402653184 | bytes 4000000 | tf_op jit(solution)/shard_map/pallas_call | solution.py:23
  (66 shorter events, 10.0 us)
Async XLA Ops:
  0.0 13.9 %collective-permute-start.10 = (bf16[128,512]{1,0:T(8,128)(2,1)}, bf16[128,512]{1,0:T(8,128)(2,1)S(1)}, u32[]{:S(2)}, u32[]{:S(2)}) collective-permute-start(bf16[128,512]{1,0:T(8,128)(2,1)} %param.16), channel_id=1, source_target_pairs={{0,16},{8,24},{16,32},{24,40},{32,48},{40,56},{48,0},{56,8},{64,80... | collective-permute-start | bytes 393224 | tf_op jit(solution)/shard_map/ppermute | solution.py:376
  1.6 12.4 %collective-permute-start.11 = (bf16[128,512]{1,0:T(8,128)(2,1)}, bf16[128,512]{1,0:T(8,128)(2,1)S(1)}, u32[]{:S(2)}, u32[]{:S(2)}) collective-permute-start(bf16[128,512]{1,0:T(8,128)(2,1)} %param.16), channel_id=1, source_target_pairs={{0,32},{8,40},{16,48},{24,56},{32,0},{40,8},{48,16},{56,24},{64,96... | collective-permute-start | bytes 393224 | tf_op jit(solution)/shard_map/ppermute | solution.py:376
  4.5 9.5 %collective-permute-start.12 = (bf16[128,512]{1,0:T(8,128)(2,1)}, bf16[128,512]{1,0:T(8,128)(2,1)S(1)}, u32[]{:S(2)}, u32[]{:S(2)}) collective-permute-start(bf16[128,512]{1,0:T(8,128)(2,1)} %param.16), channel_id=1, source_target_pairs={{0,48},{8,56},{16,0},{24,8},{32,16},{40,24},{48,32},{56,40},{64,11... | collective-permute-start | bytes 393224 | tf_op jit(solution)/shard_map/ppermute | solution.py:376
  12.9 4.0 %collective-permute-start = (f32[40,512]{1,0:T(8,128)S(1)}, f32[40,512]{1,0:T(8,128)S(1)}, u32[]{:S(2)}, u32[]{:S(2)}) collective-permute-start(f32[40,512]{1,0:T(8,128)S(1)} %get-tuple-element.22.own_ref), channel_id=1, source_target_pairs={{0,8},{8,0},{16,24},{24,16},{32,40},{40,32},{48,56},{56,48},{64,72... | collective-permute-start | bytes 245768 | tf_op jit(solution)/shard_map/ppermute | solution.py:376
  14.0 52.8 %collective-permute-start.15 = (bf16[512,512]{1,0:T(8,128)(2,1)S(1)}, bf16[512,512]{1,0:T(8,128)(2,1)S(1)}, u32[]{:S(2)}, u32[]{:S(2)}) collective-permute-start(bf16[512,512]{1,0:T(8,128)(2,1)S(1)} %constant_dynamic-update-slice_fusion.refs_0_), channel_id=1, source_target_pairs={{0,192},{8,200},{16,208},{24,216},{32,224},{40,232},{48,240},{56,2... | collective-permute-start | bytes 1572872 | tf_op jit(solution)/shard_map/ppermute | solution.py:376
  16.9 5.4 %collective-permute-start.3 = (f32[40,512]{1,0:T(8,128)S(1)}, f32[40,512]{1,0:T(8,128)S(1)}, u32[]{:S(2)}, u32[]{:S(2)}) collective-permute-start(f32[40,512]{1,0:T(8,128)S(1)} %shard_map.93.own_ref), channel_id=1, source_target_pairs={{0,48},{8,56},{16,0},{24,8},{32,16},{40,24},{48,32},{56,40},{64,11... | collective-permute-start | bytes 245768 | tf_op jit(solution)/shard_map/ppermute | solution.py:376
  17.0 6.2 %collective-permute-start.2 = (f32[40,512]{1,0:T(8,128)S(1)}, f32[40,512]{1,0:T(8,128)S(1)}, u32[]{:S(2)}, u32[]{:S(2)}) collective-permute-start(f32[40,512]{1,0:T(8,128)S(1)} %shard_map.93.own_ref), channel_id=1, source_target_pairs={{0,32},{8,40},{16,48},{24,56},{32,0},{40,8},{48,16},{56,24},{64,96... | collective-permute-start | bytes 245768 | tf_op jit(solution)/shard_map/ppermute | solution.py:376
  19.7 5.7 %collective-permute-start.1 = (f32[40,512]{1,0:T(8,128)S(1)}, f32[40,512]{1,0:T(8,128)S(1)}, u32[]{:S(2)}, u32[]{:S(2)}) collective-permute-start(f32[40,512]{1,0:T(8,128)S(1)} %shard_map.93.own_ref), channel_id=1, source_target_pairs={{0,16},{8,24},{16,32},{24,40},{32,48},{40,56},{48,0},{56,8},{64,80... | collective-permute-start | bytes 245768 | tf_op jit(solution)/shard_map/ppermute | solution.py:376
  19.7 47.6 %collective-permute-start.14 = (bf16[512,512]{1,0:T(8,128)(2,1)S(1)}, bf16[512,512]{1,0:T(8,128)(2,1)S(1)}, u32[]{:S(2)}, u32[]{:S(2)}) collective-permute-start(bf16[512,512]{1,0:T(8,128)(2,1)S(1)} %constant_dynamic-update-slice_fusion.refs_0_), channel_id=1, source_target_pairs={{0,128},{8,136},{16,144},{24,152},{32,160},{40,168},{48,176},{56,1... | collective-permute-start | bytes 1572872 | tf_op jit(solution)/shard_map/ppermute | solution.py:376
  22.3 45.2 %collective-permute-start.13 = (bf16[512,512]{1,0:T(8,128)(2,1)S(1)}, bf16[512,512]{1,0:T(8,128)(2,1)S(1)}, u32[]{:S(2)}, u32[]{:S(2)}) collective-permute-start(bf16[512,512]{1,0:T(8,128)(2,1)S(1)} %constant_dynamic-update-slice_fusion.refs_0_), channel_id=1, source_target_pairs={{0,64},{8,72},{16,80},{24,88},{32,96},{40,104},{48,112},{56,120},{... | collective-permute-start | bytes 1572872 | tf_op jit(solution)/shard_map/ppermute | solution.py:376
  25.5 23.2 %collective-permute-start.5 = (f32[40,512]{1,0:T(8,128)S(1)}, f32[40,512]{1,0:T(8,128)S(1)}, u32[]{:S(2)}, u32[]{:S(2)}) collective-permute-start(f32[40,512]{1,0:T(8,128)S(1)} %get-tuple-element.26), channel_id=1, source_target_pairs={{0,128},{8,136},{16,144},{24,152},{32,160},{40,168},{48,176},{56,1... | collective-permute-start | bytes 245768 | tf_op jit(solution)/shard_map/ppermute | solution.py:376
  26.4 23.1 %collective-permute-start.4 = (f32[40,512]{1,0:T(8,128)S(1)}, f32[40,512]{1,0:T(8,128)S(1)}, u32[]{:S(2)}, u32[]{:S(2)}) collective-permute-start(f32[40,512]{1,0:T(8,128)S(1)} %get-tuple-element.26), channel_id=1, source_target_pairs={{0,64},{8,72},{16,80},{24,88},{32,96},{40,104},{48,112},{56,120},{... | collective-permute-start | bytes 245768 | tf_op jit(solution)/shard_map/ppermute | solution.py:376
  51.4 15.4 %collective-permute-start.9 = (bf16[256,512]{1,0:T(8,128)(2,1)S(1)}, bf16[256,512]{1,0:T(8,128)(2,1)S(1)}, u32[]{:S(2)}, u32[]{:S(2)}) collective-permute-start(bf16[256,512]{1,0:T(8,128)(2,1)S(1)} %shard_map.95.own), channel_id=1, source_target_pairs={{0,6},{1,7},{2,0},{3,1},{4,2},{5,3},{6,4},{7,5},{8,14},{9,15},{10,... | collective-permute-start | bytes 786440 | tf_op jit(solution)/shard_map/ppermute | solution.py:380
  56.9 15.6 %collective-permute-start.8 = (bf16[256,512]{1,0:T(8,128)(2,1)S(1)}, bf16[256,512]{1,0:T(8,128)(2,1)S(1)}, u32[]{:S(2)}, u32[]{:S(2)}) collective-permute-start(bf16[256,512]{1,0:T(8,128)(2,1)S(1)} %shard_map.95.own), channel_id=1, source_target_pairs={{0,2},{1,3},{2,4},{3,5},{4,6},{5,7},{6,0},{7,1},{8,10},{9,11},{10,... | collective-permute-start | bytes 786440 | tf_op jit(solution)/shard_map/ppermute | solution.py:380
  66.9 13.4 %collective-permute-start.16 = (bf16[512,512]{1,0:T(8,128)(2,1)S(1)}, bf16[512,512]{1,0:T(8,128)(2,1)S(1)}, u32[]{:S(2)}, u32[]{:S(2)}) collective-permute-start(bf16[512,512]{1,0:T(8,128)(2,1)S(1)} %constant_dynamic-update-slice_fusion.refs_0_), channel_id=1, source_target_pairs={{0,8},{8,0},{16,24},{24,16},{32,40},{40,32},{48,56},{56,48},{64,72... | collective-permute-start | bytes 1572872 | tf_op jit(solution)/shard_map/ppermute | solution.py:376
  66.9 15.4 %collective-permute-start.19 = (bf16[512,512]{1,0:T(8,128)(2,1)S(1)}, bf16[512,512]{1,0:T(8,128)(2,1)S(1)}, u32[]{:S(2)}, u32[]{:S(2)}) collective-permute-start(bf16[512,512]{1,0:T(8,128)(2,1)S(1)} %collective-permute-done.15.refs_3_), channel_id=1, source_target_pairs={{0,8},{8,0},{16,24},{24,16},{32,40},{40,32},{48,56},{56,48},{64,72... | collective-permute-start | bytes 1572872 | tf_op jit(solution)/shard_map/ppermute | solution.py:376
  67.4 14.9 %collective-permute-start.18 = (bf16[512,512]{1,0:T(8,128)(2,1)S(1)}, bf16[512,512]{1,0:T(8,128)(2,1)S(1)}, u32[]{:S(2)}, u32[]{:S(2)}) collective-permute-start(bf16[512,512]{1,0:T(8,128)(2,1)S(1)} %collective-permute-done.14.refs_2_), channel_id=1, source_target_pairs={{0,8},{8,0},{16,24},{24,16},{32,40},{40,32},{48,56},{56,48},{64,72... | collective-permute-start | bytes 1572872 | tf_op jit(solution)/shard_map/ppermute | solution.py:376
  67.5 19.1 %collective-permute-start.17 = (bf16[512,512]{1,0:T(8,128)(2,1)S(1)}, bf16[512,512]{1,0:T(8,128)(2,1)S(1)}, u32[]{:S(2)}, u32[]{:S(2)}) collective-permute-start(bf16[512,512]{1,0:T(8,128)(2,1)S(1)} %collective-permute-done.13.refs_1_), channel_id=1, source_target_pairs={{0,8},{8,0},{16,24},{24,16},{32,40},{40,32},{48,56},{56,48},{64,72... | collective-permute-start | bytes 1572872 | tf_op jit(solution)/shard_map/ppermute | solution.py:376
  72.5 7.7 %collective-permute-start.7 = (bf16[256,512]{1,0:T(8,128)(2,1)S(1)}, bf16[256,512]{1,0:T(8,128)(2,1)S(1)}, u32[]{:S(2)}, u32[]{:S(2)}) collective-permute-start(bf16[256,512]{1,0:T(8,128)(2,1)S(1)} %shard_map.95.own), channel_id=1, source_target_pairs={{0,7},{1,0},{2,1},{3,2},{4,3},{5,4},{6,5},{7,6},{8,15},{9,8},{10,9... | collective-permute-start | bytes 786440 | tf_op jit(solution)/shard_map/ppermute | solution.py:380
  80.2 9.2 %collective-permute-start.6 = (bf16[256,512]{1,0:T(8,128)(2,1)S(1)}, bf16[256,512]{1,0:T(8,128)(2,1)S(1)}, u32[]{:S(2)}, u32[]{:S(2)}) collective-permute-start(bf16[256,512]{1,0:T(8,128)(2,1)S(1)} %shard_map.95.own), channel_id=1, source_target_pairs={{0,1},{1,2},{2,3},{3,4},{4,5},{5,6},{6,7},{7,0},{8,9},{9,10},{10,1... | collective-permute-start | bytes 786440 | tf_op jit(solution)/shard_map/ppermute | solution.py:380
  80.2 18.6 %collective-permute-start.21 = (bf16[256,512]{1,0:T(8,128)(2,1)S(1)}, bf16[256,512]{1,0:T(8,128)(2,1)S(1)}, u32[]{:S(2)}, u32[]{:S(2)}) collective-permute-start(bf16[256,512]{1,0:T(8,128)(2,1)S(1)} %collective-permute-done.9.down2), channel_id=1, source_target_pairs={{0,7},{1,0},{2,1},{3,2},{4,3},{5,4},{6,5},{7,6},{8,15},{9,8},{10,9... | collective-permute-start | bytes 786440 | tf_op jit(solution)/shard_map/ppermute | solution.py:380
  82.2 16.6 %collective-permute-start.20 = (bf16[256,512]{1,0:T(8,128)(2,1)S(1)}, bf16[256,512]{1,0:T(8,128)(2,1)S(1)}, u32[]{:S(2)}, u32[]{:S(2)}) collective-permute-start(bf16[256,512]{1,0:T(8,128)(2,1)S(1)} %collective-permute-done.8.up2), channel_id=1, source_target_pairs={{0,1},{1,2},{2,3},{3,4},{4,5},{5,6},{6,7},{7,0},{8,9},{9,10},{10,1... | collective-permute-start | bytes 786440 | tf_op jit(solution)/shard_map/ppermute | solution.py:380
  82.3 10.2 %collective-permute-start.23 = (bf16[128,512]{1,0:T(8,128)(2,1)S(1)}, bf16[128,512]{1,0:T(8,128)(2,1)S(1)}, u32[]{:S(2)}, u32[]{:S(2)}) collective-permute-start(bf16[128,512]{1,0:T(8,128)(2,1)S(1)} %slice.9), channel_id=1, source_target_pairs={{0,6},{1,7},{2,0},{3,1},{4,2},{5,3},{6,4},{7,5},{8,14},{9,15},{10,... | collective-permute-start | bytes 393224 | tf_op jit(solution)/shard_map/ppermute | solution.py:380
  86.5 12.3 %collective-permute-start.22 = (bf16[128,512]{1,0:T(8,128)(2,1)S(1)}, bf16[128,512]{1,0:T(8,128)(2,1)S(1)}, u32[]{:S(2)}, u32[]{:S(2)}) collective-permute-start(bf16[128,512]{1,0:T(8,128)(2,1)S(1)} %slice.8), channel_id=1, source_target_pairs={{0,2},{1,3},{2,4},{3,5},{4,6},{5,7},{6,0},{7,1},{8,10},{9,11},{10,... | collective-permute-start | bytes 393224 | tf_op jit(solution)/shard_map/ppermute | solution.py:380
  (14 other events, 153.2 us)

commit v2 on v1

--- a/solution.py
+++ b/solution.py
@@ -16,6 +16,9 @@
 ROWS = 2 * MODES
 PAY = ROWS + 8
 VMEM = pl.BlockSpec(memory_space=pltpu.VMEM)
+FLAG = 16
+SENT = 2 * ROWS + FLAG
+WROWS = 128
 PARAMS = pltpu.CompilerParams(vmem_limit_bytes=48 * 1024 * 1024)
 
 
@@ -59,12 +62,6 @@
     return jnp.min(jnp.min(where, axis=1, keepdims=True), axis=0, keepdims=True)
 
 
-def poles(decay_ref, freq_ref):
-    magnitude = jnp.exp(-decay_ref[...])
-    freq = freq_ref[...]
-    return magnitude * jnp.cos(freq), magnitude * jnp.sin(freq)
-
-
 def fill_powers(pole, table_re, table_im, count):
     def put(k, value):
         for g in range(GROUPS):
@@ -92,15 +89,10 @@
     return lax.broadcasted_iota(jnp.int32, (BLOCKS, LANES), 0)
 
 
-def ends_kernel(key_ref, value_ref, decay_ref, freq_ref, starts_ref, pay_ref, eb_ref, p256_ref,
-                sig, tre, tim, qre, qim):
-    s0 = first_start(starts_ref)
-    b0 = s0 // STEPS
-    fill_signal(key_ref, value_ref, sig)
-    pole = poles(decay_ref, freq_ref)
-    q = fill_powers(pole, tre, tim, STEPS)
-    one = (jnp.ones((MODES, CH), F32), jnp.zeros((MODES, CH), F32))
-    value = one
+def powers_kernel(pole_re, pole_im, tre, tim, qre, qim, p256_ref):
+    fill_powers((pole_re[...], pole_im[...]), tre, tim, STEPS + 1)
+    q = last_power(tre, tim)
+    value = (jnp.ones((MODES, CH), F32), jnp.zeros((MODES, CH), F32))
     for n in range(BLOCKS):
         row = (BLOCKS - 1 - n) * MODES
         for g in range(GROUPS):
@@ -110,6 +102,12 @@
         value = cmul(value, q)
     p256_ref[:MODES, :] = value[0]
     p256_ref[MODES:, :] = value[1]
+
+
+def ends_kernel(key_ref, value_ref, starts_ref, tre, tim, qre, qim, pay_ref, eb_ref, sig):
+    s0 = first_start(starts_ref)
+    b0 = s0 // STEPS
+    fill_signal(key_ref, value_ref, sig)
     blocks = block_iota()
     reach = (s0 >= TOK) | (blocks >= b0)
 
@@ -132,31 +130,31 @@
             eb_ref[g, MODES + m] = im
             w = (qre[g, pl.ds(m, BLOCKS, stride=MODES), :], qim[g, pl.ds(m, BLOCKS, stride=MODES), :])
             end = cmul(w, (re, im))
-            pay3 = pl.ds(pl.multiple_of(g * LANES, LANES), LANES)
-            pay_ref[pl.ds(m, 1), pay3] = jnp.sum(jnp.where(reach, end[0], 0.0), axis=0, keepdims=True)
-            pay_ref[pl.ds(MODES + m, 1), pay3] = jnp.sum(jnp.where(reach, end[1], 0.0), axis=0, keepdims=True)
+            lanes = pl.ds(pl.multiple_of(g * LANES, LANES), LANES)
+            pay_ref[pl.ds(m, 1), lanes] = jnp.sum(jnp.where(reach, end[0], 0.0), axis=0, keepdims=True)
+            pay_ref[pl.ds(MODES + m, 1), lanes] = jnp.sum(jnp.where(reach, end[1], 0.0), axis=0, keepdims=True)
         return unused
 
     lax.fori_loop(0, GROUPS, group, 0)
     pay_ref[ROWS:, :] = jnp.broadcast_to((s0 >= TOK).astype(F32), (PAY - ROWS, CH))
 
 
-def local_kernel(key_ref, value_ref, decay_ref, freq_ref, res_ref, skip_ref, starts_ref, eb_ref,
-                 y_ref, pz_ref, gz_ref, tre, tim, sig, qre, qim, taps, rows_):
+def last_power(tre, tim):
+    return [jnp.concatenate([t[g, STEPS * MODES:, :] for g in range(GROUPS)], axis=1) for t in (tre, tim)]
+
+
+def local_kernel(sig, tre, tim, decay_ref, res_ref, skip_ref, starts_ref, y_ref, weight_ref, taps):
     s0 = first_start(starts_ref)
     b0 = s0 // STEPS
     blocks = block_iota()
-    fill_signal(key_ref, value_ref, sig)
-    pole = poles(decay_ref, freq_ref)
-    q = fill_powers(pole, tre, tim, STEPS + 1)
-    q = (jnp.concatenate([tre[g, STEPS * MODES:, :] for g in range(GROUPS)], axis=1),
-         jnp.concatenate([tim[g, STEPS * MODES:, :] for g in range(GROUPS)], axis=1))
     y = 2.0 * decay_ref[...]
     series = jnp.ones_like(y)
     for n in range(10, 1, -1):
         series = 1.0 - y * (1.0 / n) * series
     scale = jnp.sqrt(y * series)
     weight = (res_ref[0] * scale, res_ref[1] * scale)
+    weight_ref[:MODES, :] = weight[0]
+    weight_ref[MODES:, :] = weight[1]
     for g in range(GROUPS):
         lanes = slice(g * LANES, (g + 1) * LANES)
         w_re, w_im = weight[0][:, lanes], weight[1][:, lanes]
@@ -166,48 +164,8 @@
             if k == 0:
                 row = row + skip_ref[:, lanes]
             taps[g, k:k + 1, :] = row
-    value = weight
-    for n in range(BLOCKS):
-        for g in range(GROUPS):
-            lanes = slice(g * LANES, (g + 1) * LANES)
-            qre[g, n * MODES:(n + 1) * MODES, :] = value[0][:, lanes]
-            qim[g, n * MODES:(n + 1) * MODES, :] = value[1][:, lanes]
-        value = cmul(value, q)
-    power = q
-    for n in range(3):
-        for g in range(GROUPS):
-            lanes = slice(g * LANES, (g + 1) * LANES)
-            rows_[g, n * ROWS:n * ROWS + MODES, :] = power[0][:, lanes]
-            rows_[g, n * ROWS + MODES:(n + 1) * ROWS, :] = power[1][:, lanes]
-        power = square(power)
-    for g in range(GROUPS):
-        lanes = slice(g * LANES, (g + 1) * LANES)
-        rows_[g, 3 * ROWS:3 * ROWS + MODES, :] = weight[0][:, lanes]
-        rows_[g, 3 * ROWS + MODES:4 * ROWS, :] = weight[1][:, lanes]
-
-    keeps = []
-    for n in range(3):
-        s = 1 << n
-        keeps.append((blocks >= s) & jnp.logical_not((blocks - s < b0) & (b0 <= blocks)))
-    heard = blocks <= b0
 
     def group(g, unused):
-        for m in range(MODES):
-            state = (eb_ref[g, m], eb_ref[g, MODES + m])
-            for n in range(3):
-                moved = [jnp.where(keeps[n], pltpu.roll(part, 1 << n, 0), 0.0) for part in state]
-                step = (rows_[g, n * ROWS + m:n * ROWS + m + 1, :],
-                        rows_[g, n * ROWS + MODES + m:n * ROWS + MODES + m + 1, :])
-                state = cadd(state, cmul(step, moved))
-            before = [jnp.where(blocks >= 1, pltpu.roll(part, 1, 0), 0.0) for part in state]
-            w = (rows_[g, 3 * ROWS + m:3 * ROWS + m + 1, :],
-                 rows_[g, 3 * ROWS + MODES + m:3 * ROWS + MODES + m + 1, :])
-            scaled = cmul(w, before)
-            pz_ref[g, m] = scaled[0]
-            pz_ref[g, MODES + m] = scaled[1]
-            gz_ref[g, m] = jnp.where(heard, qre[g, pl.ds(m, BLOCKS, stride=MODES), :], 0.0)
-            gz_ref[g, MODES + m] = jnp.where(heard, qim[g, pl.ds(m, BLOCKS, stride=MODES), :], 0.0)
-
         tile = 8
 
         def fir(select):
@@ -237,7 +195,75 @@
     lax.fori_loop(0, GROUPS, group, 0)
 
 
-def chip_kernel(own_ref, other_ref, p256_ref, pay_ref):
+def carry_kernel(eb_ref, tre, tim, weight_ref, starts_ref, wy_ref, pz_ref, gz_ref, later_ref, qre, qim, rows_):
+    later_ref[...] = wy_ref[...]
+    s0 = first_start(starts_ref)
+    b0 = s0 // STEPS
+    blocks = block_iota()
+    weight = (weight_ref[:MODES, :], weight_ref[MODES:, :])
+    q = last_power(tre, tim)
+    value = weight
+    for n in range(BLOCKS):
+        for g in range(GROUPS):
+            lanes = slice(g * LANES, (g + 1) * LANES)
+            qre[g, n * MODES:(n + 1) * MODES, :] = value[0][:, lanes]
+            qim[g, n * MODES:(n + 1) * MODES, :] = value[1][:, lanes]
+        value = cmul(value, q)
+    power = q
+    for n in range(3):
+        for g in range(GROUPS):
+            lanes = slice(g * LANES, (g + 1) * LANES)
+            rows_[g, n * ROWS:n * ROWS + MODES, :] = power[0][:, lanes]
+            rows_[g, n * ROWS + MODES:(n + 1) * ROWS, :] = power[1][:, lanes]
+        power = square(power)
+    for g in range(GROUPS):
+        lanes = slice(g * LANES, (g + 1) * LANES)
+        rows_[g, 3 * ROWS:3 * ROWS + MODES, :] = weight[0][:, lanes]
+        rows_[g, 3 * ROWS + MODES:4 * ROWS, :] = weight[1][:, lanes]
+
+    keeps = []
+    for n in range(3):
+        s = 1 << n
+        keeps.append((blocks >= s) & jnp.logical_not((blocks - s < b0) & (b0 <= blocks)))
+    heard = blocks <= b0
+
+    def group(g, unused):
+        for m in range(MODES):
+            state = (eb_ref[g, m], eb_ref[g, MODES + m])
+            for n in range(3):
+                moved = [jnp.where(keeps[n], pltpu.roll(part, 1 << n, 0), 0.0) for part in state]
+                step = (rows_[g, n * ROWS + m:n * ROWS + m + 1, :],
+                        rows_[g, n * ROWS + MODES + m:n * ROWS + MODES + m + 1, :])
+                state = cadd(state, cmul(step, moved))
+            before = [jnp.where(blocks >= 1, pltpu.roll(part, 1, 0), 0.0) for part in state]
+            w = (rows_[g, 3 * ROWS + m:3 * ROWS + m + 1, :],
+                 rows_[g, 3 * ROWS + MODES + m:3 * ROWS + MODES + m + 1, :])
+            scaled = cmul(w, before)
+            pz_ref[g, m] = scaled[0]
+            pz_ref[g, MODES + m] = scaled[1]
+            gz_ref[g, m] = jnp.where(heard, qre[g, pl.ds(m, BLOCKS, stride=MODES), :], 0.0)
+            gz_ref[g, MODES + m] = jnp.where(heard, qim[g, pl.ds(m, BLOCKS, stride=MODES), :], 0.0)
+
+        return unused
+
+    lax.fori_loop(0, GROUPS, group, 0)
+
+
+def put_state(ref, state, thru):
+    for part, at in zip(state, (0, MODES)):
+        high = part.astype(BF16)
+        ref[at:at + MODES, :] = high
+        ref[ROWS + at:ROWS + at + MODES, :] = (part - high.astype(F32)).astype(BF16)
+    ref[2 * ROWS:SENT, :] = jnp.broadcast_to(thru, (FLAG, CH)).astype(BF16)
+
+
+def get_state(ref):
+    parts = [ref[at:at + MODES, :].astype(F32) + ref[ROWS + at:ROWS + at + MODES, :].astype(F32)
+             for at in (0, MODES)]
+    return parts, ref[2 * ROWS:2 * ROWS + 8, :].astype(F32)[:1]
+
+
+def chip_kernel(own_ref, other_ref, p256_ref, weight_ref, sent_ref):
     core = lax.axis_index("ctx") % NC
     first = (core == 0).astype(F32)
     own, other = halves(own_ref), halves(other_ref)
@@ -246,22 +272,27 @@
     late = [first * b + (1.0 - first) * a for a, b in zip(own, other)]
     late_thru = first * other_thru + (1.0 - first) * own_thru
     moved = cmul(halves(p256_ref), early)
-    pay_ref[:MODES, :] = late_thru * moved[0] + late[0]
-    pay_ref[MODES:ROWS, :] = late_thru * moved[1] + late[1]
-    pay_ref[ROWS:, :] = jnp.broadcast_to(own_thru * other_thru, (PAY - ROWS, CH))
-
-
-def row_kernel(own_ref, one_ref, two_ref, three_ref, p256_ref, pay_ref, before_ref, factor_ref, held):
+    put_state(sent_ref, [late_thru * a + b for a, b in zip(moved, late)], own_thru * other_thru)
+    sent_ref[SENT:, :] = weight_ref[...]
+
+
+def row_kernel(own_ref, one_ref, two_ref, three_ref, p256_ref, pay_ref, before_ref, factor_ref, wy_ref,
+               held):
     mine = (lax.axis_index("ctx") // NC) % NY
     for k, ref in enumerate((own_ref, one_ref, two_ref, three_ref)):
-        held[lax.rem(mine - k + NY, NY)] = ref[...]
+        there = lax.rem(mine - k + NY, NY)
+        state, thru = get_state(ref)
+        held[there, :MODES, :] = state[0]
+        held[there, MODES:ROWS, :] = state[1]
+        held[there, ROWS:, :] = jnp.broadcast_to(thru, (PAY - ROWS, CH))
+        wy_ref[pl.ds(pl.multiple_of(there * WROWS, WROWS), WROWS), :] = ref[SENT:, :]
     p512 = square(halves(p256_ref))
     state = (jnp.zeros((MODES, CH), F32),) * 2
     factor = (jnp.ones((MODES, CH), F32), jnp.zeros((MODES, CH), F32))
     thru = jnp.ones((1, CH), F32)
     for i in range(NY):
         @pl.when(mine == i)
-        def put():
+        def put(state=state, factor=factor):
             before_ref[:MODES, :] = state[0]
             before_ref[MODES:, :] = state[1]
             factor_ref[:MODES, :] = factor[0]
@@ -327,43 +358,54 @@
         hidden_ref[:, lanes] = (query_ref[:, lanes].astype(F32) * conv[g]).astype(BF16)
 
 
-def weight_kernel(*refs):
-    pieces, out_ref = refs[:8], refs[8]
-    index = lax.axis_index("ctx")
-    core, y, x = index % NC, (index // NC) % NY, index // (NC * NY)
-    for side in range(2):
-        c = core if side == 0 else 1 - core
-        for dx in range(NX):
-            there = lax.rem(x - dx + NX, NX)
-            for dy in range(NY):
-                chip = there * NY + lax.rem(y - dy + NY, NY)
-                rows = pl.ds(pl.multiple_of((chip * NC + c) * 128, 128), 128)
-                out_ref[rows, :] = pieces[side * NX + dx][dy * 128:(dy + 1) * 128, :]
-
-
-def near_kernel(own, up1, down1, up2, down2, weight_ref, out_ref):
+def weight_kernel(token_ref, *refs):
+    pieces, out_ref = refs[:NX], refs[NX]
+    x = lax.axis_index("ctx") // (NC * NY)
+    for dx in range(NX):
+        there = lax.rem(x - dx + NX, NX)
+        rows = pl.ds(pl.multiple_of(there * NY * WROWS, NY * WROWS), NY * WROWS)
+        out_ref[rows, :] = pieces[dx][...]
+
+
+def relay_kernel(up1, down1, up2, down2, up2_ref, down2_ref, top_ref, bottom_ref, token_ref):
+    half = TOK // 2
+    up2_ref[...] = up2[...]
+    down2_ref[...] = down2[...]
+    top_ref[...] = up2[:half, :]
+    bottom_ref[...] = down2[half:, :]
+    token_ref[...] = up1[:16, :LANES] + down1[:16, :LANES]
+
+
+def project(z, hidden, own_ref, other_ref):
+    core = lax.axis_index("ctx") % NC
+    rows = pl.ds(pl.multiple_of(z * 2 * WROWS, 2 * WROWS), 2 * WROWS)
+    total = None
+    for side, weight_ref in ((core, own_ref), (1 - core, other_ref)):
+        lanes = [pl.ds(pl.multiple_of((2 * h + side) * WROWS, WROWS), WROWS) for h in range(2)]
+        part = jnp.concatenate([hidden[:, at] for at in lanes], axis=1)
+        term = jnp.dot(part, weight_ref[rows, :], preferred_element_type=F32)
+        total = term if total is None else total + term
+    return total
+
+
+def near_kernel(here, up1, down1, up2, down2, own_ref, other_ref, out_ref):
     z = lax.axis_index("tp")
     total = None
-    for k, ref in ((0, own), (1, up1), (-1, down1), (2, up2), (-2, down2)):
-        rows = pl.ds(pl.multiple_of(lax.rem(z - k + NZ, NZ) * CH, CH), CH)
-        term = jnp.dot(ref[...], weight_ref[rows, :], preferred_element_type=F32)
+    for k, ref in ((0, here), (1, up1), (-1, down1), (2, up2), (-2, down2)):
+        term = project(lax.rem(z - k + NZ, NZ), ref, own_ref, other_ref)
         total = term if total is None else total + term
     out_ref[...] = total
 
 
-def far_kernel(near_ref, up3, down3, up4, down4, weight_ref, out_ref):
+def far_kernel(near_ref, up3, down3, up4, down4, own_ref, other_ref, out_ref, last):
     z = lax.axis_index("tp")
-
-    def rows(k):
-        return pl.ds(pl.multiple_of(lax.rem(z - k + NZ, NZ) * CH, CH), CH)
-
+    half = TOK // 2
+    last[:half, :] = up4[...]
+    last[half:, :] = down4[...]
     total = near_ref[...]
-    for k, ref in ((3, up3), (-3, down3)):
-        total = total + jnp.dot(ref[...], weight_ref[rows(k), :], preferred_element_type=F32)
-    half = TOK // 2
-    last = weight_ref[rows(4), :]
-    out_ref[:half, :] = (total[:half] + jnp.dot(up4[...], last, preferred_element_type=F32)).astype(BF16)
-    out_ref[half:, :] = (total[half:] + jnp.dot(down4[...], last, preferred_element_type=F32)).astype(BF16)
+    for k, ref in ((3, up3), (-3, down3), (4, last)):
+        total = total + project(lax.rem(z - k + NZ, NZ), ref, own_ref, other_ref)
+    out_ref[...] = total.astype(BF16)
 
 
 def ctx_index(x, y, c):
@@ -390,41 +432,47 @@
     block_shape = struct(GROUPS, ROWS, BLOCKS, LANES)
     table = (GROUPS, (STEPS + 1) * MODES, LANES)
 
-    pay, eb, p256 = call(
-        ends_kernel, (pay_shape, block_shape, state_shape), (key, value, decay, freq, starts),
-        [sig, pltpu.VMEM(table, F32), pltpu.VMEM(table, F32), qs, qs], 20_000_000, 1_500_000)
+    magnitude = jnp.exp(-decay)
+    q_shape = struct(GROUPS, BLOCKS * MODES, LANES)
+    tre, tim, qre, qim, p256 = call(
+        powers_kernel, (struct(*table), struct(*table), q_shape, q_shape, state_shape),
+        (magnitude * jnp.cos(freq), magnitude * jnp.sin(freq)), (), 2_000_000_000, 5_000_000)
+    pay, eb, signal = call(
+        ends_kernel, (pay_shape, block_shape, struct(GROUPS, TOK, LANES)),
+        (key, value, starts, tre, tim, qre, qim), (), 20_000_000, 5_000_000)
     other = move(pay, 0, 0, 1)
-
-    wy = jnp.concatenate([out_weight] + [move(out_weight, 0, k, 0) for k in (1, 2, 3)], axis=0)
+    chip = call(chip_kernel, struct(SENT + WROWS, CH, dtype=BF16), (pay, other, p256, out_weight))
+    near = [move(chip, 0, k, 0) for k in (1, 2, 3)]
+    y, gain = call(
+        local_kernel, (struct(GROUPS, STEPS, BLOCKS, LANES), state_shape),
+        (signal, tre, tim, decay, residue, skip, starts),
+        [pltpu.VMEM((GROUPS, STEPS, LANES), F32)], 30_000_000, 5_000_000)
+    row, before, factor, wy = call(
+        row_kernel, (pay_shape, state_shape, state_shape, struct(NY * WROWS, CH, dtype=BF16)),
+        (chip, *near, p256), [pltpu.VMEM((NY, PAY, CH), F32)])
+    back = [move(row, k, 0, 0) for k in (1, 2)]
+    pz, gz, wy = call(
+        carry_kernel, (block_shape, block_shape, struct(NY * WROWS, CH, dtype=BF16)),
+        (eb, tre, tim, gain, starts, wy),
+        [qs, qs, pltpu.VMEM((GROUPS, 4 * ROWS, LANES), F32)], 30_000_000, 5_000_000)
     wx = [wy] + [move(wy, k, 0, 0) for k in (1, 2, 3)]
-    wo = [move(w, 0, 0, 1) for w in wx]
-    weight = call(weight_kernel, struct(NZ * CH, CH, dtype=BF16), (*wx, *wo), (), 0, 8_000_000)
-
-    chip = call(chip_kernel, pay_shape, (pay, other, p256))
-    near = [move(chip, 0, k, 0) for k in (1, 2, 3)]
-    y, pz, gz, tre, tim = call(
-        local_kernel,
-        (struct(GROUPS, STEPS, BLOCKS, LANES), block_shape, block_shape, struct(*table), struct(*table)),
-        (key, value, decay, freq, residue, skip, starts, eb),
-        [sig, qs, qs, pltpu.VMEM((GROUPS, STEPS, LANES), F32), pltpu.VMEM((GROUPS, 4 * ROWS, LANES), F32)],
-        30_000_000, 5_000_000)
-    row, before, factor = call(
-        row_kernel, (pay_shape, state_shape, state_shape), (chip, *near, p256),
-        [pltpu.VMEM((NY, PAY, CH), F32)])
-    back = [move(row, k, 0, 0) for k in (1, 2)]
     hidden = call(
         gate_kernel, struct(TOK, CH, dtype=BF16),
         (query, y, pz, gz, tre, tim, starts, pay, other, p256, before, factor, *back),
         [sig, pltpu.VMEM((GROUPS, ROWS, LANES), F32)], 20_000_000, 5_000_000)
 
-    half = TOK // 2
+    full, part = struct(TOK, CH, dtype=BF16), struct(TOK // 2, CH, dtype=BF16)
     up1, down1, up2, down2 = turn(hidden, 1), turn(hidden, -1), turn(hidden, 2), turn(hidden, -2)
+    up2, down2, top, bottom, token = call(
+        relay_kernel, (full, full, part, part, struct(16, LANES, dtype=BF16)), (up1, down1, up2, down2))
     up3, down3 = turn(up2, 1), turn(down2, -1)
-    up4, down4 = turn(up2[:half], 2), turn(down2[half:], -2)
-    total = call(near_kernel, struct(TOK, CH), (hidden, up1, down1, up2, down2, weight), (),
+    up4, down4 = turn(top, 2), turn(bottom, -2)
+    own = call(weight_kernel, struct(NZ * CH // 2, CH, dtype=BF16), (move(token, 0, 0, 1), *wx), (), 0, 4_000_000)
+    swapped = move(own, 0, 0, 1)
+    total = call(near_kernel, struct(TOK, CH), (hidden, up1, down1, up2, down2, own, swapped), (),
                  5 * 2 * TOK * CH * CH, 4_000_000)
-    return call(far_kernel, struct(TOK, CH, dtype=BF16), (total, up3, down3, up4, down4, weight), (),
-                3 * 2 * TOK * CH * CH, 4_000_000)
+    return call(far_kernel, full, (total, up3, down3, up4, down4, own, swapped),
+                [pltpu.VMEM((TOK, CH), BF16)], 3 * 2 * TOK * CH * CH, 4_000_000)
 
 
 def solution(mesh):

time: 100 us -> 80.3 us (0.80)
  the two profiles are of different devices: /device:TPU:32 before, /device:TPU:88 now
where the time goes in v2:
time: 80.3 us; the launch traced here: 80.1 us
  waiting for transfers between devices  39.4 us (49%)
  starting transfers between devices  28.7 us (36%)
  Pallas kernels  10.2 us (13%)
  other arithmetic  0.91 us (1%)
    ppermute x8, waiting for transfers between devices, turn(): return lax.ppermute(value, 'tp', [(i, (i + k) % NZ) for i in range(NZ)])  25 us
    ppermute x8, starting transfers between devices, turn(): return lax.ppermute(value, 'tp', [(i, (i + k) % NZ) for i in range(NZ)])  16.5 us
    ppermute x11, waiting for transfers between devices, move(): return lax.ppermute(value, 'ctx', pairs)  14.4 us
    ppermute x11, starting transfers between devices, move(): return lax.ppermute(value, 'ctx', pairs)  12.3 us
    pallas_call x11, Pallas kernels, call(): pl.pallas_call(kernel, out_shape=outs, in_specs=[VMEM] * len(args), out_s...  10.2 us
  transfers between devices with their start and end apart: 19, of which 11 were waited for; matrix products, arithmetic and copies ran while one was open for 0% of the time, Pallas kernels for 5%

profile of v2, /device:TPU:88, one launch (start us, length us, event | category | flops | bytes accessed | tf_op | source)
XLA Modules:
  0.0 80.1 jit_solution(8132059572761953512)
XLA Ops:
  0.0 0.9 %sine_multiply_fusion = (f32[16,512]{1,0:T(8,128)S(1)}, f32[16,512]{1,0:T(8,128)S(1)}) fusion(f32[16,512]{1,0:T(8,128)} %param.13, f32[16,512]{1,0:T(8,128)} %decay_ref.1), kind=kLoop, calls=%fused_computation | loop fusion | flops 24576 | bytes 131072 | tf_op jit(solution)/shard_map/mul | solution.py:439
  2.0 2.6 %shard_map.92 = (f32[40,512]{1,0:T(8,128)S(1)}, f32[4,32,8,128]{3,2,1,0:T(8,128)S(1)}, f32[4,256,128]{2,1,0:T(8,128)S(1)}) custom-call(bf16[256,512]{1,0:T(8,128)(2,1)S(1)} %copy-done, bf16[256,512]{1,0:T(8,128)(2,1)S(1)} %copy-done.1, s32[2,128]{1,0:T(2,128)S(1)} %bitcast.2, f32[4,528,128]{2,1,0:T(8,128)S(1)} %get-tuple-element.27.tre, ...), custom_call_target="tpu_custom_call" | custom-call | flops 20000000 | bytes 5000000 | tf_op jit(solution)/shard_map/pallas_call | solution.py:26
  4.7 1.3 %collective-permute-done.other_ref = f32[40,512]{1,0:T(8,128)S(1)} collective-permute-done((f32[40,512]{1,0:T(8,128)S(1)}, f32[40,512]{1,0:T(8,128)S(1)}, u32[]{:S(2)}, u32[]{:S(2)}) %collective-permute-start) | collective-permute-done | bytes 81952 | tf_op jit(solution)/shard_map/ppermute | solution.py:418
  6.3 2.6 %collective-permute-start.2 = (bf16[208,512]{1,0:T(8,128)(2,1)S(1)}, bf16[208,512]{1,0:T(8,128)(2,1)S(1)}, u32[]{:S(2)}, u32[]{:S(2)}) collective-permute-start(bf16[208,512]{1,0:T(8,128)(2,1)S(1)} %shard_map.94.own_ref), channel_id=1, source_target_pairs={{0,32},{8,40},{16,48},{24,56},{32,0},{40,8},{48,16},{56,24},{64,96... | collective-permute-start | bytes 638984 | tf_op jit(solution)/shard_map/ppermute | solution.py:418
  8.9 5.3 %collective-permute-done.1.one_ref = bf16[208,512]{1,0:T(8,128)(2,1)S(1)} collective-permute-done((bf16[208,512]{1,0:T(8,128)(2,1)S(1)}, bf16[208,512]{1,0:T(8,128)(2,1)S(1)}, u32[]{:S(2)}, u32[]{:S(2)}) %collective-permute-start.1) | collective-permute-done | bytes 213024 | tf_op jit(solution)/shard_map/ppermute | solution.py:418
  14.2 1.8 %collective-permute-done.2.two_ref = bf16[208,512]{1,0:T(8,128)(2,1)S(1)} collective-permute-done((bf16[208,512]{1,0:T(8,128)(2,1)S(1)}, bf16[208,512]{1,0:T(8,128)(2,1)S(1)}, u32[]{:S(2)}, u32[]{:S(2)}) %collective-permute-start.2) | collective-permute-done | bytes 213024 | tf_op jit(solution)/shard_map/ppermute | solution.py:418
  16.0 3.6 %collective-permute-done.3.three_ref = bf16[208,512]{1,0:T(8,128)(2,1)S(1)} collective-permute-done((bf16[208,512]{1,0:T(8,128)(2,1)S(1)}, bf16[208,512]{1,0:T(8,128)(2,1)S(1)}, u32[]{:S(2)}, u32[]{:S(2)}) %collective-permute-start.3) | collective-permute-done | bytes 213024 | tf_op jit(solution)/shard_map/ppermute | solution.py:418
  19.8 1.6 %collective-permute-start.4 = (f32[40,512]{1,0:T(8,128)S(1)}, f32[40,512]{1,0:T(8,128)S(1)}, u32[]{:S(2)}, u32[]{:S(2)}) collective-permute-start(f32[40,512]{1,0:T(8,128)S(1)} %get-tuple-element.42), channel_id=1, source_target_pairs={{0,64},{8,72},{16,80},{24,88},{32,96},{40,104},{48,112},{56,120},{... | collective-permute-start | bytes 245768 | tf_op jit(solution)/shard_map/ppermute | solution.py:418
  21.3 2.7 %collective-permute-start.5 = (f32[40,512]{1,0:T(8,128)S(1)}, f32[40,512]{1,0:T(8,128)S(1)}, u32[]{:S(2)}, u32[]{:S(2)}) collective-permute-start(f32[40,512]{1,0:T(8,128)S(1)} %get-tuple-element.42), channel_id=1, source_target_pairs={{0,128},{8,136},{16,144},{24,152},{32,160},{40,168},{48,176},{56,1... | collective-permute-start | bytes 245768 | tf_op jit(solution)/shard_map/ppermute | solution.py:418
  24.1 2.1 %shard_map.93 = (f32[4,32,8,128]{3,2,1,0:T(8,128)S(1)}, f32[32,512]{1,0:T(8,128)S(1)}) custom-call(f32[4,256,128]{2,1,0:T(8,128)S(1)} %get-tuple-element.31.sig, f32[4,528,128]{2,1,0:T(8,128)S(1)} %get-tuple-element.27.tre, f32[4,528,128]{2,1,0:T(8,128)S(1)} %get-tuple-element.28.tim, f32[16,512]{1,0:T(8,128)S(1)} %copy-done.3, f32[2,16,512]{2,1,0:T(8,128)S(1)} %copy-done.5, ...), custom_call_target="tpu_custom_call" | custom-call | flops 30000000 | bytes 5000000 | tf_op jit(solution)/shard_map/pallas_call | solution.py:26
  26.9 1.3 %collective-permute-done.5.two_ref = f32[40,512]{1,0:T(8,128)S(1)} collective-permute-done((f32[40,512]{1,0:T(8,128)S(1)}, f32[40,512]{1,0:T(8,128)S(1)}, u32[]{:S(2)}, u32[]{:S(2)}) %collective-permute-start.5) | collective-permute-done | bytes 81952 | tf_op jit(solution)/shard_map/ppermute | solution.py:418
  28.2 1.9 %shard_map.97.here = bf16[256,512]{1,0:T(8,128)(2,1)S(1)} custom-call(bf16[256,512]{1,0:T(8,128)(2,1)S(1)} %copy-done.2, f32[4,32,8,128]{3,2,1,0:T(8,128)S(1)} %get-tuple-element.32.y_ref, f32[4,32,8,128]{3,2,1,0:T(8,128)S(1)} %get-tuple-element.38.pz_ref, f32[4,32,8,128]{3,2,1,0:T(8,128)S(1)} %get-tuple-element.39.gz_ref, ...), custom_call_target="tpu_custom_call" | custom-call | flops 20000000 | bytes 5000000 | tf_op jit(solution)/shard_map/pallas_call | solution.py:26
  30.1 2.0 %collective-permute-start.6 = (bf16[256,512]{1,0:T(8,128)(2,1)S(1)}, bf16[256,512]{1,0:T(8,128)(2,1)S(1)}, u32[]{:S(2)}, u32[]{:S(2)}) collective-permute-start(bf16[256,512]{1,0:T(8,128)(2,1)S(1)} %shard_map.97.here), channel_id=1, source_target_pairs={{0,1},{1,2},{2,3},{3,4},{4,5},{5,6},{6,7},{7,0},{8,9},{9,10},{10,1... | collective-permute-start | bytes 786440 | tf_op jit(solution)/shard_map/ppermute | solution.py:422
  32.8 1.7 %collective-permute-start.12 = (bf16[512,512]{1,0:T(8,128)(2,1)S(1)}, bf16[512,512]{1,0:T(8,128)(2,1)S(1)}, u32[]{:S(2)}, u32[]{:S(2)}) collective-permute-start(bf16[512,512]{1,0:T(8,128)(2,1)S(1)} %get-tuple-element.46.refs_0_), channel_id=1, source_target_pairs={{0,128},{8,136},{16,144},{24,152},{32,160},{40,168},{48,176},{56,1... | collective-permute-start | bytes 1572872 | tf_op jit(solution)/shard_map/ppermute | solution.py:418
  34.5 2.2 %collective-permute-start.13 = (bf16[512,512]{1,0:T(8,128)(2,1)S(1)}, bf16[512,512]{1,0:T(8,128)(2,1)S(1)}, u32[]{:S(2)}, u32[]{:S(2)}) collective-permute-start(bf16[512,512]{1,0:T(8,128)(2,1)S(1)} %get-tuple-element.46.refs_0_), channel_id=1, source_target_pairs={{0,192},{8,200},{16,208},{24,216},{32,224},{40,232},{48,240},{56,2... | collective-permute-start | bytes 1572872 | tf_op jit(solution)/shard_map/ppermute | solution.py:418
  37.2 5.7 %collective-permute-start.8 = (bf16[256,512]{1,0:T(8,128)(2,1)S(1)}, bf16[256,512]{1,0:T(8,128)(2,1)S(1)}, u32[]{:S(2)}, u32[]{:S(2)}) collective-permute-start(bf16[256,512]{1,0:T(8,128)(2,1)S(1)} %shard_map.97.here), channel_id=1, source_target_pairs={{0,2},{1,3},{2,4},{3,5},{4,6},{5,7},{6,0},{7,1},{8,10},{9,11},{10,... | collective-permute-start | bytes 786440 | tf_op jit(solution)/shard_map/ppermute | solution.py:422
  43.0 8.4 %collective-permute-done.8.up2 = bf16[256,512]{1,0:T(8,128)(2,1)S(1)} collective-permute-done((bf16[256,512]{1,0:T(8,128)(2,1)S(1)}, bf16[256,512]{1,0:T(8,128)(2,1)S(1)}, u32[]{:S(2)}, u32[]{:S(2)}) %collective-permute-start.8) | collective-permute-done | bytes 262176 | tf_op jit(solution)/shard_map/ppermute | solution.py:422
  51.4 4.9 %collective-permute-done.9.down2 = bf16[256,512]{1,0:T(8,128)(2,1)S(1)} collective-permute-done((bf16[256,512]{1,0:T(8,128)(2,1)S(1)}, bf16[256,512]{1,0:T(8,128)(2,1)S(1)}, u32[]{:S(2)}, u32[]{:S(2)}) %collective-permute-start.9) | collective-permute-done | bytes 262176 | tf_op jit(solution)/shard_map/ppermute | solution.py:422
  56.4 1.2 %collective-permute-done.10.token_ref = bf16[16,128]{1,0:T(8,128)(2,1)S(1)} collective-permute-done((bf16[16,128]{1,0:T(8,128)(2,1)S(1)}, bf16[16,128]{1,0:T(8,128)(2,1)S(1)}, u32[]{:S(2)}, u32[]{:S(2)}) %collective-permute-start.10) | collective-permute-done | bytes 4128 | tf_op jit(solution)/shard_map/ppermute | solution.py:418
  58.2 3.0 %collective-permute-start.15 = (bf16[256,512]{1,0:T(8,128)(2,1)S(1)}, bf16[256,512]{1,0:T(8,128)(2,1)S(1)}, u32[]{:S(2)}, u32[]{:S(2)}) collective-permute-start(bf16[256,512]{1,0:T(8,128)(2,1)S(1)} %get-tuple-element.43.up2), channel_id=1, source_target_pairs={{0,1},{1,2},{2,3},{3,4},{4,5},{5,6},{6,7},{7,0},{8,9},{9,10},{10,1... | collective-permute-start | bytes 786440 | tf_op jit(solution)/shard_map/ppermute | solution.py:422
  61.2 5.6 %collective-permute-start.17 = (bf16[128,512]{1,0:T(8,128)(2,1)S(1)}, bf16[128,512]{1,0:T(8,128)(2,1)S(1)}, u32[]{:S(2)}, u32[]{:S(2)}) collective-permute-start(bf16[128,512]{1,0:T(8,128)(2,1)S(1)} %get-tuple-element.47), channel_id=1, source_target_pairs={{0,2},{1,3},{2,4},{3,5},{4,6},{5,7},{6,0},{7,1},{8,10},{9,11},{10,... | collective-permute-start | bytes 393224 | tf_op jit(solution)/shard_map/ppermute | solution.py:422
  67.7 5.3 %collective-permute-done.17.up4 = bf16[128,512]{1,0:T(8,128)(2,1)S(1)} collective-permute-done((bf16[128,512]{1,0:T(8,128)(2,1)S(1)}, bf16[128,512]{1,0:T(8,128)(2,1)S(1)}, u32[]{:S(2)}, u32[]{:S(2)}) %collective-permute-start.17) | collective-permute-done | bytes 131104 | tf_op jit(solution)/shard_map/ppermute | solution.py:422
  73.0 5.8 %collective-permute-done.18.down4 = bf16[128,512]{1,0:T(8,128)(2,1)S(1)} collective-permute-done((bf16[128,512]{1,0:T(8,128)(2,1)S(1)}, bf16[128,512]{1,0:T(8,128)(2,1)S(1)}, u32[]{:S(2)}, u32[]{:S(2)}) %collective-permute-start.18) | collective-permute-done | bytes 131104 | tf_op jit(solution)/shard_map/ppermute | solution.py:422
  78.8 1.3 %shard_map.101 = bf16[256,512]{1,0:T(8,128)(2,1)} custom-call(f32[256,512]{1,0:T(8,128)S(1)} %shard_map.100.near_ref, bf16[256,512]{1,0:T(8,128)(2,1)S(1)} %collective-permute-done.15.up3, bf16[256,512]{1,0:T(8,128)(2,1)S(1)} %collective-permute-done.16.down3, bf16[128,512]{1,0:T(8,128)(2,1)S(1)} %collective-permute-done.17.up4, ...), custom_call_target="tpu_custom_call" | custom-call | flops 402653184 | bytes 4000000 | tf_op jit(solution)/shard_map/pallas_call | solution.py:26
  (42 shorter events, 5.2 us)
Async XLA Ops:
  1.3 4.7 %copy-start.4 = (bf16[128,512]{1,0:T(8,128)(2,1)S(1)}, bf16[128,512]{1,0:T(8,128)(2,1)}, u32[]{:S(2)}) copy-start(bf16[128,512]{1,0:T(8,128)(2,1)} %weight_ref.1) | copy-start | bytes 393220
  1.9 22.1 %copy-start.3 = (f32[16,512]{1,0:T(8,128)S(1)}, f32[16,512]{1,0:T(8,128)}, u32[]{:S(2)}) copy-start(f32[16,512]{1,0:T(8,128)} %decay_ref.1) | copy-start | bytes 98308
  1.9 22.1 %copy-start.5 = (f32[2,16,512]{2,1,0:T(8,128)S(1)}, f32[2,16,512]{2,1,0:T(8,128)}, u32[]{:S(2)}) copy-start(f32[2,16,512]{2,1,0:T(8,128)} %res_ref.1) | copy-start | bytes 196612
  2.0 22.1 %copy-start.7 = (f32[512]{0:T(512)S(1)}, f32[512]{0:T(512)}, u32[]{:S(2)}) copy-start(f32[512]{0:T(512)} %param.15) | copy-start | bytes 6148
  4.6 1.4 %collective-permute-start = (f32[40,512]{1,0:T(8,128)S(1)}, f32[40,512]{1,0:T(8,128)S(1)}, u32[]{:S(2)}, u32[]{:S(2)}) collective-permute-start(f32[40,512]{1,0:T(8,128)S(1)} %get-tuple-element.35.own_ref), channel_id=1, source_target_pairs={{0,8},{8,0},{16,24},{24,16},{32,40},{40,32},{48,56},{56,48},{64,72... | collective-permute-start | bytes 245768 | tf_op jit(solution)/shard_map/ppermute | solution.py:418
  6.0 8.2 %collective-permute-start.1 = (bf16[208,512]{1,0:T(8,128)(2,1)S(1)}, bf16[208,512]{1,0:T(8,128)(2,1)S(1)}, u32[]{:S(2)}, u32[]{:S(2)}) collective-permute-start(bf16[208,512]{1,0:T(8,128)(2,1)S(1)} %shard_map.94.own_ref), channel_id=1, source_target_pairs={{0,16},{8,24},{16,32},{24,40},{32,48},{40,56},{48,0},{56,8},{64,80... | collective-permute-start | bytes 638984 | tf_op jit(solution)/shard_map/ppermute | solution.py:418
  6.3 9.6 %collective-permute-start.2 = (bf16[208,512]{1,0:T(8,128)(2,1)S(1)}, bf16[208,512]{1,0:T(8,128)(2,1)S(1)}, u32[]{:S(2)}, u32[]{:S(2)}) collective-permute-start(bf16[208,512]{1,0:T(8,128)(2,1)S(1)} %shard_map.94.own_ref), channel_id=1, source_target_pairs={{0,32},{8,40},{16,48},{24,56},{32,0},{40,8},{48,16},{56,24},{64,96... | collective-permute-start | bytes 638984 | tf_op jit(solution)/shard_map/ppermute | solution.py:418
  8.9 10.7 %collective-permute-start.3 = (bf16[208,512]{1,0:T(8,128)(2,1)S(1)}, bf16[208,512]{1,0:T(8,128)(2,1)S(1)}, u32[]{:S(2)}, u32[]{:S(2)}) collective-permute-start(bf16[208,512]{1,0:T(8,128)(2,1)S(1)} %shard_map.94.own_ref), channel_id=1, source_target_pairs={{0,48},{8,56},{16,0},{24,8},{32,16},{40,24},{48,32},{56,40},{64,11... | collective-permute-start | bytes 638984 | tf_op jit(solution)/shard_map/ppermute | solution.py:418
  19.8 7.1 %collective-permute-start.4 = (f32[40,512]{1,0:T(8,128)S(1)}, f32[40,512]{1,0:T(8,128)S(1)}, u32[]{:S(2)}, u32[]{:S(2)}) collective-permute-start(f32[40,512]{1,0:T(8,128)S(1)} %get-tuple-element.42), channel_id=1, source_target_pairs={{0,64},{8,72},{16,80},{24,88},{32,96},{40,104},{48,112},{56,120},{... | collective-permute-start | bytes 245768 | tf_op jit(solution)/shard_map/ppermute | solution.py:418
  21.3 6.8 %collective-permute-start.5 = (f32[40,512]{1,0:T(8,128)S(1)}, f32[40,512]{1,0:T(8,128)S(1)}, u32[]{:S(2)}, u32[]{:S(2)}) collective-permute-start(f32[40,512]{1,0:T(8,128)S(1)} %get-tuple-element.42), channel_id=1, source_target_pairs={{0,128},{8,136},{16,144},{24,152},{32,160},{40,168},{48,176},{56,1... | collective-permute-start | bytes 245768 | tf_op jit(solution)/shard_map/ppermute | solution.py:418
  26.2 2.0 %copy-start.2 = (bf16[256,512]{1,0:T(8,128)(2,1)S(1)}, bf16[256,512]{1,0:T(8,128)(2,1)}, u32[]{:S(2)}) copy-start(bf16[256,512]{1,0:T(8,128)(2,1)} %query_ref.1) | copy-start | bytes 786436
  30.1 7.2 %collective-permute-start.6 = (bf16[256,512]{1,0:T(8,128)(2,1)S(1)}, bf16[256,512]{1,0:T(8,128)(2,1)S(1)}, u32[]{:S(2)}, u32[]{:S(2)}) collective-permute-start(bf16[256,512]{1,0:T(8,128)(2,1)S(1)} %shard_map.97.here), channel_id=1, source_target_pairs={{0,1},{1,2},{2,3},{3,4},{4,5},{5,6},{6,7},{7,0},{8,9},{9,10},{10,1... | collective-permute-start | bytes 786440 | tf_op jit(solution)/shard_map/ppermute | solution.py:422
  32.1 10.9 %collective-permute-start.7 = (bf16[256,512]{1,0:T(8,128)(2,1)S(1)}, bf16[256,512]{1,0:T(8,128)(2,1)S(1)}, u32[]{:S(2)}, u32[]{:S(2)}) collective-permute-start(bf16[256,512]{1,0:T(8,128)(2,1)S(1)} %shard_map.97.here), channel_id=1, source_target_pairs={{0,7},{1,0},{2,1},{3,2},{4,3},{5,4},{6,5},{7,6},{8,15},{9,8},{10,9... | collective-permute-start | bytes 786440 | tf_op jit(solution)/shard_map/ppermute | solution.py:422
  32.2 25.4 %collective-permute-start.11 = (bf16[512,512]{1,0:T(8,128)(2,1)S(1)}, bf16[512,512]{1,0:T(8,128)(2,1)S(1)}, u32[]{:S(2)}, u32[]{:S(2)}) collective-permute-start(bf16[512,512]{1,0:T(8,128)(2,1)S(1)} %get-tuple-element.46.refs_0_), channel_id=1, source_target_pairs={{0,64},{8,72},{16,80},{24,88},{32,96},{40,104},{48,112},{56,120},{... | collective-permute-start | bytes 1572872 | tf_op jit(solution)/shard_map/ppermute | solution.py:418
  32.8 24.8 %collective-permute-start.12 = (bf16[512,512]{1,0:T(8,128)(2,1)S(1)}, bf16[512,512]{1,0:T(8,128)(2,1)S(1)}, u32[]{:S(2)}, u32[]{:S(2)}) collective-permute-start(bf16[512,512]{1,0:T(8,128)(2,1)S(1)} %get-tuple-element.46.refs_0_), channel_id=1, source_target_pairs={{0,128},{8,136},{16,144},{24,152},{32,160},{40,168},{48,176},{56,1... | collective-permute-start | bytes 1572872 | tf_op jit(solution)/shard_map/ppermute | solution.py:418
  34.5 23.1 %collective-permute-start.13 = (bf16[512,512]{1,0:T(8,128)(2,1)S(1)}, bf16[512,512]{1,0:T(8,128)(2,1)S(1)}, u32[]{:S(2)}, u32[]{:S(2)}) collective-permute-start(bf16[512,512]{1,0:T(8,128)(2,1)S(1)} %get-tuple-element.46.refs_0_), channel_id=1, source_target_pairs={{0,192},{8,200},{16,208},{24,216},{32,224},{40,232},{48,240},{56,2... | collective-permute-start | bytes 1572872 | tf_op jit(solution)/shard_map/ppermute | solution.py:418
  37.2 14.1 %collective-permute-start.8 = (bf16[256,512]{1,0:T(8,128)(2,1)S(1)}, bf16[256,512]{1,0:T(8,128)(2,1)S(1)}, u32[]{:S(2)}, u32[]{:S(2)}) collective-permute-start(bf16[256,512]{1,0:T(8,128)(2,1)S(1)} %shard_map.97.here), channel_id=1, source_target_pairs={{0,2},{1,3},{2,4},{3,5},{4,6},{5,7},{6,0},{7,1},{8,10},{9,11},{10,... | collective-permute-start | bytes 786440 | tf_op jit(solution)/shard_map/ppermute | solution.py:422
  42.9 13.3 %collective-permute-start.9 = (bf16[256,512]{1,0:T(8,128)(2,1)S(1)}, bf16[256,512]{1,0:T(8,128)(2,1)S(1)}, u32[]{:S(2)}, u32[]{:S(2)}) collective-permute-start(bf16[256,512]{1,0:T(8,128)(2,1)S(1)} %shard_map.97.here), channel_id=1, source_target_pairs={{0,6},{1,7},{2,0},{3,1},{4,2},{5,3},{6,4},{7,5},{8,14},{9,15},{10,... | collective-permute-start | bytes 786440 | tf_op jit(solution)/shard_map/ppermute | solution.py:422
  56.3 1.3 %collective-permute-start.10 = (bf16[16,128]{1,0:T(8,128)(2,1)S(1)}, bf16[16,128]{1,0:T(8,128)(2,1)S(1)}, u32[]{:S(2)}, u32[]{:S(2)}) collective-permute-start(bf16[16,128]{1,0:T(8,128)(2,1)S(1)} %get-tuple-element.45), channel_id=1, source_target_pairs={{0,8},{8,0},{16,24},{24,16},{32,40},{40,32},{48,56},{56,48},{64,72... | collective-permute-start | bytes 12296 | tf_op jit(solution)/shard_map/ppermute | solution.py:418
  57.8 9.1 %collective-permute-start.14 = (bf16[2048,512]{1,0:T(8,128)(2,1)S(1)}, bf16[2048,512]{1,0:T(8,128)(2,1)S(1)}, u32[]{:S(2)}, u32[]{:S(2)}) collective-permute-start(bf16[2048,512]{1,0:T(8,128)(2,1)S(1)} %shard_map.99.own_ref), channel_id=1, source_target_pairs={{0,8},{8,0},{16,24},{24,16},{32,40},{40,32},{48,56},{56,48},{64,72... | collective-permute-start | bytes 6291464 | tf_op jit(solution)/shard_map/ppermute | solution.py:418
  58.2 20.6 %collective-permute-start.15 = (bf16[256,512]{1,0:T(8,128)(2,1)S(1)}, bf16[256,512]{1,0:T(8,128)(2,1)S(1)}, u32[]{:S(2)}, u32[]{:S(2)}) collective-permute-start(bf16[256,512]{1,0:T(8,128)(2,1)S(1)} %get-tuple-element.43.up2), channel_id=1, source_target_pairs={{0,1},{1,2},{2,3},{3,4},{4,5},{5,6},{6,7},{7,0},{8,9},{9,10},{10,1... | collective-permute-start | bytes 786440 | tf_op jit(solution)/shard_map/ppermute | solution.py:422
  61.2 17.6 %collective-permute-start.16 = (bf16[256,512]{1,0:T(8,128)(2,1)S(1)}, bf16[256,512]{1,0:T(8,128)(2,1)S(1)}, u32[]{:S(2)}, u32[]{:S(2)}) collective-permute-start(bf16[256,512]{1,0:T(8,128)(2,1)S(1)} %get-tuple-element.44.down2), channel_id=1, source_target_pairs={{0,7},{1,0},{2,1},{3,2},{4,3},{5,4},{6,5},{7,6},{8,15},{9,8},{10,9... | collective-permute-start | bytes 786440 | tf_op jit(solution)/shard_map/ppermute | solution.py:422
  61.2 11.8 %collective-permute-start.17 = (bf16[128,512]{1,0:T(8,128)(2,1)S(1)}, bf16[128,512]{1,0:T(8,128)(2,1)S(1)}, u32[]{:S(2)}, u32[]{:S(2)}) collective-permute-start(bf16[128,512]{1,0:T(8,128)(2,1)S(1)} %get-tuple-element.47), channel_id=1, source_target_pairs={{0,2},{1,3},{2,4},{3,5},{4,6},{5,7},{6,0},{7,1},{8,10},{9,11},{10,... | collective-permute-start | bytes 393224 | tf_op jit(solution)/shard_map/ppermute | solution.py:422
  66.9 12.0 %collective-permute-start.18 = (bf16[128,512]{1,0:T(8,128)(2,1)S(1)}, bf16[128,512]{1,0:T(8,128)(2,1)S(1)}, u32[]{:S(2)}, u32[]{:S(2)}) collective-permute-start(bf16[128,512]{1,0:T(8,128)(2,1)S(1)} %get-tuple-element.48), channel_id=1, source_target_pairs={{0,6},{1,7},{2,0},{3,1},{4,2},{5,3},{6,4},{7,5},{8,14},{9,15},{10,... | collective-permute-start | bytes 393224 | tf_op jit(solution)/shard_map/ppermute | solution.py:422
  (3 other events, 3.0 us)

commit v3 on v2

--- a/solution.py
+++ b/solution.py
@@ -195,8 +195,8 @@
     lax.fori_loop(0, GROUPS, group, 0)
 
 
-def carry_kernel(eb_ref, tre, tim, weight_ref, starts_ref, wy_ref, pz_ref, gz_ref, later_ref, qre, qim, rows_):
-    later_ref[...] = wy_ref[...]
+def carry_kernel(eb_ref, tre, tim, weight_ref, starts_ref, after_ref,
+                 pz_ref, gz_ref, qre, qim, rows_):
     s0 = first_start(starts_ref)
     b0 = s0 // STEPS
     blocks = block_iota()
@@ -263,7 +263,7 @@
     return parts, ref[2 * ROWS:2 * ROWS + 8, :].astype(F32)[:1]
 
 
-def chip_kernel(own_ref, other_ref, p256_ref, weight_ref, sent_ref):
+def chip_kernel(own_ref, other_ref, p256_ref, sent_ref):
     core = lax.axis_index("ctx") % NC
     first = (core == 0).astype(F32)
     own, other = halves(own_ref), halves(other_ref)
@@ -273,11 +273,9 @@
     late_thru = first * other_thru + (1.0 - first) * own_thru
     moved = cmul(halves(p256_ref), early)
     put_state(sent_ref, [late_thru * a + b for a, b in zip(moved, late)], own_thru * other_thru)
-    sent_ref[SENT:, :] = weight_ref[...]
-
-
-def row_kernel(own_ref, one_ref, two_ref, three_ref, p256_ref, pay_ref, before_ref, factor_ref, wy_ref,
-               held):
+
+
+def row_kernel(own_ref, one_ref, two_ref, three_ref, p256_ref, pay_ref, before_ref, factor_ref, held):
     mine = (lax.axis_index("ctx") // NC) % NY
     for k, ref in enumerate((own_ref, one_ref, two_ref, three_ref)):
         there = lax.rem(mine - k + NY, NY)
@@ -285,7 +283,6 @@
         held[there, :MODES, :] = state[0]
         held[there, MODES:ROWS, :] = state[1]
         held[there, ROWS:, :] = jnp.broadcast_to(thru, (PAY - ROWS, CH))
-        wy_ref[pl.ds(pl.multiple_of(there * WROWS, WROWS), WROWS), :] = ref[SENT:, :]
     p512 = square(halves(p256_ref))
     state = (jnp.zeros((MODES, CH), F32),) * 2
     factor = (jnp.ones((MODES, CH), F32), jnp.zeros((MODES, CH), F32))
@@ -358,53 +355,24 @@
         hidden_ref[:, lanes] = (query_ref[:, lanes].astype(F32) * conv[g]).astype(BF16)
 
 
-def weight_kernel(token_ref, *refs):
-    pieces, out_ref = refs[:NX], refs[NX]
-    x = lax.axis_index("ctx") // (NC * NY)
-    for dx in range(NX):
-        there = lax.rem(x - dx + NX, NX)
-        rows = pl.ds(pl.multiple_of(there * NY * WROWS, NY * WROWS), NY * WROWS)
-        out_ref[rows, :] = pieces[dx][...]
-
-
-def relay_kernel(up1, down1, up2, down2, up2_ref, down2_ref, top_ref, bottom_ref, token_ref):
+def relay_kernel(up1, down1, up2, down2, up2_ref, down2_ref, top_ref, bottom_ref):
     half = TOK // 2
     up2_ref[...] = up2[...]
     down2_ref[...] = down2[...]
     top_ref[...] = up2[:half, :]
     bottom_ref[...] = down2[half:, :]
-    token_ref[...] = up1[:16, :LANES] + down1[:16, :LANES]
-
-
-def project(z, hidden, own_ref, other_ref):
-    core = lax.axis_index("ctx") % NC
-    rows = pl.ds(pl.multiple_of(z * 2 * WROWS, 2 * WROWS), 2 * WROWS)
-    total = None
-    for side, weight_ref in ((core, own_ref), (1 - core, other_ref)):
-        lanes = [pl.ds(pl.multiple_of((2 * h + side) * WROWS, WROWS), WROWS) for h in range(2)]
-        part = jnp.concatenate([hidden[:, at] for at in lanes], axis=1)
-        term = jnp.dot(part, weight_ref[rows, :], preferred_element_type=F32)
-        total = term if total is None else total + term
-    return total
-
-
-def near_kernel(here, up1, down1, up2, down2, own_ref, other_ref, out_ref):
-    z = lax.axis_index("tp")
-    total = None
-    for k, ref in ((0, here), (1, up1), (-1, down1), (2, up2), (-2, down2)):
-        term = project(lax.rem(z - k + NZ, NZ), ref, own_ref, other_ref)
-        total = term if total is None else total + term
-    out_ref[...] = total
-
-
-def far_kernel(near_ref, up3, down3, up4, down4, own_ref, other_ref, out_ref, last):
+
+
+def project_kernel(here, up1, down1, up2, down2, up3, down3, up4, down4, weight_ref, out_ref, last):
     z = lax.axis_index("tp")
     half = TOK // 2
     last[:half, :] = up4[...]
     last[half:, :] = down4[...]
-    total = near_ref[...]
-    for k, ref in ((3, up3), (-3, down3), (4, last)):
-        total = total + project(lax.rem(z - k + NZ, NZ), ref, own_ref, other_ref)
+    total = None
+    for k, hidden in enumerate((here, up1, up2, up3, last, down3, down2, down1)):
+        rows = pl.ds(pl.multiple_of(lax.rem(z - k + NZ, NZ) * CH, CH), CH)
+        term = jnp.dot(hidden[...], weight_ref[rows, :], preferred_element_type=F32)
+        total = term if total is None else total + term
     out_ref[...] = total.astype(BF16)
 
 
@@ -432,6 +400,7 @@
     block_shape = struct(GROUPS, ROWS, BLOCKS, LANES)
     table = (GROUPS, (STEPS + 1) * MODES, LANES)
 
+    weight = lax.all_gather(out_weight, "ctx", axis=0, tiled=True)
     magnitude = jnp.exp(-decay)
     q_shape = struct(GROUPS, BLOCKS * MODES, LANES)
     tre, tim, qre, qim, p256 = call(
@@ -441,21 +410,19 @@
         ends_kernel, (pay_shape, block_shape, struct(GROUPS, TOK, LANES)),
         (key, value, starts, tre, tim, qre, qim), (), 20_000_000, 5_000_000)
     other = move(pay, 0, 0, 1)
-    chip = call(chip_kernel, struct(SENT + WROWS, CH, dtype=BF16), (pay, other, p256, out_weight))
+    chip = call(chip_kernel, struct(SENT, CH, dtype=BF16), (pay, other, p256))
     near = [move(chip, 0, k, 0) for k in (1, 2, 3)]
     y, gain = call(
         local_kernel, (struct(GROUPS, STEPS, BLOCKS, LANES), state_shape),
         (signal, tre, tim, decay, residue, skip, starts),
         [pltpu.VMEM((GROUPS, STEPS, LANES), F32)], 30_000_000, 5_000_000)
-    row, before, factor, wy = call(
-        row_kernel, (pay_shape, state_shape, state_shape, struct(NY * WROWS, CH, dtype=BF16)),
+    row, before, factor = call(
+        row_kernel, (pay_shape, state_shape, state_shape),
         (chip, *near, p256), [pltpu.VMEM((NY, PAY, CH), F32)])
     back = [move(row, k, 0, 0) for k in (1, 2)]
-    pz, gz, wy = call(
-        carry_kernel, (block_shape, block_shape, struct(NY * WROWS, CH, dtype=BF16)),
-        (eb, tre, tim, gain, starts, wy),
+    pz, gz = call(
+        carry_kernel, (block_shape, block_shape), (eb, tre, tim, gain, starts, row),
         [qs, qs, pltpu.VMEM((GROUPS, 4 * ROWS, LANES), F32)], 30_000_000, 5_000_000)
-    wx = [wy] + [move(wy, k, 0, 0) for k in (1, 2, 3)]
     hidden = call(
         gate_kernel, struct(TOK, CH, dtype=BF16),
         (query, y, pz, gz, tre, tim, starts, pay, other, p256, before, factor, *back),
@@ -463,16 +430,13 @@
 
     full, part = struct(TOK, CH, dtype=BF16), struct(TOK // 2, CH, dtype=BF16)
     up1, down1, up2, down2 = turn(hidden, 1), turn(hidden, -1), turn(hidden, 2), turn(hidden, -2)
-    up2, down2, top, bottom, token = call(
-        relay_kernel, (full, full, part, part, struct(16, LANES, dtype=BF16)), (up1, down1, up2, down2))
+    up2, down2, top, bottom = call(relay_kernel, (full, full, part, part), (up1, down1, up2, down2))
     up3, down3 = turn(up2, 1), turn(down2, -1)
     up4, down4 = turn(top, 2), turn(bottom, -2)
-    own = call(weight_kernel, struct(NZ * CH // 2, CH, dtype=BF16), (move(token, 0, 0, 1), *wx), (), 0, 4_000_000)
-    swapped = move(own, 0, 0, 1)
-    total = call(near_kernel, struct(TOK, CH), (hidden, up1, down1, up2, down2, own, swapped), (),
-                 5 * 2 * TOK * CH * CH, 4_000_000)
-    return call(far_kernel, full, (total, up3, down3, up4, down4, own, swapped),
-                [pltpu.VMEM((TOK, CH), BF16)], 3 * 2 * TOK * CH * CH, 4_000_000)
+    return call(
+        project_kernel, full,
+        (hidden, up1, down1, up2, down2, up3, down3, up4, down4, weight),
+        [pltpu.VMEM((TOK, CH), BF16)], 2 * TOK * CH * CH * NZ, 7_000_000)
 
 
 def solution(mesh):

time: 80.3 us -> 81.4 us (1.014)
  the two profiles are of different devices: /device:TPU:88 before, /device:TPU:2 now
where the time goes in v3:
time: 81.4 us; the launch traced here: 81.2 us
  starting transfers between devices  27.5 us (34%)
  waiting for transfers between devices  26.6 us (33%)
  between operations  13.5 us (17%)
  Pallas kernels  12 us (15%)
  other arithmetic  0.91 us (1%)
    ppermute x8, waiting for transfers between devices, turn(): return lax.ppermute(value, 'tp', [(i, (i + k) % NZ) for i in range(NZ)])  20 us
    ppermute x8, starting transfers between devices, turn(): return lax.ppermute(value, 'tp', [(i, (i + k) % NZ) for i in range(NZ)])  17.9 us
    pallas_call x9, Pallas kernels, call(): pl.pallas_call(kernel, out_shape=outs, in_specs=[VMEM] * len(args), out_s...  12 us
    ppermute x6, starting transfers between devices, move(): return lax.ppermute(value, 'ctx', pairs)  9.54 us
    ppermute x6, waiting for transfers between devices, move(): return lax.ppermute(value, 'ctx', pairs)  5.89 us
  transfers between devices with their start and end apart: 15, of which 10 were waited for; matrix products, arithmetic and copies ran while one was open for 1% of the time, Pallas kernels for 10%

profile of v3, /device:TPU:2, one launch (start us, length us, event | category | flops | bytes accessed | tf_op | source)
XLA Modules:
  0.0 81.2 jit_solution(11744923288444766326)
XLA Ops:
  9.2 2.6 %shard_map.92 = (f32[40,512]{1,0:T(8,128)S(1)}, f32[4,32,8,128]{3,2,1,0:T(8,128)S(1)}, f32[4,256,128]{2,1,0:T(8,128)S(1)}) custom-call(bf16[256,512]{1,0:T(8,128)(2,1)S(1)} %copy-done, bf16[256,512]{1,0:T(8,128)(2,1)S(1)} %copy-done.1, s32[2,128]{1,0:T(2,128)S(1)} %bitcast.2, f32[4,528,128]{2,1,0:T(8,128)S(1)} %get-tuple-element.24.tre, ...), custom_call_target="tpu_custom_call" | custom-call | flops 20000000 | bytes 5000000 | tf_op jit(solution)/shard_map/pallas_call | solution.py:26
  12.0 1.3 %collective-permute-done.other_ref = f32[40,512]{1,0:T(8,128)S(1)} collective-permute-done((f32[40,512]{1,0:T(8,128)S(1)}, f32[40,512]{1,0:T(8,128)S(1)}, u32[]{:S(2)}, u32[]{:S(2)}) %collective-permute-start) | collective-permute-done | bytes 81952 | tf_op jit(solution)/shard_map/ppermute | solution.py:386
  13.3 1.7 %collective-permute-start.1 = (bf16[80,512]{1,0:T(8,128)(2,1)S(1)}, bf16[80,512]{1,0:T(8,128)(2,1)S(1)}, u32[]{:S(2)}, u32[]{:S(2)}) collective-permute-start(bf16[80,512]{1,0:T(8,128)(2,1)S(1)} %shard_map.94.own_ref), channel_id=1, source_target_pairs={{0,16},{8,24},{16,32},{24,40},{32,48},{40,56},{48,0},{56,8},{64,80... | collective-permute-start | bytes 245768 | tf_op jit(solution)/shard_map/ppermute | solution.py:386
  14.9 2.9 %collective-permute-start.2 = (bf16[80,512]{1,0:T(8,128)(2,1)S(1)}, bf16[80,512]{1,0:T(8,128)(2,1)S(1)}, u32[]{:S(2)}, u32[]{:S(2)}) collective-permute-start(bf16[80,512]{1,0:T(8,128)(2,1)S(1)} %shard_map.94.own_ref), channel_id=1, source_target_pairs={{0,32},{8,40},{16,48},{24,56},{32,0},{40,8},{48,16},{56,24},{64,96... | collective-permute-start | bytes 245768 | tf_op jit(solution)/shard_map/ppermute | solution.py:386
  17.8 1.3 %collective-permute-start.3 = (bf16[80,512]{1,0:T(8,128)(2,1)S(1)}, bf16[80,512]{1,0:T(8,128)(2,1)S(1)}, u32[]{:S(2)}, u32[]{:S(2)}) collective-permute-start(bf16[80,512]{1,0:T(8,128)(2,1)S(1)} %shard_map.94.own_ref), channel_id=1, source_target_pairs={{0,48},{8,56},{16,0},{24,8},{32,16},{40,24},{48,32},{56,40},{64,11... | collective-permute-start | bytes 245768 | tf_op jit(solution)/shard_map/ppermute | solution.py:386
  19.2 2.9 %collective-permute-done.2.two_ref = bf16[80,512]{1,0:T(8,128)(2,1)S(1)} collective-permute-done((bf16[80,512]{1,0:T(8,128)(2,1)S(1)}, bf16[80,512]{1,0:T(8,128)(2,1)S(1)}, u32[]{:S(2)}, u32[]{:S(2)}) %collective-permute-start.2) | collective-permute-done | bytes 81952 | tf_op jit(solution)/shard_map/ppermute | solution.py:386
  22.4 1.6 %collective-permute-start.4 = (f32[40,512]{1,0:T(8,128)S(1)}, f32[40,512]{1,0:T(8,128)S(1)}, u32[]{:S(2)}, u32[]{:S(2)}) collective-permute-start(f32[40,512]{1,0:T(8,128)S(1)} %get-tuple-element.34.after_ref), channel_id=1, source_target_pairs={{0,64},{8,72},{16,80},{24,88},{32,96},{40,104},{48,112},{56,120},{... | collective-permute-start | bytes 245768 | tf_op jit(solution)/shard_map/ppermute | solution.py:386
  24.0 2.0 %collective-permute-start.5 = (f32[40,512]{1,0:T(8,128)S(1)}, f32[40,512]{1,0:T(8,128)S(1)}, u32[]{:S(2)}, u32[]{:S(2)}) collective-permute-start(f32[40,512]{1,0:T(8,128)S(1)} %get-tuple-element.34.after_ref), channel_id=1, source_target_pairs={{0,128},{8,136},{16,144},{24,152},{32,160},{40,168},{48,176},{56,1... | collective-permute-start | bytes 245768 | tf_op jit(solution)/shard_map/ppermute | solution.py:386
  26.0 2.1 %shard_map.93 = (f32[4,32,8,128]{3,2,1,0:T(8,128)S(1)}, f32[32,512]{1,0:T(8,128)S(1)}) custom-call(f32[4,256,128]{2,1,0:T(8,128)S(1)} %get-tuple-element.28.sig, f32[4,528,128]{2,1,0:T(8,128)S(1)} %get-tuple-element.24.tre, f32[4,528,128]{2,1,0:T(8,128)S(1)} %get-tuple-element.25.tim, f32[16,512]{1,0:T(8,128)S(1)} %copy-done.3, f32[2,16,512]{2,1,0:T(8,128)S(1)} %copy-done.4, ...), custom_call_target="tpu_custom_call" | custom-call | flops 30000000 | bytes 5000000 | tf_op jit(solution)/shard_map/pallas_call | solution.py:26
  28.7 1.5 %collective-permute-done.5.two_ref = f32[40,512]{1,0:T(8,128)S(1)} collective-permute-done((f32[40,512]{1,0:T(8,128)S(1)}, f32[40,512]{1,0:T(8,128)S(1)}, u32[]{:S(2)}, u32[]{:S(2)}) %collective-permute-start.5) | collective-permute-done | bytes 81952 | tf_op jit(solution)/shard_map/ppermute | solution.py:386
  30.3 1.9 %shard_map.97.here = bf16[256,512]{1,0:T(8,128)(2,1)S(1)} custom-call(bf16[256,512]{1,0:T(8,128)(2,1)S(1)} %copy-done.2, f32[4,32,8,128]{3,2,1,0:T(8,128)S(1)} %get-tuple-element.29.y_ref, f32[4,32,8,128]{3,2,1,0:T(8,128)S(1)} %get-tuple-element.35.pz_ref, f32[4,32,8,128]{3,2,1,0:T(8,128)S(1)} %get-tuple-element.36.gz_ref, ...), custom_call_target="tpu_custom_call" | custom-call | flops 20000000 | bytes 5000000 | tf_op jit(solution)/shard_map/pallas_call | solution.py:26
  32.2 1.6 %collective-permute-start.6 = (bf16[256,512]{1,0:T(8,128)(2,1)S(1)}, bf16[256,512]{1,0:T(8,128)(2,1)S(1)}, u32[]{:S(2)}, u32[]{:S(2)}) collective-permute-start(bf16[256,512]{1,0:T(8,128)(2,1)S(1)} %shard_map.97.here), channel_id=1, source_target_pairs={{0,1},{1,2},{2,3},{3,4},{4,5},{5,6},{6,7},{7,0},{8,9},{9,10},{10,1... | collective-permute-start | bytes 786440 | tf_op jit(solution)/shard_map/ppermute | solution.py:390
  33.8 4.2 %collective-permute-start.7 = (bf16[256,512]{1,0:T(8,128)(2,1)S(1)}, bf16[256,512]{1,0:T(8,128)(2,1)S(1)}, u32[]{:S(2)}, u32[]{:S(2)}) collective-permute-start(bf16[256,512]{1,0:T(8,128)(2,1)S(1)} %shard_map.97.here), channel_id=1, source_target_pairs={{0,7},{1,0},{2,1},{3,2},{4,3},{5,4},{6,5},{7,6},{8,15},{9,8},{10,9... | collective-permute-start | bytes 786440 | tf_op jit(solution)/shard_map/ppermute | solution.py:390
  38.0 4.1 %collective-permute-start.9 = (bf16[256,512]{1,0:T(8,128)(2,1)S(1)}, bf16[256,512]{1,0:T(8,128)(2,1)S(1)}, u32[]{:S(2)}, u32[]{:S(2)}) collective-permute-start(bf16[256,512]{1,0:T(8,128)(2,1)S(1)} %shard_map.97.here), channel_id=1, source_target_pairs={{0,6},{1,7},{2,0},{3,1},{4,2},{5,3},{6,4},{7,5},{8,14},{9,15},{10,... | collective-permute-start | bytes 786440 | tf_op jit(solution)/shard_map/ppermute | solution.py:390
  42.2 5.6 %collective-permute-done.6.up1 = bf16[256,512]{1,0:T(8,128)(2,1)S(1)} collective-permute-done((bf16[256,512]{1,0:T(8,128)(2,1)S(1)}, bf16[256,512]{1,0:T(8,128)(2,1)S(1)}, u32[]{:S(2)}, u32[]{:S(2)}) %collective-permute-start.6) | collective-permute-done | bytes 262176 | tf_op jit(solution)/shard_map/ppermute | solution.py:390
  47.8 1.5 %collective-permute-done.7.down1 = bf16[256,512]{1,0:T(8,128)(2,1)S(1)} collective-permute-done((bf16[256,512]{1,0:T(8,128)(2,1)S(1)}, bf16[256,512]{1,0:T(8,128)(2,1)S(1)}, u32[]{:S(2)}, u32[]{:S(2)}) %collective-permute-start.7) | collective-permute-done | bytes 262176 | tf_op jit(solution)/shard_map/ppermute | solution.py:390
  49.3 2.1 %collective-permute-done.8.up2 = bf16[256,512]{1,0:T(8,128)(2,1)S(1)} collective-permute-done((bf16[256,512]{1,0:T(8,128)(2,1)S(1)}, bf16[256,512]{1,0:T(8,128)(2,1)S(1)}, u32[]{:S(2)}, u32[]{:S(2)}) %collective-permute-start.8) | collective-permute-done | bytes 262176 | tf_op jit(solution)/shard_map/ppermute | solution.py:390
  51.4 1.6 %collective-permute-done.9.down2 = bf16[256,512]{1,0:T(8,128)(2,1)S(1)} collective-permute-done((bf16[256,512]{1,0:T(8,128)(2,1)S(1)}, bf16[256,512]{1,0:T(8,128)(2,1)S(1)}, u32[]{:S(2)}, u32[]{:S(2)}) %collective-permute-start.9) | collective-permute-done | bytes 262176 | tf_op jit(solution)/shard_map/ppermute | solution.py:390
  53.0 2.1 %collective-permute-start.10 = (bf16[256,512]{1,0:T(8,128)(2,1)S(1)}, bf16[256,512]{1,0:T(8,128)(2,1)S(1)}, u32[]{:S(2)}, u32[]{:S(2)}) collective-permute-start(bf16[256,512]{1,0:T(8,128)(2,1)S(1)} %get-tuple-element.39.up2), channel_id=1, source_target_pairs={{0,1},{1,2},{2,3},{3,4},{4,5},{5,6},{6,7},{7,0},{8,9},{9,10},{10,1... | collective-permute-start | bytes 786440 | tf_op jit(solution)/shard_map/ppermute | solution.py:390
  55.1 1.2 %collective-permute-start.11 = (bf16[256,512]{1,0:T(8,128)(2,1)S(1)}, bf16[256,512]{1,0:T(8,128)(2,1)S(1)}, u32[]{:S(2)}, u32[]{:S(2)}) collective-permute-start(bf16[256,512]{1,0:T(8,128)(2,1)S(1)} %get-tuple-element.40.down2), channel_id=1, source_target_pairs={{0,7},{1,0},{2,1},{3,2},{4,3},{5,4},{6,5},{7,6},{8,15},{9,8},{10,9... | collective-permute-start | bytes 786440 | tf_op jit(solution)/shard_map/ppermute | solution.py:390
  56.3 4.7 %collective-permute-start.12 = (bf16[128,512]{1,0:T(8,128)(2,1)S(1)}, bf16[128,512]{1,0:T(8,128)(2,1)S(1)}, u32[]{:S(2)}, u32[]{:S(2)}) collective-permute-start(bf16[128,512]{1,0:T(8,128)(2,1)S(1)} %get-tuple-element.41), channel_id=1, source_target_pairs={{0,2},{1,3},{2,4},{3,5},{4,6},{5,7},{6,0},{7,1},{8,10},{9,11},{10,... | collective-permute-start | bytes 393224 | tf_op jit(solution)/shard_map/ppermute | solution.py:390
  61.0 5.8 %collective-permute-done.12.up4 = bf16[128,512]{1,0:T(8,128)(2,1)S(1)} collective-permute-done((bf16[128,512]{1,0:T(8,128)(2,1)S(1)}, bf16[128,512]{1,0:T(8,128)(2,1)S(1)}, u32[]{:S(2)}, u32[]{:S(2)}) %collective-permute-start.12) | collective-permute-done | bytes 131104 | tf_op jit(solution)/shard_map/ppermute | solution.py:390
  66.8 3.4 %collective-permute-done.13.down4 = bf16[128,512]{1,0:T(8,128)(2,1)S(1)} collective-permute-done((bf16[128,512]{1,0:T(8,128)(2,1)S(1)}, bf16[128,512]{1,0:T(8,128)(2,1)S(1)}, u32[]{:S(2)}, u32[]{:S(2)}) %collective-permute-start.13) | collective-permute-done | bytes 131104 | tf_op jit(solution)/shard_map/ppermute | solution.py:390
  70.2 4.1 %shard_map.99 = bf16[256,512]{1,0:T(8,128)(2,1)} custom-call(bf16[256,512]{1,0:T(8,128)(2,1)S(1)} %shard_map.97.here, bf16[256,512]{1,0:T(8,128)(2,1)S(1)} %collective-permute-done.6.up1, bf16[256,512]{1,0:T(8,128)(2,1)S(1)} %collective-permute-done.7.down1, bf16[256,512]{1,0:T(8,128)(2,1)S(1)} %get-tuple-element.39.up2, ...), custom_call_target="tpu_custom_call" | custom-call | flops 1073741824 | bytes 7000000 | tf_op jit(solution)/shard_map/pallas_call | solution.py:26
  (31 shorter events, 3.9 us)
Async XLA Ops:
  6.5 63.7 %all-gather.2.cloned.1.call-start = ((), (), s32[]{:S(2)}) async-start(), calls=%async_computation | async-start | bytes 4325376 | tf_op jit(solution)/shard_map/all_gather | solution.py:403
  8.2 1.0 %copy-start = (bf16[256,512]{1,0:T(8,128)(2,1)S(1)}, bf16[256,512]{1,0:T(8,128)(2,1)}, u32[]{:S(2)}) copy-start(bf16[256,512]{1,0:T(8,128)(2,1)} %key_ref.1) | copy-start | bytes 786436
  8.2 1.0 %copy-start.1 = (bf16[256,512]{1,0:T(8,128)(2,1)S(1)}, bf16[256,512]{1,0:T(8,128)(2,1)}, u32[]{:S(2)}) copy-start(bf16[256,512]{1,0:T(8,128)(2,1)} %value_ref.1) | copy-start | bytes 786436
  8.2 1.0 %copy-start.5 = (s32[256]{0:T(256)S(1)}, s32[256]{0:T(256)}, u32[]{:S(2)}) copy-start(s32[256]{0:T(256)} %param.17) | copy-start | bytes 3076
  9.2 16.7 %copy-start.3 = (f32[16,512]{1,0:T(8,128)S(1)}, f32[16,512]{1,0:T(8,128)}, u32[]{:S(2)}) copy-start(f32[16,512]{1,0:T(8,128)} %decay_ref.1) | copy-start | bytes 98308
  9.2 16.7 %copy-start.4 = (f32[2,16,512]{2,1,0:T(8,128)S(1)}, f32[2,16,512]{2,1,0:T(8,128)}, u32[]{:S(2)}) copy-start(f32[2,16,512]{2,1,0:T(8,128)} %res_ref.1) | copy-start | bytes 196612
  9.2 16.7 %copy-start.6 = (f32[512]{0:T(512)S(1)}, f32[512]{0:T(512)}, u32[]{:S(2)}) copy-start(f32[512]{0:T(512)} %param.15) | copy-start | bytes 6148
  11.9 1.4 %collective-permute-start = (f32[40,512]{1,0:T(8,128)S(1)}, f32[40,512]{1,0:T(8,128)S(1)}, u32[]{:S(2)}, u32[]{:S(2)}) collective-permute-start(f32[40,512]{1,0:T(8,128)S(1)} %get-tuple-element.32.own_ref), channel_id=1, source_target_pairs={{0,8},{8,0},{16,24},{24,16},{32,40},{40,32},{48,56},{56,48},{64,72... | collective-permute-start | bytes 245768 | tf_op jit(solution)/shard_map/ppermute | solution.py:386
  13.3 5.9 %collective-permute-start.1 = (bf16[80,512]{1,0:T(8,128)(2,1)S(1)}, bf16[80,512]{1,0:T(8,128)(2,1)S(1)}, u32[]{:S(2)}, u32[]{:S(2)}) collective-permute-start(bf16[80,512]{1,0:T(8,128)(2,1)S(1)} %shard_map.94.own_ref), channel_id=1, source_target_pairs={{0,16},{8,24},{16,32},{24,40},{32,48},{40,56},{48,0},{56,8},{64,80... | collective-permute-start | bytes 245768 | tf_op jit(solution)/shard_map/ppermute | solution.py:386
  14.9 7.1 %collective-permute-start.2 = (bf16[80,512]{1,0:T(8,128)(2,1)S(1)}, bf16[80,512]{1,0:T(8,128)(2,1)S(1)}, u32[]{:S(2)}, u32[]{:S(2)}) collective-permute-start(bf16[80,512]{1,0:T(8,128)(2,1)S(1)} %shard_map.94.own_ref), channel_id=1, source_target_pairs={{0,32},{8,40},{16,48},{24,56},{32,0},{40,8},{48,16},{56,24},{64,96... | collective-permute-start | bytes 245768 | tf_op jit(solution)/shard_map/ppermute | solution.py:386
  17.8 4.4 %collective-permute-start.3 = (bf16[80,512]{1,0:T(8,128)(2,1)S(1)}, bf16[80,512]{1,0:T(8,128)(2,1)S(1)}, u32[]{:S(2)}, u32[]{:S(2)}) collective-permute-start(bf16[80,512]{1,0:T(8,128)(2,1)S(1)} %shard_map.94.own_ref), channel_id=1, source_target_pairs={{0,48},{8,56},{16,0},{24,8},{32,16},{40,24},{48,32},{56,40},{64,11... | collective-permute-start | bytes 245768 | tf_op jit(solution)/shard_map/ppermute | solution.py:386
  22.4 6.3 %collective-permute-start.4 = (f32[40,512]{1,0:T(8,128)S(1)}, f32[40,512]{1,0:T(8,128)S(1)}, u32[]{:S(2)}, u32[]{:S(2)}) collective-permute-start(f32[40,512]{1,0:T(8,128)S(1)} %get-tuple-element.34.after_ref), channel_id=1, source_target_pairs={{0,64},{8,72},{16,80},{24,88},{32,96},{40,104},{48,112},{56,120},{... | collective-permute-start | bytes 245768 | tf_op jit(solution)/shard_map/ppermute | solution.py:386
  24.0 6.3 %collective-permute-start.5 = (f32[40,512]{1,0:T(8,128)S(1)}, f32[40,512]{1,0:T(8,128)S(1)}, u32[]{:S(2)}, u32[]{:S(2)}) collective-permute-start(f32[40,512]{1,0:T(8,128)S(1)} %get-tuple-element.34.after_ref), channel_id=1, source_target_pairs={{0,128},{8,136},{16,144},{24,152},{32,160},{40,168},{48,176},{56,1... | collective-permute-start | bytes 245768 | tf_op jit(solution)/shard_map/ppermute | solution.py:386
  28.0 2.2 %copy-start.2 = (bf16[256,512]{1,0:T(8,128)(2,1)S(1)}, bf16[256,512]{1,0:T(8,128)(2,1)}, u32[]{:S(2)}) copy-start(bf16[256,512]{1,0:T(8,128)(2,1)} %query_ref.1) | copy-start | bytes 786436
  32.2 15.6 %collective-permute-start.6 = (bf16[256,512]{1,0:T(8,128)(2,1)S(1)}, bf16[256,512]{1,0:T(8,128)(2,1)S(1)}, u32[]{:S(2)}, u32[]{:S(2)}) collective-permute-start(bf16[256,512]{1,0:T(8,128)(2,1)S(1)} %shard_map.97.here), channel_id=1, source_target_pairs={{0,1},{1,2},{2,3},{3,4},{4,5},{5,6},{6,7},{7,0},{8,9},{9,10},{10,1... | collective-permute-start | bytes 786440 | tf_op jit(solution)/shard_map/ppermute | solution.py:390
  33.8 15.4 %collective-permute-start.7 = (bf16[256,512]{1,0:T(8,128)(2,1)S(1)}, bf16[256,512]{1,0:T(8,128)(2,1)S(1)}, u32[]{:S(2)}, u32[]{:S(2)}) collective-permute-start(bf16[256,512]{1,0:T(8,128)(2,1)S(1)} %shard_map.97.here), channel_id=1, source_target_pairs={{0,7},{1,0},{2,1},{3,2},{4,3},{5,4},{6,5},{7,6},{8,15},{9,8},{10,9... | collective-permute-start | bytes 786440 | tf_op jit(solution)/shard_map/ppermute | solution.py:390
  38.0 13.4 %collective-permute-start.8 = (bf16[256,512]{1,0:T(8,128)(2,1)S(1)}, bf16[256,512]{1,0:T(8,128)(2,1)S(1)}, u32[]{:S(2)}, u32[]{:S(2)}) collective-permute-start(bf16[256,512]{1,0:T(8,128)(2,1)S(1)} %shard_map.97.here), channel_id=1, source_target_pairs={{0,2},{1,3},{2,4},{3,5},{4,6},{5,7},{6,0},{7,1},{8,10},{9,11},{10,... | collective-permute-start | bytes 786440 | tf_op jit(solution)/shard_map/ppermute | solution.py:390
  38.0 14.9 %collective-permute-start.9 = (bf16[256,512]{1,0:T(8,128)(2,1)S(1)}, bf16[256,512]{1,0:T(8,128)(2,1)S(1)}, u32[]{:S(2)}, u32[]{:S(2)}) collective-permute-start(bf16[256,512]{1,0:T(8,128)(2,1)S(1)} %shard_map.97.here), channel_id=1, source_target_pairs={{0,6},{1,7},{2,0},{3,1},{4,2},{5,3},{6,4},{7,5},{8,14},{9,15},{10,... | collective-permute-start | bytes 786440 | tf_op jit(solution)/shard_map/ppermute | solution.py:390
  53.0 17.2 %collective-permute-start.10 = (bf16[256,512]{1,0:T(8,128)(2,1)S(1)}, bf16[256,512]{1,0:T(8,128)(2,1)S(1)}, u32[]{:S(2)}, u32[]{:S(2)}) collective-permute-start(bf16[256,512]{1,0:T(8,128)(2,1)S(1)} %get-tuple-element.39.up2), channel_id=1, source_target_pairs={{0,1},{1,2},{2,3},{3,4},{4,5},{5,6},{6,7},{7,0},{8,9},{9,10},{10,1... | collective-permute-start | bytes 786440 | tf_op jit(solution)/shard_map/ppermute | solution.py:390
  55.1 15.1 %collective-permute-start.11 = (bf16[256,512]{1,0:T(8,128)(2,1)S(1)}, bf16[256,512]{1,0:T(8,128)(2,1)S(1)}, u32[]{:S(2)}, u32[]{:S(2)}) collective-permute-start(bf16[256,512]{1,0:T(8,128)(2,1)S(1)} %get-tuple-element.40.down2), channel_id=1, source_target_pairs={{0,7},{1,0},{2,1},{3,2},{4,3},{5,4},{6,5},{7,6},{8,15},{9,8},{10,9... | collective-permute-start | bytes 786440 | tf_op jit(solution)/shard_map/ppermute | solution.py:390
  56.3 10.5 %collective-permute-start.12 = (bf16[128,512]{1,0:T(8,128)(2,1)S(1)}, bf16[128,512]{1,0:T(8,128)(2,1)S(1)}, u32[]{:S(2)}, u32[]{:S(2)}) collective-permute-start(bf16[128,512]{1,0:T(8,128)(2,1)S(1)} %get-tuple-element.41), channel_id=1, source_target_pairs={{0,2},{1,3},{2,4},{3,5},{4,6},{5,7},{6,0},{7,1},{8,10},{9,11},{10,... | collective-permute-start | bytes 393224 | tf_op jit(solution)/shard_map/ppermute | solution.py:390
  61.0 9.2 %collective-permute-start.13 = (bf16[128,512]{1,0:T(8,128)(2,1)S(1)}, bf16[128,512]{1,0:T(8,128)(2,1)S(1)}, u32[]{:S(2)}, u32[]{:S(2)}) collective-permute-start(bf16[128,512]{1,0:T(8,128)(2,1)S(1)} %get-tuple-element.42), channel_id=1, source_target_pairs={{0,6},{1,7},{2,0},{3,1},{4,2},{5,3},{6,4},{7,5},{8,14},{9,15},{10,... | collective-permute-start | bytes 393224 | tf_op jit(solution)/shard_map/ppermute | solution.py:390
Sparse Core Ops, SparseCore 0:
  9.9 53.7 all-gather.1

commit v4 on v3

--- a/solution.py
+++ b/solution.py
@@ -19,7 +19,9 @@
 FLAG = 16
 SENT = 2 * ROWS + FLAG
 WROWS = 128
-PARAMS = pltpu.CompilerParams(vmem_limit_bytes=48 * 1024 * 1024)
+FOLD = 4
+THIN = TOK // FOLD
+PARAMS = pltpu.CompilerParams(vmem_limit_bytes=24 * 1024 * 1024)
 
 
 def call(kernel, outs, args, scratch=(), flops=0, nbytes=0):
@@ -143,7 +145,8 @@
     return [jnp.concatenate([t[g, STEPS * MODES:, :] for g in range(GROUPS)], axis=1) for t in (tre, tim)]
 
 
-def local_kernel(sig, tre, tim, decay_ref, res_ref, skip_ref, starts_ref, y_ref, weight_ref, taps):
+def local_kernel(sig, tre, tim, decay_ref, res_ref, skip_ref, starts_ref, after_ref,
+                 y_ref, weight_ref, taps):
     s0 = first_start(starts_ref)
     b0 = s0 // STEPS
     blocks = block_iota()
@@ -195,8 +198,7 @@
     lax.fori_loop(0, GROUPS, group, 0)
 
 
-def carry_kernel(eb_ref, tre, tim, weight_ref, starts_ref, after_ref,
-                 pz_ref, gz_ref, qre, qim, rows_):
+def carry_kernel(eb_ref, tre, tim, weight_ref, starts_ref, pz_ref, gz_ref, qre, qim, rows_):
     s0 = first_start(starts_ref)
     b0 = s0 // STEPS
     blocks = block_iota()
@@ -273,6 +275,16 @@
     late_thru = first * other_thru + (1.0 - first) * own_thru
     moved = cmul(halves(p256_ref), early)
     put_state(sent_ref, [late_thru * a + b for a, b in zip(moved, late)], own_thru * other_thru)
+
+
+def put_pair(out_ref, side, own_ref, other_ref):
+    rows = own_ref.shape[0]
+    out_ref[pl.ds(pl.multiple_of(side * rows, rows), rows), :] = own_ref[...]
+    out_ref[pl.ds(pl.multiple_of((1 - side) * rows, rows), rows), :] = other_ref[...]
+
+
+def pair_kernel(own_ref, pair_ref, after_ref, out_ref):
+    put_pair(out_ref, lax.axis_index("ctx") // (NC * NY) % 2, own_ref, pair_ref)
 
 
 def row_kernel(own_ref, one_ref, two_ref, three_ref, p256_ref, pay_ref, before_ref, factor_ref, held):
@@ -352,28 +364,72 @@
     lax.fori_loop(0, GROUPS, group, 0)
     for g in range(GROUPS):
         lanes = slice(g * LANES, (g + 1) * LANES)
-        hidden_ref[:, lanes] = (query_ref[:, lanes].astype(F32) * conv[g]).astype(BF16)
-
-
-def relay_kernel(up1, down1, up2, down2, up2_ref, down2_ref, top_ref, bottom_ref):
-    half = TOK // 2
-    up2_ref[...] = up2[...]
-    down2_ref[...] = down2[...]
-    top_ref[...] = up2[:half, :]
-    bottom_ref[...] = down2[half:, :]
-
-
-def project_kernel(here, up1, down1, up2, down2, up3, down3, up4, down4, weight_ref, out_ref, last):
-    z = lax.axis_index("tp")
-    half = TOK // 2
-    last[:half, :] = up4[...]
-    last[half:, :] = down4[...]
-    total = None
-    for k, hidden in enumerate((here, up1, up2, up3, last, down3, down2, down1)):
-        rows = pl.ds(pl.multiple_of(lax.rem(z - k + NZ, NZ) * CH, CH), CH)
-        term = jnp.dot(hidden[...], weight_ref[rows, :], preferred_element_type=F32)
-        total = term if total is None else total + term
-    out_ref[...] = total.astype(BF16)
+        gated = (query_ref[:, lanes].astype(F32) * conv[g]).astype(BF16)
+        for q in range(FOLD):
+            hidden_ref[:, q * CH + g * LANES:q * CH + (g + 1) * LANES] = gated[q * THIN:(q + 1) * THIN]
+
+
+def four_kernel(both_ref, pair_ref, after_ref, even_ref, odd_ref):
+    side = (lax.axis_index("ctx") // NC) % 2
+    even_ref[...] = jnp.where(side == 0, both_ref[...], pair_ref[...])
+    odd_ref[...] = jnp.where(side == 0, pair_ref[...], both_ref[...])
+
+
+def eight_kernel(even_ref, even_x, odd_ref, odd_y, after_up, after_down, even_out, odd_out):
+    n = even_ref.shape[0]
+    for at, ref, out in ((0, even_ref, even_out), (0, odd_ref, odd_out), (n, even_x, even_out), (n, odd_y, odd_out)):
+        out[at:at + n, :] = ref[...]
+
+
+def join_kernel(even_ref, odd_ref, even_far, odd_far, after_up, after_down, out_ref):
+    n = even_ref.shape[0]
+    for at, ref in enumerate((even_ref, odd_ref, even_far, odd_far)):
+        out_ref[at * n:(at + 1) * n, :] = ref[...]
+
+
+def places(k):
+    index = lax.axis_index("ctx")
+    xb, yb = index // (NC * NY * 2), (index // NC) % NY // 2
+    block = lax.rem(lax.axis_index("tp") - k + NZ, NZ)
+    dx = (block // 4 != xb).astype(jnp.int32)
+    dy = (lax.rem(block, 2) != yb).astype(jnp.int32)
+    i = lax.rem(block // 2, 2)
+    found = []
+    for h in range(2):
+        far, near = (dy, dx) if h == 0 else (dx, dy)
+        at = far * 8 * WROWS + h * 4 * WROWS + near * 2 * WROWS + i * WROWS
+        found.append(pl.ds(pl.multiple_of(at, WROWS), WROWS))
+    return found
+
+
+def most_kernel(here, up1, down1, up2, down2, up3, down3, own_ref, total_ref, left):
+    core = lax.axis_index("ctx") % NC
+    for k, ref in enumerate((here, up1, up2, up3, None, down3, down2, down1)):
+        for h, lanes in enumerate(places(k)):
+            for c in range(NC):
+                side = jnp.where(core == c, 0, 1)
+                if ref is None:
+                    left[side, :, lanes] = jnp.zeros((TOK, WROWS), BF16)
+                    continue
+                for q in range(FOLD):
+                    at = slice(q * CH + (NC * h + c) * WROWS, q * CH + (NC * h + c + 1) * WROWS)
+                    left[side, q * THIN:(q + 1) * THIN, lanes] = ref[:, at]
+    total_ref[...] = jnp.dot(left[0], own_ref[...], preferred_element_type=F32)
+
+
+def rest_kernel(total_ref, left, up4, down4, own_ref, other_ref, out_ref, last, rows):
+    core = lax.axis_index("ctx") % NC
+    for h, at in enumerate(places(4)):
+        for c in range(NC):
+            lanes = slice((NC * h + c) * WROWS, (NC * h + c + 1) * WROWS)
+            for q in range(FOLD):
+                middle = q * THIN + THIN // 2
+                source = slice(q * CH + (NC * h + c) * WROWS, q * CH + (NC * h + c + 1) * WROWS)
+                last[q * THIN:middle, lanes] = up4[:, source]
+                last[middle:(q + 1) * THIN, lanes] = down4[:, source]
+            rows[lanes, :] = jnp.where(core == c, own_ref[at, :], other_ref[at, :])
+    out_ref[...] = (total_ref[...] + jnp.dot(left[1], other_ref[...], preferred_element_type=F32)
+                    + jnp.dot(last[...], rows[...], preferred_element_type=F32)).astype(BF16)
 
 
 def ctx_index(x, y, c):
@@ -382,6 +438,12 @@
 
 def move(value, dx, dy, dc):
     pairs = [(ctx_index(x, y, c), ctx_index(x + dx, y + dy, c + dc))
+             for x in range(NX) for y in range(NY) for c in range(NC)]
+    return lax.ppermute(value, "ctx", pairs)
+
+
+def trade(value, dx, dy):
+    pairs = [(ctx_index(x, y, c), ctx_index(x ^ dx, y ^ dy, c))
              for x in range(NX) for y in range(NY) for c in range(NC)]
     return lax.ppermute(value, "ctx", pairs)
 
@@ -400,7 +462,6 @@
     block_shape = struct(GROUPS, ROWS, BLOCKS, LANES)
     table = (GROUPS, (STEPS + 1) * MODES, LANES)
 
-    weight = lax.all_gather(out_weight, "ctx", axis=0, tiled=True)
     magnitude = jnp.exp(-decay)
     q_shape = struct(GROUPS, BLOCKS * MODES, LANES)
     tre, tim, qre, qim, p256 = call(
@@ -412,31 +473,40 @@
     other = move(pay, 0, 0, 1)
     chip = call(chip_kernel, struct(SENT, CH, dtype=BF16), (pay, other, p256))
     near = [move(chip, 0, k, 0) for k in (1, 2, 3)]
-    y, gain = call(
-        local_kernel, (struct(GROUPS, STEPS, BLOCKS, LANES), state_shape),
-        (signal, tre, tim, decay, residue, skip, starts),
-        [pltpu.VMEM((GROUPS, STEPS, LANES), F32)], 30_000_000, 5_000_000)
     row, before, factor = call(
         row_kernel, (pay_shape, state_shape, state_shape),
         (chip, *near, p256), [pltpu.VMEM((NY, PAY, CH), F32)])
     back = [move(row, k, 0, 0) for k in (1, 2)]
+    y, gain = call(
+        local_kernel, (struct(GROUPS, STEPS, BLOCKS, LANES), state_shape),
+        (signal, tre, tim, decay, residue, skip, starts, chip),
+        [pltpu.VMEM((GROUPS, STEPS, LANES), F32)], 30_000_000, 5_000_000)
     pz, gz = call(
-        carry_kernel, (block_shape, block_shape), (eb, tre, tim, gain, starts, row),
+        carry_kernel, (block_shape, block_shape), (eb, tre, tim, gain, starts),
         [qs, qs, pltpu.VMEM((GROUPS, 4 * ROWS, LANES), F32)], 30_000_000, 5_000_000)
     hidden = call(
-        gate_kernel, struct(TOK, CH, dtype=BF16),
+        gate_kernel, struct(THIN, FOLD * CH, dtype=BF16),
         (query, y, pz, gz, tre, tim, starts, pay, other, p256, before, factor, *back),
         [sig, pltpu.VMEM((GROUPS, ROWS, LANES), F32)], 20_000_000, 5_000_000)
 
-    full, part = struct(TOK, CH, dtype=BF16), struct(TOK // 2, CH, dtype=BF16)
-    up1, down1, up2, down2 = turn(hidden, 1), turn(hidden, -1), turn(hidden, 2), turn(hidden, -2)
-    up2, down2, top, bottom = call(relay_kernel, (full, full, part, part), (up1, down1, up2, down2))
+    both = call(pair_kernel, struct(2 * WROWS, CH, dtype=BF16), (out_weight, trade(out_weight, 1, 0), row))
+    w2, w4 = [struct(n * WROWS, CH, dtype=BF16) for n in (2, 4)]
+    even, odd = call(four_kernel, (w2, w2), (both, trade(both, 0, 1), hidden), (), 0, 2_000_000)
+    half = THIN // 2
+    up1, down1 = turn(hidden, 1), turn(hidden, -1)
+    even, odd = call(
+        eight_kernel, (w4, w4), (even, trade(even, 2, 0), odd, trade(odd, 0, 2), up1, down1), (), 0, 4_000_000)
+    up2, down2 = turn(up1, 1), turn(down1, -1)
     up3, down3 = turn(up2, 1), turn(down2, -1)
-    up4, down4 = turn(top, 2), turn(bottom, -2)
+    up4, down4 = turn(up3[:half], 1), turn(down3[half:], -1)
+    own = call(join_kernel, struct(NZ * CH // 2, CH, dtype=BF16),
+               (even, odd, trade(even, 0, 2), trade(odd, 2, 0), up3, down3), (), 0, 4_000_000)
+    total, left = call(
+        most_kernel, (struct(TOK, CH), struct(NC, TOK, NZ * CH // NC, dtype=BF16)),
+        (hidden, up1, down1, up2, down2, up3, down3, own), (), TOK * CH * CH * NZ, 7_000_000)
     return call(
-        project_kernel, full,
-        (hidden, up1, down1, up2, down2, up3, down3, up4, down4, weight),
-        [pltpu.VMEM((TOK, CH), BF16)], 2 * TOK * CH * CH * NZ, 7_000_000)
+        rest_kernel, struct(TOK, CH, dtype=BF16), (total, left, up4, down4, own, move(own, 0, 0, 1)),
+        [pltpu.VMEM((TOK, CH), BF16), pltpu.VMEM((CH, CH), BF16)], TOK * CH * CH * NZ, 7_000_000)
 
 
 def solution(mesh):

time: 81.4 us -> 68.1 us (0.84)
  the two profiles are of different devices: /device:TPU:2 before, /device:TPU:1 now
where the time goes in v4:
time: 68.1 us; the launch traced here: 67.9 us
  starting transfers between devices  33.4 us (49%)
  waiting for transfers between devices  21.7 us (32%)
  Pallas kernels  11 us (16%)
  other arithmetic  0.91 us (1%)
  local copies, waits for them, and re-layouts  0.71 us (1%)
    ppermute x7, starting transfers between devices, move(): return lax.ppermute(value, 'ctx', pairs)  14.4 us
    ppermute x8, starting transfers between devices, turn(): return lax.ppermute(value, 'tp', [(i, (i + k) % NZ) for i in range(NZ)])  13.4 us
    ppermute x8, waiting for transfers between devices, turn(): return lax.ppermute(value, 'tp', [(i, (i + k) % NZ) for i in range(NZ)])  12.5 us
    pallas_call x13, Pallas kernels, call(): pl.pallas_call(kernel, out_shape=outs, in_specs=[VMEM] * len(args), out_s...  11 us
    ppermute x7, waiting for transfers between devices, move(): return lax.ppermute(value, 'ctx', pairs)  8.94 us
    ppermute x6, starting transfers between devices, trade(): return lax.ppermute(value, 'ctx', pairs)  5.61 us
  transfers between devices with their start and end apart: 21, of which 12 were waited for; matrix products, arithmetic and copies ran while one was open for 0% of the time, Pallas kernels for 9%

profile of v4, /device:TPU:1, one launch (start us, length us, event | category | flops | bytes accessed | tf_op | source)
XLA Modules:
  0.0 67.9 jit_solution(335401007867875592)
XLA Ops:
  2.0 2.6 %shard_map.92 = (f32[40,512]{1,0:T(8,128)S(1)}, f32[4,32,8,128]{3,2,1,0:T(8,128)S(1)}, f32[4,256,128]{2,1,0:T(8,128)S(1)}) custom-call(bf16[256,512]{1,0:T(8,128)(2,1)S(1)} %copy-done, bf16[256,512]{1,0:T(8,128)(2,1)S(1)} %copy-done.1, s32[2,128]{1,0:T(2,128)S(1)} %bitcast.2, f32[4,528,128]{2,1,0:T(8,128)S(1)} %get-tuple-element.26.tre, ...), custom_call_target="tpu_custom_call" | custom-call | flops 20000000 | bytes 5000000 | tf_op jit(solution)/shard_map/pallas_call | solution.py:28
  4.6 3.3 %collective-permute-start = (f32[40,512]{1,0:T(8,128)S(1)}, f32[40,512]{1,0:T(8,128)S(1)}, u32[]{:S(2)}, u32[]{:S(2)}) collective-permute-start(f32[40,512]{1,0:T(8,128)S(1)} %get-tuple-element.31.own_ref), channel_id=1, source_target_pairs={{0,8},{8,0},{16,24},{24,16},{32,40},{40,32},{48,56},{56,48},{64,72... | collective-permute-start | bytes 245768 | tf_op jit(solution)/shard_map/ppermute | solution.py:442
  8.9 1.4 %collective-permute-start.3 = (bf16[80,512]{1,0:T(8,128)(2,1)S(1)}, bf16[80,512]{1,0:T(8,128)(2,1)S(1)}, u32[]{:S(2)}, u32[]{:S(2)}) collective-permute-start(bf16[80,512]{1,0:T(8,128)(2,1)S(1)} %shard_map.93.after_ref.own_ref), channel_id=1, source_target_pairs={{0,48},{8,56},{16,0},{24,8},{32,16},{40,24},{48,32},{56,40},{64,11... | collective-permute-start | bytes 245768 | tf_op jit(solution)/shard_map/ppermute | solution.py:442
  11.3 1.3 %collective-permute-done.3.three_ref = bf16[80,512]{1,0:T(8,128)(2,1)S(1)} collective-permute-done((bf16[80,512]{1,0:T(8,128)(2,1)S(1)}, bf16[80,512]{1,0:T(8,128)(2,1)S(1)}, u32[]{:S(2)}, u32[]{:S(2)}) %collective-permute-start.3) | collective-permute-done | bytes 81952 | tf_op jit(solution)/shard_map/ppermute | solution.py:442
  12.6 2.5 %collective-permute-done.2.two_ref = bf16[80,512]{1,0:T(8,128)(2,1)S(1)} collective-permute-done((bf16[80,512]{1,0:T(8,128)(2,1)S(1)}, bf16[80,512]{1,0:T(8,128)(2,1)S(1)}, u32[]{:S(2)}, u32[]{:S(2)}) %collective-permute-start.2) | collective-permute-done | bytes 81952 | tf_op jit(solution)/shard_map/ppermute | solution.py:442
  15.2 2.4 %collective-permute-done.1.one_ref = bf16[80,512]{1,0:T(8,128)(2,1)S(1)} collective-permute-done((bf16[80,512]{1,0:T(8,128)(2,1)S(1)}, bf16[80,512]{1,0:T(8,128)(2,1)S(1)}, u32[]{:S(2)}, u32[]{:S(2)}) %collective-permute-start.1) | collective-permute-done | bytes 81952 | tf_op jit(solution)/shard_map/ppermute | solution.py:442
  17.9 2.5 %collective-permute-start.5 = (f32[40,512]{1,0:T(8,128)S(1)}, f32[40,512]{1,0:T(8,128)S(1)}, u32[]{:S(2)}, u32[]{:S(2)}) collective-permute-start(f32[40,512]{1,0:T(8,128)S(1)} %get-tuple-element.40.after_ref), channel_id=1, source_target_pairs={{0,128},{8,136},{16,144},{24,152},{32,160},{40,168},{48,176},{56,1... | collective-permute-start | bytes 245768 | tf_op jit(solution)/shard_map/ppermute | solution.py:442
  20.7 2.1 %shard_map.94 = (f32[4,32,8,128]{3,2,1,0:T(8,128)S(1)}, f32[32,512]{1,0:T(8,128)S(1)}) custom-call(f32[4,256,128]{2,1,0:T(8,128)S(1)} %get-tuple-element.30.sig, f32[4,528,128]{2,1,0:T(8,128)S(1)} %get-tuple-element.26.tre, f32[4,528,128]{2,1,0:T(8,128)S(1)} %get-tuple-element.27.tim, f32[16,512]{1,0:T(8,128)S(1)} %copy-done.3, f32[2,16,512]{2,1,0:T(8,128)S(1)} %copy-done.5, ...), custom_call_target="tpu_custom_call" | custom-call | flops 30000000 | bytes 5000000 | tf_op jit(solution)/shard_map/pallas_call | solution.py:28
  23.5 1.8 %collective-permute-done.4.one_ref = f32[40,512]{1,0:T(8,128)S(1)} collective-permute-done((f32[40,512]{1,0:T(8,128)S(1)}, f32[40,512]{1,0:T(8,128)S(1)}, u32[]{:S(2)}, u32[]{:S(2)}) %collective-permute-start.4) | collective-permute-done | bytes 81952 | tf_op jit(solution)/shard_map/ppermute | solution.py:442
  25.3 1.9 %shard_map.97.after_ref.here = bf16[64,2048]{1,0:T(8,128)(2,1)S(1)} custom-call(bf16[256,512]{1,0:T(8,128)(2,1)S(1)} %copy-done.2, f32[4,32,8,128]{3,2,1,0:T(8,128)S(1)} %get-tuple-element.33.y_ref, f32[4,32,8,128]{3,2,1,0:T(8,128)S(1)} %get-tuple-element.36.pz_ref, f32[4,32,8,128]{3,2,1,0:T(8,128)S(1)} %get-tuple-element.37.gz_ref, ...), custom_call_target="tpu_custom_call" | custom-call | flops 20000000 | bytes 5000000 | tf_op jit(solution)/shard_map/pallas_call | solution.py:28
  27.2 5.6 %collective-permute-start.7 = (bf16[64,2048]{1,0:T(8,128)(2,1)S(1)}, bf16[64,2048]{1,0:T(8,128)(2,1)S(1)}, u32[]{:S(2)}, u32[]{:S(2)}) collective-permute-start(bf16[64,2048]{1,0:T(8,128)(2,1)S(1)} %shard_map.97.after_ref.here), channel_id=1, source_target_pairs={{0,7},{1,0},{2,1},{3,2},{4,3},{5,4},{6,5},{7,6},{8,15},{9,8},{10,9... | collective-permute-start | bytes 786440 | tf_op jit(solution)/shard_map/ppermute | solution.py:452
  34.3 2.2 %collective-permute-done.7.after_down.down1 = bf16[64,2048]{1,0:T(8,128)(2,1)S(1)} collective-permute-done((bf16[64,2048]{1,0:T(8,128)(2,1)S(1)}, bf16[64,2048]{1,0:T(8,128)(2,1)S(1)}, u32[]{:S(2)}, u32[]{:S(2)}) %collective-permute-start.7) | collective-permute-done | bytes 262176 | tf_op jit(solution)/shard_map/ppermute | solution.py:452
  36.5 3.4 %collective-permute-start.9 = (bf16[64,2048]{1,0:T(8,128)(2,1)S(1)}, bf16[64,2048]{1,0:T(8,128)(2,1)S(1)}, u32[]{:S(2)}, u32[]{:S(2)}) collective-permute-start(bf16[64,2048]{1,0:T(8,128)(2,1)S(1)} %collective-permute-done.7.after_down.down1), channel_id=1, source_target_pairs={{0,7},{1,0},{2,1},{3,2},{4,3},{5,4},{6,5},{7,6},{8,15},{9,8},{10,9... | collective-permute-start | bytes 786440 | tf_op jit(solution)/shard_map/ppermute | solution.py:452
  40.3 1.2 %collective-permute-start.16 = (bf16[512,512]{1,0:T(8,128)(2,1)S(1)}, bf16[512,512]{1,0:T(8,128)(2,1)S(1)}, u32[]{:S(2)}, u32[]{:S(2)}) collective-permute-start(bf16[512,512]{1,0:T(8,128)(2,1)S(1)} %get-tuple-element.43.even_ref), channel_id=1, source_target_pairs={{0,32},{8,40},{16,48},{24,56},{32,0},{40,8},{48,16},{56,24},{64,96... | collective-permute-start | bytes 1572872 | tf_op jit(solution)/shard_map/ppermute | solution.py:448
  41.5 2.9 %collective-permute-start.17 = (bf16[512,512]{1,0:T(8,128)(2,1)S(1)}, bf16[512,512]{1,0:T(8,128)(2,1)S(1)}, u32[]{:S(2)}, u32[]{:S(2)}) collective-permute-start(bf16[512,512]{1,0:T(8,128)(2,1)S(1)} %get-tuple-element.44.odd_ref), channel_id=1, source_target_pairs={{0,128},{8,136},{16,144},{24,152},{32,160},{40,168},{48,176},{56,1... | collective-permute-start | bytes 1572872 | tf_op jit(solution)/shard_map/ppermute | solution.py:448
  44.4 2.7 %collective-permute-start.11 = (bf16[64,2048]{1,0:T(8,128)(2,1)S(1)}, bf16[64,2048]{1,0:T(8,128)(2,1)S(1)}, u32[]{:S(2)}, u32[]{:S(2)}) collective-permute-start(bf16[64,2048]{1,0:T(8,128)(2,1)S(1)} %collective-permute-done.9.down2), channel_id=1, source_target_pairs={{0,7},{1,0},{2,1},{3,2},{4,3},{5,4},{6,5},{7,6},{8,15},{9,8},{10,9... | collective-permute-start | bytes 786440 | tf_op jit(solution)/shard_map/ppermute | solution.py:452
  47.1 3.3 %collective-permute-done.11.after_down.down3 = bf16[64,2048]{1,0:T(8,128)(2,1)S(1)} collective-permute-done((bf16[64,2048]{1,0:T(8,128)(2,1)S(1)}, bf16[64,2048]{1,0:T(8,128)(2,1)S(1)}, u32[]{:S(2)}, u32[]{:S(2)}) %collective-permute-start.11) | collective-permute-done | bytes 262176 | tf_op jit(solution)/shard_map/ppermute | solution.py:452
  50.4 3.4 %collective-permute-done.10.after_up.up3 = bf16[64,2048]{1,0:T(8,128)(2,1)S(1)} collective-permute-done((bf16[64,2048]{1,0:T(8,128)(2,1)S(1)}, bf16[64,2048]{1,0:T(8,128)(2,1)S(1)}, u32[]{:S(2)}, u32[]{:S(2)}) %collective-permute-start.10) | collective-permute-done | bytes 262176 | tf_op jit(solution)/shard_map/ppermute | solution.py:452
  54.0 5.8 %collective-permute-start.20 = (bf16[2048,512]{1,0:T(8,128)(2,1)S(1)}, bf16[2048,512]{1,0:T(8,128)(2,1)S(1)}, u32[]{:S(2)}, u32[]{:S(2)}) collective-permute-start(bf16[2048,512]{1,0:T(8,128)(2,1)S(1)} %shard_map.101.own_ref), channel_id=1, source_target_pairs={{0,8},{8,0},{16,24},{24,16},{32,40},{40,32},{48,56},{56,48},{64,72... | collective-permute-start | bytes 6291464 | tf_op jit(solution)/shard_map/ppermute | solution.py:442
  60.3 1.1 %collective-permute-start.18 = (bf16[32,2048]{1,0:T(8,128)(2,1)S(1)}, bf16[32,2048]{1,0:T(8,128)(2,1)S(1)}, u32[]{:S(2)}, u32[]{:S(2)}) collective-permute-start(bf16[32,2048]{1,0:T(8,128)(2,1)S(1)} %slice.8), channel_id=1, source_target_pairs={{0,1},{1,2},{2,3},{3,4},{4,5},{5,6},{6,7},{7,0},{8,9},{9,10},{10,1... | collective-permute-start | bytes 393224 | tf_op jit(solution)/shard_map/ppermute | solution.py:452
  61.4 1.4 %shard_map.102 = (f32[256,512]{1,0:T(8,128)S(1)}, bf16[2,256,2048]{2,1,0:T(8,128)(2,1)S(1)}) custom-call(bf16[64,2048]{1,0:T(8,128)(2,1)S(1)} %shard_map.97.after_ref.here, bf16[64,2048]{1,0:T(8,128)(2,1)S(1)} %collective-permute-done.6.after_up.up1, bf16[64,2048]{1,0:T(8,128)(2,1)S(1)} %collective-permute-done.7.after_down.down1, ...), custom_call_target="tpu_custom_call" | custom-call | flops 536870912 | bytes 7000000 | tf_op jit(solution)/shard_map/pallas_call | solution.py:28
  62.8 2.2 %collective-permute-done.19.down4 = bf16[32,2048]{1,0:T(8,128)(2,1)S(1)} collective-permute-done((bf16[32,2048]{1,0:T(8,128)(2,1)S(1)}, bf16[32,2048]{1,0:T(8,128)(2,1)S(1)}, u32[]{:S(2)}, u32[]{:S(2)}) %collective-permute-start.19) | collective-permute-done | bytes 131104 | tf_op jit(solution)/shard_map/ppermute | solution.py:452
  65.0 1.4 %collective-permute-done.18.up4 = bf16[32,2048]{1,0:T(8,128)(2,1)S(1)} collective-permute-done((bf16[32,2048]{1,0:T(8,128)(2,1)S(1)}, bf16[32,2048]{1,0:T(8,128)(2,1)S(1)}, u32[]{:S(2)}, u32[]{:S(2)}) %collective-permute-start.18) | collective-permute-done | bytes 131104 | tf_op jit(solution)/shard_map/ppermute | solution.py:452
  66.4 1.6 %shard_map.103 = bf16[256,512]{1,0:T(8,128)(2,1)} custom-call(f32[256,512]{1,0:T(8,128)S(1)} %get-tuple-element.45.total_ref, bf16[2,256,2048]{2,1,0:T(8,128)(2,1)S(1)} %get-tuple-element.46.left, bf16[32,2048]{1,0:T(8,128)(2,1)S(1)} %collective-permute-done.18.up4, bf16[32,2048]{1,0:T(8,128)(2,1)S(1)} %collective-permute-done.19.down4, ...), custom_call_target="tpu_custom_call" | custom-call | flops 536870912 | bytes 7000000 | tf_op jit(solution)/shard_map/pallas_call | solution.py:28
  (50 shorter events, 7.6 us)
Async XLA Ops:
  1.9 18.8 %copy-start.3 = (f32[16,512]{1,0:T(8,128)S(1)}, f32[16,512]{1,0:T(8,128)}, u32[]{:S(2)}) copy-start(f32[16,512]{1,0:T(8,128)} %decay_ref.1) | copy-start | bytes 98308
  1.9 18.8 %copy-start.5 = (f32[2,16,512]{2,1,0:T(8,128)S(1)}, f32[2,16,512]{2,1,0:T(8,128)}, u32[]{:S(2)}) copy-start(f32[2,16,512]{2,1,0:T(8,128)} %res_ref.1) | copy-start | bytes 196612
  2.0 18.8 %copy-start.7 = (f32[512]{0:T(512)S(1)}, f32[512]{0:T(512)}, u32[]{:S(2)}) copy-start(f32[512]{0:T(512)} %param.15) | copy-start | bytes 6148
  4.6 4.3 %collective-permute-start = (f32[40,512]{1,0:T(8,128)S(1)}, f32[40,512]{1,0:T(8,128)S(1)}, u32[]{:S(2)}, u32[]{:S(2)}) collective-permute-start(f32[40,512]{1,0:T(8,128)S(1)} %get-tuple-element.31.own_ref), channel_id=1, source_target_pairs={{0,8},{8,0},{16,24},{24,16},{32,40},{40,32},{48,56},{56,48},{64,72... | collective-permute-start | bytes 245768 | tf_op jit(solution)/shard_map/ppermute | solution.py:442
  7.9 9.8 %collective-permute-start.12 = (bf16[128,512]{1,0:T(8,128)(2,1)S(1)}, bf16[128,512]{1,0:T(8,128)(2,1)S(1)}, u32[]{:S(2)}, u32[]{:S(2)}) collective-permute-start(bf16[128,512]{1,0:T(8,128)(2,1)S(1)} %copy-done.4), channel_id=1, source_target_pairs={{0,64},{8,72},{16,80},{24,88},{32,96},{40,104},{48,112},{56,120},{... | collective-permute-start | bytes 393224 | tf_op jit(solution)/shard_map/ppermute | solution.py:448
  8.9 3.8 %collective-permute-start.3 = (bf16[80,512]{1,0:T(8,128)(2,1)S(1)}, bf16[80,512]{1,0:T(8,128)(2,1)S(1)}, u32[]{:S(2)}, u32[]{:S(2)}) collective-permute-start(bf16[80,512]{1,0:T(8,128)(2,1)S(1)} %shard_map.93.after_ref.own_ref), channel_id=1, source_target_pairs={{0,48},{8,56},{16,0},{24,8},{32,16},{40,24},{48,32},{56,40},{64,11... | collective-permute-start | bytes 245768 | tf_op jit(solution)/shard_map/ppermute | solution.py:442
  10.3 4.9 %collective-permute-start.2 = (bf16[80,512]{1,0:T(8,128)(2,1)S(1)}, bf16[80,512]{1,0:T(8,128)(2,1)S(1)}, u32[]{:S(2)}, u32[]{:S(2)}) collective-permute-start(bf16[80,512]{1,0:T(8,128)(2,1)S(1)} %shard_map.93.after_ref.own_ref), channel_id=1, source_target_pairs={{0,32},{8,40},{16,48},{24,56},{32,0},{40,8},{48,16},{56,24},{64,96... | collective-permute-start | bytes 245768 | tf_op jit(solution)/shard_map/ppermute | solution.py:442
  10.7 6.9 %collective-permute-start.1 = (bf16[80,512]{1,0:T(8,128)(2,1)S(1)}, bf16[80,512]{1,0:T(8,128)(2,1)S(1)}, u32[]{:S(2)}, u32[]{:S(2)}) collective-permute-start(bf16[80,512]{1,0:T(8,128)(2,1)S(1)} %shard_map.93.after_ref.own_ref), channel_id=1, source_target_pairs={{0,16},{8,24},{16,32},{24,40},{32,48},{40,56},{48,0},{56,8},{64,80... | collective-permute-start | bytes 245768 | tf_op jit(solution)/shard_map/ppermute | solution.py:442
  17.8 15.1 %collective-permute-start.13 = (bf16[256,512]{1,0:T(8,128)(2,1)S(1)}, bf16[256,512]{1,0:T(8,128)(2,1)S(1)}, u32[]{:S(2)}, u32[]{:S(2)}) collective-permute-start(bf16[256,512]{1,0:T(8,128)(2,1)S(1)} %shard_map.98.both_ref), channel_id=1, source_target_pairs={{0,16},{8,24},{16,0},{24,8},{32,48},{40,56},{48,32},{56,40},{64,80... | collective-permute-start | bytes 786440 | tf_op jit(solution)/shard_map/ppermute | solution.py:448
  17.9 5.6 %collective-permute-start.5 = (f32[40,512]{1,0:T(8,128)S(1)}, f32[40,512]{1,0:T(8,128)S(1)}, u32[]{:S(2)}, u32[]{:S(2)}) collective-permute-start(f32[40,512]{1,0:T(8,128)S(1)} %get-tuple-element.40.after_ref), channel_id=1, source_target_pairs={{0,128},{8,136},{16,144},{24,152},{32,160},{40,168},{48,176},{56,1... | collective-permute-start | bytes 245768 | tf_op jit(solution)/shard_map/ppermute | solution.py:442
  20.4 4.9 %collective-permute-start.4 = (f32[40,512]{1,0:T(8,128)S(1)}, f32[40,512]{1,0:T(8,128)S(1)}, u32[]{:S(2)}, u32[]{:S(2)}) collective-permute-start(f32[40,512]{1,0:T(8,128)S(1)} %get-tuple-element.40.after_ref), channel_id=1, source_target_pairs={{0,64},{8,72},{16,80},{24,88},{32,96},{40,104},{48,112},{56,120},{... | collective-permute-start | bytes 245768 | tf_op jit(solution)/shard_map/ppermute | solution.py:442
  27.2 9.3 %collective-permute-start.7 = (bf16[64,2048]{1,0:T(8,128)(2,1)S(1)}, bf16[64,2048]{1,0:T(8,128)(2,1)S(1)}, u32[]{:S(2)}, u32[]{:S(2)}) collective-permute-start(bf16[64,2048]{1,0:T(8,128)(2,1)S(1)} %shard_map.97.after_ref.here), channel_id=1, source_target_pairs={{0,7},{1,0},{2,1},{3,2},{4,3},{5,4},{6,5},{7,6},{8,15},{9,8},{10,9... | collective-permute-start | bytes 786440 | tf_op jit(solution)/shard_map/ppermute | solution.py:452
  32.9 7.1 %collective-permute-start.6 = (bf16[64,2048]{1,0:T(8,128)(2,1)S(1)}, bf16[64,2048]{1,0:T(8,128)(2,1)S(1)}, u32[]{:S(2)}, u32[]{:S(2)}) collective-permute-start(bf16[64,2048]{1,0:T(8,128)(2,1)S(1)} %shard_map.97.after_ref.here), channel_id=1, source_target_pairs={{0,1},{1,2},{2,3},{3,4},{4,5},{5,6},{6,7},{7,0},{8,9},{9,10},{10,1... | collective-permute-start | bytes 786440 | tf_op jit(solution)/shard_map/ppermute | solution.py:452
  32.9 7.2 %collective-permute-start.14 = (bf16[256,512]{1,0:T(8,128)(2,1)S(1)}, bf16[256,512]{1,0:T(8,128)(2,1)S(1)}, u32[]{:S(2)}, u32[]{:S(2)}) collective-permute-start(bf16[256,512]{1,0:T(8,128)(2,1)S(1)} %get-tuple-element.41.even_ref), channel_id=1, source_target_pairs={{0,128},{8,136},{16,144},{24,152},{32,160},{40,168},{48,176},{56,1... | collective-permute-start | bytes 786440 | tf_op jit(solution)/shard_map/ppermute | solution.py:448
  33.2 7.0 %collective-permute-start.15 = (bf16[256,512]{1,0:T(8,128)(2,1)S(1)}, bf16[256,512]{1,0:T(8,128)(2,1)S(1)}, u32[]{:S(2)}, u32[]{:S(2)}) collective-permute-start(bf16[256,512]{1,0:T(8,128)(2,1)S(1)} %get-tuple-element.42.odd_ref), channel_id=1, source_target_pairs={{0,32},{8,40},{16,48},{24,56},{32,0},{40,8},{48,16},{56,24},{64,96... | collective-permute-start | bytes 786440 | tf_op jit(solution)/shard_map/ppermute | solution.py:448
  36.5 7.9 %collective-permute-start.9 = (bf16[64,2048]{1,0:T(8,128)(2,1)S(1)}, bf16[64,2048]{1,0:T(8,128)(2,1)S(1)}, u32[]{:S(2)}, u32[]{:S(2)}) collective-permute-start(bf16[64,2048]{1,0:T(8,128)(2,1)S(1)} %collective-permute-done.7.after_down.down1), channel_id=1, source_target_pairs={{0,7},{1,0},{2,1},{3,2},{4,3},{5,4},{6,5},{7,6},{8,15},{9,8},{10,9... | collective-permute-start | bytes 786440 | tf_op jit(solution)/shard_map/ppermute | solution.py:452
  39.9 7.1 %collective-permute-start.8 = (bf16[64,2048]{1,0:T(8,128)(2,1)S(1)}, bf16[64,2048]{1,0:T(8,128)(2,1)S(1)}, u32[]{:S(2)}, u32[]{:S(2)}) collective-permute-start(bf16[64,2048]{1,0:T(8,128)(2,1)S(1)} %collective-permute-done.6.after_up.up1), channel_id=1, source_target_pairs={{0,1},{1,2},{2,3},{3,4},{4,5},{5,6},{6,7},{7,0},{8,9},{9,10},{10,1... | collective-permute-start | bytes 786440 | tf_op jit(solution)/shard_map/ppermute | solution.py:452
  40.3 13.5 %collective-permute-start.16 = (bf16[512,512]{1,0:T(8,128)(2,1)S(1)}, bf16[512,512]{1,0:T(8,128)(2,1)S(1)}, u32[]{:S(2)}, u32[]{:S(2)}) collective-permute-start(bf16[512,512]{1,0:T(8,128)(2,1)S(1)} %get-tuple-element.43.even_ref), channel_id=1, source_target_pairs={{0,32},{8,40},{16,48},{24,56},{32,0},{40,8},{48,16},{56,24},{64,96... | collective-permute-start | bytes 1572872 | tf_op jit(solution)/shard_map/ppermute | solution.py:448
  41.5 12.3 %collective-permute-start.17 = (bf16[512,512]{1,0:T(8,128)(2,1)S(1)}, bf16[512,512]{1,0:T(8,128)(2,1)S(1)}, u32[]{:S(2)}, u32[]{:S(2)}) collective-permute-start(bf16[512,512]{1,0:T(8,128)(2,1)S(1)} %get-tuple-element.44.odd_ref), channel_id=1, source_target_pairs={{0,128},{8,136},{16,144},{24,152},{32,160},{40,168},{48,176},{56,1... | collective-permute-start | bytes 1572872 | tf_op jit(solution)/shard_map/ppermute | solution.py:448
  44.4 6.0 %collective-permute-start.11 = (bf16[64,2048]{1,0:T(8,128)(2,1)S(1)}, bf16[64,2048]{1,0:T(8,128)(2,1)S(1)}, u32[]{:S(2)}, u32[]{:S(2)}) collective-permute-start(bf16[64,2048]{1,0:T(8,128)(2,1)S(1)} %collective-permute-done.9.down2), channel_id=1, source_target_pairs={{0,7},{1,0},{2,1},{3,2},{4,3},{5,4},{6,5},{7,6},{8,15},{9,8},{10,9... | collective-permute-start | bytes 786440 | tf_op jit(solution)/shard_map/ppermute | solution.py:452
  47.1 6.7 %collective-permute-start.10 = (bf16[64,2048]{1,0:T(8,128)(2,1)S(1)}, bf16[64,2048]{1,0:T(8,128)(2,1)S(1)}, u32[]{:S(2)}, u32[]{:S(2)}) collective-permute-start(bf16[64,2048]{1,0:T(8,128)(2,1)S(1)} %collective-permute-done.8.up2), channel_id=1, source_target_pairs={{0,1},{1,2},{2,3},{3,4},{4,5},{5,6},{6,7},{7,0},{8,9},{9,10},{10,1... | collective-permute-start | bytes 786440 | tf_op jit(solution)/shard_map/ppermute | solution.py:452
  54.0 12.4 %collective-permute-start.20 = (bf16[2048,512]{1,0:T(8,128)(2,1)S(1)}, bf16[2048,512]{1,0:T(8,128)(2,1)S(1)}, u32[]{:S(2)}, u32[]{:S(2)}) collective-permute-start(bf16[2048,512]{1,0:T(8,128)(2,1)S(1)} %shard_map.101.own_ref), channel_id=1, source_target_pairs={{0,8},{8,0},{16,24},{24,16},{32,40},{40,32},{48,56},{56,48},{64,72... | collective-permute-start | bytes 6291464 | tf_op jit(solution)/shard_map/ppermute | solution.py:442
  59.8 5.2 %collective-permute-start.19 = (bf16[32,2048]{1,0:T(8,128)(2,1)S(1)}, bf16[32,2048]{1,0:T(8,128)(2,1)S(1)}, u32[]{:S(2)}, u32[]{:S(2)}) collective-permute-start(bf16[32,2048]{1,0:T(8,128)(2,1)S(1)} %slice.9), channel_id=1, source_target_pairs={{0,7},{1,0},{2,1},{3,2},{4,3},{5,4},{6,5},{7,6},{8,15},{9,8},{10,9... | collective-permute-start | bytes 393224 | tf_op jit(solution)/shard_map/ppermute | solution.py:452
  60.3 6.1 %collective-permute-start.18 = (bf16[32,2048]{1,0:T(8,128)(2,1)S(1)}, bf16[32,2048]{1,0:T(8,128)(2,1)S(1)}, u32[]{:S(2)}, u32[]{:S(2)}) collective-permute-start(bf16[32,2048]{1,0:T(8,128)(2,1)S(1)} %slice.8), channel_id=1, source_target_pairs={{0,1},{1,2},{2,3},{3,4},{4,5},{5,6},{6,7},{7,0},{8,9},{9,10},{10,1... | collective-permute-start | bytes 393224 | tf_op jit(solution)/shard_map/ppermute | solution.py:452
  (5 other events, 12.1 us)

commit v5 on v4

--- a/solution.py
+++ b/solution.py
@@ -125,7 +125,7 @@
             return tuple(out)
 
         zero = jnp.zeros((BLOCKS, LANES), F32)
-        acc = lax.fori_loop(0, STEPS, step, (zero,) * ROWS, unroll=4)
+        acc = lax.fori_loop(0, STEPS, step, (zero,) * ROWS, unroll=8)
         for m in range(MODES):
             re, im = acc[2 * m], acc[2 * m + 1]
             eb_ref[g, m] = re
@@ -359,7 +359,7 @@
             conv[g, pl.ds(j, BLOCKS, stride=STEPS), :] = y_ref[g, j] + jnp.where(late, 0.0, total)
             return unused
 
-        return lax.fori_loop(0, STEPS, step, unused, unroll=4)
+        return lax.fori_loop(0, STEPS, step, unused, unroll=16)
 
     lax.fori_loop(0, GROUPS, group, 0)
     for g in range(GROUPS):
@@ -375,16 +375,18 @@
     odd_ref[...] = jnp.where(side == 0, pair_ref[...], both_ref[...])
 
 
-def eight_kernel(even_ref, even_x, odd_ref, odd_y, after_up, after_down, even_out, odd_out):
+def eight_kernel(even_ref, even_x, odd_ref, odd_y, after_up, after_down, all_ref, even_out, odd_out):
     n = even_ref.shape[0]
     for at, ref, out in ((0, even_ref, even_out), (0, odd_ref, odd_out), (n, even_x, even_out), (n, odd_y, odd_out)):
         out[at:at + n, :] = ref[...]
-
-
-def join_kernel(even_ref, odd_ref, even_far, odd_far, after_up, after_down, out_ref):
+        start = at if out is even_out else 2 * n + at
+        all_ref[start:start + n, :] = ref[...]
+
+
+def join_kernel(even_ref, odd_ref, after_up, after_down, out_ref):
     n = even_ref.shape[0]
-    for at, ref in enumerate((even_ref, odd_ref, even_far, odd_far)):
-        out_ref[at * n:(at + 1) * n, :] = ref[...]
+    out_ref[:n, :] = even_ref[...]
+    out_ref[n:, :] = odd_ref[...]
 
 
 def places(k):
@@ -402,8 +404,9 @@
     return found
 
 
-def most_kernel(here, up1, down1, up2, down2, up3, down3, own_ref, total_ref, left):
+def most_kernel(here, up1, down1, up2, down2, up3, down3, near_own, far_own, near_other, total_ref, left_ref, left):
     core = lax.axis_index("ctx") % NC
+    wide = 8 * WROWS
     for k, ref in enumerate((here, up1, up2, up3, None, down3, down2, down1)):
         for h, lanes in enumerate(places(k)):
             for c in range(NC):
@@ -414,21 +417,31 @@
                 for q in range(FOLD):
                     at = slice(q * CH + (NC * h + c) * WROWS, q * CH + (NC * h + c + 1) * WROWS)
                     left[side, q * THIN:(q + 1) * THIN, lanes] = ref[:, at]
-    total_ref[...] = jnp.dot(left[0], own_ref[...], preferred_element_type=F32)
-
-
-def rest_kernel(total_ref, left, up4, down4, own_ref, other_ref, out_ref, last, rows):
+    total_ref[...] = (jnp.dot(left[0, :, :wide], near_own[...], preferred_element_type=F32)
+                      + jnp.dot(left[0, :, wide:], far_own[...], preferred_element_type=F32)
+                      + jnp.dot(left[1, :, :wide], near_other[...], preferred_element_type=F32))
+    left_ref[...] = left[1, :, wide:]
+
+
+def last_kernel(up4, down4, out_ref):
+    for q in range(FOLD):
+        middle = q * THIN + THIN // 2
+        lanes = slice(q * CH, (q + 1) * CH)
+        out_ref[q * THIN:middle, :] = up4[:, lanes]
+        out_ref[middle:(q + 1) * THIN, :] = down4[:, lanes]
+
+
+def rest_kernel(total_ref, left, last, near_own, near_other, own_ref, other_ref, out_ref, rows):
     core = lax.axis_index("ctx") % NC
-    for h, at in enumerate(places(4)):
+    wide = 8 * WROWS
+    for h, place in enumerate(places(4)):
+        far = place.start >= wide
+        at = pl.ds(pl.multiple_of(jnp.where(far, place.start - wide, place.start), WROWS), WROWS)
         for c in range(NC):
             lanes = slice((NC * h + c) * WROWS, (NC * h + c + 1) * WROWS)
-            for q in range(FOLD):
-                middle = q * THIN + THIN // 2
-                source = slice(q * CH + (NC * h + c) * WROWS, q * CH + (NC * h + c + 1) * WROWS)
-                last[q * THIN:middle, lanes] = up4[:, source]
-                last[middle:(q + 1) * THIN, lanes] = down4[:, source]
-            rows[lanes, :] = jnp.where(core == c, own_ref[at, :], other_ref[at, :])
-    out_ref[...] = (total_ref[...] + jnp.dot(left[1], other_ref[...], preferred_element_type=F32)
+            rows[lanes, :] = jnp.where(core == c, jnp.where(far, own_ref[at, :], near_own[at, :]),
+                                       jnp.where(far, other_ref[at, :], near_other[at, :]))
+    out_ref[...] = (total_ref[...] + jnp.dot(left[...], other_ref[...], preferred_element_type=F32)
                     + jnp.dot(last[...], rows[...], preferred_element_type=F32)).astype(BF16)
 
 
@@ -487,26 +500,28 @@
     hidden = call(
         gate_kernel, struct(THIN, FOLD * CH, dtype=BF16),
         (query, y, pz, gz, tre, tim, starts, pay, other, p256, before, factor, *back),
-        [sig, pltpu.VMEM((GROUPS, ROWS, LANES), F32)], 20_000_000, 5_000_000)
+        [sig, pltpu.VMEM((GROUPS, ROWS, LANES), F32)], 2_000_000_000, 5_000_000)
 
     both = call(pair_kernel, struct(2 * WROWS, CH, dtype=BF16), (out_weight, trade(out_weight, 1, 0), row))
-    w2, w4 = [struct(n * WROWS, CH, dtype=BF16) for n in (2, 4)]
+    w2, w4, w8 = [struct(n * WROWS, CH, dtype=BF16) for n in (2, 4, 8)]
     even, odd = call(four_kernel, (w2, w2), (both, trade(both, 0, 1), hidden), (), 0, 2_000_000)
     half = THIN // 2
     up1, down1 = turn(hidden, 1), turn(hidden, -1)
-    even, odd = call(
-        eight_kernel, (w4, w4), (even, trade(even, 2, 0), odd, trade(odd, 0, 2), up1, down1), (), 0, 4_000_000)
+    near, even, odd = call(
+        eight_kernel, (w8, w4, w4), (even, trade(even, 2, 0), odd, trade(odd, 0, 2), up1, down1), (), 0, 4_000_000)
     up2, down2 = turn(up1, 1), turn(down1, -1)
     up3, down3 = turn(up2, 1), turn(down2, -1)
     up4, down4 = turn(up3[:half], 1), turn(down3[half:], -1)
-    own = call(join_kernel, struct(NZ * CH // 2, CH, dtype=BF16),
-               (even, odd, trade(even, 0, 2), trade(odd, 2, 0), up3, down3), (), 0, 4_000_000)
+    far = call(join_kernel, w8, (trade(even, 0, 2), trade(odd, 2, 0), up3, down3), (), 0, 2_000_000)
+    near_other = move(near, 0, 0, 1)
     total, left = call(
-        most_kernel, (struct(TOK, CH), struct(NC, TOK, NZ * CH // NC, dtype=BF16)),
-        (hidden, up1, down1, up2, down2, up3, down3, own), (), TOK * CH * CH * NZ, 7_000_000)
+        most_kernel, (struct(TOK, CH), struct(TOK, 8 * WROWS, dtype=BF16)),
+        (hidden, up1, down1, up2, down2, up3, down3, near, far, near_other),
+        [pltpu.VMEM((NC, TOK, NZ * CH // NC), BF16)], 1_000_000_000, 7_000_000)
+    last = call(last_kernel, struct(TOK, CH, dtype=BF16), (up4, down4), (), 20_000_000_000, 1_000_000)
     return call(
-        rest_kernel, struct(TOK, CH, dtype=BF16), (total, left, up4, down4, own, move(own, 0, 0, 1)),
-        [pltpu.VMEM((TOK, CH), BF16), pltpu.VMEM((CH, CH), BF16)], TOK * CH * CH * NZ, 7_000_000)
+        rest_kernel, struct(TOK, CH, dtype=BF16), (total, left, last, near, near_other, far, move(far, 0, 0, 1)),
+        [pltpu.VMEM((CH, CH), BF16)], TOK * CH * CH * NZ, 7_000_000)
 
 
 def solution(mesh):

time: 68.1 us -> 64.7 us (0.950)
  waiting for transfers between devices: 21.7 us -> 11.7 us
  starting transfers between devices: 33.4 us -> 40.5 us
    ppermute x8, waiting for transfers between devices: 12.5 us -> 3.99 us  [turn(): return lax.ppermute(value, 'tp', [(i, (i + k) % NZ) for i in range(NZ)])]
    ppermute x6, starting transfers between devices: 5.61 us -> 9.44 us  [trade(): return lax.ppermute(value, 'ctx', pairs)]
    ppermute x7 -> x8, waiting for transfers between devices: 8.94 us -> 5.42 us  [move(): return lax.ppermute(value, 'ctx', pairs)]
    ppermute x7 -> x8, starting transfers between devices: 14.4 us -> 16.8 us  [move(): return lax.ppermute(value, 'ctx', pairs)]
    ppermute x6, waiting for transfers between devices: 0.29 us -> 2.3 us  [trade(): return lax.ppermute(value, 'ctx', pairs)]
    ppermute x8, starting transfers between devices: 13.4 us -> 14.3 us  [turn(): return lax.ppermute(value, 'tp', [(i, (i + k) % NZ) for i in range(NZ)])]
    pallas_call x13 -> x14, Pallas kernels: 11 us -> 10.5 us  [call(): pl.pallas_call(kernel, out_shape=outs, in_specs=[VMEM] * len(args), out_s...]
  transfers between devices with their start and end apart: 21 -> 22, of which waited for: 12 -> 7; matrix products, arithmetic and copies ran while one was open for 0% -> 0% of each run, Pallas kernels for 9% -> 10%
where the time goes in v5:
time: 64.7 us; the launch traced here: 64.6 us
  starting transfers between devices  40.5 us (63%)
  waiting for transfers between devices  11.7 us (18%)
  Pallas kernels  10.5 us (16%)
  other arithmetic  0.91 us (1%)
  local copies, waits for them, and re-layouts  0.75 us (1%)
    ppermute x8, starting transfers between devices, move(): return lax.ppermute(value, 'ctx', pairs)  16.8 us
    ppermute x8, starting transfers between devices, turn(): return lax.ppermute(value, 'tp', [(i, (i + k) % NZ) for i in range(NZ)])  14.3 us
    pallas_call x14, Pallas kernels, call(): pl.pallas_call(kernel, out_shape=outs, in_specs=[VMEM] * len(args), out_s...  10.5 us
    ppermute x6, starting transfers between devices, trade(): return lax.ppermute(value, 'ctx', pairs)  9.44 us
    ppermute x8, waiting for transfers between devices, move(): return lax.ppermute(value, 'ctx', pairs)  5.42 us
    ppermute x8, waiting for transfers between devices, turn(): return lax.ppermute(value, 'tp', [(i, (i + k) % NZ) for i in range(NZ)])  3.99 us
    ppermute x6, waiting for transfers between devices, trade(): return lax.ppermute(value, 'ctx', pairs)  2.3 us
  transfers between devices with their start and end apart: 22, of which 7 were waited for; matrix products, arithmetic and copies ran while one was open for 0% of the time, Pallas kernels for 10%

profile of v5, /device:TPU:1, one launch (start us, length us, event | category | flops | bytes accessed | tf_op | source)
XLA Modules:
  0.0 64.6 jit_solution(13450915294297797125)
XLA Ops:
  2.0 2.3 %shard_map.92 = (f32[40,512]{1,0:T(8,128)S(1)}, f32[4,32,8,128]{3,2,1,0:T(8,128)S(1)}, f32[4,256,128]{2,1,0:T(8,128)S(1)}) custom-call(bf16[256,512]{1,0:T(8,128)(2,1)S(1)} %copy-done, bf16[256,512]{1,0:T(8,128)(2,1)S(1)} %copy-done.1, s32[2,128]{1,0:T(2,128)S(1)} %bitcast.2, f32[4,528,128]{2,1,0:T(8,128)S(1)} %get-tuple-element.27.tre, ...), custom_call_target="tpu_custom_call" | custom-call | flops 20000000 | bytes 5000000 | tf_op jit(solution)/shard_map/pallas_call | solution.py:28
  4.2 3.3 %collective-permute-start = (f32[40,512]{1,0:T(8,128)S(1)}, f32[40,512]{1,0:T(8,128)S(1)}, u32[]{:S(2)}, u32[]{:S(2)}) collective-permute-start(f32[40,512]{1,0:T(8,128)S(1)} %get-tuple-element.32.own_ref), channel_id=1, source_target_pairs={{0,8},{8,0},{16,24},{24,16},{32,40},{40,32},{48,56},{56,48},{64,72... | collective-permute-start | bytes 245768 | tf_op jit(solution)/shard_map/ppermute | solution.py:455
  8.6 2.2 %collective-permute-start.2 = (bf16[80,512]{1,0:T(8,128)(2,1)S(1)}, bf16[80,512]{1,0:T(8,128)(2,1)S(1)}, u32[]{:S(2)}, u32[]{:S(2)}) collective-permute-start(bf16[80,512]{1,0:T(8,128)(2,1)S(1)} %shard_map.93.after_ref.own_ref), channel_id=1, source_target_pairs={{0,32},{8,40},{16,48},{24,56},{32,0},{40,8},{48,16},{56,24},{64,96... | collective-permute-start | bytes 245768 | tf_op jit(solution)/shard_map/ppermute | solution.py:455
  10.8 1.1 %collective-permute-start.3 = (bf16[80,512]{1,0:T(8,128)(2,1)S(1)}, bf16[80,512]{1,0:T(8,128)(2,1)S(1)}, u32[]{:S(2)}, u32[]{:S(2)}) collective-permute-start(bf16[80,512]{1,0:T(8,128)(2,1)S(1)} %shard_map.93.after_ref.own_ref), channel_id=1, source_target_pairs={{0,48},{8,56},{16,0},{24,8},{32,16},{40,24},{48,32},{56,40},{64,11... | collective-permute-start | bytes 245768 | tf_op jit(solution)/shard_map/ppermute | solution.py:455
  11.9 1.2 %collective-permute-start.12 = (bf16[128,512]{1,0:T(8,128)(2,1)S(1)}, bf16[128,512]{1,0:T(8,128)(2,1)S(1)}, u32[]{:S(2)}, u32[]{:S(2)}) collective-permute-start(bf16[128,512]{1,0:T(8,128)(2,1)S(1)} %copy-done.3), channel_id=1, source_target_pairs={{0,64},{8,72},{16,80},{24,88},{32,96},{40,104},{48,112},{56,120},{... | collective-permute-start | bytes 393224 | tf_op jit(solution)/shard_map/ppermute | solution.py:461
  13.1 1.2 %collective-permute-done.1.one_ref = bf16[80,512]{1,0:T(8,128)(2,1)S(1)} collective-permute-done((bf16[80,512]{1,0:T(8,128)(2,1)S(1)}, bf16[80,512]{1,0:T(8,128)(2,1)S(1)}, u32[]{:S(2)}, u32[]{:S(2)}) %collective-permute-start.1) | collective-permute-done | bytes 81952 | tf_op jit(solution)/shard_map/ppermute | solution.py:455
  16.2 2.5 %collective-permute-start.5 = (f32[40,512]{1,0:T(8,128)S(1)}, f32[40,512]{1,0:T(8,128)S(1)}, u32[]{:S(2)}, u32[]{:S(2)}) collective-permute-start(f32[40,512]{1,0:T(8,128)S(1)} %get-tuple-element.41.after_ref), channel_id=1, source_target_pairs={{0,128},{8,136},{16,144},{24,152},{32,160},{40,168},{48,176},{56,1... | collective-permute-start | bytes 245768 | tf_op jit(solution)/shard_map/ppermute | solution.py:455
  18.6 2.1 %shard_map.94 = (f32[4,32,8,128]{3,2,1,0:T(8,128)S(1)}, f32[32,512]{1,0:T(8,128)S(1)}) custom-call(f32[4,256,128]{2,1,0:T(8,128)S(1)} %get-tuple-element.31.sig, f32[4,528,128]{2,1,0:T(8,128)S(1)} %get-tuple-element.27.tre, f32[4,528,128]{2,1,0:T(8,128)S(1)} %get-tuple-element.28.tim, f32[16,512]{1,0:T(8,128)S(1)} %copy-done.2, f32[2,16,512]{2,1,0:T(8,128)S(1)} %copy-done.4, ...), custom_call_target="tpu_custom_call" | custom-call | flops 30000000 | bytes 5000000 | tf_op jit(solution)/shard_map/pallas_call | solution.py:28
  21.7 1.7 %shard_map.97.after_ref.here = bf16[64,2048]{1,0:T(8,128)(2,1)S(1)} custom-call(bf16[256,512]{1,0:T(8,128)(2,1)S(1)} %copy-done.7, f32[4,32,8,128]{3,2,1,0:T(8,128)S(1)} %get-tuple-element.34.y_ref, f32[4,32,8,128]{3,2,1,0:T(8,128)S(1)} %get-tuple-element.37.pz_ref, f32[4,32,8,128]{3,2,1,0:T(8,128)S(1)} %get-tuple-element.38.gz_ref, ...), custom_call_target="tpu_custom_call" | custom-call | flops 2000000000 | bytes 5000000 | tf_op jit(solution)/shard_map/pallas_call | solution.py:28
  23.4 1.7 %collective-permute-start.6 = (bf16[64,2048]{1,0:T(8,128)(2,1)S(1)}, bf16[64,2048]{1,0:T(8,128)(2,1)S(1)}, u32[]{:S(2)}, u32[]{:S(2)}) collective-permute-start(bf16[64,2048]{1,0:T(8,128)(2,1)S(1)} %shard_map.97.after_ref.here), channel_id=1, source_target_pairs={{0,1},{1,2},{2,3},{3,4},{4,5},{5,6},{6,7},{7,0},{8,9},{9,10},{10,1... | collective-permute-start | bytes 786440 | tf_op jit(solution)/shard_map/ppermute | solution.py:465
  25.1 4.0 %collective-permute-start.7 = (bf16[64,2048]{1,0:T(8,128)(2,1)S(1)}, bf16[64,2048]{1,0:T(8,128)(2,1)S(1)}, u32[]{:S(2)}, u32[]{:S(2)}) collective-permute-start(bf16[64,2048]{1,0:T(8,128)(2,1)S(1)} %shard_map.97.after_ref.here), channel_id=1, source_target_pairs={{0,7},{1,0},{2,1},{3,2},{4,3},{5,4},{6,5},{7,6},{8,15},{9,8},{10,9... | collective-permute-start | bytes 786440 | tf_op jit(solution)/shard_map/ppermute | solution.py:465
  29.2 2.1 %collective-permute-start.14 = (bf16[256,512]{1,0:T(8,128)(2,1)S(1)}, bf16[256,512]{1,0:T(8,128)(2,1)S(1)}, u32[]{:S(2)}, u32[]{:S(2)}) collective-permute-start(bf16[256,512]{1,0:T(8,128)(2,1)S(1)} %get-tuple-element.42.even_ref), channel_id=1, source_target_pairs={{0,128},{8,136},{16,144},{24,152},{32,160},{40,168},{48,176},{56,1... | collective-permute-start | bytes 786440 | tf_op jit(solution)/shard_map/ppermute | solution.py:461
  31.3 2.0 %collective-permute-start.15 = (bf16[256,512]{1,0:T(8,128)(2,1)S(1)}, bf16[256,512]{1,0:T(8,128)(2,1)S(1)}, u32[]{:S(2)}, u32[]{:S(2)}) collective-permute-start(bf16[256,512]{1,0:T(8,128)(2,1)S(1)} %get-tuple-element.43.odd_ref), channel_id=1, source_target_pairs={{0,32},{8,40},{16,48},{24,56},{32,0},{40,8},{48,16},{56,24},{64,96... | collective-permute-start | bytes 786440 | tf_op jit(solution)/shard_map/ppermute | solution.py:461
  33.4 2.7 %collective-permute-start.9 = (bf16[64,2048]{1,0:T(8,128)(2,1)S(1)}, bf16[64,2048]{1,0:T(8,128)(2,1)S(1)}, u32[]{:S(2)}, u32[]{:S(2)}) collective-permute-start(bf16[64,2048]{1,0:T(8,128)(2,1)S(1)} %collective-permute-done.7.after_down.down1), channel_id=1, source_target_pairs={{0,7},{1,0},{2,1},{3,2},{4,3},{5,4},{6,5},{7,6},{8,15},{9,8},{10,9... | collective-permute-start | bytes 786440 | tf_op jit(solution)/shard_map/ppermute | solution.py:465
  36.1 2.3 %collective-permute-done.15.odd_y = bf16[256,512]{1,0:T(8,128)(2,1)S(1)} collective-permute-done((bf16[256,512]{1,0:T(8,128)(2,1)S(1)}, bf16[256,512]{1,0:T(8,128)(2,1)S(1)}, u32[]{:S(2)}, u32[]{:S(2)}) %collective-permute-start.15) | collective-permute-done | bytes 262176 | tf_op jit(solution)/shard_map/ppermute | solution.py:461
  38.5 2.3 %collective-permute-start.16 = (bf16[512,512]{1,0:T(8,128)(2,1)S(1)}, bf16[512,512]{1,0:T(8,128)(2,1)S(1)}, u32[]{:S(2)}, u32[]{:S(2)}) collective-permute-start(bf16[512,512]{1,0:T(8,128)(2,1)S(1)} %get-tuple-element.45), channel_id=1, source_target_pairs={{0,32},{8,40},{16,48},{24,56},{32,0},{40,8},{48,16},{56,24},{64,96... | collective-permute-start | bytes 1572872 | tf_op jit(solution)/shard_map/ppermute | solution.py:461
  40.8 1.6 %collective-permute-start.17 = (bf16[512,512]{1,0:T(8,128)(2,1)S(1)}, bf16[512,512]{1,0:T(8,128)(2,1)S(1)}, u32[]{:S(2)}, u32[]{:S(2)}) collective-permute-start(bf16[512,512]{1,0:T(8,128)(2,1)S(1)} %get-tuple-element.46), channel_id=1, source_target_pairs={{0,128},{8,136},{16,144},{24,152},{32,160},{40,168},{48,176},{56,1... | collective-permute-start | bytes 1572872 | tf_op jit(solution)/shard_map/ppermute | solution.py:461
  42.4 3.1 %collective-permute-start.11 = (bf16[64,2048]{1,0:T(8,128)(2,1)S(1)}, bf16[64,2048]{1,0:T(8,128)(2,1)S(1)}, u32[]{:S(2)}, u32[]{:S(2)}) collective-permute-start(bf16[64,2048]{1,0:T(8,128)(2,1)S(1)} %collective-permute-done.9.down2), channel_id=1, source_target_pairs={{0,7},{1,0},{2,1},{3,2},{4,3},{5,4},{6,5},{7,6},{8,15},{9,8},{10,9... | collective-permute-start | bytes 786440 | tf_op jit(solution)/shard_map/ppermute | solution.py:465
  45.4 4.0 %collective-permute-done.10.after_up.up3 = bf16[64,2048]{1,0:T(8,128)(2,1)S(1)} collective-permute-done((bf16[64,2048]{1,0:T(8,128)(2,1)S(1)}, bf16[64,2048]{1,0:T(8,128)(2,1)S(1)}, u32[]{:S(2)}, u32[]{:S(2)}) %collective-permute-start.10) | collective-permute-done | bytes 262176 | tf_op jit(solution)/shard_map/ppermute | solution.py:465
  49.6 2.7 %collective-permute-start.20 = (bf16[32,2048]{1,0:T(8,128)(2,1)S(1)}, bf16[32,2048]{1,0:T(8,128)(2,1)S(1)}, u32[]{:S(2)}, u32[]{:S(2)}) collective-permute-start(bf16[32,2048]{1,0:T(8,128)(2,1)S(1)} %slice.9), channel_id=1, source_target_pairs={{0,7},{1,0},{2,1},{3,2},{4,3},{5,4},{6,5},{7,6},{8,15},{9,8},{10,9... | collective-permute-start | bytes 393224 | tf_op jit(solution)/shard_map/ppermute | solution.py:465
  52.3 7.0 %collective-permute-start.18 = (bf16[1024,512]{1,0:T(8,128)(2,1)S(1)}, bf16[1024,512]{1,0:T(8,128)(2,1)S(1)}, u32[]{:S(2)}, u32[]{:S(2)}) collective-permute-start(bf16[1024,512]{1,0:T(8,128)(2,1)S(1)} %get-tuple-element.44.near_own), channel_id=1, source_target_pairs={{0,8},{8,0},{16,24},{24,16},{32,40},{40,32},{48,56},{56,48},{64,72... | collective-permute-start | bytes 3145736 | tf_op jit(solution)/shard_map/ppermute | solution.py:455
  59.5 2.1 %collective-permute-done.18.near_other = bf16[1024,512]{1,0:T(8,128)(2,1)S(1)} collective-permute-done((bf16[1024,512]{1,0:T(8,128)(2,1)S(1)}, bf16[1024,512]{1,0:T(8,128)(2,1)S(1)}, u32[]{:S(2)}, u32[]{:S(2)}) %collective-permute-start.18) | collective-permute-done | bytes 1048608 | tf_op jit(solution)/shard_map/ppermute | solution.py:455
  61.6 1.7 %shard_map.102 = (f32[256,512]{1,0:T(8,128)S(1)}, bf16[256,1024]{1,0:T(8,128)(2,1)S(1)}) custom-call(bf16[64,2048]{1,0:T(8,128)(2,1)S(1)} %shard_map.97.after_ref.here, bf16[64,2048]{1,0:T(8,128)(2,1)S(1)} %collective-permute-done.6.after_up.up1, bf16[64,2048]{1,0:T(8,128)(2,1)S(1)} %collective-permute-done.7.after_down.down1, ...), custom_call_target="tpu_custom_call" | custom-call | flops 1000000000 | bytes 7000000 | tf_op jit(solution)/shard_map/pallas_call | solution.py:28
  63.3 1.3 %shard_map.104 = bf16[256,512]{1,0:T(8,128)(2,1)} custom-call(f32[256,512]{1,0:T(8,128)S(1)} %get-tuple-element.47.total_ref, bf16[256,1024]{1,0:T(8,128)(2,1)S(1)} %get-tuple-element.48.left, bf16[256,512]{1,0:T(8,128)(2,1)S(1)} %shard_map.103.last, bf16[1024,512]{1,0:T(8,128)(2,1)S(1)} %get-tuple-element.44.near_own, ...), custom_call_target="tpu_custom_call" | custom-call | flops 536870912 | bytes 7000000 | tf_op jit(solution)/shard_map/pallas_call | solution.py:28
  (53 shorter events, 6.3 us)
Async XLA Ops:
  1.9 16.7 %copy-start.2 = (f32[16,512]{1,0:T(8,128)S(1)}, f32[16,512]{1,0:T(8,128)}, u32[]{:S(2)}) copy-start(f32[16,512]{1,0:T(8,128)} %decay_ref.1) | copy-start | bytes 98308
  2.0 16.7 %copy-start.4 = (f32[2,16,512]{2,1,0:T(8,128)S(1)}, f32[2,16,512]{2,1,0:T(8,128)}, u32[]{:S(2)}) copy-start(f32[2,16,512]{2,1,0:T(8,128)} %res_ref.1) | copy-start | bytes 196612
  4.2 4.3 %collective-permute-start = (f32[40,512]{1,0:T(8,128)S(1)}, f32[40,512]{1,0:T(8,128)S(1)}, u32[]{:S(2)}, u32[]{:S(2)}) collective-permute-start(f32[40,512]{1,0:T(8,128)S(1)} %get-tuple-element.32.own_ref), channel_id=1, source_target_pairs={{0,8},{8,0},{16,24},{24,16},{32,40},{40,32},{48,56},{56,48},{64,72... | collective-permute-start | bytes 245768 | tf_op jit(solution)/shard_map/ppermute | solution.py:455
  8.5 5.8 %collective-permute-start.1 = (bf16[80,512]{1,0:T(8,128)(2,1)S(1)}, bf16[80,512]{1,0:T(8,128)(2,1)S(1)}, u32[]{:S(2)}, u32[]{:S(2)}) collective-permute-start(bf16[80,512]{1,0:T(8,128)(2,1)S(1)} %shard_map.93.after_ref.own_ref), channel_id=1, source_target_pairs={{0,16},{8,24},{16,32},{24,40},{32,48},{40,56},{48,0},{56,8},{64,80... | collective-permute-start | bytes 245768 | tf_op jit(solution)/shard_map/ppermute | solution.py:455
  8.6 6.1 %collective-permute-start.2 = (bf16[80,512]{1,0:T(8,128)(2,1)S(1)}, bf16[80,512]{1,0:T(8,128)(2,1)S(1)}, u32[]{:S(2)}, u32[]{:S(2)}) collective-permute-start(bf16[80,512]{1,0:T(8,128)(2,1)S(1)} %shard_map.93.after_ref.own_ref), channel_id=1, source_target_pairs={{0,32},{8,40},{16,48},{24,56},{32,0},{40,8},{48,16},{56,24},{64,96... | collective-permute-start | bytes 245768 | tf_op jit(solution)/shard_map/ppermute | solution.py:455
  10.8 4.7 %collective-permute-start.3 = (bf16[80,512]{1,0:T(8,128)(2,1)S(1)}, bf16[80,512]{1,0:T(8,128)(2,1)S(1)}, u32[]{:S(2)}, u32[]{:S(2)}) collective-permute-start(bf16[80,512]{1,0:T(8,128)(2,1)S(1)} %shard_map.93.after_ref.own_ref), channel_id=1, source_target_pairs={{0,48},{8,56},{16,0},{24,8},{32,16},{40,24},{48,32},{56,40},{64,11... | collective-permute-start | bytes 245768 | tf_op jit(solution)/shard_map/ppermute | solution.py:455
  11.9 9.6 %collective-permute-start.12 = (bf16[128,512]{1,0:T(8,128)(2,1)S(1)}, bf16[128,512]{1,0:T(8,128)(2,1)S(1)}, u32[]{:S(2)}, u32[]{:S(2)}) collective-permute-start(bf16[128,512]{1,0:T(8,128)(2,1)S(1)} %copy-done.3), channel_id=1, source_target_pairs={{0,64},{8,72},{16,80},{24,88},{32,96},{40,104},{48,112},{56,120},{... | collective-permute-start | bytes 393224 | tf_op jit(solution)/shard_map/ppermute | solution.py:461
  15.6 6.0 %collective-permute-start.4 = (f32[40,512]{1,0:T(8,128)S(1)}, f32[40,512]{1,0:T(8,128)S(1)}, u32[]{:S(2)}, u32[]{:S(2)}) collective-permute-start(f32[40,512]{1,0:T(8,128)S(1)} %get-tuple-element.41.after_ref), channel_id=1, source_target_pairs={{0,64},{8,72},{16,80},{24,88},{32,96},{40,104},{48,112},{56,120},{... | collective-permute-start | bytes 245768 | tf_op jit(solution)/shard_map/ppermute | solution.py:455
  16.2 5.5 %collective-permute-start.5 = (f32[40,512]{1,0:T(8,128)S(1)}, f32[40,512]{1,0:T(8,128)S(1)}, u32[]{:S(2)}, u32[]{:S(2)}) collective-permute-start(f32[40,512]{1,0:T(8,128)S(1)} %get-tuple-element.41.after_ref), channel_id=1, source_target_pairs={{0,128},{8,136},{16,144},{24,152},{32,160},{40,168},{48,176},{56,1... | collective-permute-start | bytes 245768 | tf_op jit(solution)/shard_map/ppermute | solution.py:455
  21.5 7.7 %collective-permute-start.13 = (bf16[256,512]{1,0:T(8,128)(2,1)S(1)}, bf16[256,512]{1,0:T(8,128)(2,1)S(1)}, u32[]{:S(2)}, u32[]{:S(2)}) collective-permute-start(bf16[256,512]{1,0:T(8,128)(2,1)S(1)} %shard_map.98.both_ref), channel_id=1, source_target_pairs={{0,16},{8,24},{16,0},{24,8},{32,48},{40,56},{48,32},{56,40},{64,80... | collective-permute-start | bytes 786440 | tf_op jit(solution)/shard_map/ppermute | solution.py:461
  23.4 10.0 %collective-permute-start.6 = (bf16[64,2048]{1,0:T(8,128)(2,1)S(1)}, bf16[64,2048]{1,0:T(8,128)(2,1)S(1)}, u32[]{:S(2)}, u32[]{:S(2)}) collective-permute-start(bf16[64,2048]{1,0:T(8,128)(2,1)S(1)} %shard_map.97.after_ref.here), channel_id=1, source_target_pairs={{0,1},{1,2},{2,3},{3,4},{4,5},{5,6},{6,7},{7,0},{8,9},{9,10},{10,1... | collective-permute-start | bytes 786440 | tf_op jit(solution)/shard_map/ppermute | solution.py:465
  25.1 8.3 %collective-permute-start.7 = (bf16[64,2048]{1,0:T(8,128)(2,1)S(1)}, bf16[64,2048]{1,0:T(8,128)(2,1)S(1)}, u32[]{:S(2)}, u32[]{:S(2)}) collective-permute-start(bf16[64,2048]{1,0:T(8,128)(2,1)S(1)} %shard_map.97.after_ref.here), channel_id=1, source_target_pairs={{0,7},{1,0},{2,1},{3,2},{4,3},{5,4},{6,5},{7,6},{8,15},{9,8},{10,9... | collective-permute-start | bytes 786440 | tf_op jit(solution)/shard_map/ppermute | solution.py:465
  29.2 6.9 %collective-permute-start.14 = (bf16[256,512]{1,0:T(8,128)(2,1)S(1)}, bf16[256,512]{1,0:T(8,128)(2,1)S(1)}, u32[]{:S(2)}, u32[]{:S(2)}) collective-permute-start(bf16[256,512]{1,0:T(8,128)(2,1)S(1)} %get-tuple-element.42.even_ref), channel_id=1, source_target_pairs={{0,128},{8,136},{16,144},{24,152},{32,160},{40,168},{48,176},{56,1... | collective-permute-start | bytes 786440 | tf_op jit(solution)/shard_map/ppermute | solution.py:461
  31.3 7.0 %collective-permute-start.15 = (bf16[256,512]{1,0:T(8,128)(2,1)S(1)}, bf16[256,512]{1,0:T(8,128)(2,1)S(1)}, u32[]{:S(2)}, u32[]{:S(2)}) collective-permute-start(bf16[256,512]{1,0:T(8,128)(2,1)S(1)} %get-tuple-element.43.odd_ref), channel_id=1, source_target_pairs={{0,32},{8,40},{16,48},{24,56},{32,0},{40,8},{48,16},{56,24},{64,96... | collective-permute-start | bytes 786440 | tf_op jit(solution)/shard_map/ppermute | solution.py:461
  33.4 9.0 %collective-permute-start.8 = (bf16[64,2048]{1,0:T(8,128)(2,1)S(1)}, bf16[64,2048]{1,0:T(8,128)(2,1)S(1)}, u32[]{:S(2)}, u32[]{:S(2)}) collective-permute-start(bf16[64,2048]{1,0:T(8,128)(2,1)S(1)} %collective-permute-done.6.after_up.up1), channel_id=1, source_target_pairs={{0,1},{1,2},{2,3},{3,4},{4,5},{5,6},{6,7},{7,0},{8,9},{9,10},{10,1... | collective-permute-start | bytes 786440 | tf_op jit(solution)/shard_map/ppermute | solution.py:465
  33.4 9.0 %collective-permute-start.9 = (bf16[64,2048]{1,0:T(8,128)(2,1)S(1)}, bf16[64,2048]{1,0:T(8,128)(2,1)S(1)}, u32[]{:S(2)}, u32[]{:S(2)}) collective-permute-start(bf16[64,2048]{1,0:T(8,128)(2,1)S(1)} %collective-permute-done.7.after_down.down1), channel_id=1, source_target_pairs={{0,7},{1,0},{2,1},{3,2},{4,3},{5,4},{6,5},{7,6},{8,15},{9,8},{10,9... | collective-permute-start | bytes 786440 | tf_op jit(solution)/shard_map/ppermute | solution.py:465
  38.5 20.8 %collective-permute-start.16 = (bf16[512,512]{1,0:T(8,128)(2,1)S(1)}, bf16[512,512]{1,0:T(8,128)(2,1)S(1)}, u32[]{:S(2)}, u32[]{:S(2)}) collective-permute-start(bf16[512,512]{1,0:T(8,128)(2,1)S(1)} %get-tuple-element.45), channel_id=1, source_target_pairs={{0,32},{8,40},{16,48},{24,56},{32,0},{40,8},{48,16},{56,24},{64,96... | collective-permute-start | bytes 1572872 | tf_op jit(solution)/shard_map/ppermute | solution.py:461
  40.8 18.5 %collective-permute-start.17 = (bf16[512,512]{1,0:T(8,128)(2,1)S(1)}, bf16[512,512]{1,0:T(8,128)(2,1)S(1)}, u32[]{:S(2)}, u32[]{:S(2)}) collective-permute-start(bf16[512,512]{1,0:T(8,128)(2,1)S(1)} %get-tuple-element.46), channel_id=1, source_target_pairs={{0,128},{8,136},{16,144},{24,152},{32,160},{40,168},{48,176},{56,1... | collective-permute-start | bytes 1572872 | tf_op jit(solution)/shard_map/ppermute | solution.py:461
  42.4 7.0 %collective-permute-start.10 = (bf16[64,2048]{1,0:T(8,128)(2,1)S(1)}, bf16[64,2048]{1,0:T(8,128)(2,1)S(1)}, u32[]{:S(2)}, u32[]{:S(2)}) collective-permute-start(bf16[64,2048]{1,0:T(8,128)(2,1)S(1)} %collective-permute-done.8.up2), channel_id=1, source_target_pairs={{0,1},{1,2},{2,3},{3,4},{4,5},{5,6},{6,7},{7,0},{8,9},{9,10},{10,1... | collective-permute-start | bytes 786440 | tf_op jit(solution)/shard_map/ppermute | solution.py:465
  42.4 7.1 %collective-permute-start.11 = (bf16[64,2048]{1,0:T(8,128)(2,1)S(1)}, bf16[64,2048]{1,0:T(8,128)(2,1)S(1)}, u32[]{:S(2)}, u32[]{:S(2)}) collective-permute-start(bf16[64,2048]{1,0:T(8,128)(2,1)S(1)} %collective-permute-done.9.down2), channel_id=1, source_target_pairs={{0,7},{1,0},{2,1},{3,2},{4,3},{5,4},{6,5},{7,6},{8,15},{9,8},{10,9... | collective-permute-start | bytes 786440 | tf_op jit(solution)/shard_map/ppermute | solution.py:465
  49.4 10.1 %collective-permute-start.19 = (bf16[32,2048]{1,0:T(8,128)(2,1)S(1)}, bf16[32,2048]{1,0:T(8,128)(2,1)S(1)}, u32[]{:S(2)}, u32[]{:S(2)}) collective-permute-start(bf16[32,2048]{1,0:T(8,128)(2,1)S(1)} %slice.8), channel_id=1, source_target_pairs={{0,1},{1,2},{2,3},{3,4},{4,5},{5,6},{6,7},{7,0},{8,9},{9,10},{10,1... | collective-permute-start | bytes 393224 | tf_op jit(solution)/shard_map/ppermute | solution.py:465
  49.6 10.0 %collective-permute-start.20 = (bf16[32,2048]{1,0:T(8,128)(2,1)S(1)}, bf16[32,2048]{1,0:T(8,128)(2,1)S(1)}, u32[]{:S(2)}, u32[]{:S(2)}) collective-permute-start(bf16[32,2048]{1,0:T(8,128)(2,1)S(1)} %slice.9), channel_id=1, source_target_pairs={{0,7},{1,0},{2,1},{3,2},{4,3},{5,4},{6,5},{7,6},{8,15},{9,8},{10,9... | collective-permute-start | bytes 393224 | tf_op jit(solution)/shard_map/ppermute | solution.py:465
  52.3 9.3 %collective-permute-start.18 = (bf16[1024,512]{1,0:T(8,128)(2,1)S(1)}, bf16[1024,512]{1,0:T(8,128)(2,1)S(1)}, u32[]{:S(2)}, u32[]{:S(2)}) collective-permute-start(bf16[1024,512]{1,0:T(8,128)(2,1)S(1)} %get-tuple-element.44.near_own), channel_id=1, source_target_pairs={{0,8},{8,0},{16,24},{24,16},{32,40},{40,32},{48,56},{56,48},{64,72... | collective-permute-start | bytes 3145736 | tf_op jit(solution)/shard_map/ppermute | solution.py:455
  59.4 3.9 %collective-permute-start.21 = (bf16[1024,512]{1,0:T(8,128)(2,1)S(1)}, bf16[1024,512]{1,0:T(8,128)(2,1)S(1)}, u32[]{:S(2)}, u32[]{:S(2)}) collective-permute-start(bf16[1024,512]{1,0:T(8,128)(2,1)S(1)} %shard_map.101.far_own.own_ref), channel_id=1, source_target_pairs={{0,8},{8,0},{16,24},{24,16},{32,40},{40,32},{48,56},{56,48},{64,72... | collective-permute-start | bytes 3145736 | tf_op jit(solution)/shard_map/ppermute | solution.py:455
  (6 other events, 30.5 us)

commit v6 on v5

--- a/solution.py
+++ b/solution.py
@@ -262,7 +262,7 @@
 def get_state(ref):
     parts = [ref[at:at + MODES, :].astype(F32) + ref[ROWS + at:ROWS + at + MODES, :].astype(F32)
              for at in (0, MODES)]
-    return parts, ref[2 * ROWS:2 * ROWS + 8, :].astype(F32)[:1]
+    return parts, ref[2 * ROWS:SENT, :].astype(F32)[:1]
 
 
 def chip_kernel(own_ref, other_ref, p256_ref, sent_ref):
@@ -479,7 +479,7 @@
     q_shape = struct(GROUPS, BLOCKS * MODES, LANES)
     tre, tim, qre, qim, p256 = call(
         powers_kernel, (struct(*table), struct(*table), q_shape, q_shape, state_shape),
-        (magnitude * jnp.cos(freq), magnitude * jnp.sin(freq)), (), 2_000_000_000, 5_000_000)
+        (magnitude * jnp.cos(freq), magnitude * jnp.sin(freq)), (), 300000000, 5_000_000)
     pay, eb, signal = call(
         ends_kernel, (pay_shape, block_shape, struct(GROUPS, TOK, LANES)),
         (key, value, starts, tre, tim, qre, qim), (), 20_000_000, 5_000_000)
@@ -517,8 +517,8 @@
     total, left = call(
         most_kernel, (struct(TOK, CH), struct(TOK, 8 * WROWS, dtype=BF16)),
         (hidden, up1, down1, up2, down2, up3, down3, near, far, near_other),
-        [pltpu.VMEM((NC, TOK, NZ * CH // NC), BF16)], 1_000_000_000, 7_000_000)
-    last = call(last_kernel, struct(TOK, CH, dtype=BF16), (up4, down4), (), 20_000_000_000, 1_000_000)
+        [pltpu.VMEM((NC, TOK, NZ * CH // NC), BF16)], 8000000000, 7_000_000)
+    last = call(last_kernel, struct(TOK, CH, dtype=BF16), (up4, down4), (), 8000000000, 1_000_000)
     return call(
         rest_kernel, struct(TOK, CH, dtype=BF16), (total, left, last, near, near_other, far, move(far, 0, 0, 1)),
         [pltpu.VMEM((CH, CH), BF16)], TOK * CH * CH * NZ, 7_000_000)

time: 64.7 us -> 62.6 us (0.968); the launches traced: 64.6 us -> 61.4 us
  waiting for transfers between devices: 11.7 us -> 6.27 us
  starting transfers between devices: 40.5 us -> 43.4 us
  local copies, waits for them, and re-layouts: 0.75 us -> 0.09 us
    ppermute x8, waiting for transfers between devices: 3.99 us -> 0.02 us  [turn(): return lax.ppermute(value, 'tp', [(i, (i + k) % NZ) for i in range(NZ)])]
    ppermute x8, starting transfers between devices: 16.8 us -> 19.7 us  [move(): return lax.ppermute(value, 'ctx', pairs)]
    ppermute x8, waiting for transfers between devices: 5.42 us -> 3.95 us  [move(): return lax.ppermute(value, 'ctx', pairs)]
    unnamed x16, local copies, waits for them, and re-layouts: 0.73 us -> 0.07 us
  transfers between devices with their start and end apart: 22 -> 22, of which waited for: 7 -> 6; matrix products, arithmetic and copies ran while one was open for 0% -> 0% of each run, Pallas kernels for 10% -> 11%
where the time goes in v6:
time: 62.6 us; the launch traced here: 61.4 us
  starting transfers between devices  43.4 us (69%)
  Pallas kernels  10.5 us (17%)
  waiting for transfers between devices  6.27 us (10%)
  other arithmetic  0.97 us (2%)
    ppermute x8, starting transfers between devices, move(): return lax.ppermute(value, 'ctx', pairs)  19.7 us
    ppermute x8, starting transfers between devices, turn(): return lax.ppermute(value, 'tp', [(i, (i + k) % NZ) for i in range(NZ)])  14.3 us
    pallas_call x14, Pallas kernels, call(): pl.pallas_call(kernel, out_shape=outs, in_specs=[VMEM] * len(args), out_s...  10.5 us
    ppermute x6, starting transfers between devices, trade(): return lax.ppermute(value, 'ctx', pairs)  9.44 us
    ppermute x8, waiting for transfers between devices, move(): return lax.ppermute(value, 'ctx', pairs)  3.95 us
    ppermute x6, waiting for transfers between devices, trade(): return lax.ppermute(value, 'ctx', pairs)  2.3 us
  transfers between devices with their start and end apart: 22, of which 6 were waited for; matrix products, arithmetic and copies ran while one was open for 0% of the time, Pallas kernels for 11%

profile of v6, /device:TPU:1, one launch (start us, length us, event | category | flops | bytes accessed | tf_op | source)
XLA Modules:
  0.0 61.4 jit_solution(8858461719752441633)
XLA Ops:
  0.0 1.0 %sine_multiply_fusion = (f32[16,512]{1,0:T(8,128)S(1)}, f32[16,512]{1,0:T(8,128)S(1)}) fusion(f32[16,512]{1,0:T(8,128)} %param.13, f32[16,512]{1,0:T(8,128)} %decay_ref.1), kind=kLoop, calls=%fused_computation | loop fusion | flops 24576 | bytes 131072 | tf_op jit(solution)/shard_map/mul | solution.py:482
  1.4 2.3 %shard_map.92 = (f32[40,512]{1,0:T(8,128)S(1)}, f32[4,32,8,128]{3,2,1,0:T(8,128)S(1)}, f32[4,256,128]{2,1,0:T(8,128)S(1)}) custom-call(bf16[256,512]{1,0:T(8,128)(2,1)S(1)} %copy-done, bf16[256,512]{1,0:T(8,128)(2,1)S(1)} %copy-done.1, s32[2,128]{1,0:T(2,128)S(1)} %bitcast.2, f32[4,528,128]{2,1,0:T(8,128)S(1)} %get-tuple-element.27.tre, ...), custom_call_target="tpu_custom_call" | custom-call | flops 20000000 | bytes 5000000 | tf_op jit(solution)/shard_map/pallas_call | solution.py:28
  3.6 3.3 %collective-permute-start = (f32[40,512]{1,0:T(8,128)S(1)}, f32[40,512]{1,0:T(8,128)S(1)}, u32[]{:S(2)}, u32[]{:S(2)}) collective-permute-start(f32[40,512]{1,0:T(8,128)S(1)} %get-tuple-element.32.own_ref), channel_id=1, source_target_pairs={{0,8},{8,0},{16,24},{24,16},{32,40},{40,32},{48,56},{56,48},{64,72... | collective-permute-start | bytes 245768 | tf_op jit(solution)/shard_map/ppermute | solution.py:455
  8.0 2.2 %collective-permute-start.2 = (bf16[80,512]{1,0:T(8,128)(2,1)S(1)}, bf16[80,512]{1,0:T(8,128)(2,1)S(1)}, u32[]{:S(2)}, u32[]{:S(2)}) collective-permute-start(bf16[80,512]{1,0:T(8,128)(2,1)S(1)} %shard_map.93.after_ref.own_ref), channel_id=1, source_target_pairs={{0,32},{8,40},{16,48},{24,56},{32,0},{40,8},{48,16},{56,24},{64,96... | collective-permute-start | bytes 245768 | tf_op jit(solution)/shard_map/ppermute | solution.py:455
  10.2 1.1 %collective-permute-start.3 = (bf16[80,512]{1,0:T(8,128)(2,1)S(1)}, bf16[80,512]{1,0:T(8,128)(2,1)S(1)}, u32[]{:S(2)}, u32[]{:S(2)}) collective-permute-start(bf16[80,512]{1,0:T(8,128)(2,1)S(1)} %shard_map.93.after_ref.own_ref), channel_id=1, source_target_pairs={{0,48},{8,56},{16,0},{24,8},{32,16},{40,24},{48,32},{56,40},{64,11... | collective-permute-start | bytes 245768 | tf_op jit(solution)/shard_map/ppermute | solution.py:455
  11.3 1.2 %collective-permute-start.12 = (bf16[128,512]{1,0:T(8,128)(2,1)S(1)}, bf16[128,512]{1,0:T(8,128)(2,1)S(1)}, u32[]{:S(2)}, u32[]{:S(2)}) collective-permute-start(bf16[128,512]{1,0:T(8,128)(2,1)S(1)} %copy-done.3), channel_id=1, source_target_pairs={{0,64},{8,72},{16,80},{24,88},{32,96},{40,104},{48,112},{56,120},{... | collective-permute-start | bytes 393224 | tf_op jit(solution)/shard_map/ppermute | solution.py:461
  12.5 1.2 %collective-permute-done.1.one_ref = bf16[80,512]{1,0:T(8,128)(2,1)S(1)} collective-permute-done((bf16[80,512]{1,0:T(8,128)(2,1)S(1)}, bf16[80,512]{1,0:T(8,128)(2,1)S(1)}, u32[]{:S(2)}, u32[]{:S(2)}) %collective-permute-start.1) | collective-permute-done | bytes 81952 | tf_op jit(solution)/shard_map/ppermute | solution.py:455
  15.6 2.5 %collective-permute-start.5 = (f32[40,512]{1,0:T(8,128)S(1)}, f32[40,512]{1,0:T(8,128)S(1)}, u32[]{:S(2)}, u32[]{:S(2)}) collective-permute-start(f32[40,512]{1,0:T(8,128)S(1)} %get-tuple-element.41.after_ref), channel_id=1, source_target_pairs={{0,128},{8,136},{16,144},{24,152},{32,160},{40,168},{48,176},{56,1... | collective-permute-start | bytes 245768 | tf_op jit(solution)/shard_map/ppermute | solution.py:455
  18.1 2.1 %shard_map.94 = (f32[4,32,8,128]{3,2,1,0:T(8,128)S(1)}, f32[32,512]{1,0:T(8,128)S(1)}) custom-call(f32[4,256,128]{2,1,0:T(8,128)S(1)} %get-tuple-element.31.sig, f32[4,528,128]{2,1,0:T(8,128)S(1)} %get-tuple-element.27.tre, f32[4,528,128]{2,1,0:T(8,128)S(1)} %get-tuple-element.28.tim, f32[16,512]{1,0:T(8,128)S(1)} %copy-done.2, f32[2,16,512]{2,1,0:T(8,128)S(1)} %copy-done.4, ...), custom_call_target="tpu_custom_call" | custom-call | flops 30000000 | bytes 5000000 | tf_op jit(solution)/shard_map/pallas_call | solution.py:28
  21.1 1.7 %shard_map.97.after_ref.here = bf16[64,2048]{1,0:T(8,128)(2,1)S(1)} custom-call(bf16[256,512]{1,0:T(8,128)(2,1)S(1)} %copy-done.7, f32[4,32,8,128]{3,2,1,0:T(8,128)S(1)} %get-tuple-element.34.y_ref, f32[4,32,8,128]{3,2,1,0:T(8,128)S(1)} %get-tuple-element.37.pz_ref, f32[4,32,8,128]{3,2,1,0:T(8,128)S(1)} %get-tuple-element.38.gz_ref, ...), custom_call_target="tpu_custom_call" | custom-call | flops 2000000000 | bytes 5000000 | tf_op jit(solution)/shard_map/pallas_call | solution.py:28
  22.8 1.7 %collective-permute-start.6 = (bf16[64,2048]{1,0:T(8,128)(2,1)S(1)}, bf16[64,2048]{1,0:T(8,128)(2,1)S(1)}, u32[]{:S(2)}, u32[]{:S(2)}) collective-permute-start(bf16[64,2048]{1,0:T(8,128)(2,1)S(1)} %shard_map.97.after_ref.here), channel_id=1, source_target_pairs={{0,1},{1,2},{2,3},{3,4},{4,5},{5,6},{6,7},{7,0},{8,9},{9,10},{10,1... | collective-permute-start | bytes 786440 | tf_op jit(solution)/shard_map/ppermute | solution.py:465
  24.5 4.0 %collective-permute-start.7 = (bf16[64,2048]{1,0:T(8,128)(2,1)S(1)}, bf16[64,2048]{1,0:T(8,128)(2,1)S(1)}, u32[]{:S(2)}, u32[]{:S(2)}) collective-permute-start(bf16[64,2048]{1,0:T(8,128)(2,1)S(1)} %shard_map.97.after_ref.here), channel_id=1, source_target_pairs={{0,7},{1,0},{2,1},{3,2},{4,3},{5,4},{6,5},{7,6},{8,15},{9,8},{10,9... | collective-permute-start | bytes 786440 | tf_op jit(solution)/shard_map/ppermute | solution.py:465
  28.6 2.2 %collective-permute-start.14 = (bf16[256,512]{1,0:T(8,128)(2,1)S(1)}, bf16[256,512]{1,0:T(8,128)(2,1)S(1)}, u32[]{:S(2)}, u32[]{:S(2)}) collective-permute-start(bf16[256,512]{1,0:T(8,128)(2,1)S(1)} %get-tuple-element.42.even_ref), channel_id=1, source_target_pairs={{0,128},{8,136},{16,144},{24,152},{32,160},{40,168},{48,176},{56,1... | collective-permute-start | bytes 786440 | tf_op jit(solution)/shard_map/ppermute | solution.py:461
  30.8 2.0 %collective-permute-start.15 = (bf16[256,512]{1,0:T(8,128)(2,1)S(1)}, bf16[256,512]{1,0:T(8,128)(2,1)S(1)}, u32[]{:S(2)}, u32[]{:S(2)}) collective-permute-start(bf16[256,512]{1,0:T(8,128)(2,1)S(1)} %get-tuple-element.43.odd_ref), channel_id=1, source_target_pairs={{0,32},{8,40},{16,48},{24,56},{32,0},{40,8},{48,16},{56,24},{64,96... | collective-permute-start | bytes 786440 | tf_op jit(solution)/shard_map/ppermute | solution.py:461
  32.8 2.7 %collective-permute-start.9 = (bf16[64,2048]{1,0:T(8,128)(2,1)S(1)}, bf16[64,2048]{1,0:T(8,128)(2,1)S(1)}, u32[]{:S(2)}, u32[]{:S(2)}) collective-permute-start(bf16[64,2048]{1,0:T(8,128)(2,1)S(1)} %collective-permute-done.7.after_down.down1), channel_id=1, source_target_pairs={{0,7},{1,0},{2,1},{3,2},{4,3},{5,4},{6,5},{7,6},{8,15},{9,8},{10,9... | collective-permute-start | bytes 786440 | tf_op jit(solution)/shard_map/ppermute | solution.py:465
  35.5 2.3 %collective-permute-done.15.odd_y = bf16[256,512]{1,0:T(8,128)(2,1)S(1)} collective-permute-done((bf16[256,512]{1,0:T(8,128)(2,1)S(1)}, bf16[256,512]{1,0:T(8,128)(2,1)S(1)}, u32[]{:S(2)}, u32[]{:S(2)}) %collective-permute-start.15) | collective-permute-done | bytes 262176 | tf_op jit(solution)/shard_map/ppermute | solution.py:461
  37.9 2.3 %collective-permute-start.16 = (bf16[512,512]{1,0:T(8,128)(2,1)S(1)}, bf16[512,512]{1,0:T(8,128)(2,1)S(1)}, u32[]{:S(2)}, u32[]{:S(2)}) collective-permute-start(bf16[512,512]{1,0:T(8,128)(2,1)S(1)} %get-tuple-element.45), channel_id=1, source_target_pairs={{0,32},{8,40},{16,48},{24,56},{32,0},{40,8},{48,16},{56,24},{64,96... | collective-permute-start | bytes 1572872 | tf_op jit(solution)/shard_map/ppermute | solution.py:461
  40.2 1.5 %collective-permute-start.17 = (bf16[512,512]{1,0:T(8,128)(2,1)S(1)}, bf16[512,512]{1,0:T(8,128)(2,1)S(1)}, u32[]{:S(2)}, u32[]{:S(2)}) collective-permute-start(bf16[512,512]{1,0:T(8,128)(2,1)S(1)} %get-tuple-element.46), channel_id=1, source_target_pairs={{0,128},{8,136},{16,144},{24,152},{32,160},{40,168},{48,176},{56,1... | collective-permute-start | bytes 1572872 | tf_op jit(solution)/shard_map/ppermute | solution.py:461
  41.8 3.1 %collective-permute-start.11 = (bf16[64,2048]{1,0:T(8,128)(2,1)S(1)}, bf16[64,2048]{1,0:T(8,128)(2,1)S(1)}, u32[]{:S(2)}, u32[]{:S(2)}) collective-permute-start(bf16[64,2048]{1,0:T(8,128)(2,1)S(1)} %collective-permute-done.9.down2), channel_id=1, source_target_pairs={{0,7},{1,0},{2,1},{3,2},{4,3},{5,4},{6,5},{7,6},{8,15},{9,8},{10,9... | collective-permute-start | bytes 786440 | tf_op jit(solution)/shard_map/ppermute | solution.py:465
  44.9 5.1 %collective-permute-start.18 = (bf16[1024,512]{1,0:T(8,128)(2,1)S(1)}, bf16[1024,512]{1,0:T(8,128)(2,1)S(1)}, u32[]{:S(2)}, u32[]{:S(2)}) collective-permute-start(bf16[1024,512]{1,0:T(8,128)(2,1)S(1)} %get-tuple-element.44.near_own), channel_id=1, source_target_pairs={{0,8},{8,0},{16,24},{24,16},{32,40},{40,32},{48,56},{56,48},{64,72... | collective-permute-start | bytes 3145736 | tf_op jit(solution)/shard_map/ppermute | solution.py:455
  50.1 2.7 %collective-permute-start.20 = (bf16[32,2048]{1,0:T(8,128)(2,1)S(1)}, bf16[32,2048]{1,0:T(8,128)(2,1)S(1)}, u32[]{:S(2)}, u32[]{:S(2)}) collective-permute-start(bf16[32,2048]{1,0:T(8,128)(2,1)S(1)} %slice.9), channel_id=1, source_target_pairs={{0,7},{1,0},{2,1},{3,2},{4,3},{5,4},{6,5},{7,6},{8,15},{9,8},{10,9... | collective-permute-start | bytes 393224 | tf_op jit(solution)/shard_map/ppermute | solution.py:465
  52.9 5.0 %collective-permute-start.21 = (bf16[1024,512]{1,0:T(8,128)(2,1)S(1)}, bf16[1024,512]{1,0:T(8,128)(2,1)S(1)}, u32[]{:S(2)}, u32[]{:S(2)}) collective-permute-start(bf16[1024,512]{1,0:T(8,128)(2,1)S(1)} %shard_map.101.far_own.own_ref), channel_id=1, source_target_pairs={{0,8},{8,0},{16,24},{24,16},{32,40},{40,32},{48,56},{56,48},{64,72... | collective-permute-start | bytes 3145736 | tf_op jit(solution)/shard_map/ppermute | solution.py:455
  57.9 1.7 %shard_map.102 = (f32[256,512]{1,0:T(8,128)S(1)}, bf16[256,1024]{1,0:T(8,128)(2,1)S(1)}) custom-call(bf16[64,2048]{1,0:T(8,128)(2,1)S(1)} %shard_map.97.after_ref.here, bf16[64,2048]{1,0:T(8,128)(2,1)S(1)} %collective-permute-done.6.after_up.up1, bf16[64,2048]{1,0:T(8,128)(2,1)S(1)} %collective-permute-done.7.after_down.down1, ...), custom_call_target="tpu_custom_call" | custom-call | flops 8000000000 | bytes 7000000 | tf_op jit(solution)/shard_map/pallas_call | solution.py:28
  60.1 1.3 %shard_map.104 = bf16[256,512]{1,0:T(8,128)(2,1)} custom-call(f32[256,512]{1,0:T(8,128)S(1)} %get-tuple-element.47.total_ref, bf16[256,1024]{1,0:T(8,128)(2,1)S(1)} %get-tuple-element.48.left, bf16[256,512]{1,0:T(8,128)(2,1)S(1)} %shard_map.103.last, bf16[1024,512]{1,0:T(8,128)(2,1)S(1)} %get-tuple-element.44.near_own, ...), custom_call_target="tpu_custom_call" | custom-call | flops 536870912 | bytes 7000000 | tf_op jit(solution)/shard_map/pallas_call | solution.py:28
  (53 shorter events, 5.2 us)
Async XLA Ops:
  1.4 16.7 %copy-start.2 = (f32[16,512]{1,0:T(8,128)S(1)}, f32[16,512]{1,0:T(8,128)}, u32[]{:S(2)}) copy-start(f32[16,512]{1,0:T(8,128)} %decay_ref.1) | copy-start | bytes 98308
  1.4 16.7 %copy-start.4 = (f32[2,16,512]{2,1,0:T(8,128)S(1)}, f32[2,16,512]{2,1,0:T(8,128)}, u32[]{:S(2)}) copy-start(f32[2,16,512]{2,1,0:T(8,128)} %res_ref.1) | copy-start | bytes 196612
  3.6 4.2 %collective-permute-start = (f32[40,512]{1,0:T(8,128)S(1)}, f32[40,512]{1,0:T(8,128)S(1)}, u32[]{:S(2)}, u32[]{:S(2)}) collective-permute-start(f32[40,512]{1,0:T(8,128)S(1)} %get-tuple-element.32.own_ref), channel_id=1, source_target_pairs={{0,8},{8,0},{16,24},{24,16},{32,40},{40,32},{48,56},{56,48},{64,72... | collective-permute-start | bytes 245768 | tf_op jit(solution)/shard_map/ppermute | solution.py:455
  7.9 5.8 %collective-permute-start.1 = (bf16[80,512]{1,0:T(8,128)(2,1)S(1)}, bf16[80,512]{1,0:T(8,128)(2,1)S(1)}, u32[]{:S(2)}, u32[]{:S(2)}) collective-permute-start(bf16[80,512]{1,0:T(8,128)(2,1)S(1)} %shard_map.93.after_ref.own_ref), channel_id=1, source_target_pairs={{0,16},{8,24},{16,32},{24,40},{32,48},{40,56},{48,0},{56,8},{64,80... | collective-permute-start | bytes 245768 | tf_op jit(solution)/shard_map/ppermute | solution.py:455
  8.0 6.1 %collective-permute-start.2 = (bf16[80,512]{1,0:T(8,128)(2,1)S(1)}, bf16[80,512]{1,0:T(8,128)(2,1)S(1)}, u32[]{:S(2)}, u32[]{:S(2)}) collective-permute-start(bf16[80,512]{1,0:T(8,128)(2,1)S(1)} %shard_map.93.after_ref.own_ref), channel_id=1, source_target_pairs={{0,32},{8,40},{16,48},{24,56},{32,0},{40,8},{48,16},{56,24},{64,96... | collective-permute-start | bytes 245768 | tf_op jit(solution)/shard_map/ppermute | solution.py:455
  10.2 4.7 %collective-permute-start.3 = (bf16[80,512]{1,0:T(8,128)(2,1)S(1)}, bf16[80,512]{1,0:T(8,128)(2,1)S(1)}, u32[]{:S(2)}, u32[]{:S(2)}) collective-permute-start(bf16[80,512]{1,0:T(8,128)(2,1)S(1)} %shard_map.93.after_ref.own_ref), channel_id=1, source_target_pairs={{0,48},{8,56},{16,0},{24,8},{32,16},{40,24},{48,32},{56,40},{64,11... | collective-permute-start | bytes 245768 | tf_op jit(solution)/shard_map/ppermute | solution.py:455
  11.3 9.6 %collective-permute-start.12 = (bf16[128,512]{1,0:T(8,128)(2,1)S(1)}, bf16[128,512]{1,0:T(8,128)(2,1)S(1)}, u32[]{:S(2)}, u32[]{:S(2)}) collective-permute-start(bf16[128,512]{1,0:T(8,128)(2,1)S(1)} %copy-done.3), channel_id=1, source_target_pairs={{0,64},{8,72},{16,80},{24,88},{32,96},{40,104},{48,112},{56,120},{... | collective-permute-start | bytes 393224 | tf_op jit(solution)/shard_map/ppermute | solution.py:461
  15.1 6.0 %collective-permute-start.4 = (f32[40,512]{1,0:T(8,128)S(1)}, f32[40,512]{1,0:T(8,128)S(1)}, u32[]{:S(2)}, u32[]{:S(2)}) collective-permute-start(f32[40,512]{1,0:T(8,128)S(1)} %get-tuple-element.41.after_ref), channel_id=1, source_target_pairs={{0,64},{8,72},{16,80},{24,88},{32,96},{40,104},{48,112},{56,120},{... | collective-permute-start | bytes 245768 | tf_op jit(solution)/shard_map/ppermute | solution.py:455
  15.6 5.5 %collective-permute-start.5 = (f32[40,512]{1,0:T(8,128)S(1)}, f32[40,512]{1,0:T(8,128)S(1)}, u32[]{:S(2)}, u32[]{:S(2)}) collective-permute-start(f32[40,512]{1,0:T(8,128)S(1)} %get-tuple-element.41.after_ref), channel_id=1, source_target_pairs={{0,128},{8,136},{16,144},{24,152},{32,160},{40,168},{48,176},{56,1... | collective-permute-start | bytes 245768 | tf_op jit(solution)/shard_map/ppermute | solution.py:455
  20.9 7.7 %collective-permute-start.13 = (bf16[256,512]{1,0:T(8,128)(2,1)S(1)}, bf16[256,512]{1,0:T(8,128)(2,1)S(1)}, u32[]{:S(2)}, u32[]{:S(2)}) collective-permute-start(bf16[256,512]{1,0:T(8,128)(2,1)S(1)} %shard_map.98.both_ref), channel_id=1, source_target_pairs={{0,16},{8,24},{16,0},{24,8},{32,48},{40,56},{48,32},{56,40},{64,80... | collective-permute-start | bytes 786440 | tf_op jit(solution)/shard_map/ppermute | solution.py:461
  22.8 10.0 %collective-permute-start.6 = (bf16[64,2048]{1,0:T(8,128)(2,1)S(1)}, bf16[64,2048]{1,0:T(8,128)(2,1)S(1)}, u32[]{:S(2)}, u32[]{:S(2)}) collective-permute-start(bf16[64,2048]{1,0:T(8,128)(2,1)S(1)} %shard_map.97.after_ref.here), channel_id=1, source_target_pairs={{0,1},{1,2},{2,3},{3,4},{4,5},{5,6},{6,7},{7,0},{8,9},{9,10},{10,1... | collective-permute-start | bytes 786440 | tf_op jit(solution)/shard_map/ppermute | solution.py:465
  24.5 8.3 %collective-permute-start.7 = (bf16[64,2048]{1,0:T(8,128)(2,1)S(1)}, bf16[64,2048]{1,0:T(8,128)(2,1)S(1)}, u32[]{:S(2)}, u32[]{:S(2)}) collective-permute-start(bf16[64,2048]{1,0:T(8,128)(2,1)S(1)} %shard_map.97.after_ref.here), channel_id=1, source_target_pairs={{0,7},{1,0},{2,1},{3,2},{4,3},{5,4},{6,5},{7,6},{8,15},{9,8},{10,9... | collective-permute-start | bytes 786440 | tf_op jit(solution)/shard_map/ppermute | solution.py:465
  28.6 6.9 %collective-permute-start.14 = (bf16[256,512]{1,0:T(8,128)(2,1)S(1)}, bf16[256,512]{1,0:T(8,128)(2,1)S(1)}, u32[]{:S(2)}, u32[]{:S(2)}) collective-permute-start(bf16[256,512]{1,0:T(8,128)(2,1)S(1)} %get-tuple-element.42.even_ref), channel_id=1, source_target_pairs={{0,128},{8,136},{16,144},{24,152},{32,160},{40,168},{48,176},{56,1... | collective-permute-start | bytes 786440 | tf_op jit(solution)/shard_map/ppermute | solution.py:461
  30.8 7.0 %collective-permute-start.15 = (bf16[256,512]{1,0:T(8,128)(2,1)S(1)}, bf16[256,512]{1,0:T(8,128)(2,1)S(1)}, u32[]{:S(2)}, u32[]{:S(2)}) collective-permute-start(bf16[256,512]{1,0:T(8,128)(2,1)S(1)} %get-tuple-element.43.odd_ref), channel_id=1, source_target_pairs={{0,32},{8,40},{16,48},{24,56},{32,0},{40,8},{48,16},{56,24},{64,96... | collective-permute-start | bytes 786440 | tf_op jit(solution)/shard_map/ppermute | solution.py:461
  32.8 9.0 %collective-permute-start.8 = (bf16[64,2048]{1,0:T(8,128)(2,1)S(1)}, bf16[64,2048]{1,0:T(8,128)(2,1)S(1)}, u32[]{:S(2)}, u32[]{:S(2)}) collective-permute-start(bf16[64,2048]{1,0:T(8,128)(2,1)S(1)} %collective-permute-done.6.after_up.up1), channel_id=1, source_target_pairs={{0,1},{1,2},{2,3},{3,4},{4,5},{5,6},{6,7},{7,0},{8,9},{9,10},{10,1... | collective-permute-start | bytes 786440 | tf_op jit(solution)/shard_map/ppermute | solution.py:465
  32.8 9.0 %collective-permute-start.9 = (bf16[64,2048]{1,0:T(8,128)(2,1)S(1)}, bf16[64,2048]{1,0:T(8,128)(2,1)S(1)}, u32[]{:S(2)}, u32[]{:S(2)}) collective-permute-start(bf16[64,2048]{1,0:T(8,128)(2,1)S(1)} %collective-permute-done.7.after_down.down1), channel_id=1, source_target_pairs={{0,7},{1,0},{2,1},{3,2},{4,3},{5,4},{6,5},{7,6},{8,15},{9,8},{10,9... | collective-permute-start | bytes 786440 | tf_op jit(solution)/shard_map/ppermute | solution.py:465
  37.9 14.9 %collective-permute-start.16 = (bf16[512,512]{1,0:T(8,128)(2,1)S(1)}, bf16[512,512]{1,0:T(8,128)(2,1)S(1)}, u32[]{:S(2)}, u32[]{:S(2)}) collective-permute-start(bf16[512,512]{1,0:T(8,128)(2,1)S(1)} %get-tuple-element.45), channel_id=1, source_target_pairs={{0,32},{8,40},{16,48},{24,56},{32,0},{40,8},{48,16},{56,24},{64,96... | collective-permute-start | bytes 1572872 | tf_op jit(solution)/shard_map/ppermute | solution.py:461
  40.2 12.5 %collective-permute-start.17 = (bf16[512,512]{1,0:T(8,128)(2,1)S(1)}, bf16[512,512]{1,0:T(8,128)(2,1)S(1)}, u32[]{:S(2)}, u32[]{:S(2)}) collective-permute-start(bf16[512,512]{1,0:T(8,128)(2,1)S(1)} %get-tuple-element.46), channel_id=1, source_target_pairs={{0,128},{8,136},{16,144},{24,152},{32,160},{40,168},{48,176},{56,1... | collective-permute-start | bytes 1572872 | tf_op jit(solution)/shard_map/ppermute | solution.py:461
  41.8 8.1 %collective-permute-start.10 = (bf16[64,2048]{1,0:T(8,128)(2,1)S(1)}, bf16[64,2048]{1,0:T(8,128)(2,1)S(1)}, u32[]{:S(2)}, u32[]{:S(2)}) collective-permute-start(bf16[64,2048]{1,0:T(8,128)(2,1)S(1)} %collective-permute-done.8.up2), channel_id=1, source_target_pairs={{0,1},{1,2},{2,3},{3,4},{4,5},{5,6},{6,7},{7,0},{8,9},{9,10},{10,1... | collective-permute-start | bytes 786440 | tf_op jit(solution)/shard_map/ppermute | solution.py:465
  41.8 8.2 %collective-permute-start.11 = (bf16[64,2048]{1,0:T(8,128)(2,1)S(1)}, bf16[64,2048]{1,0:T(8,128)(2,1)S(1)}, u32[]{:S(2)}, u32[]{:S(2)}) collective-permute-start(bf16[64,2048]{1,0:T(8,128)(2,1)S(1)} %collective-permute-done.9.down2), channel_id=1, source_target_pairs={{0,7},{1,0},{2,1},{3,2},{4,3},{5,4},{6,5},{7,6},{8,15},{9,8},{10,9... | collective-permute-start | bytes 786440 | tf_op jit(solution)/shard_map/ppermute | solution.py:465
  44.9 13.0 %collective-permute-start.18 = (bf16[1024,512]{1,0:T(8,128)(2,1)S(1)}, bf16[1024,512]{1,0:T(8,128)(2,1)S(1)}, u32[]{:S(2)}, u32[]{:S(2)}) collective-permute-start(bf16[1024,512]{1,0:T(8,128)(2,1)S(1)} %get-tuple-element.44.near_own), channel_id=1, source_target_pairs={{0,8},{8,0},{16,24},{24,16},{32,40},{40,32},{48,56},{56,48},{64,72... | collective-permute-start | bytes 3145736 | tf_op jit(solution)/shard_map/ppermute | solution.py:455
  49.9 7.9 %collective-permute-start.19 = (bf16[32,2048]{1,0:T(8,128)(2,1)S(1)}, bf16[32,2048]{1,0:T(8,128)(2,1)S(1)}, u32[]{:S(2)}, u32[]{:S(2)}) collective-permute-start(bf16[32,2048]{1,0:T(8,128)(2,1)S(1)} %slice.8), channel_id=1, source_target_pairs={{0,1},{1,2},{2,3},{3,4},{4,5},{5,6},{6,7},{7,0},{8,9},{9,10},{10,1... | collective-permute-start | bytes 393224 | tf_op jit(solution)/shard_map/ppermute | solution.py:465
  50.1 7.8 %collective-permute-start.20 = (bf16[32,2048]{1,0:T(8,128)(2,1)S(1)}, bf16[32,2048]{1,0:T(8,128)(2,1)S(1)}, u32[]{:S(2)}, u32[]{:S(2)}) collective-permute-start(bf16[32,2048]{1,0:T(8,128)(2,1)S(1)} %slice.9), channel_id=1, source_target_pairs={{0,7},{1,0},{2,1},{3,2},{4,3},{5,4},{6,5},{7,6},{8,15},{9,8},{10,9... | collective-permute-start | bytes 393224 | tf_op jit(solution)/shard_map/ppermute | solution.py:465
  52.9 7.3 %collective-permute-start.21 = (bf16[1024,512]{1,0:T(8,128)(2,1)S(1)}, bf16[1024,512]{1,0:T(8,128)(2,1)S(1)}, u32[]{:S(2)}, u32[]{:S(2)}) collective-permute-start(bf16[1024,512]{1,0:T(8,128)(2,1)S(1)} %shard_map.101.far_own.own_ref), channel_id=1, source_target_pairs={{0,8},{8,0},{16,24},{24,16},{32,40},{40,32},{48,56},{56,48},{64,72... | collective-permute-start | bytes 3145736 | tf_op jit(solution)/shard_map/ppermute | solution.py:455
  (6 other events, 31.5 us)

commit v7 on v6

--- a/solution.py
+++ b/solution.py
@@ -19,7 +19,7 @@
 FLAG = 16
 SENT = 2 * ROWS + FLAG
 WROWS = 128
-FOLD = 4
+FOLD = 8
 THIN = TOK // FOLD
 PARAMS = pltpu.CompilerParams(vmem_limit_bytes=24 * 1024 * 1024)
 
@@ -284,10 +284,10 @@
 
 
 def pair_kernel(own_ref, pair_ref, after_ref, out_ref):
-    put_pair(out_ref, lax.axis_index("ctx") // (NC * NY) % 2, own_ref, pair_ref)
-
-
-def row_kernel(own_ref, one_ref, two_ref, three_ref, p256_ref, pay_ref, before_ref, factor_ref, held):
+    put_pair(out_ref, lax.axis_index("ctx") // (NC * NY * 2), own_ref, pair_ref)
+
+
+def row_kernel(own_ref, one_ref, two_ref, three_ref, p256_ref, after_ref, pay_ref, before_ref, factor_ref, held):
     mine = (lax.axis_index("ctx") // NC) % NY
     for k, ref in enumerate((own_ref, one_ref, two_ref, three_ref)):
         there = lax.rem(mine - k + NY, NY)
@@ -370,7 +370,7 @@
 
 
 def four_kernel(both_ref, pair_ref, after_ref, even_ref, odd_ref):
-    side = (lax.axis_index("ctx") // NC) % 2
+    side = (lax.axis_index("ctx") // NC) % NY // 2
     even_ref[...] = jnp.where(side == 0, both_ref[...], pair_ref[...])
     odd_ref[...] = jnp.where(side == 0, pair_ref[...], both_ref[...])
 
@@ -391,15 +391,15 @@
 
 def places(k):
     index = lax.axis_index("ctx")
-    xb, yb = index // (NC * NY * 2), (index // NC) % NY // 2
+    x, y = index // (NC * NY), (index // NC) % NY
     block = lax.rem(lax.axis_index("tp") - k + NZ, NZ)
-    dx = (block // 4 != xb).astype(jnp.int32)
-    dy = (lax.rem(block, 2) != yb).astype(jnp.int32)
-    i = lax.rem(block // 2, 2)
+    odd, i = lax.rem(block, 2), block // 4
+    dx = (lax.rem(block // 2, 2) != lax.rem(x, 2)).astype(jnp.int32)
     found = []
     for h in range(2):
-        far, near = (dy, dx) if h == 0 else (dx, dy)
-        at = far * 8 * WROWS + h * 4 * WROWS + near * 2 * WROWS + i * WROWS
+        dy = (lax.rem(y, 2) != h).astype(jnp.int32)
+        far, near = jnp.where(odd == 1, dx, dy), jnp.where(odd == 1, dy, dx)
+        at = far * 8 * WROWS + odd * 4 * WROWS + near * 2 * WROWS + i * WROWS
         found.append(pl.ds(pl.multiple_of(at, WROWS), WROWS))
     return found
 
@@ -423,7 +423,7 @@
     left_ref[...] = left[1, :, wide:]
 
 
-def last_kernel(up4, down4, out_ref):
+def last_kernel(up4, down4, after_ref, out_ref):
     for q in range(FOLD):
         middle = q * THIN + THIN // 2
         lanes = slice(q * CH, (q + 1) * CH)
@@ -479,21 +479,21 @@
     q_shape = struct(GROUPS, BLOCKS * MODES, LANES)
     tre, tim, qre, qim, p256 = call(
         powers_kernel, (struct(*table), struct(*table), q_shape, q_shape, state_shape),
-        (magnitude * jnp.cos(freq), magnitude * jnp.sin(freq)), (), 300000000, 5_000_000)
+        (magnitude * jnp.cos(freq), magnitude * jnp.sin(freq)), (), 300_000_000, 5_000_000)
     pay, eb, signal = call(
         ends_kernel, (pay_shape, block_shape, struct(GROUPS, TOK, LANES)),
         (key, value, starts, tre, tim, qre, qim), (), 20_000_000, 5_000_000)
     other = move(pay, 0, 0, 1)
     chip = call(chip_kernel, struct(SENT, CH, dtype=BF16), (pay, other, p256))
     near = [move(chip, 0, k, 0) for k in (1, 2, 3)]
-    row, before, factor = call(
-        row_kernel, (pay_shape, state_shape, state_shape),
-        (chip, *near, p256), [pltpu.VMEM((NY, PAY, CH), F32)])
-    back = [move(row, k, 0, 0) for k in (1, 2)]
     y, gain = call(
         local_kernel, (struct(GROUPS, STEPS, BLOCKS, LANES), state_shape),
         (signal, tre, tim, decay, residue, skip, starts, chip),
         [pltpu.VMEM((GROUPS, STEPS, LANES), F32)], 30_000_000, 5_000_000)
+    row, before, factor = call(
+        row_kernel, (pay_shape, state_shape, state_shape),
+        (chip, *near, p256, gain), [pltpu.VMEM((NY, PAY, CH), F32)])
+    back = [move(row, k, 0, 0) for k in (1, 2)]
     pz, gz = call(
         carry_kernel, (block_shape, block_shape), (eb, tre, tim, gain, starts),
         [qs, qs, pltpu.VMEM((GROUPS, 4 * ROWS, LANES), F32)], 30_000_000, 5_000_000)
@@ -502,23 +502,23 @@
         (query, y, pz, gz, tre, tim, starts, pay, other, p256, before, factor, *back),
         [sig, pltpu.VMEM((GROUPS, ROWS, LANES), F32)], 2_000_000_000, 5_000_000)
 
-    both = call(pair_kernel, struct(2 * WROWS, CH, dtype=BF16), (out_weight, trade(out_weight, 1, 0), row))
+    both = call(pair_kernel, struct(2 * WROWS, CH, dtype=BF16), (out_weight, trade(out_weight, 2, 0), row))
     w2, w4, w8 = [struct(n * WROWS, CH, dtype=BF16) for n in (2, 4, 8)]
-    even, odd = call(four_kernel, (w2, w2), (both, trade(both, 0, 1), hidden), (), 0, 2_000_000)
+    even, odd = call(four_kernel, (w2, w2), (both, trade(both, 0, 2), hidden), (), 0, 2_000_000)
     half = THIN // 2
     up1, down1 = turn(hidden, 1), turn(hidden, -1)
     near, even, odd = call(
-        eight_kernel, (w8, w4, w4), (even, trade(even, 2, 0), odd, trade(odd, 0, 2), up1, down1), (), 0, 4_000_000)
+        eight_kernel, (w8, w4, w4), (even, trade(even, 1, 0), odd, trade(odd, 0, 1), up1, down1), (), 0, 4_000_000)
     up2, down2 = turn(up1, 1), turn(down1, -1)
     up3, down3 = turn(up2, 1), turn(down2, -1)
     up4, down4 = turn(up3[:half], 1), turn(down3[half:], -1)
-    far = call(join_kernel, w8, (trade(even, 0, 2), trade(odd, 2, 0), up3, down3), (), 0, 2_000_000)
+    far = call(join_kernel, w8, (trade(even, 0, 1), trade(odd, 1, 0), up3, down3), (), 10000000000, 2_000_000)
     near_other = move(near, 0, 0, 1)
     total, left = call(
         most_kernel, (struct(TOK, CH), struct(TOK, 8 * WROWS, dtype=BF16)),
         (hidden, up1, down1, up2, down2, up3, down3, near, far, near_other),
         [pltpu.VMEM((NC, TOK, NZ * CH // NC), BF16)], 8000000000, 7_000_000)
-    last = call(last_kernel, struct(TOK, CH, dtype=BF16), (up4, down4), (), 8000000000, 1_000_000)
+    last = call(last_kernel, struct(TOK, CH, dtype=BF16), (up4, down4, total), (), 8000000000, 1_000_000)
     return call(
         rest_kernel, struct(TOK, CH, dtype=BF16), (total, left, last, near, near_other, far, move(far, 0, 0, 1)),
         [pltpu.VMEM((CH, CH), BF16)], TOK * CH * CH * NZ, 7_000_000)

time: 62.6 us -> 59.7 us (0.954)
  starting transfers between devices: 43.4 us -> 40.1 us
  waiting for transfers between devices: 6.27 us -> 7 us
    ppermute x8, waiting for transfers between devices: 0.02 us -> 4.97 us  [turn(): return lax.ppermute(value, 'tp', [(i, (i + k) % NZ) for i in range(NZ)])]
    ppermute x6, starting transfers between devices: 9.44 us -> 5.63 us  [trade(): return lax.ppermute(value, 'ctx', pairs)]
    ppermute x6, waiting for transfers between devices: 2.3 us -> 0.02 us  [trade(): return lax.ppermute(value, 'ctx', pairs)]
    ppermute x8, waiting for transfers between devices: 3.95 us -> 2.01 us  [move(): return lax.ppermute(value, 'ctx', pairs)]
    ppermute x8, starting transfers between devices: 19.7 us -> 20.5 us  [move(): return lax.ppermute(value, 'ctx', pairs)]
where the time goes in v7:
time: 59.7 us; the launch traced here: 58.8 us
  starting transfers between devices  40.1 us (67%)
  Pallas kernels  10.5 us (18%)
  waiting for transfers between devices  7 us (12%)
  other arithmetic  0.97 us (2%)
    ppermute x8, starting transfers between devices, move(): return lax.ppermute(value, 'ctx', pairs)  20.5 us
    ppermute x8, starting transfers between devices, turn(): return lax.ppermute(value, 'tp', [(i, (i + k) % NZ) for i in range(NZ)])  13.9 us
    pallas_call x14, Pallas kernels, call(): pl.pallas_call(kernel, out_shape=outs, in_specs=[VMEM] * len(args), out_s...  10.5 us
    ppermute x6, starting transfers between devices, trade(): return lax.ppermute(value, 'ctx', pairs)  5.63 us
    ppermute x8, waiting for transfers between devices, turn(): return lax.ppermute(value, 'tp', [(i, (i + k) % NZ) for i in range(NZ)])  4.97 us
    ppermute x8, waiting for transfers between devices, move(): return lax.ppermute(value, 'ctx', pairs)  2.01 us
  transfers between devices with their start and end apart: 22, of which 6 were waited for; matrix products, arithmetic and copies ran while one was open for 0% of the time, Pallas kernels for 11%

profile of v7, /device:TPU:1, one launch (start us, length us, event | category | flops | bytes accessed | tf_op | source)
XLA Modules:
  0.0 58.8 jit_solution(6829153340908393347)
XLA Ops:
  0.0 1.0 %sine_multiply_fusion = (f32[16,512]{1,0:T(8,128)S(1)}, f32[16,512]{1,0:T(8,128)S(1)}) fusion(f32[16,512]{1,0:T(8,128)} %param.13, f32[16,512]{1,0:T(8,128)} %decay_ref.1), kind=kLoop, calls=%fused_computation | loop fusion | flops 24576 | bytes 131072 | tf_op jit(solution)/shard_map/mul | solution.py:482
  1.4 2.3 %shard_map.92 = (f32[40,512]{1,0:T(8,128)S(1)}, f32[4,32,8,128]{3,2,1,0:T(8,128)S(1)}, f32[4,256,128]{2,1,0:T(8,128)S(1)}) custom-call(bf16[256,512]{1,0:T(8,128)(2,1)S(1)} %copy-done, bf16[256,512]{1,0:T(8,128)(2,1)S(1)} %copy-done.1, s32[2,128]{1,0:T(2,128)S(1)} %bitcast.2, f32[4,528,128]{2,1,0:T(8,128)S(1)} %get-tuple-element.27.tre, ...), custom_call_target="tpu_custom_call" | custom-call | flops 20000000 | bytes 5000000 | tf_op jit(solution)/shard_map/pallas_call | solution.py:28
  3.6 3.3 %collective-permute-start = (f32[40,512]{1,0:T(8,128)S(1)}, f32[40,512]{1,0:T(8,128)S(1)}, u32[]{:S(2)}, u32[]{:S(2)}) collective-permute-start(f32[40,512]{1,0:T(8,128)S(1)} %get-tuple-element.32.own_ref), channel_id=1, source_target_pairs={{0,8},{8,0},{16,24},{24,16},{32,40},{40,32},{48,56},{56,48},{64,72... | collective-permute-start | bytes 245768 | tf_op jit(solution)/shard_map/ppermute | solution.py:455
  7.0 1.0 %collective-permute-start.12 = (bf16[128,512]{1,0:T(8,128)(2,1)S(1)}, bf16[128,512]{1,0:T(8,128)(2,1)S(1)}, u32[]{:S(2)}, u32[]{:S(2)}) collective-permute-start(bf16[128,512]{1,0:T(8,128)(2,1)S(1)} %copy-done.3), channel_id=1, source_target_pairs={{0,128},{8,136},{16,144},{24,152},{32,160},{40,168},{48,176},{56,1... | collective-permute-start | bytes 393224 | tf_op jit(solution)/shard_map/ppermute | solution.py:461
  8.1 1.4 %collective-permute-start.1 = (bf16[80,512]{1,0:T(8,128)(2,1)S(1)}, bf16[80,512]{1,0:T(8,128)(2,1)S(1)}, u32[]{:S(2)}, u32[]{:S(2)}) collective-permute-start(bf16[80,512]{1,0:T(8,128)(2,1)S(1)} %shard_map.93.after_ref.own_ref), channel_id=1, source_target_pairs={{0,16},{8,24},{16,32},{24,40},{32,48},{40,56},{48,0},{56,8},{64,80... | collective-permute-start | bytes 245768 | tf_op jit(solution)/shard_map/ppermute | solution.py:455
  9.4 2.6 %collective-permute-start.2 = (bf16[80,512]{1,0:T(8,128)(2,1)S(1)}, bf16[80,512]{1,0:T(8,128)(2,1)S(1)}, u32[]{:S(2)}, u32[]{:S(2)}) collective-permute-start(bf16[80,512]{1,0:T(8,128)(2,1)S(1)} %shard_map.93.after_ref.own_ref), channel_id=1, source_target_pairs={{0,32},{8,40},{16,48},{24,56},{32,0},{40,8},{48,16},{56,24},{64,96... | collective-permute-start | bytes 245768 | tf_op jit(solution)/shard_map/ppermute | solution.py:455
  12.1 1.1 %collective-permute-start.3 = (bf16[80,512]{1,0:T(8,128)(2,1)S(1)}, bf16[80,512]{1,0:T(8,128)(2,1)S(1)}, u32[]{:S(2)}, u32[]{:S(2)}) collective-permute-start(bf16[80,512]{1,0:T(8,128)(2,1)S(1)} %shard_map.93.after_ref.own_ref), channel_id=1, source_target_pairs={{0,48},{8,56},{16,0},{24,8},{32,16},{40,24},{48,32},{56,40},{64,11... | collective-permute-start | bytes 245768 | tf_op jit(solution)/shard_map/ppermute | solution.py:455
  13.1 2.1 %shard_map.94 = (f32[4,32,8,128]{3,2,1,0:T(8,128)S(1)}, f32[32,512]{1,0:T(8,128)S(1)}) custom-call(f32[4,256,128]{2,1,0:T(8,128)S(1)} %get-tuple-element.31.sig, f32[4,528,128]{2,1,0:T(8,128)S(1)} %get-tuple-element.27.tre, f32[4,528,128]{2,1,0:T(8,128)S(1)} %get-tuple-element.28.tim, f32[16,512]{1,0:T(8,128)S(1)} %copy-done.2, f32[2,16,512]{2,1,0:T(8,128)S(1)} %copy-done.4, ...), custom_call_target="tpu_custom_call" | custom-call | flops 30000000 | bytes 5000000 | tf_op jit(solution)/shard_map/pallas_call | solution.py:28
  16.6 1.7 %collective-permute-start.5 = (f32[40,512]{1,0:T(8,128)S(1)}, f32[40,512]{1,0:T(8,128)S(1)}, u32[]{:S(2)}, u32[]{:S(2)}) collective-permute-start(f32[40,512]{1,0:T(8,128)S(1)} %get-tuple-element.41.after_ref), channel_id=1, source_target_pairs={{0,128},{8,136},{16,144},{24,152},{32,160},{40,168},{48,176},{56,1... | collective-permute-start | bytes 245768 | tf_op jit(solution)/shard_map/ppermute | solution.py:455
  18.3 2.0 %collective-permute-start.13 = (bf16[256,512]{1,0:T(8,128)(2,1)S(1)}, bf16[256,512]{1,0:T(8,128)(2,1)S(1)}, u32[]{:S(2)}, u32[]{:S(2)}) collective-permute-start(bf16[256,512]{1,0:T(8,128)(2,1)S(1)} %shard_map.98.both_ref), channel_id=1, source_target_pairs={{0,32},{8,40},{16,48},{24,56},{32,0},{40,8},{48,16},{56,24},{64,96... | collective-permute-start | bytes 786440 | tf_op jit(solution)/shard_map/ppermute | solution.py:461
  21.7 1.7 %shard_map.97.after_ref.here = bf16[32,4096]{1,0:T(8,128)(2,1)S(1)} custom-call(bf16[256,512]{1,0:T(8,128)(2,1)S(1)} %copy-done.7, f32[4,32,8,128]{3,2,1,0:T(8,128)S(1)} %get-tuple-element.34.y_ref, f32[4,32,8,128]{3,2,1,0:T(8,128)S(1)} %get-tuple-element.37.pz_ref, f32[4,32,8,128]{3,2,1,0:T(8,128)S(1)} %get-tuple-element.38.gz_ref, ...), custom_call_target="tpu_custom_call" | custom-call | flops 2000000000 | bytes 5000000 | tf_op jit(solution)/shard_map/pallas_call | solution.py:28
  23.4 1.7 %collective-permute-start.6 = (bf16[32,4096]{1,0:T(8,128)(2,1)S(1)}, bf16[32,4096]{1,0:T(8,128)(2,1)S(1)}, u32[]{:S(2)}, u32[]{:S(2)}) collective-permute-start(bf16[32,4096]{1,0:T(8,128)(2,1)S(1)} %shard_map.97.after_ref.here), channel_id=1, source_target_pairs={{0,1},{1,2},{2,3},{3,4},{4,5},{5,6},{6,7},{7,0},{8,9},{9,10},{10,1... | collective-permute-start | bytes 786440 | tf_op jit(solution)/shard_map/ppermute | solution.py:465
  25.1 4.0 %collective-permute-start.7 = (bf16[32,4096]{1,0:T(8,128)(2,1)S(1)}, bf16[32,4096]{1,0:T(8,128)(2,1)S(1)}, u32[]{:S(2)}, u32[]{:S(2)}) collective-permute-start(bf16[32,4096]{1,0:T(8,128)(2,1)S(1)} %shard_map.97.after_ref.here), channel_id=1, source_target_pairs={{0,7},{1,0},{2,1},{3,2},{4,3},{5,4},{6,5},{7,6},{8,15},{9,8},{10,9... | collective-permute-start | bytes 786440 | tf_op jit(solution)/shard_map/ppermute | solution.py:465
  29.2 0.9 %collective-permute-start.14 = (bf16[256,512]{1,0:T(8,128)(2,1)S(1)}, bf16[256,512]{1,0:T(8,128)(2,1)S(1)}, u32[]{:S(2)}, u32[]{:S(2)}) collective-permute-start(bf16[256,512]{1,0:T(8,128)(2,1)S(1)} %get-tuple-element.42.even_ref), channel_id=1, source_target_pairs={{0,64},{8,72},{16,80},{24,88},{32,96},{40,104},{48,112},{56,120},{... | collective-permute-start | bytes 786440 | tf_op jit(solution)/shard_map/ppermute | solution.py:461
  30.4 2.7 %collective-permute-done.6.after_up.up1 = bf16[32,4096]{1,0:T(8,128)(2,1)S(1)} collective-permute-done((bf16[32,4096]{1,0:T(8,128)(2,1)S(1)}, bf16[32,4096]{1,0:T(8,128)(2,1)S(1)}, u32[]{:S(2)}, u32[]{:S(2)}) %collective-permute-start.6) | collective-permute-done | bytes 262176 | tf_op jit(solution)/shard_map/ppermute | solution.py:465
  33.1 2.7 %collective-permute-start.9 = (bf16[32,4096]{1,0:T(8,128)(2,1)S(1)}, bf16[32,4096]{1,0:T(8,128)(2,1)S(1)}, u32[]{:S(2)}, u32[]{:S(2)}) collective-permute-start(bf16[32,4096]{1,0:T(8,128)(2,1)S(1)} %collective-permute-done.7.after_down.down1), channel_id=1, source_target_pairs={{0,7},{1,0},{2,1},{3,2},{4,3},{5,4},{6,5},{7,6},{8,15},{9,8},{10,9... | collective-permute-start | bytes 786440 | tf_op jit(solution)/shard_map/ppermute | solution.py:465
  36.3 1.0 %collective-permute-start.17 = (bf16[512,512]{1,0:T(8,128)(2,1)S(1)}, bf16[512,512]{1,0:T(8,128)(2,1)S(1)}, u32[]{:S(2)}, u32[]{:S(2)}) collective-permute-start(bf16[512,512]{1,0:T(8,128)(2,1)S(1)} %get-tuple-element.46), channel_id=1, source_target_pairs={{0,64},{8,72},{16,80},{24,88},{32,96},{40,104},{48,112},{56,120},{... | collective-permute-start | bytes 1572872 | tf_op jit(solution)/shard_map/ppermute | solution.py:461
  37.3 2.2 %collective-permute-done.8.up2 = bf16[32,4096]{1,0:T(8,128)(2,1)S(1)} collective-permute-done((bf16[32,4096]{1,0:T(8,128)(2,1)S(1)}, bf16[32,4096]{1,0:T(8,128)(2,1)S(1)}, u32[]{:S(2)}, u32[]{:S(2)}) %collective-permute-start.8) | collective-permute-done | bytes 262176 | tf_op jit(solution)/shard_map/ppermute | solution.py:465
  39.6 2.7 %collective-permute-start.11 = (bf16[32,4096]{1,0:T(8,128)(2,1)S(1)}, bf16[32,4096]{1,0:T(8,128)(2,1)S(1)}, u32[]{:S(2)}, u32[]{:S(2)}) collective-permute-start(bf16[32,4096]{1,0:T(8,128)(2,1)S(1)} %collective-permute-done.9.down2), channel_id=1, source_target_pairs={{0,7},{1,0},{2,1},{3,2},{4,3},{5,4},{6,5},{7,6},{8,15},{9,8},{10,9... | collective-permute-start | bytes 786440 | tf_op jit(solution)/shard_map/ppermute | solution.py:465
  42.2 5.1 %collective-permute-start.18 = (bf16[1024,512]{1,0:T(8,128)(2,1)S(1)}, bf16[1024,512]{1,0:T(8,128)(2,1)S(1)}, u32[]{:S(2)}, u32[]{:S(2)}) collective-permute-start(bf16[1024,512]{1,0:T(8,128)(2,1)S(1)} %get-tuple-element.44.near_own), channel_id=1, source_target_pairs={{0,8},{8,0},{16,24},{24,16},{32,40},{40,32},{48,56},{56,48},{64,72... | collective-permute-start | bytes 3145736 | tf_op jit(solution)/shard_map/ppermute | solution.py:455
  47.5 2.7 %collective-permute-start.20 = (bf16[16,4096]{1,0:T(8,128)(2,1)S(1)}, bf16[16,4096]{1,0:T(8,128)(2,1)S(1)}, u32[]{:S(2)}, u32[]{:S(2)}) collective-permute-start(bf16[16,4096]{1,0:T(8,128)(2,1)S(1)} %slice.9), channel_id=1, source_target_pairs={{0,7},{1,0},{2,1},{3,2},{4,3},{5,4},{6,5},{7,6},{8,15},{9,8},{10,9... | collective-permute-start | bytes 393224 | tf_op jit(solution)/shard_map/ppermute | solution.py:465
  50.3 4.9 %collective-permute-start.21 = (bf16[1024,512]{1,0:T(8,128)(2,1)S(1)}, bf16[1024,512]{1,0:T(8,128)(2,1)S(1)}, u32[]{:S(2)}, u32[]{:S(2)}) collective-permute-start(bf16[1024,512]{1,0:T(8,128)(2,1)S(1)} %shard_map.101.far_own.own_ref), channel_id=1, source_target_pairs={{0,8},{8,0},{16,24},{24,16},{32,40},{40,32},{48,56},{56,48},{64,72... | collective-permute-start | bytes 3145736 | tf_op jit(solution)/shard_map/ppermute | solution.py:455
  55.2 1.6 %shard_map.102 = (f32[256,512]{1,0:T(8,128)S(1)}, bf16[256,1024]{1,0:T(8,128)(2,1)S(1)}) custom-call(bf16[32,4096]{1,0:T(8,128)(2,1)S(1)} %shard_map.97.after_ref.here, bf16[32,4096]{1,0:T(8,128)(2,1)S(1)} %collective-permute-done.6.after_up.up1, bf16[32,4096]{1,0:T(8,128)(2,1)S(1)} %collective-permute-done.7.after_down.down1, ...), custom_call_target="tpu_custom_call" | custom-call | flops 8000000000 | bytes 7000000 | tf_op jit(solution)/shard_map/pallas_call | solution.py:28
  57.5 1.3 %shard_map.104 = bf16[256,512]{1,0:T(8,128)(2,1)} custom-call(f32[256,512]{1,0:T(8,128)S(1)} %get-tuple-element.47.after_ref.total_ref, bf16[256,1024]{1,0:T(8,128)(2,1)S(1)} %get-tuple-element.48.left, bf16[256,512]{1,0:T(8,128)(2,1)S(1)} %shard_map.103.last, bf16[1024,512]{1,0:T(8,128)(2,1)S(1)} %get-tuple-element.44.near_own, ...), custom_call_target="tpu_custom_call" | custom-call | flops 536870912 | bytes 7000000 | tf_op jit(solution)/shard_map/pallas_call | solution.py:28
  (53 shorter events, 4.7 us)
Async XLA Ops:
  1.4 11.8 %copy-start.2 = (f32[16,512]{1,0:T(8,128)S(1)}, f32[16,512]{1,0:T(8,128)}, u32[]{:S(2)}) copy-start(f32[16,512]{1,0:T(8,128)} %decay_ref.1) | copy-start | bytes 98308
  1.4 11.8 %copy-start.4 = (f32[2,16,512]{2,1,0:T(8,128)S(1)}, f32[2,16,512]{2,1,0:T(8,128)}, u32[]{:S(2)}) copy-start(f32[2,16,512]{2,1,0:T(8,128)} %res_ref.1) | copy-start | bytes 196612
  3.6 4.4 %collective-permute-start = (f32[40,512]{1,0:T(8,128)S(1)}, f32[40,512]{1,0:T(8,128)S(1)}, u32[]{:S(2)}, u32[]{:S(2)}) collective-permute-start(f32[40,512]{1,0:T(8,128)S(1)} %get-tuple-element.32.own_ref), channel_id=1, source_target_pairs={{0,8},{8,0},{16,24},{24,16},{32,40},{40,32},{48,56},{56,48},{64,72... | collective-permute-start | bytes 245768 | tf_op jit(solution)/shard_map/ppermute | solution.py:455
  7.0 11.3 %collective-permute-start.12 = (bf16[128,512]{1,0:T(8,128)(2,1)S(1)}, bf16[128,512]{1,0:T(8,128)(2,1)S(1)}, u32[]{:S(2)}, u32[]{:S(2)}) collective-permute-start(bf16[128,512]{1,0:T(8,128)(2,1)S(1)} %copy-done.3), channel_id=1, source_target_pairs={{0,128},{8,136},{16,144},{24,152},{32,160},{40,168},{48,176},{56,1... | collective-permute-start | bytes 393224 | tf_op jit(solution)/shard_map/ppermute | solution.py:461
  8.1 7.2 %collective-permute-start.1 = (bf16[80,512]{1,0:T(8,128)(2,1)S(1)}, bf16[80,512]{1,0:T(8,128)(2,1)S(1)}, u32[]{:S(2)}, u32[]{:S(2)}) collective-permute-start(bf16[80,512]{1,0:T(8,128)(2,1)S(1)} %shard_map.93.after_ref.own_ref), channel_id=1, source_target_pairs={{0,16},{8,24},{16,32},{24,40},{32,48},{40,56},{48,0},{56,8},{64,80... | collective-permute-start | bytes 245768 | tf_op jit(solution)/shard_map/ppermute | solution.py:455
  9.4 6.6 %collective-permute-start.2 = (bf16[80,512]{1,0:T(8,128)(2,1)S(1)}, bf16[80,512]{1,0:T(8,128)(2,1)S(1)}, u32[]{:S(2)}, u32[]{:S(2)}) collective-permute-start(bf16[80,512]{1,0:T(8,128)(2,1)S(1)} %shard_map.93.after_ref.own_ref), channel_id=1, source_target_pairs={{0,32},{8,40},{16,48},{24,56},{32,0},{40,8},{48,16},{56,24},{64,96... | collective-permute-start | bytes 245768 | tf_op jit(solution)/shard_map/ppermute | solution.py:455
  12.1 4.0 %collective-permute-start.3 = (bf16[80,512]{1,0:T(8,128)(2,1)S(1)}, bf16[80,512]{1,0:T(8,128)(2,1)S(1)}, u32[]{:S(2)}, u32[]{:S(2)}) collective-permute-start(bf16[80,512]{1,0:T(8,128)(2,1)S(1)} %shard_map.93.after_ref.own_ref), channel_id=1, source_target_pairs={{0,48},{8,56},{16,0},{24,8},{32,16},{40,24},{48,32},{56,40},{64,11... | collective-permute-start | bytes 245768 | tf_op jit(solution)/shard_map/ppermute | solution.py:455
  16.2 5.4 %collective-permute-start.4 = (f32[40,512]{1,0:T(8,128)S(1)}, f32[40,512]{1,0:T(8,128)S(1)}, u32[]{:S(2)}, u32[]{:S(2)}) collective-permute-start(f32[40,512]{1,0:T(8,128)S(1)} %get-tuple-element.41.after_ref), channel_id=1, source_target_pairs={{0,64},{8,72},{16,80},{24,88},{32,96},{40,104},{48,112},{56,120},{... | collective-permute-start | bytes 245768 | tf_op jit(solution)/shard_map/ppermute | solution.py:455
  16.6 5.1 %collective-permute-start.5 = (f32[40,512]{1,0:T(8,128)S(1)}, f32[40,512]{1,0:T(8,128)S(1)}, u32[]{:S(2)}, u32[]{:S(2)}) collective-permute-start(f32[40,512]{1,0:T(8,128)S(1)} %get-tuple-element.41.after_ref), channel_id=1, source_target_pairs={{0,128},{8,136},{16,144},{24,152},{32,160},{40,168},{48,176},{56,1... | collective-permute-start | bytes 245768 | tf_op jit(solution)/shard_map/ppermute | solution.py:455
  18.3 10.8 %collective-permute-start.13 = (bf16[256,512]{1,0:T(8,128)(2,1)S(1)}, bf16[256,512]{1,0:T(8,128)(2,1)S(1)}, u32[]{:S(2)}, u32[]{:S(2)}) collective-permute-start(bf16[256,512]{1,0:T(8,128)(2,1)S(1)} %shard_map.98.both_ref), channel_id=1, source_target_pairs={{0,32},{8,40},{16,48},{24,56},{32,0},{40,8},{48,16},{56,24},{64,96... | collective-permute-start | bytes 786440 | tf_op jit(solution)/shard_map/ppermute | solution.py:461
  23.4 9.7 %collective-permute-start.6 = (bf16[32,4096]{1,0:T(8,128)(2,1)S(1)}, bf16[32,4096]{1,0:T(8,128)(2,1)S(1)}, u32[]{:S(2)}, u32[]{:S(2)}) collective-permute-start(bf16[32,4096]{1,0:T(8,128)(2,1)S(1)} %shard_map.97.after_ref.here), channel_id=1, source_target_pairs={{0,1},{1,2},{2,3},{3,4},{4,5},{5,6},{6,7},{7,0},{8,9},{9,10},{10,1... | collective-permute-start | bytes 786440 | tf_op jit(solution)/shard_map/ppermute | solution.py:465
  25.1 8.0 %collective-permute-start.7 = (bf16[32,4096]{1,0:T(8,128)(2,1)S(1)}, bf16[32,4096]{1,0:T(8,128)(2,1)S(1)}, u32[]{:S(2)}, u32[]{:S(2)}) collective-permute-start(bf16[32,4096]{1,0:T(8,128)(2,1)S(1)} %shard_map.97.after_ref.here), channel_id=1, source_target_pairs={{0,7},{1,0},{2,1},{3,2},{4,3},{5,4},{6,5},{7,6},{8,15},{9,8},{10,9... | collective-permute-start | bytes 786440 | tf_op jit(solution)/shard_map/ppermute | solution.py:465
  29.2 6.6 %collective-permute-start.14 = (bf16[256,512]{1,0:T(8,128)(2,1)S(1)}, bf16[256,512]{1,0:T(8,128)(2,1)S(1)}, u32[]{:S(2)}, u32[]{:S(2)}) collective-permute-start(bf16[256,512]{1,0:T(8,128)(2,1)S(1)} %get-tuple-element.42.even_ref), channel_id=1, source_target_pairs={{0,64},{8,72},{16,80},{24,88},{32,96},{40,104},{48,112},{56,120},{... | collective-permute-start | bytes 786440 | tf_op jit(solution)/shard_map/ppermute | solution.py:461
  30.1 5.7 %collective-permute-start.15 = (bf16[256,512]{1,0:T(8,128)(2,1)S(1)}, bf16[256,512]{1,0:T(8,128)(2,1)S(1)}, u32[]{:S(2)}, u32[]{:S(2)}) collective-permute-start(bf16[256,512]{1,0:T(8,128)(2,1)S(1)} %get-tuple-element.43.odd_ref), channel_id=1, source_target_pairs={{0,16},{8,24},{16,0},{24,8},{32,48},{40,56},{48,32},{56,40},{64,80... | collective-permute-start | bytes 786440 | tf_op jit(solution)/shard_map/ppermute | solution.py:461
  33.1 6.4 %collective-permute-start.8 = (bf16[32,4096]{1,0:T(8,128)(2,1)S(1)}, bf16[32,4096]{1,0:T(8,128)(2,1)S(1)}, u32[]{:S(2)}, u32[]{:S(2)}) collective-permute-start(bf16[32,4096]{1,0:T(8,128)(2,1)S(1)} %collective-permute-done.6.after_up.up1), channel_id=1, source_target_pairs={{0,1},{1,2},{2,3},{3,4},{4,5},{5,6},{6,7},{7,0},{8,9},{9,10},{10,1... | collective-permute-start | bytes 786440 | tf_op jit(solution)/shard_map/ppermute | solution.py:465
  33.1 6.4 %collective-permute-start.9 = (bf16[32,4096]{1,0:T(8,128)(2,1)S(1)}, bf16[32,4096]{1,0:T(8,128)(2,1)S(1)}, u32[]{:S(2)}, u32[]{:S(2)}) collective-permute-start(bf16[32,4096]{1,0:T(8,128)(2,1)S(1)} %collective-permute-done.7.after_down.down1), channel_id=1, source_target_pairs={{0,7},{1,0},{2,1},{3,2},{4,3},{5,4},{6,5},{7,6},{8,15},{9,8},{10,9... | collective-permute-start | bytes 786440 | tf_op jit(solution)/shard_map/ppermute | solution.py:465
  35.9 14.2 %collective-permute-start.16 = (bf16[512,512]{1,0:T(8,128)(2,1)S(1)}, bf16[512,512]{1,0:T(8,128)(2,1)S(1)}, u32[]{:S(2)}, u32[]{:S(2)}) collective-permute-start(bf16[512,512]{1,0:T(8,128)(2,1)S(1)} %get-tuple-element.45), channel_id=1, source_target_pairs={{0,16},{8,24},{16,0},{24,8},{32,48},{40,56},{48,32},{56,40},{64,80... | collective-permute-start | bytes 1572872 | tf_op jit(solution)/shard_map/ppermute | solution.py:461
  36.3 13.9 %collective-permute-start.17 = (bf16[512,512]{1,0:T(8,128)(2,1)S(1)}, bf16[512,512]{1,0:T(8,128)(2,1)S(1)}, u32[]{:S(2)}, u32[]{:S(2)}) collective-permute-start(bf16[512,512]{1,0:T(8,128)(2,1)S(1)} %get-tuple-element.46), channel_id=1, source_target_pairs={{0,64},{8,72},{16,80},{24,88},{32,96},{40,104},{48,112},{56,120},{... | collective-permute-start | bytes 1572872 | tf_op jit(solution)/shard_map/ppermute | solution.py:461
  39.6 7.8 %collective-permute-start.10 = (bf16[32,4096]{1,0:T(8,128)(2,1)S(1)}, bf16[32,4096]{1,0:T(8,128)(2,1)S(1)}, u32[]{:S(2)}, u32[]{:S(2)}) collective-permute-start(bf16[32,4096]{1,0:T(8,128)(2,1)S(1)} %collective-permute-done.8.up2), channel_id=1, source_target_pairs={{0,1},{1,2},{2,3},{3,4},{4,5},{5,6},{6,7},{7,0},{8,9},{9,10},{10,1... | collective-permute-start | bytes 786440 | tf_op jit(solution)/shard_map/ppermute | solution.py:465
  39.6 7.9 %collective-permute-start.11 = (bf16[32,4096]{1,0:T(8,128)(2,1)S(1)}, bf16[32,4096]{1,0:T(8,128)(2,1)S(1)}, u32[]{:S(2)}, u32[]{:S(2)}) collective-permute-start(bf16[32,4096]{1,0:T(8,128)(2,1)S(1)} %collective-permute-done.9.down2), channel_id=1, source_target_pairs={{0,7},{1,0},{2,1},{3,2},{4,3},{5,4},{6,5},{7,6},{8,15},{9,8},{10,9... | collective-permute-start | bytes 786440 | tf_op jit(solution)/shard_map/ppermute | solution.py:465
  42.2 13.0 %collective-permute-start.18 = (bf16[1024,512]{1,0:T(8,128)(2,1)S(1)}, bf16[1024,512]{1,0:T(8,128)(2,1)S(1)}, u32[]{:S(2)}, u32[]{:S(2)}) collective-permute-start(bf16[1024,512]{1,0:T(8,128)(2,1)S(1)} %get-tuple-element.44.near_own), channel_id=1, source_target_pairs={{0,8},{8,0},{16,24},{24,16},{32,40},{40,32},{48,56},{56,48},{64,72... | collective-permute-start | bytes 3145736 | tf_op jit(solution)/shard_map/ppermute | solution.py:455
  47.3 9.5 %collective-permute-start.19 = (bf16[16,4096]{1,0:T(8,128)(2,1)S(1)}, bf16[16,4096]{1,0:T(8,128)(2,1)S(1)}, u32[]{:S(2)}, u32[]{:S(2)}) collective-permute-start(bf16[16,4096]{1,0:T(8,128)(2,1)S(1)} %slice.8), channel_id=1, source_target_pairs={{0,1},{1,2},{2,3},{3,4},{4,5},{5,6},{6,7},{7,0},{8,9},{9,10},{10,1... | collective-permute-start | bytes 393224 | tf_op jit(solution)/shard_map/ppermute | solution.py:465
  47.5 9.4 %collective-permute-start.20 = (bf16[16,4096]{1,0:T(8,128)(2,1)S(1)}, bf16[16,4096]{1,0:T(8,128)(2,1)S(1)}, u32[]{:S(2)}, u32[]{:S(2)}) collective-permute-start(bf16[16,4096]{1,0:T(8,128)(2,1)S(1)} %slice.9), channel_id=1, source_target_pairs={{0,7},{1,0},{2,1},{3,2},{4,3},{5,4},{6,5},{7,6},{8,15},{9,8},{10,9... | collective-permute-start | bytes 393224 | tf_op jit(solution)/shard_map/ppermute | solution.py:465
  50.3 7.2 %collective-permute-start.21 = (bf16[1024,512]{1,0:T(8,128)(2,1)S(1)}, bf16[1024,512]{1,0:T(8,128)(2,1)S(1)}, u32[]{:S(2)}, u32[]{:S(2)}) collective-permute-start(bf16[1024,512]{1,0:T(8,128)(2,1)S(1)} %shard_map.101.far_own.own_ref), channel_id=1, source_target_pairs={{0,8},{8,0},{16,24},{24,16},{32,40},{40,32},{48,56},{56,48},{64,72... | collective-permute-start | bytes 3145736 | tf_op jit(solution)/shard_map/ppermute | solution.py:455
  (6 other events, 22.7 us)

commit v8 on v7

--- a/solution.py
+++ b/solution.py
@@ -91,27 +91,18 @@
     return lax.broadcasted_iota(jnp.int32, (BLOCKS, LANES), 0)
 
 
-def powers_kernel(pole_re, pole_im, tre, tim, qre, qim, p256_ref):
+def powers_kernel(pole_re, pole_im, tre, tim, p256_ref):
     fill_powers((pole_re[...], pole_im[...]), tre, tim, STEPS + 1)
-    q = last_power(tre, tim)
-    value = (jnp.ones((MODES, CH), F32), jnp.zeros((MODES, CH), F32))
-    for n in range(BLOCKS):
-        row = (BLOCKS - 1 - n) * MODES
-        for g in range(GROUPS):
-            lanes = slice(g * LANES, (g + 1) * LANES)
-            qre[g, row:row + MODES, :] = value[0][:, lanes]
-            qim[g, row:row + MODES, :] = value[1][:, lanes]
-        value = cmul(value, q)
+    value = square(square(square(last_power(tre, tim))))
     p256_ref[:MODES, :] = value[0]
     p256_ref[MODES:, :] = value[1]
 
 
-def ends_kernel(key_ref, value_ref, starts_ref, tre, tim, qre, qim, pay_ref, eb_ref, sig):
+def ends_kernel(key_ref, value_ref, starts_ref, tre, tim, pay_ref, eb_ref, sig):
     s0 = first_start(starts_ref)
     b0 = s0 // STEPS
     fill_signal(key_ref, value_ref, sig)
     blocks = block_iota()
-    reach = (s0 >= TOK) | (blocks >= b0)
 
     def group(g, unused):
         def step(j, acc):
@@ -127,14 +118,17 @@
         zero = jnp.zeros((BLOCKS, LANES), F32)
         acc = lax.fori_loop(0, STEPS, step, (zero,) * ROWS, unroll=8)
         for m in range(MODES):
-            re, im = acc[2 * m], acc[2 * m + 1]
-            eb_ref[g, m] = re
-            eb_ref[g, MODES + m] = im
-            w = (qre[g, pl.ds(m, BLOCKS, stride=MODES), :], qim[g, pl.ds(m, BLOCKS, stride=MODES), :])
-            end = cmul(w, (re, im))
-            lanes = pl.ds(pl.multiple_of(g * LANES, LANES), LANES)
-            pay_ref[pl.ds(m, 1), lanes] = jnp.sum(jnp.where(reach, end[0], 0.0), axis=0, keepdims=True)
-            pay_ref[pl.ds(MODES + m, 1), lanes] = jnp.sum(jnp.where(reach, end[1], 0.0), axis=0, keepdims=True)
+            eb_ref[g, m * BLOCKS:(m + 1) * BLOCKS, :] = acc[2 * m]
+            eb_ref[g, (MODES + m) * BLOCKS:(MODES + m + 1) * BLOCKS, :] = acc[2 * m + 1]
+        q = (tre[g, STEPS * MODES:, :], tim[g, STEPS * MODES:, :])
+        state = (jnp.zeros((MODES, LANES), F32),) * 2
+        for n in range(BLOCKS):
+            state = [jnp.where(b0 == n, 0.0, part) for part in state]
+            add = [eb_ref[g, pl.ds(at * BLOCKS + n, MODES, stride=BLOCKS), :] for at in (0, MODES)]
+            state = cadd(cmul(q, state), add)
+        lanes = pl.ds(pl.multiple_of(g * LANES, LANES), LANES)
+        pay_ref[:MODES, lanes] = state[0]
+        pay_ref[MODES:ROWS, lanes] = state[1]
         return unused
 
     lax.fori_loop(0, GROUPS, group, 0)
@@ -231,7 +225,8 @@
 
     def group(g, unused):
         for m in range(MODES):
-            state = (eb_ref[g, m], eb_ref[g, MODES + m])
+            state = (eb_ref[g, m * BLOCKS:(m + 1) * BLOCKS, :],
+                     eb_ref[g, (MODES + m) * BLOCKS:(MODES + m + 1) * BLOCKS, :])
             for n in range(3):
                 moved = [jnp.where(keeps[n], pltpu.roll(part, 1 << n, 0), 0.0) for part in state]
                 step = (rows_[g, n * ROWS + m:n * ROWS + m + 1, :],
@@ -284,7 +279,7 @@
 
 
 def pair_kernel(own_ref, pair_ref, after_ref, out_ref):
-    put_pair(out_ref, lax.axis_index("ctx") // (NC * NY * 2), own_ref, pair_ref)
+    put_pair(out_ref, lax.axis_index("ctx") // (NC * NY) % 2, own_ref, pair_ref)
 
 
 def row_kernel(own_ref, one_ref, two_ref, three_ref, p256_ref, after_ref, pay_ref, before_ref, factor_ref, held):
@@ -393,8 +388,8 @@
     index = lax.axis_index("ctx")
     x, y = index // (NC * NY), (index // NC) % NY
     block = lax.rem(lax.axis_index("tp") - k + NZ, NZ)
-    odd, i = lax.rem(block, 2), block // 4
-    dx = (lax.rem(block // 2, 2) != lax.rem(x, 2)).astype(jnp.int32)
+    odd, i = lax.rem(block, 2), lax.rem(block // 2, 2)
+    dx = (block // 4 != x // 2).astype(jnp.int32)
     found = []
     for h in range(2):
         dy = (lax.rem(y, 2) != h).astype(jnp.int32)
@@ -476,13 +471,12 @@
     table = (GROUPS, (STEPS + 1) * MODES, LANES)
 
     magnitude = jnp.exp(-decay)
-    q_shape = struct(GROUPS, BLOCKS * MODES, LANES)
-    tre, tim, qre, qim, p256 = call(
-        powers_kernel, (struct(*table), struct(*table), q_shape, q_shape, state_shape),
+    tre, tim, p256 = call(
+        powers_kernel, (struct(*table), struct(*table), state_shape),
         (magnitude * jnp.cos(freq), magnitude * jnp.sin(freq)), (), 300_000_000, 5_000_000)
     pay, eb, signal = call(
-        ends_kernel, (pay_shape, block_shape, struct(GROUPS, TOK, LANES)),
-        (key, value, starts, tre, tim, qre, qim), (), 20_000_000, 5_000_000)
+        ends_kernel, (pay_shape, struct(GROUPS, ROWS * BLOCKS, LANES), struct(GROUPS, TOK, LANES)),
+        (key, value, starts, tre, tim), (), 20_000_000, 5_000_000)
     other = move(pay, 0, 0, 1)
     chip = call(chip_kernel, struct(SENT, CH, dtype=BF16), (pay, other, p256))
     near = [move(chip, 0, k, 0) for k in (1, 2, 3)]
@@ -502,17 +496,17 @@
         (query, y, pz, gz, tre, tim, starts, pay, other, p256, before, factor, *back),
         [sig, pltpu.VMEM((GROUPS, ROWS, LANES), F32)], 2_000_000_000, 5_000_000)
 
-    both = call(pair_kernel, struct(2 * WROWS, CH, dtype=BF16), (out_weight, trade(out_weight, 2, 0), row))
+    both = call(pair_kernel, struct(2 * WROWS, CH, dtype=BF16), (out_weight, trade(out_weight, 1, 0), row))
     w2, w4, w8 = [struct(n * WROWS, CH, dtype=BF16) for n in (2, 4, 8)]
     even, odd = call(four_kernel, (w2, w2), (both, trade(both, 0, 2), hidden), (), 0, 2_000_000)
     half = THIN // 2
     up1, down1 = turn(hidden, 1), turn(hidden, -1)
     near, even, odd = call(
-        eight_kernel, (w8, w4, w4), (even, trade(even, 1, 0), odd, trade(odd, 0, 1), up1, down1), (), 0, 4_000_000)
+        eight_kernel, (w8, w4, w4), (even, trade(even, 2, 0), odd, trade(odd, 0, 1), up1, down1), (), 0, 4_000_000)
     up2, down2 = turn(up1, 1), turn(down1, -1)
     up3, down3 = turn(up2, 1), turn(down2, -1)
     up4, down4 = turn(up3[:half], 1), turn(down3[half:], -1)
-    far = call(join_kernel, w8, (trade(even, 0, 1), trade(odd, 1, 0), up3, down3), (), 10000000000, 2_000_000)
+    far = call(join_kernel, w8, (trade(even, 0, 1), trade(odd, 2, 0), up3, down3), (), 10000000000, 2_000_000)
     near_other = move(near, 0, 0, 1)
     total, left = call(
         most_kernel, (struct(TOK, CH), struct(TOK, 8 * WROWS, dtype=BF16)),

time: 59.7 us -> 58.8 us (0.985)
  waiting for transfers between devices: 7 us -> 5.85 us
    ppermute x8, waiting for transfers between devices: 4.97 us -> 2.16 us  [turn(): return lax.ppermute(value, 'tp', [(i, (i + k) % NZ) for i in range(NZ)])]
    ppermute x6, starting transfers between devices: 5.63 us -> 6.64 us  [trade(): return lax.ppermute(value, 'ctx', pairs)]
    ppermute x6, waiting for transfers between devices: 0.02 us -> 0.95 us  [trade(): return lax.ppermute(value, 'ctx', pairs)]
    ppermute x8, starting transfers between devices: 20.5 us -> 19.6 us  [move(): return lax.ppermute(value, 'ctx', pairs)]
    ppermute x8, waiting for transfers between devices: 2.01 us -> 2.74 us  [move(): return lax.ppermute(value, 'ctx', pairs)]
  transfers between devices with their start and end apart: 22 -> 22, of which waited for: 6 -> 7; matrix products, arithmetic and copies ran while one was open for 0% -> 0% of each run, Pallas kernels for 11% -> 11%
where the time goes in v8:
time: 58.8 us; the launch traced here: 57.9 us
  starting transfers between devices  40.2 us (68%)
  Pallas kernels  10.3 us (18%)
  waiting for transfers between devices  5.85 us (10%)
  other arithmetic  0.97 us (2%)
    ppermute x8, starting transfers between devices, move(): return lax.ppermute(value, 'ctx', pairs)  19.6 us
    ppermute x8, starting transfers between devices, turn(): return lax.ppermute(value, 'tp', [(i, (i + k) % NZ) for i in range(NZ)])  13.9 us
    pallas_call x14, Pallas kernels, call(): pl.pallas_call(kernel, out_shape=outs, in_specs=[VMEM] * len(args), out_s...  10.3 us
    ppermute x6, starting transfers between devices, trade(): return lax.ppermute(value, 'ctx', pairs)  6.64 us
    ppermute x8, waiting for transfers between devices, move(): return lax.ppermute(value, 'ctx', pairs)  2.74 us
    ppermute x8, waiting for transfers between devices, turn(): return lax.ppermute(value, 'tp', [(i, (i + k) % NZ) for i in range(NZ)])  2.16 us
  transfers between devices with their start and end apart: 22, of which 7 were waited for; matrix products, arithmetic and copies ran while one was open for 0% of the time, Pallas kernels for 11%

profile of v8, /device:TPU:1, one launch (start us, length us, event | category | flops | bytes accessed | tf_op | source)
XLA Modules:
  0.0 57.9 jit_solution(18199548417233580629)
XLA Ops:
  0.0 1.0 %sine_multiply_fusion = (f32[16,512]{1,0:T(8,128)S(1)}, f32[16,512]{1,0:T(8,128)S(1)}) fusion(f32[16,512]{1,0:T(8,128)} %param.13, f32[16,512]{1,0:T(8,128)} %decay_ref.1), kind=kLoop, calls=%fused_computation | loop fusion | flops 24576 | bytes 131072 | tf_op jit(solution)/shard_map/mul | solution.py:476
  1.4 2.2 %shard_map.92 = (f32[40,512]{1,0:T(8,128)S(1)}, f32[4,256,128]{2,1,0:T(8,128)S(1)}, f32[4,256,128]{2,1,0:T(8,128)S(1)}) custom-call(bf16[256,512]{1,0:T(8,128)(2,1)S(1)} %copy-done, bf16[256,512]{1,0:T(8,128)(2,1)S(1)} %copy-done.1, s32[2,128]{1,0:T(2,128)S(1)} %bitcast.2, f32[4,528,128]{2,1,0:T(8,128)S(1)} %get-tuple-element.25.tre, ...), custom_call_target="tpu_custom_call" | custom-call | flops 20000000 | bytes 5000000 | tf_op jit(solution)/shard_map/pallas_call | solution.py:28
  3.5 3.3 %collective-permute-start = (f32[40,512]{1,0:T(8,128)S(1)}, f32[40,512]{1,0:T(8,128)S(1)}, u32[]{:S(2)}, u32[]{:S(2)}) collective-permute-start(f32[40,512]{1,0:T(8,128)S(1)} %get-tuple-element.28.own_ref), channel_id=1, source_target_pairs={{0,8},{8,0},{16,24},{24,16},{32,40},{40,32},{48,56},{56,48},{64,72... | collective-permute-start | bytes 245768 | tf_op jit(solution)/shard_map/ppermute | solution.py:450
  6.8 0.9 %collective-permute-done.other_ref = f32[40,512]{1,0:T(8,128)S(1)} collective-permute-done((f32[40,512]{1,0:T(8,128)S(1)}, f32[40,512]{1,0:T(8,128)S(1)}, u32[]{:S(2)}, u32[]{:S(2)}) %collective-permute-start) | collective-permute-done | bytes 81952 | tf_op jit(solution)/shard_map/ppermute | solution.py:450
  7.9 2.5 %collective-permute-start.2 = (bf16[80,512]{1,0:T(8,128)(2,1)S(1)}, bf16[80,512]{1,0:T(8,128)(2,1)S(1)}, u32[]{:S(2)}, u32[]{:S(2)}) collective-permute-start(bf16[80,512]{1,0:T(8,128)(2,1)S(1)} %shard_map.93.after_ref.own_ref), channel_id=1, source_target_pairs={{0,32},{8,40},{16,48},{24,56},{32,0},{40,8},{48,16},{56,24},{64,96... | collective-permute-start | bytes 245768 | tf_op jit(solution)/shard_map/ppermute | solution.py:450
  10.4 1.1 %collective-permute-start.3 = (bf16[80,512]{1,0:T(8,128)(2,1)S(1)}, bf16[80,512]{1,0:T(8,128)(2,1)S(1)}, u32[]{:S(2)}, u32[]{:S(2)}) collective-permute-start(bf16[80,512]{1,0:T(8,128)(2,1)S(1)} %shard_map.93.after_ref.own_ref), channel_id=1, source_target_pairs={{0,48},{8,56},{16,0},{24,8},{32,16},{40,24},{48,32},{56,40},{64,11... | collective-permute-start | bytes 245768 | tf_op jit(solution)/shard_map/ppermute | solution.py:450
  11.5 2.1 %shard_map.94 = (f32[4,32,8,128]{3,2,1,0:T(8,128)S(1)}, f32[32,512]{1,0:T(8,128)S(1)}) custom-call(f32[4,256,128]{2,1,0:T(8,128)S(1)} %get-tuple-element.27.sig, f32[4,528,128]{2,1,0:T(8,128)S(1)} %get-tuple-element.25.tre, f32[4,528,128]{2,1,0:T(8,128)S(1)} %get-tuple-element.26.tim, f32[16,512]{1,0:T(8,128)S(1)} %copy-done.2, f32[2,16,512]{2,1,0:T(8,128)S(1)} %copy-done.4, ...), custom_call_target="tpu_custom_call" | custom-call | flops 30000000 | bytes 5000000 | tf_op jit(solution)/shard_map/pallas_call | solution.py:28
  14.9 1.0 %collective-permute-start.4 = (f32[40,512]{1,0:T(8,128)S(1)}, f32[40,512]{1,0:T(8,128)S(1)}, u32[]{:S(2)}, u32[]{:S(2)}) collective-permute-start(f32[40,512]{1,0:T(8,128)S(1)} %get-tuple-element.37.after_ref), channel_id=1, source_target_pairs={{0,64},{8,72},{16,80},{24,88},{32,96},{40,104},{48,112},{56,120},{... | collective-permute-start | bytes 245768 | tf_op jit(solution)/shard_map/ppermute | solution.py:450
  15.9 2.0 %collective-permute-start.5 = (f32[40,512]{1,0:T(8,128)S(1)}, f32[40,512]{1,0:T(8,128)S(1)}, u32[]{:S(2)}, u32[]{:S(2)}) collective-permute-start(f32[40,512]{1,0:T(8,128)S(1)} %get-tuple-element.37.after_ref), channel_id=1, source_target_pairs={{0,128},{8,136},{16,144},{24,152},{32,160},{40,168},{48,176},{56,1... | collective-permute-start | bytes 245768 | tf_op jit(solution)/shard_map/ppermute | solution.py:450
  18.0 2.0 %collective-permute-start.13 = (bf16[256,512]{1,0:T(8,128)(2,1)S(1)}, bf16[256,512]{1,0:T(8,128)(2,1)S(1)}, u32[]{:S(2)}, u32[]{:S(2)}) collective-permute-start(bf16[256,512]{1,0:T(8,128)(2,1)S(1)} %shard_map.98.both_ref), channel_id=1, source_target_pairs={{0,32},{8,40},{16,48},{24,56},{32,0},{40,8},{48,16},{56,24},{64,96... | collective-permute-start | bytes 786440 | tf_op jit(solution)/shard_map/ppermute | solution.py:456
  20.9 1.7 %shard_map.97.after_ref.here = bf16[32,4096]{1,0:T(8,128)(2,1)S(1)} custom-call(bf16[256,512]{1,0:T(8,128)(2,1)S(1)} %copy-done.7, f32[4,32,8,128]{3,2,1,0:T(8,128)S(1)} %get-tuple-element.30.y_ref, f32[4,32,8,128]{3,2,1,0:T(8,128)S(1)} %get-tuple-element.33.pz_ref, f32[4,32,8,128]{3,2,1,0:T(8,128)S(1)} %get-tuple-element.34.gz_ref, ...), custom_call_target="tpu_custom_call" | custom-call | flops 2000000000 | bytes 5000000 | tf_op jit(solution)/shard_map/pallas_call | solution.py:28
  22.6 1.7 %collective-permute-start.6 = (bf16[32,4096]{1,0:T(8,128)(2,1)S(1)}, bf16[32,4096]{1,0:T(8,128)(2,1)S(1)}, u32[]{:S(2)}, u32[]{:S(2)}) collective-permute-start(bf16[32,4096]{1,0:T(8,128)(2,1)S(1)} %shard_map.97.after_ref.here), channel_id=1, source_target_pairs={{0,1},{1,2},{2,3},{3,4},{4,5},{5,6},{6,7},{7,0},{8,9},{9,10},{10,1... | collective-permute-start | bytes 786440 | tf_op jit(solution)/shard_map/ppermute | solution.py:460
  24.3 4.0 %collective-permute-start.7 = (bf16[32,4096]{1,0:T(8,128)(2,1)S(1)}, bf16[32,4096]{1,0:T(8,128)(2,1)S(1)}, u32[]{:S(2)}, u32[]{:S(2)}) collective-permute-start(bf16[32,4096]{1,0:T(8,128)(2,1)S(1)} %shard_map.97.after_ref.here), channel_id=1, source_target_pairs={{0,7},{1,0},{2,1},{3,2},{4,3},{5,4},{6,5},{7,6},{8,15},{9,8},{10,9... | collective-permute-start | bytes 786440 | tf_op jit(solution)/shard_map/ppermute | solution.py:460
  28.5 2.2 %collective-permute-start.14 = (bf16[256,512]{1,0:T(8,128)(2,1)S(1)}, bf16[256,512]{1,0:T(8,128)(2,1)S(1)}, u32[]{:S(2)}, u32[]{:S(2)}) collective-permute-start(bf16[256,512]{1,0:T(8,128)(2,1)S(1)} %get-tuple-element.38.even_ref), channel_id=1, source_target_pairs={{0,128},{8,136},{16,144},{24,152},{32,160},{40,168},{48,176},{56,1... | collective-permute-start | bytes 786440 | tf_op jit(solution)/shard_map/ppermute | solution.py:456
  31.2 1.3 %collective-permute-done.6.after_up.up1 = bf16[32,4096]{1,0:T(8,128)(2,1)S(1)} collective-permute-done((bf16[32,4096]{1,0:T(8,128)(2,1)S(1)}, bf16[32,4096]{1,0:T(8,128)(2,1)S(1)}, u32[]{:S(2)}, u32[]{:S(2)}) %collective-permute-start.6) | collective-permute-done | bytes 262176 | tf_op jit(solution)/shard_map/ppermute | solution.py:460
  32.6 2.7 %collective-permute-start.9 = (bf16[32,4096]{1,0:T(8,128)(2,1)S(1)}, bf16[32,4096]{1,0:T(8,128)(2,1)S(1)}, u32[]{:S(2)}, u32[]{:S(2)}) collective-permute-start(bf16[32,4096]{1,0:T(8,128)(2,1)S(1)} %collective-permute-done.7.after_down.down1), channel_id=1, source_target_pairs={{0,7},{1,0},{2,1},{3,2},{4,3},{5,4},{6,5},{7,6},{8,15},{9,8},{10,9... | collective-permute-start | bytes 786440 | tf_op jit(solution)/shard_map/ppermute | solution.py:460
  35.3 0.9 %collective-permute-done.15.odd_y = bf16[256,512]{1,0:T(8,128)(2,1)S(1)} collective-permute-done((bf16[256,512]{1,0:T(8,128)(2,1)S(1)}, bf16[256,512]{1,0:T(8,128)(2,1)S(1)}, u32[]{:S(2)}, u32[]{:S(2)}) %collective-permute-start.15) | collective-permute-done | bytes 262176 | tf_op jit(solution)/shard_map/ppermute | solution.py:456
  37.0 1.2 %collective-permute-start.17 = (bf16[512,512]{1,0:T(8,128)(2,1)S(1)}, bf16[512,512]{1,0:T(8,128)(2,1)S(1)}, u32[]{:S(2)}, u32[]{:S(2)}) collective-permute-start(bf16[512,512]{1,0:T(8,128)(2,1)S(1)} %get-tuple-element.42), channel_id=1, source_target_pairs={{0,128},{8,136},{16,144},{24,152},{32,160},{40,168},{48,176},{56,1... | collective-permute-start | bytes 1572872 | tf_op jit(solution)/shard_map/ppermute | solution.py:456
  39.0 2.7 %collective-permute-start.11 = (bf16[32,4096]{1,0:T(8,128)(2,1)S(1)}, bf16[32,4096]{1,0:T(8,128)(2,1)S(1)}, u32[]{:S(2)}, u32[]{:S(2)}) collective-permute-start(bf16[32,4096]{1,0:T(8,128)(2,1)S(1)} %collective-permute-done.9.down2), channel_id=1, source_target_pairs={{0,7},{1,0},{2,1},{3,2},{4,3},{5,4},{6,5},{7,6},{8,15},{9,8},{10,9... | collective-permute-start | bytes 786440 | tf_op jit(solution)/shard_map/ppermute | solution.py:460
  41.7 4.7 %collective-permute-start.18 = (bf16[1024,512]{1,0:T(8,128)(2,1)S(1)}, bf16[1024,512]{1,0:T(8,128)(2,1)S(1)}, u32[]{:S(2)}, u32[]{:S(2)}) collective-permute-start(bf16[1024,512]{1,0:T(8,128)(2,1)S(1)} %get-tuple-element.40.near_own), channel_id=1, source_target_pairs={{0,8},{8,0},{16,24},{24,16},{32,40},{40,32},{48,56},{56,48},{64,72... | collective-permute-start | bytes 3145736 | tf_op jit(solution)/shard_map/ppermute | solution.py:450
  46.5 2.7 %collective-permute-start.20 = (bf16[16,4096]{1,0:T(8,128)(2,1)S(1)}, bf16[16,4096]{1,0:T(8,128)(2,1)S(1)}, u32[]{:S(2)}, u32[]{:S(2)}) collective-permute-start(bf16[16,4096]{1,0:T(8,128)(2,1)S(1)} %slice.9), channel_id=1, source_target_pairs={{0,7},{1,0},{2,1},{3,2},{4,3},{5,4},{6,5},{7,6},{8,15},{9,8},{10,9... | collective-permute-start | bytes 393224 | tf_op jit(solution)/shard_map/ppermute | solution.py:460
  49.3 5.0 %collective-permute-start.21 = (bf16[1024,512]{1,0:T(8,128)(2,1)S(1)}, bf16[1024,512]{1,0:T(8,128)(2,1)S(1)}, u32[]{:S(2)}, u32[]{:S(2)}) collective-permute-start(bf16[1024,512]{1,0:T(8,128)(2,1)S(1)} %shard_map.101.far_own.own_ref), channel_id=1, source_target_pairs={{0,8},{8,0},{16,24},{24,16},{32,40},{40,32},{48,56},{56,48},{64,72... | collective-permute-start | bytes 3145736 | tf_op jit(solution)/shard_map/ppermute | solution.py:450
  54.3 1.6 %shard_map.102 = (f32[256,512]{1,0:T(8,128)S(1)}, bf16[256,1024]{1,0:T(8,128)(2,1)S(1)}) custom-call(bf16[32,4096]{1,0:T(8,128)(2,1)S(1)} %shard_map.97.after_ref.here, bf16[32,4096]{1,0:T(8,128)(2,1)S(1)} %collective-permute-done.6.after_up.up1, bf16[32,4096]{1,0:T(8,128)(2,1)S(1)} %collective-permute-done.7.after_down.down1, ...), custom_call_target="tpu_custom_call" | custom-call | flops 8000000000 | bytes 7000000 | tf_op jit(solution)/shard_map/pallas_call | solution.py:28
  56.6 1.3 %shard_map.104 = bf16[256,512]{1,0:T(8,128)(2,1)} custom-call(f32[256,512]{1,0:T(8,128)S(1)} %get-tuple-element.43.after_ref.total_ref, bf16[256,1024]{1,0:T(8,128)(2,1)S(1)} %get-tuple-element.44.left, bf16[256,512]{1,0:T(8,128)(2,1)S(1)} %shard_map.103.last, bf16[1024,512]{1,0:T(8,128)(2,1)S(1)} %get-tuple-element.40.near_own, ...), custom_call_target="tpu_custom_call" | custom-call | flops 536870912 | bytes 7000000 | tf_op jit(solution)/shard_map/pallas_call | solution.py:28
  (53 shorter events, 5.8 us)
Async XLA Ops:
  1.3 10.2 %copy-start.2 = (f32[16,512]{1,0:T(8,128)S(1)}, f32[16,512]{1,0:T(8,128)}, u32[]{:S(2)}) copy-start(f32[16,512]{1,0:T(8,128)} %decay_ref.1) | copy-start | bytes 98308
  1.3 10.2 %copy-start.4 = (f32[2,16,512]{2,1,0:T(8,128)S(1)}, f32[2,16,512]{2,1,0:T(8,128)}, u32[]{:S(2)}) copy-start(f32[2,16,512]{2,1,0:T(8,128)} %res_ref.1) | copy-start | bytes 196612
  3.5 4.2 %collective-permute-start = (f32[40,512]{1,0:T(8,128)S(1)}, f32[40,512]{1,0:T(8,128)S(1)}, u32[]{:S(2)}, u32[]{:S(2)}) collective-permute-start(f32[40,512]{1,0:T(8,128)S(1)} %get-tuple-element.28.own_ref), channel_id=1, source_target_pairs={{0,8},{8,0},{16,24},{24,16},{32,40},{40,32},{48,56},{56,48},{64,72... | collective-permute-start | bytes 245768 | tf_op jit(solution)/shard_map/ppermute | solution.py:450
  6.8 11.1 %collective-permute-start.12 = (bf16[128,512]{1,0:T(8,128)(2,1)S(1)}, bf16[128,512]{1,0:T(8,128)(2,1)S(1)}, u32[]{:S(2)}, u32[]{:S(2)}) collective-permute-start(bf16[128,512]{1,0:T(8,128)(2,1)S(1)} %copy-done.3), channel_id=1, source_target_pairs={{0,64},{8,72},{16,80},{24,88},{32,96},{40,104},{48,112},{56,120},{... | collective-permute-start | bytes 393224 | tf_op jit(solution)/shard_map/ppermute | solution.py:456
  7.8 5.8 %collective-permute-start.1 = (bf16[80,512]{1,0:T(8,128)(2,1)S(1)}, bf16[80,512]{1,0:T(8,128)(2,1)S(1)}, u32[]{:S(2)}, u32[]{:S(2)}) collective-permute-start(bf16[80,512]{1,0:T(8,128)(2,1)S(1)} %shard_map.93.after_ref.own_ref), channel_id=1, source_target_pairs={{0,16},{8,24},{16,32},{24,40},{32,48},{40,56},{48,0},{56,8},{64,80... | collective-permute-start | bytes 245768 | tf_op jit(solution)/shard_map/ppermute | solution.py:450
  7.9 6.5 %collective-permute-start.2 = (bf16[80,512]{1,0:T(8,128)(2,1)S(1)}, bf16[80,512]{1,0:T(8,128)(2,1)S(1)}, u32[]{:S(2)}, u32[]{:S(2)}) collective-permute-start(bf16[80,512]{1,0:T(8,128)(2,1)S(1)} %shard_map.93.after_ref.own_ref), channel_id=1, source_target_pairs={{0,32},{8,40},{16,48},{24,56},{32,0},{40,8},{48,16},{56,24},{64,96... | collective-permute-start | bytes 245768 | tf_op jit(solution)/shard_map/ppermute | solution.py:450
  10.4 4.4 %collective-permute-start.3 = (bf16[80,512]{1,0:T(8,128)(2,1)S(1)}, bf16[80,512]{1,0:T(8,128)(2,1)S(1)}, u32[]{:S(2)}, u32[]{:S(2)}) collective-permute-start(bf16[80,512]{1,0:T(8,128)(2,1)S(1)} %shard_map.93.after_ref.own_ref), channel_id=1, source_target_pairs={{0,48},{8,56},{16,0},{24,8},{32,16},{40,24},{48,32},{56,40},{64,11... | collective-permute-start | bytes 245768 | tf_op jit(solution)/shard_map/ppermute | solution.py:450
  14.9 5.7 %collective-permute-start.4 = (f32[40,512]{1,0:T(8,128)S(1)}, f32[40,512]{1,0:T(8,128)S(1)}, u32[]{:S(2)}, u32[]{:S(2)}) collective-permute-start(f32[40,512]{1,0:T(8,128)S(1)} %get-tuple-element.37.after_ref), channel_id=1, source_target_pairs={{0,64},{8,72},{16,80},{24,88},{32,96},{40,104},{48,112},{56,120},{... | collective-permute-start | bytes 245768 | tf_op jit(solution)/shard_map/ppermute | solution.py:450
  15.9 4.8 %collective-permute-start.5 = (f32[40,512]{1,0:T(8,128)S(1)}, f32[40,512]{1,0:T(8,128)S(1)}, u32[]{:S(2)}, u32[]{:S(2)}) collective-permute-start(f32[40,512]{1,0:T(8,128)S(1)} %get-tuple-element.37.after_ref), channel_id=1, source_target_pairs={{0,128},{8,136},{16,144},{24,152},{32,160},{40,168},{48,176},{56,1... | collective-permute-start | bytes 245768 | tf_op jit(solution)/shard_map/ppermute | solution.py:450
  18.0 10.4 %collective-permute-start.13 = (bf16[256,512]{1,0:T(8,128)(2,1)S(1)}, bf16[256,512]{1,0:T(8,128)(2,1)S(1)}, u32[]{:S(2)}, u32[]{:S(2)}) collective-permute-start(bf16[256,512]{1,0:T(8,128)(2,1)S(1)} %shard_map.98.both_ref), channel_id=1, source_target_pairs={{0,32},{8,40},{16,48},{24,56},{32,0},{40,8},{48,16},{56,24},{64,96... | collective-permute-start | bytes 786440 | tf_op jit(solution)/shard_map/ppermute | solution.py:456
  22.6 9.9 %collective-permute-start.6 = (bf16[32,4096]{1,0:T(8,128)(2,1)S(1)}, bf16[32,4096]{1,0:T(8,128)(2,1)S(1)}, u32[]{:S(2)}, u32[]{:S(2)}) collective-permute-start(bf16[32,4096]{1,0:T(8,128)(2,1)S(1)} %shard_map.97.after_ref.here), channel_id=1, source_target_pairs={{0,1},{1,2},{2,3},{3,4},{4,5},{5,6},{6,7},{7,0},{8,9},{9,10},{10,1... | collective-permute-start | bytes 786440 | tf_op jit(solution)/shard_map/ppermute | solution.py:460
  24.3 8.2 %collective-permute-start.7 = (bf16[32,4096]{1,0:T(8,128)(2,1)S(1)}, bf16[32,4096]{1,0:T(8,128)(2,1)S(1)}, u32[]{:S(2)}, u32[]{:S(2)}) collective-permute-start(bf16[32,4096]{1,0:T(8,128)(2,1)S(1)} %shard_map.97.after_ref.here), channel_id=1, source_target_pairs={{0,7},{1,0},{2,1},{3,2},{4,3},{5,4},{6,5},{7,6},{8,15},{9,8},{10,9... | collective-permute-start | bytes 786440 | tf_op jit(solution)/shard_map/ppermute | solution.py:460
  28.5 6.8 %collective-permute-start.14 = (bf16[256,512]{1,0:T(8,128)(2,1)S(1)}, bf16[256,512]{1,0:T(8,128)(2,1)S(1)}, u32[]{:S(2)}, u32[]{:S(2)}) collective-permute-start(bf16[256,512]{1,0:T(8,128)(2,1)S(1)} %get-tuple-element.38.even_ref), channel_id=1, source_target_pairs={{0,128},{8,136},{16,144},{24,152},{32,160},{40,168},{48,176},{56,1... | collective-permute-start | bytes 786440 | tf_op jit(solution)/shard_map/ppermute | solution.py:456
  30.7 5.5 %collective-permute-start.15 = (bf16[256,512]{1,0:T(8,128)(2,1)S(1)}, bf16[256,512]{1,0:T(8,128)(2,1)S(1)}, u32[]{:S(2)}, u32[]{:S(2)}) collective-permute-start(bf16[256,512]{1,0:T(8,128)(2,1)S(1)} %get-tuple-element.39.odd_ref), channel_id=1, source_target_pairs={{0,16},{8,24},{16,0},{24,8},{32,48},{40,56},{48,32},{56,40},{64,80... | collective-permute-start | bytes 786440 | tf_op jit(solution)/shard_map/ppermute | solution.py:456
  32.6 6.4 %collective-permute-start.8 = (bf16[32,4096]{1,0:T(8,128)(2,1)S(1)}, bf16[32,4096]{1,0:T(8,128)(2,1)S(1)}, u32[]{:S(2)}, u32[]{:S(2)}) collective-permute-start(bf16[32,4096]{1,0:T(8,128)(2,1)S(1)} %collective-permute-done.6.after_up.up1), channel_id=1, source_target_pairs={{0,1},{1,2},{2,3},{3,4},{4,5},{5,6},{6,7},{7,0},{8,9},{9,10},{10,1... | collective-permute-start | bytes 786440 | tf_op jit(solution)/shard_map/ppermute | solution.py:460
  32.6 6.4 %collective-permute-start.9 = (bf16[32,4096]{1,0:T(8,128)(2,1)S(1)}, bf16[32,4096]{1,0:T(8,128)(2,1)S(1)}, u32[]{:S(2)}, u32[]{:S(2)}) collective-permute-start(bf16[32,4096]{1,0:T(8,128)(2,1)S(1)} %collective-permute-done.7.after_down.down1), channel_id=1, source_target_pairs={{0,7},{1,0},{2,1},{3,2},{4,3},{5,4},{6,5},{7,6},{8,15},{9,8},{10,9... | collective-permute-start | bytes 786440 | tf_op jit(solution)/shard_map/ppermute | solution.py:460
  36.3 12.9 %collective-permute-start.16 = (bf16[512,512]{1,0:T(8,128)(2,1)S(1)}, bf16[512,512]{1,0:T(8,128)(2,1)S(1)}, u32[]{:S(2)}, u32[]{:S(2)}) collective-permute-start(bf16[512,512]{1,0:T(8,128)(2,1)S(1)} %get-tuple-element.41), channel_id=1, source_target_pairs={{0,16},{8,24},{16,0},{24,8},{32,48},{40,56},{48,32},{56,40},{64,80... | collective-permute-start | bytes 1572872 | tf_op jit(solution)/shard_map/ppermute | solution.py:456
  37.0 12.3 %collective-permute-start.17 = (bf16[512,512]{1,0:T(8,128)(2,1)S(1)}, bf16[512,512]{1,0:T(8,128)(2,1)S(1)}, u32[]{:S(2)}, u32[]{:S(2)}) collective-permute-start(bf16[512,512]{1,0:T(8,128)(2,1)S(1)} %get-tuple-element.42), channel_id=1, source_target_pairs={{0,128},{8,136},{16,144},{24,152},{32,160},{40,168},{48,176},{56,1... | collective-permute-start | bytes 1572872 | tf_op jit(solution)/shard_map/ppermute | solution.py:456
  39.0 7.4 %collective-permute-start.10 = (bf16[32,4096]{1,0:T(8,128)(2,1)S(1)}, bf16[32,4096]{1,0:T(8,128)(2,1)S(1)}, u32[]{:S(2)}, u32[]{:S(2)}) collective-permute-start(bf16[32,4096]{1,0:T(8,128)(2,1)S(1)} %collective-permute-done.8.up2), channel_id=1, source_target_pairs={{0,1},{1,2},{2,3},{3,4},{4,5},{5,6},{6,7},{7,0},{8,9},{9,10},{10,1... | collective-permute-start | bytes 786440 | tf_op jit(solution)/shard_map/ppermute | solution.py:460
  39.0 7.5 %collective-permute-start.11 = (bf16[32,4096]{1,0:T(8,128)(2,1)S(1)}, bf16[32,4096]{1,0:T(8,128)(2,1)S(1)}, u32[]{:S(2)}, u32[]{:S(2)}) collective-permute-start(bf16[32,4096]{1,0:T(8,128)(2,1)S(1)} %collective-permute-done.9.down2), channel_id=1, source_target_pairs={{0,7},{1,0},{2,1},{3,2},{4,3},{5,4},{6,5},{7,6},{8,15},{9,8},{10,9... | collective-permute-start | bytes 786440 | tf_op jit(solution)/shard_map/ppermute | solution.py:460
  41.7 12.6 %collective-permute-start.18 = (bf16[1024,512]{1,0:T(8,128)(2,1)S(1)}, bf16[1024,512]{1,0:T(8,128)(2,1)S(1)}, u32[]{:S(2)}, u32[]{:S(2)}) collective-permute-start(bf16[1024,512]{1,0:T(8,128)(2,1)S(1)} %get-tuple-element.40.near_own), channel_id=1, source_target_pairs={{0,8},{8,0},{16,24},{24,16},{32,40},{40,32},{48,56},{56,48},{64,72... | collective-permute-start | bytes 3145736 | tf_op jit(solution)/shard_map/ppermute | solution.py:450
  46.4 9.5 %collective-permute-start.19 = (bf16[16,4096]{1,0:T(8,128)(2,1)S(1)}, bf16[16,4096]{1,0:T(8,128)(2,1)S(1)}, u32[]{:S(2)}, u32[]{:S(2)}) collective-permute-start(bf16[16,4096]{1,0:T(8,128)(2,1)S(1)} %slice.8), channel_id=1, source_target_pairs={{0,1},{1,2},{2,3},{3,4},{4,5},{5,6},{6,7},{7,0},{8,9},{9,10},{10,1... | collective-permute-start | bytes 393224 | tf_op jit(solution)/shard_map/ppermute | solution.py:460
  46.5 9.4 %collective-permute-start.20 = (bf16[16,4096]{1,0:T(8,128)(2,1)S(1)}, bf16[16,4096]{1,0:T(8,128)(2,1)S(1)}, u32[]{:S(2)}, u32[]{:S(2)}) collective-permute-start(bf16[16,4096]{1,0:T(8,128)(2,1)S(1)} %slice.9), channel_id=1, source_target_pairs={{0,7},{1,0},{2,1},{3,2},{4,3},{5,4},{6,5},{7,6},{8,15},{9,8},{10,9... | collective-permute-start | bytes 393224 | tf_op jit(solution)/shard_map/ppermute | solution.py:460
  49.3 7.2 %collective-permute-start.21 = (bf16[1024,512]{1,0:T(8,128)(2,1)S(1)}, bf16[1024,512]{1,0:T(8,128)(2,1)S(1)}, u32[]{:S(2)}, u32[]{:S(2)}) collective-permute-start(bf16[1024,512]{1,0:T(8,128)(2,1)S(1)} %shard_map.101.far_own.own_ref), channel_id=1, source_target_pairs={{0,8},{8,0},{16,24},{24,16},{32,40},{40,32},{48,56},{56,48},{64,72... | collective-permute-start | bytes 3145736 | tf_op jit(solution)/shard_map/ppermute | solution.py:450
  (6 other events, 20.5 us)

commit v9 on v8

--- a/solution.py
+++ b/solution.py
@@ -13,6 +13,7 @@
 GROUPS = CH // LANES
 STEPS = 32
 BLOCKS = TOK // STEPS
+HALF = STEPS // 2
 ROWS = 2 * MODES
 PAY = ROWS + 8
 VMEM = pl.BlockSpec(memory_space=pltpu.VMEM)
@@ -98,6 +99,10 @@
     p256_ref[MODES:, :] = value[1]
 
 
+def table_row(tre, tim, g, at):
+    return [jnp.broadcast_to(t[g, pl.ds(at, 1), :], (BLOCKS, LANES)) for t in (tre, tim)]
+
+
 def ends_kernel(key_ref, value_ref, starts_ref, tre, tim, pay_ref, eb_ref, sig):
     s0 = first_start(starts_ref)
     b0 = s0 // STEPS
@@ -105,33 +110,41 @@
     blocks = block_iota()
 
     def group(g, unused):
-        def step(j, acc):
-            x = sig[g, pl.ds(j, BLOCKS, stride=STEPS), :]
-            x = jnp.where((blocks * STEPS + j >= s0) | (blocks != b0), x, 0.0)
-            base = (STEPS - 1 - j) * MODES
-            out = []
-            for m in range(MODES):
-                out.append(acc[2 * m] + tre[g, pl.ds(base + m, 1), :] * x)
-                out.append(acc[2 * m + 1] + tim[g, pl.ds(base + m, 1), :] * x)
-            return tuple(out)
-
         zero = jnp.zeros((BLOCKS, LANES), F32)
-        acc = lax.fori_loop(0, STEPS, step, (zero,) * ROWS, unroll=8)
-        for m in range(MODES):
-            eb_ref[g, m * BLOCKS:(m + 1) * BLOCKS, :] = acc[2 * m]
-            eb_ref[g, (MODES + m) * BLOCKS:(MODES + m + 1) * BLOCKS, :] = acc[2 * m + 1]
+        for low in range(0, MODES, MODES // 2):
+            def step(j, acc, low=low):
+                xs = []
+                for at in (j, j + HALF):
+                    x = sig[g, pl.ds(at, BLOCKS, stride=STEPS), :]
+                    xs.append(jnp.where((blocks * STEPS + at >= s0) | (blocks != b0), x, 0.0))
+                base = (HALF - 1 - j) * MODES + low
+                out = []
+                for m in range(MODES // 2):
+                    row = table_row(tre, tim, g, base + m)
+                    for n in range(4):
+                        out.append(acc[4 * m + n] + row[n % 2] * xs[n // 2])
+                return tuple(out)
+
+            acc = lax.fori_loop(0, HALF, step, (zero,) * (2 * MODES), unroll=16)
+            for m in range(MODES // 2):
+                row = table_row(tre, tim, g, HALF * MODES + low + m)
+                end = cadd(cmul(row, acc[4 * m:4 * m + 2]), acc[4 * m + 2:4 * m + 4])
+                at = low + m
+                eb_ref[g, at * BLOCKS:(at + 1) * BLOCKS, :] = end[0]
+                eb_ref[g, (MODES + at) * BLOCKS:(MODES + at + 1) * BLOCKS, :] = end[1]
         q = (tre[g, STEPS * MODES:, :], tim[g, STEPS * MODES:, :])
         state = (jnp.zeros((MODES, LANES), F32),) * 2
         for n in range(BLOCKS):
             state = [jnp.where(b0 == n, 0.0, part) for part in state]
             add = [eb_ref[g, pl.ds(at * BLOCKS + n, MODES, stride=BLOCKS), :] for at in (0, MODES)]
             state = cadd(cmul(q, state), add)
-        lanes = pl.ds(pl.multiple_of(g * LANES, LANES), LANES)
+        lanes = slice(g * LANES, (g + 1) * LANES)
         pay_ref[:MODES, lanes] = state[0]
         pay_ref[MODES:ROWS, lanes] = state[1]
         return unused
 
-    lax.fori_loop(0, GROUPS, group, 0)
+    for g in range(GROUPS):
+        group(g, 0)
     pay_ref[ROWS:, :] = jnp.broadcast_to((s0 >= TOK).astype(F32), (PAY - ROWS, CH))
 
 
@@ -356,7 +369,8 @@
 
         return lax.fori_loop(0, STEPS, step, unused, unroll=16)
 
-    lax.fori_loop(0, GROUPS, group, 0)
+    for g in range(GROUPS):
+        group(g, 0)
     for g in range(GROUPS):
         lanes = slice(g * LANES, (g + 1) * LANES)
         gated = (query_ref[:, lanes].astype(F32) * conv[g]).astype(BF16)

time: 58.8 us -> 58.6 us (level)
  no operation moved by 1% of the time
where the time goes in v9:
time: 58.6 us; the launch traced here: 57.6 us
  starting transfers between devices  40.2 us (69%)
  Pallas kernels  10.1 us (17%)
  waiting for transfers between devices  5.85 us (10%)
  other arithmetic  0.97 us (2%)
    ppermute x8, starting transfers between devices, move(): return lax.ppermute(value, 'ctx', pairs)  19.6 us
    ppermute x8, starting transfers between devices, turn(): return lax.ppermute(value, 'tp', [(i, (i + k) % NZ) for i in range(NZ)])  13.9 us
    pallas_call x14, Pallas kernels, call(): pl.pallas_call(kernel, out_shape=outs, in_specs=[VMEM] * len(args), out_s...  10.1 us
    ppermute x6, starting transfers between devices, trade(): return lax.ppermute(value, 'ctx', pairs)  6.64 us
    ppermute x8, waiting for transfers between devices, move(): return lax.ppermute(value, 'ctx', pairs)  2.74 us
    ppermute x8, waiting for transfers between devices, turn(): return lax.ppermute(value, 'tp', [(i, (i + k) % NZ) for i in range(NZ)])  2.16 us
  transfers between devices with their start and end apart: 22, of which 7 were waited for; matrix products, arithmetic and copies ran while one was open for 0% of the time, Pallas kernels for 11%

profile of v9, /device:TPU:1, one launch (start us, length us, event | category | flops | bytes accessed | tf_op | source)
XLA Modules:
  0.0 57.6 jit_solution(7271793758990647537)
XLA Ops:
  0.0 1.0 %sine_multiply_fusion = (f32[16,512]{1,0:T(8,128)S(1)}, f32[16,512]{1,0:T(8,128)S(1)}) fusion(f32[16,512]{1,0:T(8,128)} %param.13, f32[16,512]{1,0:T(8,128)} %decay_ref.1), kind=kLoop, calls=%fused_computation | loop fusion | flops 24576 | bytes 131072 | tf_op jit(solution)/shard_map/mul | solution.py:490
  1.4 2.0 %shard_map.92 = (f32[40,512]{1,0:T(8,128)S(1)}, f32[4,256,128]{2,1,0:T(8,128)S(1)}, f32[4,256,128]{2,1,0:T(8,128)S(1)}) custom-call(bf16[256,512]{1,0:T(8,128)(2,1)S(1)} %copy-done, bf16[256,512]{1,0:T(8,128)(2,1)S(1)} %copy-done.1, s32[2,128]{1,0:T(2,128)S(1)} %bitcast.2, f32[4,528,128]{2,1,0:T(8,128)S(1)} %get-tuple-element.25.tre, ...), custom_call_target="tpu_custom_call" | custom-call | flops 20000000 | bytes 5000000 | tf_op jit(solution)/shard_map/pallas_call | solution.py:29
  3.3 3.3 %collective-permute-start = (f32[40,512]{1,0:T(8,128)S(1)}, f32[40,512]{1,0:T(8,128)S(1)}, u32[]{:S(2)}, u32[]{:S(2)}) collective-permute-start(f32[40,512]{1,0:T(8,128)S(1)} %get-tuple-element.28.own_ref), channel_id=1, source_target_pairs={{0,8},{8,0},{16,24},{24,16},{32,40},{40,32},{48,56},{56,48},{64,72... | collective-permute-start | bytes 245768 | tf_op jit(solution)/shard_map/ppermute | solution.py:464
  6.7 0.9 %collective-permute-done.other_ref = f32[40,512]{1,0:T(8,128)S(1)} collective-permute-done((f32[40,512]{1,0:T(8,128)S(1)}, f32[40,512]{1,0:T(8,128)S(1)}, u32[]{:S(2)}, u32[]{:S(2)}) %collective-permute-start) | collective-permute-done | bytes 81952 | tf_op jit(solution)/shard_map/ppermute | solution.py:464
  7.7 2.5 %collective-permute-start.2 = (bf16[80,512]{1,0:T(8,128)(2,1)S(1)}, bf16[80,512]{1,0:T(8,128)(2,1)S(1)}, u32[]{:S(2)}, u32[]{:S(2)}) collective-permute-start(bf16[80,512]{1,0:T(8,128)(2,1)S(1)} %shard_map.93.after_ref.own_ref), channel_id=1, source_target_pairs={{0,32},{8,40},{16,48},{24,56},{32,0},{40,8},{48,16},{56,24},{64,96... | collective-permute-start | bytes 245768 | tf_op jit(solution)/shard_map/ppermute | solution.py:464
  10.2 1.1 %collective-permute-start.3 = (bf16[80,512]{1,0:T(8,128)(2,1)S(1)}, bf16[80,512]{1,0:T(8,128)(2,1)S(1)}, u32[]{:S(2)}, u32[]{:S(2)}) collective-permute-start(bf16[80,512]{1,0:T(8,128)(2,1)S(1)} %shard_map.93.after_ref.own_ref), channel_id=1, source_target_pairs={{0,48},{8,56},{16,0},{24,8},{32,16},{40,24},{48,32},{56,40},{64,11... | collective-permute-start | bytes 245768 | tf_op jit(solution)/shard_map/ppermute | solution.py:464
  11.3 2.1 %shard_map.94 = (f32[4,32,8,128]{3,2,1,0:T(8,128)S(1)}, f32[32,512]{1,0:T(8,128)S(1)}) custom-call(f32[4,256,128]{2,1,0:T(8,128)S(1)} %get-tuple-element.27.sig, f32[4,528,128]{2,1,0:T(8,128)S(1)} %get-tuple-element.25.tre, f32[4,528,128]{2,1,0:T(8,128)S(1)} %get-tuple-element.26.tim, f32[16,512]{1,0:T(8,128)S(1)} %copy-done.2, f32[2,16,512]{2,1,0:T(8,128)S(1)} %copy-done.4, ...), custom_call_target="tpu_custom_call" | custom-call | flops 30000000 | bytes 5000000 | tf_op jit(solution)/shard_map/pallas_call | solution.py:29
  14.7 1.0 %collective-permute-start.4 = (f32[40,512]{1,0:T(8,128)S(1)}, f32[40,512]{1,0:T(8,128)S(1)}, u32[]{:S(2)}, u32[]{:S(2)}) collective-permute-start(f32[40,512]{1,0:T(8,128)S(1)} %get-tuple-element.37.after_ref), channel_id=1, source_target_pairs={{0,64},{8,72},{16,80},{24,88},{32,96},{40,104},{48,112},{56,120},{... | collective-permute-start | bytes 245768 | tf_op jit(solution)/shard_map/ppermute | solution.py:464
  15.7 2.0 %collective-permute-start.5 = (f32[40,512]{1,0:T(8,128)S(1)}, f32[40,512]{1,0:T(8,128)S(1)}, u32[]{:S(2)}, u32[]{:S(2)}) collective-permute-start(f32[40,512]{1,0:T(8,128)S(1)} %get-tuple-element.37.after_ref), channel_id=1, source_target_pairs={{0,128},{8,136},{16,144},{24,152},{32,160},{40,168},{48,176},{56,1... | collective-permute-start | bytes 245768 | tf_op jit(solution)/shard_map/ppermute | solution.py:464
  17.8 2.0 %collective-permute-start.13 = (bf16[256,512]{1,0:T(8,128)(2,1)S(1)}, bf16[256,512]{1,0:T(8,128)(2,1)S(1)}, u32[]{:S(2)}, u32[]{:S(2)}) collective-permute-start(bf16[256,512]{1,0:T(8,128)(2,1)S(1)} %shard_map.98.both_ref), channel_id=1, source_target_pairs={{0,32},{8,40},{16,48},{24,56},{32,0},{40,8},{48,16},{56,24},{64,96... | collective-permute-start | bytes 786440 | tf_op jit(solution)/shard_map/ppermute | solution.py:470
  20.7 1.7 %shard_map.97.after_ref.here = bf16[32,4096]{1,0:T(8,128)(2,1)S(1)} custom-call(bf16[256,512]{1,0:T(8,128)(2,1)S(1)} %copy-done.7, f32[4,32,8,128]{3,2,1,0:T(8,128)S(1)} %get-tuple-element.30.y_ref, f32[4,32,8,128]{3,2,1,0:T(8,128)S(1)} %get-tuple-element.33.pz_ref, f32[4,32,8,128]{3,2,1,0:T(8,128)S(1)} %get-tuple-element.34.gz_ref, ...), custom_call_target="tpu_custom_call" | custom-call | flops 2000000000 | bytes 5000000 | tf_op jit(solution)/shard_map/pallas_call | solution.py:29
  22.4 1.7 %collective-permute-start.6 = (bf16[32,4096]{1,0:T(8,128)(2,1)S(1)}, bf16[32,4096]{1,0:T(8,128)(2,1)S(1)}, u32[]{:S(2)}, u32[]{:S(2)}) collective-permute-start(bf16[32,4096]{1,0:T(8,128)(2,1)S(1)} %shard_map.97.after_ref.here), channel_id=1, source_target_pairs={{0,1},{1,2},{2,3},{3,4},{4,5},{5,6},{6,7},{7,0},{8,9},{9,10},{10,1... | collective-permute-start | bytes 786440 | tf_op jit(solution)/shard_map/ppermute | solution.py:474
  24.1 4.0 %collective-permute-start.7 = (bf16[32,4096]{1,0:T(8,128)(2,1)S(1)}, bf16[32,4096]{1,0:T(8,128)(2,1)S(1)}, u32[]{:S(2)}, u32[]{:S(2)}) collective-permute-start(bf16[32,4096]{1,0:T(8,128)(2,1)S(1)} %shard_map.97.after_ref.here), channel_id=1, source_target_pairs={{0,7},{1,0},{2,1},{3,2},{4,3},{5,4},{6,5},{7,6},{8,15},{9,8},{10,9... | collective-permute-start | bytes 786440 | tf_op jit(solution)/shard_map/ppermute | solution.py:474
  28.2 2.2 %collective-permute-start.14 = (bf16[256,512]{1,0:T(8,128)(2,1)S(1)}, bf16[256,512]{1,0:T(8,128)(2,1)S(1)}, u32[]{:S(2)}, u32[]{:S(2)}) collective-permute-start(bf16[256,512]{1,0:T(8,128)(2,1)S(1)} %get-tuple-element.38.even_ref), channel_id=1, source_target_pairs={{0,128},{8,136},{16,144},{24,152},{32,160},{40,168},{48,176},{56,1... | collective-permute-start | bytes 786440 | tf_op jit(solution)/shard_map/ppermute | solution.py:470
  31.0 1.3 %collective-permute-done.6.after_up.up1 = bf16[32,4096]{1,0:T(8,128)(2,1)S(1)} collective-permute-done((bf16[32,4096]{1,0:T(8,128)(2,1)S(1)}, bf16[32,4096]{1,0:T(8,128)(2,1)S(1)}, u32[]{:S(2)}, u32[]{:S(2)}) %collective-permute-start.6) | collective-permute-done | bytes 262176 | tf_op jit(solution)/shard_map/ppermute | solution.py:474
  32.3 2.7 %collective-permute-start.9 = (bf16[32,4096]{1,0:T(8,128)(2,1)S(1)}, bf16[32,4096]{1,0:T(8,128)(2,1)S(1)}, u32[]{:S(2)}, u32[]{:S(2)}) collective-permute-start(bf16[32,4096]{1,0:T(8,128)(2,1)S(1)} %collective-permute-done.7.after_down.down1), channel_id=1, source_target_pairs={{0,7},{1,0},{2,1},{3,2},{4,3},{5,4},{6,5},{7,6},{8,15},{9,8},{10,9... | collective-permute-start | bytes 786440 | tf_op jit(solution)/shard_map/ppermute | solution.py:474
  35.0 0.9 %collective-permute-done.15.odd_y = bf16[256,512]{1,0:T(8,128)(2,1)S(1)} collective-permute-done((bf16[256,512]{1,0:T(8,128)(2,1)S(1)}, bf16[256,512]{1,0:T(8,128)(2,1)S(1)}, u32[]{:S(2)}, u32[]{:S(2)}) %collective-permute-start.15) | collective-permute-done | bytes 262176 | tf_op jit(solution)/shard_map/ppermute | solution.py:470
  36.7 1.2 %collective-permute-start.17 = (bf16[512,512]{1,0:T(8,128)(2,1)S(1)}, bf16[512,512]{1,0:T(8,128)(2,1)S(1)}, u32[]{:S(2)}, u32[]{:S(2)}) collective-permute-start(bf16[512,512]{1,0:T(8,128)(2,1)S(1)} %get-tuple-element.42), channel_id=1, source_target_pairs={{0,128},{8,136},{16,144},{24,152},{32,160},{40,168},{48,176},{56,1... | collective-permute-start | bytes 1572872 | tf_op jit(solution)/shard_map/ppermute | solution.py:470
  38.8 2.7 %collective-permute-start.11 = (bf16[32,4096]{1,0:T(8,128)(2,1)S(1)}, bf16[32,4096]{1,0:T(8,128)(2,1)S(1)}, u32[]{:S(2)}, u32[]{:S(2)}) collective-permute-start(bf16[32,4096]{1,0:T(8,128)(2,1)S(1)} %collective-permute-done.9.down2), channel_id=1, source_target_pairs={{0,7},{1,0},{2,1},{3,2},{4,3},{5,4},{6,5},{7,6},{8,15},{9,8},{10,9... | collective-permute-start | bytes 786440 | tf_op jit(solution)/shard_map/ppermute | solution.py:474
  41.4 4.7 %collective-permute-start.18 = (bf16[1024,512]{1,0:T(8,128)(2,1)S(1)}, bf16[1024,512]{1,0:T(8,128)(2,1)S(1)}, u32[]{:S(2)}, u32[]{:S(2)}) collective-permute-start(bf16[1024,512]{1,0:T(8,128)(2,1)S(1)} %get-tuple-element.40.near_own), channel_id=1, source_target_pairs={{0,8},{8,0},{16,24},{24,16},{32,40},{40,32},{48,56},{56,48},{64,72... | collective-permute-start | bytes 3145736 | tf_op jit(solution)/shard_map/ppermute | solution.py:464
  46.3 2.7 %collective-permute-start.20 = (bf16[16,4096]{1,0:T(8,128)(2,1)S(1)}, bf16[16,4096]{1,0:T(8,128)(2,1)S(1)}, u32[]{:S(2)}, u32[]{:S(2)}) collective-permute-start(bf16[16,4096]{1,0:T(8,128)(2,1)S(1)} %slice.9), channel_id=1, source_target_pairs={{0,7},{1,0},{2,1},{3,2},{4,3},{5,4},{6,5},{7,6},{8,15},{9,8},{10,9... | collective-permute-start | bytes 393224 | tf_op jit(solution)/shard_map/ppermute | solution.py:474
  49.1 5.0 %collective-permute-start.21 = (bf16[1024,512]{1,0:T(8,128)(2,1)S(1)}, bf16[1024,512]{1,0:T(8,128)(2,1)S(1)}, u32[]{:S(2)}, u32[]{:S(2)}) collective-permute-start(bf16[1024,512]{1,0:T(8,128)(2,1)S(1)} %shard_map.101.far_own.own_ref), channel_id=1, source_target_pairs={{0,8},{8,0},{16,24},{24,16},{32,40},{40,32},{48,56},{56,48},{64,72... | collective-permute-start | bytes 3145736 | tf_op jit(solution)/shard_map/ppermute | solution.py:464
  54.1 1.6 %shard_map.102 = (f32[256,512]{1,0:T(8,128)S(1)}, bf16[256,1024]{1,0:T(8,128)(2,1)S(1)}) custom-call(bf16[32,4096]{1,0:T(8,128)(2,1)S(1)} %shard_map.97.after_ref.here, bf16[32,4096]{1,0:T(8,128)(2,1)S(1)} %collective-permute-done.6.after_up.up1, bf16[32,4096]{1,0:T(8,128)(2,1)S(1)} %collective-permute-done.7.after_down.down1, ...), custom_call_target="tpu_custom_call" | custom-call | flops 8000000000 | bytes 7000000 | tf_op jit(solution)/shard_map/pallas_call | solution.py:29
  56.3 1.3 %shard_map.104 = bf16[256,512]{1,0:T(8,128)(2,1)} custom-call(f32[256,512]{1,0:T(8,128)S(1)} %get-tuple-element.43.after_ref.total_ref, bf16[256,1024]{1,0:T(8,128)(2,1)S(1)} %get-tuple-element.44.left, bf16[256,512]{1,0:T(8,128)(2,1)S(1)} %shard_map.103.last, bf16[1024,512]{1,0:T(8,128)(2,1)S(1)} %get-tuple-element.40.near_own, ...), custom_call_target="tpu_custom_call" | custom-call | flops 536870912 | bytes 7000000 | tf_op jit(solution)/shard_map/pallas_call | solution.py:29
  (53 shorter events, 5.8 us)
Async XLA Ops:
  1.3 10.0 %copy-start.2 = (f32[16,512]{1,0:T(8,128)S(1)}, f32[16,512]{1,0:T(8,128)}, u32[]{:S(2)}) copy-start(f32[16,512]{1,0:T(8,128)} %decay_ref.1) | copy-start | bytes 98308
  1.3 10.0 %copy-start.4 = (f32[2,16,512]{2,1,0:T(8,128)S(1)}, f32[2,16,512]{2,1,0:T(8,128)}, u32[]{:S(2)}) copy-start(f32[2,16,512]{2,1,0:T(8,128)} %res_ref.1) | copy-start | bytes 196612
  3.3 4.2 %collective-permute-start = (f32[40,512]{1,0:T(8,128)S(1)}, f32[40,512]{1,0:T(8,128)S(1)}, u32[]{:S(2)}, u32[]{:S(2)}) collective-permute-start(f32[40,512]{1,0:T(8,128)S(1)} %get-tuple-element.28.own_ref), channel_id=1, source_target_pairs={{0,8},{8,0},{16,24},{24,16},{32,40},{40,32},{48,56},{56,48},{64,72... | collective-permute-start | bytes 245768 | tf_op jit(solution)/shard_map/ppermute | solution.py:464
  6.6 11.1 %collective-permute-start.12 = (bf16[128,512]{1,0:T(8,128)(2,1)S(1)}, bf16[128,512]{1,0:T(8,128)(2,1)S(1)}, u32[]{:S(2)}, u32[]{:S(2)}) collective-permute-start(bf16[128,512]{1,0:T(8,128)(2,1)S(1)} %copy-done.3), channel_id=1, source_target_pairs={{0,64},{8,72},{16,80},{24,88},{32,96},{40,104},{48,112},{56,120},{... | collective-permute-start | bytes 393224 | tf_op jit(solution)/shard_map/ppermute | solution.py:470
  7.6 5.8 %collective-permute-start.1 = (bf16[80,512]{1,0:T(8,128)(2,1)S(1)}, bf16[80,512]{1,0:T(8,128)(2,1)S(1)}, u32[]{:S(2)}, u32[]{:S(2)}) collective-permute-start(bf16[80,512]{1,0:T(8,128)(2,1)S(1)} %shard_map.93.after_ref.own_ref), channel_id=1, source_target_pairs={{0,16},{8,24},{16,32},{24,40},{32,48},{40,56},{48,0},{56,8},{64,80... | collective-permute-start | bytes 245768 | tf_op jit(solution)/shard_map/ppermute | solution.py:464
  7.7 6.5 %collective-permute-start.2 = (bf16[80,512]{1,0:T(8,128)(2,1)S(1)}, bf16[80,512]{1,0:T(8,128)(2,1)S(1)}, u32[]{:S(2)}, u32[]{:S(2)}) collective-permute-start(bf16[80,512]{1,0:T(8,128)(2,1)S(1)} %shard_map.93.after_ref.own_ref), channel_id=1, source_target_pairs={{0,32},{8,40},{16,48},{24,56},{32,0},{40,8},{48,16},{56,24},{64,96... | collective-permute-start | bytes 245768 | tf_op jit(solution)/shard_map/ppermute | solution.py:464
  10.2 4.4 %collective-permute-start.3 = (bf16[80,512]{1,0:T(8,128)(2,1)S(1)}, bf16[80,512]{1,0:T(8,128)(2,1)S(1)}, u32[]{:S(2)}, u32[]{:S(2)}) collective-permute-start(bf16[80,512]{1,0:T(8,128)(2,1)S(1)} %shard_map.93.after_ref.own_ref), channel_id=1, source_target_pairs={{0,48},{8,56},{16,0},{24,8},{32,16},{40,24},{48,32},{56,40},{64,11... | collective-permute-start | bytes 245768 | tf_op jit(solution)/shard_map/ppermute | solution.py:464
  14.7 5.7 %collective-permute-start.4 = (f32[40,512]{1,0:T(8,128)S(1)}, f32[40,512]{1,0:T(8,128)S(1)}, u32[]{:S(2)}, u32[]{:S(2)}) collective-permute-start(f32[40,512]{1,0:T(8,128)S(1)} %get-tuple-element.37.after_ref), channel_id=1, source_target_pairs={{0,64},{8,72},{16,80},{24,88},{32,96},{40,104},{48,112},{56,120},{... | collective-permute-start | bytes 245768 | tf_op jit(solution)/shard_map/ppermute | solution.py:464
  15.7 4.8 %collective-permute-start.5 = (f32[40,512]{1,0:T(8,128)S(1)}, f32[40,512]{1,0:T(8,128)S(1)}, u32[]{:S(2)}, u32[]{:S(2)}) collective-permute-start(f32[40,512]{1,0:T(8,128)S(1)} %get-tuple-element.37.after_ref), channel_id=1, source_target_pairs={{0,128},{8,136},{16,144},{24,152},{32,160},{40,168},{48,176},{56,1... | collective-permute-start | bytes 245768 | tf_op jit(solution)/shard_map/ppermute | solution.py:464
  17.8 10.4 %collective-permute-start.13 = (bf16[256,512]{1,0:T(8,128)(2,1)S(1)}, bf16[256,512]{1,0:T(8,128)(2,1)S(1)}, u32[]{:S(2)}, u32[]{:S(2)}) collective-permute-start(bf16[256,512]{1,0:T(8,128)(2,1)S(1)} %shard_map.98.both_ref), channel_id=1, source_target_pairs={{0,32},{8,40},{16,48},{24,56},{32,0},{40,8},{48,16},{56,24},{64,96... | collective-permute-start | bytes 786440 | tf_op jit(solution)/shard_map/ppermute | solution.py:470
  22.4 9.9 %collective-permute-start.6 = (bf16[32,4096]{1,0:T(8,128)(2,1)S(1)}, bf16[32,4096]{1,0:T(8,128)(2,1)S(1)}, u32[]{:S(2)}, u32[]{:S(2)}) collective-permute-start(bf16[32,4096]{1,0:T(8,128)(2,1)S(1)} %shard_map.97.after_ref.here), channel_id=1, source_target_pairs={{0,1},{1,2},{2,3},{3,4},{4,5},{5,6},{6,7},{7,0},{8,9},{9,10},{10,1... | collective-permute-start | bytes 786440 | tf_op jit(solution)/shard_map/ppermute | solution.py:474
  24.1 8.2 %collective-permute-start.7 = (bf16[32,4096]{1,0:T(8,128)(2,1)S(1)}, bf16[32,4096]{1,0:T(8,128)(2,1)S(1)}, u32[]{:S(2)}, u32[]{:S(2)}) collective-permute-start(bf16[32,4096]{1,0:T(8,128)(2,1)S(1)} %shard_map.97.after_ref.here), channel_id=1, source_target_pairs={{0,7},{1,0},{2,1},{3,2},{4,3},{5,4},{6,5},{7,6},{8,15},{9,8},{10,9... | collective-permute-start | bytes 786440 | tf_op jit(solution)/shard_map/ppermute | solution.py:474
  28.2 6.8 %collective-permute-start.14 = (bf16[256,512]{1,0:T(8,128)(2,1)S(1)}, bf16[256,512]{1,0:T(8,128)(2,1)S(1)}, u32[]{:S(2)}, u32[]{:S(2)}) collective-permute-start(bf16[256,512]{1,0:T(8,128)(2,1)S(1)} %get-tuple-element.38.even_ref), channel_id=1, source_target_pairs={{0,128},{8,136},{16,144},{24,152},{32,160},{40,168},{48,176},{56,1... | collective-permute-start | bytes 786440 | tf_op jit(solution)/shard_map/ppermute | solution.py:470
  30.4 5.5 %collective-permute-start.15 = (bf16[256,512]{1,0:T(8,128)(2,1)S(1)}, bf16[256,512]{1,0:T(8,128)(2,1)S(1)}, u32[]{:S(2)}, u32[]{:S(2)}) collective-permute-start(bf16[256,512]{1,0:T(8,128)(2,1)S(1)} %get-tuple-element.39.odd_ref), channel_id=1, source_target_pairs={{0,16},{8,24},{16,0},{24,8},{32,48},{40,56},{48,32},{56,40},{64,80... | collective-permute-start | bytes 786440 | tf_op jit(solution)/shard_map/ppermute | solution.py:470
  32.3 6.4 %collective-permute-start.8 = (bf16[32,4096]{1,0:T(8,128)(2,1)S(1)}, bf16[32,4096]{1,0:T(8,128)(2,1)S(1)}, u32[]{:S(2)}, u32[]{:S(2)}) collective-permute-start(bf16[32,4096]{1,0:T(8,128)(2,1)S(1)} %collective-permute-done.6.after_up.up1), channel_id=1, source_target_pairs={{0,1},{1,2},{2,3},{3,4},{4,5},{5,6},{6,7},{7,0},{8,9},{9,10},{10,1... | collective-permute-start | bytes 786440 | tf_op jit(solution)/shard_map/ppermute | solution.py:474
  32.3 6.4 %collective-permute-start.9 = (bf16[32,4096]{1,0:T(8,128)(2,1)S(1)}, bf16[32,4096]{1,0:T(8,128)(2,1)S(1)}, u32[]{:S(2)}, u32[]{:S(2)}) collective-permute-start(bf16[32,4096]{1,0:T(8,128)(2,1)S(1)} %collective-permute-done.7.after_down.down1), channel_id=1, source_target_pairs={{0,7},{1,0},{2,1},{3,2},{4,3},{5,4},{6,5},{7,6},{8,15},{9,8},{10,9... | collective-permute-start | bytes 786440 | tf_op jit(solution)/shard_map/ppermute | solution.py:474
  36.1 12.9 %collective-permute-start.16 = (bf16[512,512]{1,0:T(8,128)(2,1)S(1)}, bf16[512,512]{1,0:T(8,128)(2,1)S(1)}, u32[]{:S(2)}, u32[]{:S(2)}) collective-permute-start(bf16[512,512]{1,0:T(8,128)(2,1)S(1)} %get-tuple-element.41), channel_id=1, source_target_pairs={{0,16},{8,24},{16,0},{24,8},{32,48},{40,56},{48,32},{56,40},{64,80... | collective-permute-start | bytes 1572872 | tf_op jit(solution)/shard_map/ppermute | solution.py:470
  36.7 12.3 %collective-permute-start.17 = (bf16[512,512]{1,0:T(8,128)(2,1)S(1)}, bf16[512,512]{1,0:T(8,128)(2,1)S(1)}, u32[]{:S(2)}, u32[]{:S(2)}) collective-permute-start(bf16[512,512]{1,0:T(8,128)(2,1)S(1)} %get-tuple-element.42), channel_id=1, source_target_pairs={{0,128},{8,136},{16,144},{24,152},{32,160},{40,168},{48,176},{56,1... | collective-permute-start | bytes 1572872 | tf_op jit(solution)/shard_map/ppermute | solution.py:470
  38.8 7.4 %collective-permute-start.10 = (bf16[32,4096]{1,0:T(8,128)(2,1)S(1)}, bf16[32,4096]{1,0:T(8,128)(2,1)S(1)}, u32[]{:S(2)}, u32[]{:S(2)}) collective-permute-start(bf16[32,4096]{1,0:T(8,128)(2,1)S(1)} %collective-permute-done.8.up2), channel_id=1, source_target_pairs={{0,1},{1,2},{2,3},{3,4},{4,5},{5,6},{6,7},{7,0},{8,9},{9,10},{10,1... | collective-permute-start | bytes 786440 | tf_op jit(solution)/shard_map/ppermute | solution.py:474
  38.8 7.5 %collective-permute-start.11 = (bf16[32,4096]{1,0:T(8,128)(2,1)S(1)}, bf16[32,4096]{1,0:T(8,128)(2,1)S(1)}, u32[]{:S(2)}, u32[]{:S(2)}) collective-permute-start(bf16[32,4096]{1,0:T(8,128)(2,1)S(1)} %collective-permute-done.9.down2), channel_id=1, source_target_pairs={{0,7},{1,0},{2,1},{3,2},{4,3},{5,4},{6,5},{7,6},{8,15},{9,8},{10,9... | collective-permute-start | bytes 786440 | tf_op jit(solution)/shard_map/ppermute | solution.py:474
  41.4 12.6 %collective-permute-start.18 = (bf16[1024,512]{1,0:T(8,128)(2,1)S(1)}, bf16[1024,512]{1,0:T(8,128)(2,1)S(1)}, u32[]{:S(2)}, u32[]{:S(2)}) collective-permute-start(bf16[1024,512]{1,0:T(8,128)(2,1)S(1)} %get-tuple-element.40.near_own), channel_id=1, source_target_pairs={{0,8},{8,0},{16,24},{24,16},{32,40},{40,32},{48,56},{56,48},{64,72... | collective-permute-start | bytes 3145736 | tf_op jit(solution)/shard_map/ppermute | solution.py:464
  46.2 9.5 %collective-permute-start.19 = (bf16[16,4096]{1,0:T(8,128)(2,1)S(1)}, bf16[16,4096]{1,0:T(8,128)(2,1)S(1)}, u32[]{:S(2)}, u32[]{:S(2)}) collective-permute-start(bf16[16,4096]{1,0:T(8,128)(2,1)S(1)} %slice.8), channel_id=1, source_target_pairs={{0,1},{1,2},{2,3},{3,4},{4,5},{5,6},{6,7},{7,0},{8,9},{9,10},{10,1... | collective-permute-start | bytes 393224 | tf_op jit(solution)/shard_map/ppermute | solution.py:474
  46.3 9.4 %collective-permute-start.20 = (bf16[16,4096]{1,0:T(8,128)(2,1)S(1)}, bf16[16,4096]{1,0:T(8,128)(2,1)S(1)}, u32[]{:S(2)}, u32[]{:S(2)}) collective-permute-start(bf16[16,4096]{1,0:T(8,128)(2,1)S(1)} %slice.9), channel_id=1, source_target_pairs={{0,7},{1,0},{2,1},{3,2},{4,3},{5,4},{6,5},{7,6},{8,15},{9,8},{10,9... | collective-permute-start | bytes 393224 | tf_op jit(solution)/shard_map/ppermute | solution.py:474
  49.1 7.2 %collective-permute-start.21 = (bf16[1024,512]{1,0:T(8,128)(2,1)S(1)}, bf16[1024,512]{1,0:T(8,128)(2,1)S(1)}, u32[]{:S(2)}, u32[]{:S(2)}) collective-permute-start(bf16[1024,512]{1,0:T(8,128)(2,1)S(1)} %shard_map.101.far_own.own_ref), channel_id=1, source_target_pairs={{0,8},{8,0},{16,24},{24,16},{32,40},{40,32},{48,56},{56,48},{64,72... | collective-permute-start | bytes 3145736 | tf_op jit(solution)/shard_map/ppermute | solution.py:464
  (6 other events, 20.1 us)

commit v10 on v9

--- a/solution.py
+++ b/solution.py
@@ -85,7 +85,7 @@
 def fill_signal(key_ref, value_ref, sig):
     for g in range(GROUPS):
         lanes = slice(g * LANES, (g + 1) * LANES)
-        sig[g] = key_ref[:, lanes].astype(F32) * value_ref[:, lanes].astype(F32)
+        sig[g, :TOK, :] = key_ref[:, lanes].astype(F32) * value_ref[:, lanes].astype(F32)
 
 
 def block_iota():
@@ -373,7 +373,7 @@
         group(g, 0)
     for g in range(GROUPS):
         lanes = slice(g * LANES, (g + 1) * LANES)
-        gated = (query_ref[:, lanes].astype(F32) * conv[g]).astype(BF16)
+        gated = (query_ref[:, lanes].astype(F32) * conv[g, :TOK, :]).astype(BF16)
         for q in range(FOLD):
             hidden_ref[:, q * CH + g * LANES:q * CH + (g + 1) * LANES] = gated[q * THIN:(q + 1) * THIN]
 
@@ -477,8 +477,8 @@
 def shards(query, key, value, decay, freq, residue, skip, out_weight, doc_starts):
     starts = doc_starts.reshape(TOK // LANES, LANES)
     skip = skip.reshape(1, CH)
-    sig = pltpu.VMEM((GROUPS, TOK, LANES), F32)
-    qs = pltpu.VMEM((GROUPS, BLOCKS * MODES, LANES), F32)
+    sig = pltpu.VMEM((GROUPS, TOK + STEPS, LANES), F32)
+    qs = pltpu.VMEM((GROUPS, (BLOCKS + 1) * MODES, LANES), F32)
     state_shape = struct(ROWS, CH)
     pay_shape = struct(PAY, CH)
     block_shape = struct(GROUPS, ROWS, BLOCKS, LANES)
@@ -489,7 +489,7 @@
         powers_kernel, (struct(*table), struct(*table), state_shape),
         (magnitude * jnp.cos(freq), magnitude * jnp.sin(freq)), (), 300_000_000, 5_000_000)
     pay, eb, signal = call(
-        ends_kernel, (pay_shape, struct(GROUPS, ROWS * BLOCKS, LANES), struct(GROUPS, TOK, LANES)),
+        ends_kernel, (pay_shape, struct(GROUPS, (ROWS + 1) * BLOCKS, LANES), struct(GROUPS, TOK + STEPS, LANES)),
         (key, value, starts, tre, tim), (), 20_000_000, 5_000_000)
     other = move(pay, 0, 0, 1)
     chip = call(chip_kernel, struct(SENT, CH, dtype=BF16), (pay, other, p256))

time: 58.6 us -> 58.6 us (level)
  no operation moved by 1% of the time
where the time goes in v10:
time: 58.6 us; the launch traced here: 57.6 us
  starting transfers between devices  40.2 us (69%)
  Pallas kernels  10.1 us (17%)
  waiting for transfers between devices  5.84 us (10%)
  other arithmetic  0.97 us (2%)
    ppermute x8, starting transfers between devices, move(): return lax.ppermute(value, 'ctx', pairs)  19.6 us
    ppermute x8, starting transfers between devices, turn(): return lax.ppermute(value, 'tp', [(i, (i + k) % NZ) for i in range(NZ)])  13.9 us
    pallas_call x14, Pallas kernels, call(): pl.pallas_call(kernel, out_shape=outs, in_specs=[VMEM] * len(args), out_s...  10.1 us
    ppermute x6, starting transfers between devices, trade(): return lax.ppermute(value, 'ctx', pairs)  6.64 us
    ppermute x8, waiting for transfers between devices, move(): return lax.ppermute(value, 'ctx', pairs)  2.72 us
    ppermute x8, waiting for transfers between devices, turn(): return lax.ppermute(value, 'tp', [(i, (i + k) % NZ) for i in range(NZ)])  2.16 us
  transfers between devices with their start and end apart: 22, of which 7 were waited for; matrix products, arithmetic and copies ran while one was open for 0% of the time, Pallas kernels for 11%

profile of v10, /device:TPU:1, one launch (start us, length us, event | category | flops | bytes accessed | tf_op | source)
XLA Modules:
  0.0 57.6 jit_solution(13135360256603240570)
XLA Ops:
  0.0 1.0 %sine_multiply_fusion = (f32[16,512]{1,0:T(8,128)S(1)}, f32[16,512]{1,0:T(8,128)S(1)}) fusion(f32[16,512]{1,0:T(8,128)} %param.13, f32[16,512]{1,0:T(8,128)} %decay_ref.1), kind=kLoop, calls=%fused_computation | loop fusion | flops 24576 | bytes 131072 | tf_op jit(solution)/shard_map/mul | solution.py:490
  1.4 2.0 %shard_map.92 = (f32[40,512]{1,0:T(8,128)S(1)}, f32[4,264,128]{2,1,0:T(8,128)S(1)}, f32[4,288,128]{2,1,0:T(8,128)S(1)}) custom-call(bf16[256,512]{1,0:T(8,128)(2,1)S(1)} %copy-done, bf16[256,512]{1,0:T(8,128)(2,1)S(1)} %copy-done.1, s32[2,128]{1,0:T(2,128)S(1)} %bitcast.2, f32[4,528,128]{2,1,0:T(8,128)S(1)} %get-tuple-element.25.tre, ...), custom_call_target="tpu_custom_call" | custom-call | flops 20000000 | bytes 5000000 | tf_op jit(solution)/shard_map/pallas_call | solution.py:29
  3.3 3.3 %collective-permute-start = (f32[40,512]{1,0:T(8,128)S(1)}, f32[40,512]{1,0:T(8,128)S(1)}, u32[]{:S(2)}, u32[]{:S(2)}) collective-permute-start(f32[40,512]{1,0:T(8,128)S(1)} %get-tuple-element.28.own_ref), channel_id=1, source_target_pairs={{0,8},{8,0},{16,24},{24,16},{32,40},{40,32},{48,56},{56,48},{64,72... | collective-permute-start | bytes 245768 | tf_op jit(solution)/shard_map/ppermute | solution.py:464
  6.6 0.9 %collective-permute-done.other_ref = f32[40,512]{1,0:T(8,128)S(1)} collective-permute-done((f32[40,512]{1,0:T(8,128)S(1)}, f32[40,512]{1,0:T(8,128)S(1)}, u32[]{:S(2)}, u32[]{:S(2)}) %collective-permute-start) | collective-permute-done | bytes 81952 | tf_op jit(solution)/shard_map/ppermute | solution.py:464
  7.7 2.5 %collective-permute-start.2 = (bf16[80,512]{1,0:T(8,128)(2,1)S(1)}, bf16[80,512]{1,0:T(8,128)(2,1)S(1)}, u32[]{:S(2)}, u32[]{:S(2)}) collective-permute-start(bf16[80,512]{1,0:T(8,128)(2,1)S(1)} %shard_map.93.after_ref.own_ref), channel_id=1, source_target_pairs={{0,32},{8,40},{16,48},{24,56},{32,0},{40,8},{48,16},{56,24},{64,96... | collective-permute-start | bytes 245768 | tf_op jit(solution)/shard_map/ppermute | solution.py:464
  10.2 1.1 %collective-permute-start.3 = (bf16[80,512]{1,0:T(8,128)(2,1)S(1)}, bf16[80,512]{1,0:T(8,128)(2,1)S(1)}, u32[]{:S(2)}, u32[]{:S(2)}) collective-permute-start(bf16[80,512]{1,0:T(8,128)(2,1)S(1)} %shard_map.93.after_ref.own_ref), channel_id=1, source_target_pairs={{0,48},{8,56},{16,0},{24,8},{32,16},{40,24},{48,32},{56,40},{64,11... | collective-permute-start | bytes 245768 | tf_op jit(solution)/shard_map/ppermute | solution.py:464
  11.3 2.1 %shard_map.94 = (f32[4,32,8,128]{3,2,1,0:T(8,128)S(1)}, f32[32,512]{1,0:T(8,128)S(1)}) custom-call(f32[4,288,128]{2,1,0:T(8,128)S(1)} %get-tuple-element.27.sig, f32[4,528,128]{2,1,0:T(8,128)S(1)} %get-tuple-element.25.tre, f32[4,528,128]{2,1,0:T(8,128)S(1)} %get-tuple-element.26.tim, f32[16,512]{1,0:T(8,128)S(1)} %copy-done.2, f32[2,16,512]{2,1,0:T(8,128)S(1)} %copy-done.4, ...), custom_call_target="tpu_custom_call" | custom-call | flops 30000000 | bytes 5000000 | tf_op jit(solution)/shard_map/pallas_call | solution.py:29
  14.7 1.0 %collective-permute-start.4 = (f32[40,512]{1,0:T(8,128)S(1)}, f32[40,512]{1,0:T(8,128)S(1)}, u32[]{:S(2)}, u32[]{:S(2)}) collective-permute-start(f32[40,512]{1,0:T(8,128)S(1)} %get-tuple-element.37.after_ref), channel_id=1, source_target_pairs={{0,64},{8,72},{16,80},{24,88},{32,96},{40,104},{48,112},{56,120},{... | collective-permute-start | bytes 245768 | tf_op jit(solution)/shard_map/ppermute | solution.py:464
  15.7 2.0 %collective-permute-start.5 = (f32[40,512]{1,0:T(8,128)S(1)}, f32[40,512]{1,0:T(8,128)S(1)}, u32[]{:S(2)}, u32[]{:S(2)}) collective-permute-start(f32[40,512]{1,0:T(8,128)S(1)} %get-tuple-element.37.after_ref), channel_id=1, source_target_pairs={{0,128},{8,136},{16,144},{24,152},{32,160},{40,168},{48,176},{56,1... | collective-permute-start | bytes 245768 | tf_op jit(solution)/shard_map/ppermute | solution.py:464
  17.8 2.0 %collective-permute-start.13 = (bf16[256,512]{1,0:T(8,128)(2,1)S(1)}, bf16[256,512]{1,0:T(8,128)(2,1)S(1)}, u32[]{:S(2)}, u32[]{:S(2)}) collective-permute-start(bf16[256,512]{1,0:T(8,128)(2,1)S(1)} %shard_map.98.both_ref), channel_id=1, source_target_pairs={{0,32},{8,40},{16,48},{24,56},{32,0},{40,8},{48,16},{56,24},{64,96... | collective-permute-start | bytes 786440 | tf_op jit(solution)/shard_map/ppermute | solution.py:470
  20.7 1.7 %shard_map.97.after_ref.here = bf16[32,4096]{1,0:T(8,128)(2,1)S(1)} custom-call(bf16[256,512]{1,0:T(8,128)(2,1)S(1)} %copy-done.7, f32[4,32,8,128]{3,2,1,0:T(8,128)S(1)} %get-tuple-element.30.y_ref, f32[4,32,8,128]{3,2,1,0:T(8,128)S(1)} %get-tuple-element.33.pz_ref, f32[4,32,8,128]{3,2,1,0:T(8,128)S(1)} %get-tuple-element.34.gz_ref, ...), custom_call_target="tpu_custom_call" | custom-call | flops 2000000000 | bytes 5000000 | tf_op jit(solution)/shard_map/pallas_call | solution.py:29
  22.4 1.7 %collective-permute-start.6 = (bf16[32,4096]{1,0:T(8,128)(2,1)S(1)}, bf16[32,4096]{1,0:T(8,128)(2,1)S(1)}, u32[]{:S(2)}, u32[]{:S(2)}) collective-permute-start(bf16[32,4096]{1,0:T(8,128)(2,1)S(1)} %shard_map.97.after_ref.here), channel_id=1, source_target_pairs={{0,1},{1,2},{2,3},{3,4},{4,5},{5,6},{6,7},{7,0},{8,9},{9,10},{10,1... | collective-permute-start | bytes 786440 | tf_op jit(solution)/shard_map/ppermute | solution.py:474
  24.1 4.0 %collective-permute-start.7 = (bf16[32,4096]{1,0:T(8,128)(2,1)S(1)}, bf16[32,4096]{1,0:T(8,128)(2,1)S(1)}, u32[]{:S(2)}, u32[]{:S(2)}) collective-permute-start(bf16[32,4096]{1,0:T(8,128)(2,1)S(1)} %shard_map.97.after_ref.here), channel_id=1, source_target_pairs={{0,7},{1,0},{2,1},{3,2},{4,3},{5,4},{6,5},{7,6},{8,15},{9,8},{10,9... | collective-permute-start | bytes 786440 | tf_op jit(solution)/shard_map/ppermute | solution.py:474
  28.2 2.2 %collective-permute-start.14 = (bf16[256,512]{1,0:T(8,128)(2,1)S(1)}, bf16[256,512]{1,0:T(8,128)(2,1)S(1)}, u32[]{:S(2)}, u32[]{:S(2)}) collective-permute-start(bf16[256,512]{1,0:T(8,128)(2,1)S(1)} %get-tuple-element.38.even_ref), channel_id=1, source_target_pairs={{0,128},{8,136},{16,144},{24,152},{32,160},{40,168},{48,176},{56,1... | collective-permute-start | bytes 786440 | tf_op jit(solution)/shard_map/ppermute | solution.py:470
  31.0 1.3 %collective-permute-done.6.after_up.up1 = bf16[32,4096]{1,0:T(8,128)(2,1)S(1)} collective-permute-done((bf16[32,4096]{1,0:T(8,128)(2,1)S(1)}, bf16[32,4096]{1,0:T(8,128)(2,1)S(1)}, u32[]{:S(2)}, u32[]{:S(2)}) %collective-permute-start.6) | collective-permute-done | bytes 262176 | tf_op jit(solution)/shard_map/ppermute | solution.py:474
  32.3 2.7 %collective-permute-start.9 = (bf16[32,4096]{1,0:T(8,128)(2,1)S(1)}, bf16[32,4096]{1,0:T(8,128)(2,1)S(1)}, u32[]{:S(2)}, u32[]{:S(2)}) collective-permute-start(bf16[32,4096]{1,0:T(8,128)(2,1)S(1)} %collective-permute-done.7.after_down.down1), channel_id=1, source_target_pairs={{0,7},{1,0},{2,1},{3,2},{4,3},{5,4},{6,5},{7,6},{8,15},{9,8},{10,9... | collective-permute-start | bytes 786440 | tf_op jit(solution)/shard_map/ppermute | solution.py:474
  35.0 0.9 %collective-permute-done.15.odd_y = bf16[256,512]{1,0:T(8,128)(2,1)S(1)} collective-permute-done((bf16[256,512]{1,0:T(8,128)(2,1)S(1)}, bf16[256,512]{1,0:T(8,128)(2,1)S(1)}, u32[]{:S(2)}, u32[]{:S(2)}) %collective-permute-start.15) | collective-permute-done | bytes 262176 | tf_op jit(solution)/shard_map/ppermute | solution.py:470
  36.7 1.2 %collective-permute-start.17 = (bf16[512,512]{1,0:T(8,128)(2,1)S(1)}, bf16[512,512]{1,0:T(8,128)(2,1)S(1)}, u32[]{:S(2)}, u32[]{:S(2)}) collective-permute-start(bf16[512,512]{1,0:T(8,128)(2,1)S(1)} %get-tuple-element.42), channel_id=1, source_target_pairs={{0,128},{8,136},{16,144},{24,152},{32,160},{40,168},{48,176},{56,1... | collective-permute-start | bytes 1572872 | tf_op jit(solution)/shard_map/ppermute | solution.py:470
  38.8 2.7 %collective-permute-start.11 = (bf16[32,4096]{1,0:T(8,128)(2,1)S(1)}, bf16[32,4096]{1,0:T(8,128)(2,1)S(1)}, u32[]{:S(2)}, u32[]{:S(2)}) collective-permute-start(bf16[32,4096]{1,0:T(8,128)(2,1)S(1)} %collective-permute-done.9.down2), channel_id=1, source_target_pairs={{0,7},{1,0},{2,1},{3,2},{4,3},{5,4},{6,5},{7,6},{8,15},{9,8},{10,9... | collective-permute-start | bytes 786440 | tf_op jit(solution)/shard_map/ppermute | solution.py:474
  41.4 4.7 %collective-permute-start.18 = (bf16[1024,512]{1,0:T(8,128)(2,1)S(1)}, bf16[1024,512]{1,0:T(8,128)(2,1)S(1)}, u32[]{:S(2)}, u32[]{:S(2)}) collective-permute-start(bf16[1024,512]{1,0:T(8,128)(2,1)S(1)} %get-tuple-element.40.near_own), channel_id=1, source_target_pairs={{0,8},{8,0},{16,24},{24,16},{32,40},{40,32},{48,56},{56,48},{64,72... | collective-permute-start | bytes 3145736 | tf_op jit(solution)/shard_map/ppermute | solution.py:464
  46.3 2.7 %collective-permute-start.20 = (bf16[16,4096]{1,0:T(8,128)(2,1)S(1)}, bf16[16,4096]{1,0:T(8,128)(2,1)S(1)}, u32[]{:S(2)}, u32[]{:S(2)}) collective-permute-start(bf16[16,4096]{1,0:T(8,128)(2,1)S(1)} %slice.9), channel_id=1, source_target_pairs={{0,7},{1,0},{2,1},{3,2},{4,3},{5,4},{6,5},{7,6},{8,15},{9,8},{10,9... | collective-permute-start | bytes 393224 | tf_op jit(solution)/shard_map/ppermute | solution.py:474
  49.1 5.0 %collective-permute-start.21 = (bf16[1024,512]{1,0:T(8,128)(2,1)S(1)}, bf16[1024,512]{1,0:T(8,128)(2,1)S(1)}, u32[]{:S(2)}, u32[]{:S(2)}) collective-permute-start(bf16[1024,512]{1,0:T(8,128)(2,1)S(1)} %shard_map.101.far_own.own_ref), channel_id=1, source_target_pairs={{0,8},{8,0},{16,24},{24,16},{32,40},{40,32},{48,56},{56,48},{64,72... | collective-permute-start | bytes 3145736 | tf_op jit(solution)/shard_map/ppermute | solution.py:464
  54.1 1.6 %shard_map.102 = (f32[256,512]{1,0:T(8,128)S(1)}, bf16[256,1024]{1,0:T(8,128)(2,1)S(1)}) custom-call(bf16[32,4096]{1,0:T(8,128)(2,1)S(1)} %shard_map.97.after_ref.here, bf16[32,4096]{1,0:T(8,128)(2,1)S(1)} %collective-permute-done.6.after_up.up1, bf16[32,4096]{1,0:T(8,128)(2,1)S(1)} %collective-permute-done.7.after_down.down1, ...), custom_call_target="tpu_custom_call" | custom-call | flops 8000000000 | bytes 7000000 | tf_op jit(solution)/shard_map/pallas_call | solution.py:29
  56.4 1.3 %shard_map.104 = bf16[256,512]{1,0:T(8,128)(2,1)} custom-call(f32[256,512]{1,0:T(8,128)S(1)} %get-tuple-element.43.after_ref.total_ref, bf16[256,1024]{1,0:T(8,128)(2,1)S(1)} %get-tuple-element.44.left, bf16[256,512]{1,0:T(8,128)(2,1)S(1)} %shard_map.103.last, bf16[1024,512]{1,0:T(8,128)(2,1)S(1)} %get-tuple-element.40.near_own, ...), custom_call_target="tpu_custom_call" | custom-call | flops 536870912 | bytes 7000000 | tf_op jit(solution)/shard_map/pallas_call | solution.py:29
  (53 shorter events, 5.8 us)
Async XLA Ops:
  1.3 10.0 %copy-start.2 = (f32[16,512]{1,0:T(8,128)S(1)}, f32[16,512]{1,0:T(8,128)}, u32[]{:S(2)}) copy-start(f32[16,512]{1,0:T(8,128)} %decay_ref.1) | copy-start | bytes 98308
  1.3 10.0 %copy-start.4 = (f32[2,16,512]{2,1,0:T(8,128)S(1)}, f32[2,16,512]{2,1,0:T(8,128)}, u32[]{:S(2)}) copy-start(f32[2,16,512]{2,1,0:T(8,128)} %res_ref.1) | copy-start | bytes 196612
  3.3 4.2 %collective-permute-start = (f32[40,512]{1,0:T(8,128)S(1)}, f32[40,512]{1,0:T(8,128)S(1)}, u32[]{:S(2)}, u32[]{:S(2)}) collective-permute-start(f32[40,512]{1,0:T(8,128)S(1)} %get-tuple-element.28.own_ref), channel_id=1, source_target_pairs={{0,8},{8,0},{16,24},{24,16},{32,40},{40,32},{48,56},{56,48},{64,72... | collective-permute-start | bytes 245768 | tf_op jit(solution)/shard_map/ppermute | solution.py:464
  6.6 11.1 %collective-permute-start.12 = (bf16[128,512]{1,0:T(8,128)(2,1)S(1)}, bf16[128,512]{1,0:T(8,128)(2,1)S(1)}, u32[]{:S(2)}, u32[]{:S(2)}) collective-permute-start(bf16[128,512]{1,0:T(8,128)(2,1)S(1)} %copy-done.3), channel_id=1, source_target_pairs={{0,64},{8,72},{16,80},{24,88},{32,96},{40,104},{48,112},{56,120},{... | collective-permute-start | bytes 393224 | tf_op jit(solution)/shard_map/ppermute | solution.py:470
  7.6 5.8 %collective-permute-start.1 = (bf16[80,512]{1,0:T(8,128)(2,1)S(1)}, bf16[80,512]{1,0:T(8,128)(2,1)S(1)}, u32[]{:S(2)}, u32[]{:S(2)}) collective-permute-start(bf16[80,512]{1,0:T(8,128)(2,1)S(1)} %shard_map.93.after_ref.own_ref), channel_id=1, source_target_pairs={{0,16},{8,24},{16,32},{24,40},{32,48},{40,56},{48,0},{56,8},{64,80... | collective-permute-start | bytes 245768 | tf_op jit(solution)/shard_map/ppermute | solution.py:464
  7.7 6.5 %collective-permute-start.2 = (bf16[80,512]{1,0:T(8,128)(2,1)S(1)}, bf16[80,512]{1,0:T(8,128)(2,1)S(1)}, u32[]{:S(2)}, u32[]{:S(2)}) collective-permute-start(bf16[80,512]{1,0:T(8,128)(2,1)S(1)} %shard_map.93.after_ref.own_ref), channel_id=1, source_target_pairs={{0,32},{8,40},{16,48},{24,56},{32,0},{40,8},{48,16},{56,24},{64,96... | collective-permute-start | bytes 245768 | tf_op jit(solution)/shard_map/ppermute | solution.py:464
  10.2 4.4 %collective-permute-start.3 = (bf16[80,512]{1,0:T(8,128)(2,1)S(1)}, bf16[80,512]{1,0:T(8,128)(2,1)S(1)}, u32[]{:S(2)}, u32[]{:S(2)}) collective-permute-start(bf16[80,512]{1,0:T(8,128)(2,1)S(1)} %shard_map.93.after_ref.own_ref), channel_id=1, source_target_pairs={{0,48},{8,56},{16,0},{24,8},{32,16},{40,24},{48,32},{56,40},{64,11... | collective-permute-start | bytes 245768 | tf_op jit(solution)/shard_map/ppermute | solution.py:464
  14.7 5.8 %collective-permute-start.4 = (f32[40,512]{1,0:T(8,128)S(1)}, f32[40,512]{1,0:T(8,128)S(1)}, u32[]{:S(2)}, u32[]{:S(2)}) collective-permute-start(f32[40,512]{1,0:T(8,128)S(1)} %get-tuple-element.37.after_ref), channel_id=1, source_target_pairs={{0,64},{8,72},{16,80},{24,88},{32,96},{40,104},{48,112},{56,120},{... | collective-permute-start | bytes 245768 | tf_op jit(solution)/shard_map/ppermute | solution.py:464
  15.7 4.8 %collective-permute-start.5 = (f32[40,512]{1,0:T(8,128)S(1)}, f32[40,512]{1,0:T(8,128)S(1)}, u32[]{:S(2)}, u32[]{:S(2)}) collective-permute-start(f32[40,512]{1,0:T(8,128)S(1)} %get-tuple-element.37.after_ref), channel_id=1, source_target_pairs={{0,128},{8,136},{16,144},{24,152},{32,160},{40,168},{48,176},{56,1... | collective-permute-start | bytes 245768 | tf_op jit(solution)/shard_map/ppermute | solution.py:464
  17.8 10.4 %collective-permute-start.13 = (bf16[256,512]{1,0:T(8,128)(2,1)S(1)}, bf16[256,512]{1,0:T(8,128)(2,1)S(1)}, u32[]{:S(2)}, u32[]{:S(2)}) collective-permute-start(bf16[256,512]{1,0:T(8,128)(2,1)S(1)} %shard_map.98.both_ref), channel_id=1, source_target_pairs={{0,32},{8,40},{16,48},{24,56},{32,0},{40,8},{48,16},{56,24},{64,96... | collective-permute-start | bytes 786440 | tf_op jit(solution)/shard_map/ppermute | solution.py:470
  22.4 9.9 %collective-permute-start.6 = (bf16[32,4096]{1,0:T(8,128)(2,1)S(1)}, bf16[32,4096]{1,0:T(8,128)(2,1)S(1)}, u32[]{:S(2)}, u32[]{:S(2)}) collective-permute-start(bf16[32,4096]{1,0:T(8,128)(2,1)S(1)} %shard_map.97.after_ref.here), channel_id=1, source_target_pairs={{0,1},{1,2},{2,3},{3,4},{4,5},{5,6},{6,7},{7,0},{8,9},{9,10},{10,1... | collective-permute-start | bytes 786440 | tf_op jit(solution)/shard_map/ppermute | solution.py:474
  24.1 8.2 %collective-permute-start.7 = (bf16[32,4096]{1,0:T(8,128)(2,1)S(1)}, bf16[32,4096]{1,0:T(8,128)(2,1)S(1)}, u32[]{:S(2)}, u32[]{:S(2)}) collective-permute-start(bf16[32,4096]{1,0:T(8,128)(2,1)S(1)} %shard_map.97.after_ref.here), channel_id=1, source_target_pairs={{0,7},{1,0},{2,1},{3,2},{4,3},{5,4},{6,5},{7,6},{8,15},{9,8},{10,9... | collective-permute-start | bytes 786440 | tf_op jit(solution)/shard_map/ppermute | solution.py:474
  28.2 6.8 %collective-permute-start.14 = (bf16[256,512]{1,0:T(8,128)(2,1)S(1)}, bf16[256,512]{1,0:T(8,128)(2,1)S(1)}, u32[]{:S(2)}, u32[]{:S(2)}) collective-permute-start(bf16[256,512]{1,0:T(8,128)(2,1)S(1)} %get-tuple-element.38.even_ref), channel_id=1, source_target_pairs={{0,128},{8,136},{16,144},{24,152},{32,160},{40,168},{48,176},{56,1... | collective-permute-start | bytes 786440 | tf_op jit(solution)/shard_map/ppermute | solution.py:470
  30.4 5.5 %collective-permute-start.15 = (bf16[256,512]{1,0:T(8,128)(2,1)S(1)}, bf16[256,512]{1,0:T(8,128)(2,1)S(1)}, u32[]{:S(2)}, u32[]{:S(2)}) collective-permute-start(bf16[256,512]{1,0:T(8,128)(2,1)S(1)} %get-tuple-element.39.odd_ref), channel_id=1, source_target_pairs={{0,16},{8,24},{16,0},{24,8},{32,48},{40,56},{48,32},{56,40},{64,80... | collective-permute-start | bytes 786440 | tf_op jit(solution)/shard_map/ppermute | solution.py:470
  32.3 6.4 %collective-permute-start.8 = (bf16[32,4096]{1,0:T(8,128)(2,1)S(1)}, bf16[32,4096]{1,0:T(8,128)(2,1)S(1)}, u32[]{:S(2)}, u32[]{:S(2)}) collective-permute-start(bf16[32,4096]{1,0:T(8,128)(2,1)S(1)} %collective-permute-done.6.after_up.up1), channel_id=1, source_target_pairs={{0,1},{1,2},{2,3},{3,4},{4,5},{5,6},{6,7},{7,0},{8,9},{9,10},{10,1... | collective-permute-start | bytes 786440 | tf_op jit(solution)/shard_map/ppermute | solution.py:474
  32.3 6.4 %collective-permute-start.9 = (bf16[32,4096]{1,0:T(8,128)(2,1)S(1)}, bf16[32,4096]{1,0:T(8,128)(2,1)S(1)}, u32[]{:S(2)}, u32[]{:S(2)}) collective-permute-start(bf16[32,4096]{1,0:T(8,128)(2,1)S(1)} %collective-permute-done.7.after_down.down1), channel_id=1, source_target_pairs={{0,7},{1,0},{2,1},{3,2},{4,3},{5,4},{6,5},{7,6},{8,15},{9,8},{10,9... | collective-permute-start | bytes 786440 | tf_op jit(solution)/shard_map/ppermute | solution.py:474
  36.1 12.9 %collective-permute-start.16 = (bf16[512,512]{1,0:T(8,128)(2,1)S(1)}, bf16[512,512]{1,0:T(8,128)(2,1)S(1)}, u32[]{:S(2)}, u32[]{:S(2)}) collective-permute-start(bf16[512,512]{1,0:T(8,128)(2,1)S(1)} %get-tuple-element.41), channel_id=1, source_target_pairs={{0,16},{8,24},{16,0},{24,8},{32,48},{40,56},{48,32},{56,40},{64,80... | collective-permute-start | bytes 1572872 | tf_op jit(solution)/shard_map/ppermute | solution.py:470
  36.7 12.3 %collective-permute-start.17 = (bf16[512,512]{1,0:T(8,128)(2,1)S(1)}, bf16[512,512]{1,0:T(8,128)(2,1)S(1)}, u32[]{:S(2)}, u32[]{:S(2)}) collective-permute-start(bf16[512,512]{1,0:T(8,128)(2,1)S(1)} %get-tuple-element.42), channel_id=1, source_target_pairs={{0,128},{8,136},{16,144},{24,152},{32,160},{40,168},{48,176},{56,1... | collective-permute-start | bytes 1572872 | tf_op jit(solution)/shard_map/ppermute | solution.py:470
  38.8 7.4 %collective-permute-start.10 = (bf16[32,4096]{1,0:T(8,128)(2,1)S(1)}, bf16[32,4096]{1,0:T(8,128)(2,1)S(1)}, u32[]{:S(2)}, u32[]{:S(2)}) collective-permute-start(bf16[32,4096]{1,0:T(8,128)(2,1)S(1)} %collective-permute-done.8.up2), channel_id=1, source_target_pairs={{0,1},{1,2},{2,3},{3,4},{4,5},{5,6},{6,7},{7,0},{8,9},{9,10},{10,1... | collective-permute-start | bytes 786440 | tf_op jit(solution)/shard_map/ppermute | solution.py:474
  38.8 7.5 %collective-permute-start.11 = (bf16[32,4096]{1,0:T(8,128)(2,1)S(1)}, bf16[32,4096]{1,0:T(8,128)(2,1)S(1)}, u32[]{:S(2)}, u32[]{:S(2)}) collective-permute-start(bf16[32,4096]{1,0:T(8,128)(2,1)S(1)} %collective-permute-done.9.down2), channel_id=1, source_target_pairs={{0,7},{1,0},{2,1},{3,2},{4,3},{5,4},{6,5},{7,6},{8,15},{9,8},{10,9... | collective-permute-start | bytes 786440 | tf_op jit(solution)/shard_map/ppermute | solution.py:474
  41.4 12.6 %collective-permute-start.18 = (bf16[1024,512]{1,0:T(8,128)(2,1)S(1)}, bf16[1024,512]{1,0:T(8,128)(2,1)S(1)}, u32[]{:S(2)}, u32[]{:S(2)}) collective-permute-start(bf16[1024,512]{1,0:T(8,128)(2,1)S(1)} %get-tuple-element.40.near_own), channel_id=1, source_target_pairs={{0,8},{8,0},{16,24},{24,16},{32,40},{40,32},{48,56},{56,48},{64,72... | collective-permute-start | bytes 3145736 | tf_op jit(solution)/shard_map/ppermute | solution.py:464
  46.2 9.5 %collective-permute-start.19 = (bf16[16,4096]{1,0:T(8,128)(2,1)S(1)}, bf16[16,4096]{1,0:T(8,128)(2,1)S(1)}, u32[]{:S(2)}, u32[]{:S(2)}) collective-permute-start(bf16[16,4096]{1,0:T(8,128)(2,1)S(1)} %slice.8), channel_id=1, source_target_pairs={{0,1},{1,2},{2,3},{3,4},{4,5},{5,6},{6,7},{7,0},{8,9},{9,10},{10,1... | collective-permute-start | bytes 393224 | tf_op jit(solution)/shard_map/ppermute | solution.py:474
  46.3 9.4 %collective-permute-start.20 = (bf16[16,4096]{1,0:T(8,128)(2,1)S(1)}, bf16[16,4096]{1,0:T(8,128)(2,1)S(1)}, u32[]{:S(2)}, u32[]{:S(2)}) collective-permute-start(bf16[16,4096]{1,0:T(8,128)(2,1)S(1)} %slice.9), channel_id=1, source_target_pairs={{0,7},{1,0},{2,1},{3,2},{4,3},{5,4},{6,5},{7,6},{8,15},{9,8},{10,9... | collective-permute-start | bytes 393224 | tf_op jit(solution)/shard_map/ppermute | solution.py:474
  49.1 7.2 %collective-permute-start.21 = (bf16[1024,512]{1,0:T(8,128)(2,1)S(1)}, bf16[1024,512]{1,0:T(8,128)(2,1)S(1)}, u32[]{:S(2)}, u32[]{:S(2)}) collective-permute-start(bf16[1024,512]{1,0:T(8,128)(2,1)S(1)} %shard_map.101.far_own.own_ref), channel_id=1, source_target_pairs={{0,8},{8,0},{16,24},{24,16},{32,40},{40,32},{48,56},{56,48},{64,72... | collective-permute-start | bytes 3145736 | tf_op jit(solution)/shard_map/ppermute | solution.py:464
  (6 other events, 20.1 us)
